TPU v7x, 512 devices: a whole 4x4x16 slice. The times are simulated.
512 devices in a mesh: pipe: 64 (over y, z_hi, x), expert: 8 (over z_lo, core).
Axes of the slice: x: 4, y: 4, z: 16 (z_hi: 4, z_lo: 4; z = z_hi * 4 + z_lo), core: 2. Of those that a mesh axis runs over, the one named last changes fastest.
Arguments:
- stash_a: bfloat16 [64, 2, 64, 3584], P('pipe', None, 'expert'), may hold values from -6 to 6
- stash_b: bfloat16 [64, 2, 64, 3584], P('pipe', None, 'expert'), may hold values from -6 to 6
- ids_a: int32 [64, 2, 64, 8], P('pipe', None, 'expert'), may hold values from 0 to 255, all different within a row
- ids_b: int32 [64, 2, 64, 8], P('pipe', None, 'expert'), may hold values from 0 to 255, all different within a row
- arriving_a: bfloat16 [64, 64, 3584], P('pipe', 'expert'), may hold values from -6 to 6
- arriving_b: bfloat16 [64, 64, 3584], P('pipe', 'expert'), may hold values from -6 to 6
- head_a: bfloat16 [1, 64, 3584], P(None, 'expert'), may hold values from -6 to 6
- head_b: bfloat16 [1, 64, 3584], P(None, 'expert'), may hold values from -6 to 6
- w_gate: bfloat16 [64, 3584, 1024], P('pipe', None, 'expert'), may hold values from -0.09375 to 0.09375
- w_up: bfloat16 [64, 3584, 1024], P('pipe', None, 'expert'), may hold values from -0.09375 to 0.09375
- w_down: bfloat16 [64, 1024, 3584], P('pipe', 'expert'), may hold values from -0.09375 to 0.09375
- router: bfloat16 [64, 256, 3584], P('pipe', 'expert'), may hold values from -2 to 2
Outputs:
- leaving_a: bfloat16 [64, 64, 3584], P('pipe', 'expert')
- leaving_b: bfloat16 [64, 64, 3584], P('pipe', 'expert')
- router_grad: float32 [64, 256, 3584], P('pipe', 'expert')
Inputs may be any that keep to these rules, and one draw needn't show every extreme that they name: `ids_a`: each row names 8 different experts. `ids_b`: each row names 8 different experts.
All inputs are finite; a program needn't handle non-finite values.
Results may differ from a plain program's by a relative error of at most 0.019.
Values may be sent and summed in bfloat16 or wider, within the bound.
No kernel may reach another device: no remote copies, remote signals or barrier semaphores. Data moves between devices by JAX's collectives and lax.ppermute only.
A program may use at most 64 MiB of HBM per device.

v0:
```python
import jax
import jax.numpy as jnp
from jax import lax
from jax.sharding import PartitionSpec as P

EXPERTS = 256
TOPK = 8


z_weight = 0.01
balance_weight = 1.0


def passed_along(block, axis, distance):
    devices = range(lax.axis_size(axis))
    route = [(i - distance, i) for i in devices if i - distance in devices]
    return lax.ppermute(block, axis, route)


def mirror_half(members):
    pipe_count = lax.axis_size("pipe")
    packed = jnp.concatenate([member.reshape(pipe_count, -1) for member in members], axis=1)
    spread_out = lax.all_to_all(packed, "pipe", split_axis=0, concat_axis=0, tiled=True)
    returned = lax.all_to_all(spread_out[::-1], "pipe", split_axis=0, concat_axis=0, tiled=True)
    results = []
    offset_col = 0
    for member in members:
        span_cols = member.size // pipe_count
        results.append(returned[:, offset_col : offset_col + span_cols].reshape(member.shape))
        offset_col = offset_col + span_cols
    return tuple(results)


def mirror_full(values):
    pipe_count = lax.axis_size("pipe")
    packed = values.reshape(pipe_count, -1)
    spread_out = lax.all_to_all(
        packed.astype(jnp.bfloat16), "pipe", split_axis=0, concat_axis=0, tiled=True
    ).astype(packed.dtype)
    returned = lax.all_to_all(
        spread_out[::-1].astype(jnp.bfloat16), "pipe", split_axis=0, concat_axis=0, tiled=True
    ).astype(jnp.float32)
    return returned.reshape(values.shape)


def local_counts(chosen):
    flat_ids = chosen.reshape(chosen.shape[0], -1)
    matches = (flat_ids[:, :, None] == jnp.arange(EXPERTS, dtype=jnp.int32)[None, None, :]).astype(
        jnp.float32
    )
    return jnp.sum(matches, axis=1)


def router_slopes(logits, share_own):
    peak_val = lax.pmax(jnp.max(logits, axis=-1), "expert")
    expo_terms = jnp.exp(logits - peak_val[..., None])
    denom_sum, weighted = lax.psum(
        (jnp.sum(expo_terms, axis=-1), jnp.sum(expo_terms * share_own[:, None, :], axis=-1)),
        "expert",
    )
    probs = expo_terms / denom_sum[..., None]
    log_total = peak_val + jnp.log(denom_sum)
    mean_share = weighted / denom_sum
    slopes = (
        (2.0 * z_weight * log_total - balance_weight * mean_share)[..., None]
        + balance_weight * share_own[:, None, :]
    ) * probs
    return slopes.astype(jnp.bfloat16)


def expert_rows(grads, gate_pre, up_pre, gate_weight, up_weight, down_weight):
    hidden_grad = lax.dot_general(
        lax.all_gather(grads, "expert", axis=0, tiled=True),
        down_weight,
        (((1,), (1,)), ((), ())),
        preferred_element_type=jnp.float32,
    )
    gate_sig = jax.nn.sigmoid(gate_pre)
    d_gate = (hidden_grad * up_pre * gate_sig * (1.0 + gate_pre * (1.0 - gate_sig))).astype(
        jnp.bfloat16
    )
    d_up = (hidden_grad * gate_pre * gate_sig).astype(jnp.bfloat16)
    result = lax.dot_general(
        d_gate, gate_weight, (((1,), (1,)), ((), ())), preferred_element_type=jnp.float32
    )
    terms = result + lax.dot_general(
        d_up, up_weight, (((1,), (1,)), ((), ())), preferred_element_type=jnp.float32
    )
    summed = lax.psum_scatter(
        terms.astype(jnp.bfloat16), "expert", scatter_dimension=0, tiled=True
    ).astype(jnp.float32)
    return (grads.astype(jnp.float32) + summed).astype(jnp.bfloat16)


def shards(
    stash_a,
    stash_b,
    ids_a,
    ids_b,
    arriving_a,
    arriving_b,
    head_a,
    head_b,
    w_gate,
    w_up,
    w_down,
    router,
):
    stash_a = stash_a[0]
    stash_b = stash_b[0]
    ids_a = ids_a[0]
    ids_b = ids_b[0]
    arriving_a = arriving_a[0]
    arriving_b = arriving_b[0]
    w_gate = w_gate[0]
    w_up = w_up[0]
    w_down = w_down[0]
    router = router[0]
    ticks_count = stash_a.shape[0]
    token_count = stash_a.shape[1] * lax.axis_size("expert")
    scale_share = EXPERTS / (token_count * TOPK)
    count_a, count_b = lax.psum((local_counts(ids_a), local_counts(ids_b)), "expert")
    share_a = count_a * scale_share
    share_b = count_b * scale_share
    gate_b_w, up_b_w, down_b_w, router_b = mirror_half((w_gate, w_up, w_down, router))
    inputs_a, inputs_b = (
        lax.all_gather(stash_a, "expert", axis=1, tiled=True),
        lax.all_gather(stash_b, "expert", axis=1, tiled=True),
    )
    own_count = router.shape[0]
    first_expert = lax.axis_index("expert") * own_count
    own_a = lax.dynamic_slice_in_dim(share_a, first_expert, own_count, 1)
    own_b = lax.dynamic_slice_in_dim(share_b, first_expert, own_count, 1)
    logits_a = jnp.einsum("tmd,ed->tme", inputs_a, router, preferred_element_type=jnp.float32)
    logits_b = jnp.einsum("tmd,ed->tme", inputs_b, router_b, preferred_element_type=jnp.float32)
    slopes = router_slopes(
        jnp.concatenate([logits_a, logits_b], axis=0), jnp.concatenate([own_a, own_b], axis=0)
    )
    grad_a = jnp.einsum(
        "tme,tmd->ed", slopes[:ticks_count], inputs_a, preferred_element_type=jnp.float32
    )
    grad_b = jnp.einsum(
        "tme,tmd->ed", slopes[ticks_count:], inputs_b, preferred_element_type=jnp.float32
    )
    gate_a = jnp.einsum("tmd,dh->tmh", inputs_a, w_gate, preferred_element_type=jnp.float32)
    up_a = jnp.einsum("tmd,dh->tmh", inputs_a, w_up, preferred_element_type=jnp.float32)
    gate_b = jnp.einsum("tmd,dh->tmh", inputs_b, gate_b_w, preferred_element_type=jnp.float32)
    up_b = jnp.einsum("tmd,dh->tmh", inputs_b, up_b_w, preferred_element_type=jnp.float32)
    section_index = lax.axis_index("pipe")
    top_section = lax.axis_size("pipe") - 1
    grads_a = arriving_a
    grads_b = arriving_b
    out_a = arriving_a
    out_b = arriving_b
    for moment in range(ticks_count):
        out_a = expert_rows(grads_a, gate_a[moment], up_a[moment], w_gate, w_up, w_down)
        out_b = expert_rows(grads_b, gate_b[moment], up_b[moment], gate_b_w, up_b_w, down_b_w)
        if moment + 1 < ticks_count:
            moved_a = passed_along(out_a, "pipe", -1)
            moved_b = passed_along(out_b, "pipe", 1)
            grads_a = jnp.where(section_index == top_section, head_a[moment], moved_a)
            grads_b = jnp.where(section_index == 0, head_b[moment], moved_b)
    router_grad = grad_a + mirror_full(grad_b)
    return (out_a[None], out_b[None], router_grad[None])


def solution(mesh):
    placed = (
        P("pipe", None, "expert", None),
        P("pipe", None, "expert", None),
        P("pipe", None, "expert", None),
        P("pipe", None, "expert", None),
        P("pipe", "expert", None),
        P("pipe", "expert", None),
        P(None, "expert", None),
        P(None, "expert", None),
        P("pipe", None, "expert"),
        P("pipe", None, "expert"),
        P("pipe", "expert", None),
        P("pipe", "expert", None),
    )
    return jax.shard_map(
        shards,
        mesh=mesh,
        in_specs=placed,
        out_specs=(P("pipe", "expert", None), P("pipe", "expert", None), P("pipe", "expert", None)),
        check_vma=False,
    )
```

profile of v0, /device:TPU:6, one launch (start us, length us, event | category | flops | bytes accessed | tf_op | source)
XLA Modules:
  0.0 741.3 jit_solution(17055047867594935294)
XLA Ops:
  7.2 1.6 reshape_squeeze.12
  8.8 1.5 reshape_squeeze.13
  11.7 2.7 maximum_bitcast_fusion
  14.9 5.4 reduce.2
  20.3 4.4 reshape.74
  24.7 157.0 %all_to_all.39 = bf16[64,2,11648]{2,1,0:T(2,128)(2,1)} all-to-all(bf16[64,2,11648]{2,1,0:T(2,128)(2,1)} %reshape.74), channel_id=1, replica_groups=mesh['pipe'=64,'expert'=8] {'pipe'}, dimensions={0} | all-to-all | bytes 5963776 | tf_op jit(solution)/shard_map/all_to_all | solution.py:23
  181.8 16.9 %reshape.75 = bf16[64,1,23296]{2,1,0:T(2,128)(2,1)} reshape(bf16[64,2,11648]{2,1,0:T(2,128)(2,1)} %all_to_all.39) | data formatting | bytes 5963776
  198.7 4.7 copy.33
  203.3 81.4 %rev.6 = bf16[64,23296]{1,0:T(8,128)(2,1)} reverse(bf16[64,23296]{1,0:T(8,128)(2,1)} %bitcast.191), dimensions={0} | reverse | bytes 5963776 | tf_op jit(solution)/shard_map/rev | solution.py:24
  284.8 5.4 reduce.3
  290.2 4.4 reshape.76
  294.6 11.5 %all-to-all-start.1 = ((bf16[64,2,11648]{2,1,0:T(2,128)(2,1)}), bf16[64,2,11648]{2,1,0:T(2,128)(2,1)}, u32[]{:S(2)}, u32[]{:S(2)}) async-start(bf16[64,2,11648]{2,1,0:T(2,128)(2,1)} %reshape.76), calls=%async_computation.3 | async-start | bytes 5963776 | tf_op jit(solution)/shard_map/all_to_all | solution.py:24
  306.2 138.9 %all-gather = bf16[1,64,3584]{2,1,0:T(8,128)(2,1)S(1)} all-gather(bf16[1,8,3584]{2,1,0:T(8,128)(2,1)S(1)} %copy-done.18), channel_id=2, replica_groups=mesh['pipe'=64,'expert'=8] {'expert'}, dimensions={1}, use_global_device_ids=true | all-gather | bytes 516096 | tf_op jit(solution)/shard_map/all_gather | solution.py:73
  445.5 16.5 %all-gather.1 = bf16[1,2,64,3584]{3,2,1,0:T(8,128)(2,1)S(1)} all-gather(bf16[1,2,8,3584]{3,2,1,0:T(8,128)(2,1)S(1)} %copy-done.19), channel_id=3, replica_groups=mesh['pipe'=64,'expert'=8] {'expert'}, dimensions={2}, use_global_device_ids=true | all-gather | bytes 1032192 | tf_op jit(solution)/shard_map/all_gather | solution.py:127
  465.0 14.7 %all-reduce.1 = (f32[2,256]{1,0:T(2,128)S(1)}, f32[2,256]{1,0:T(2,128)S(1)}) all-reduce(f32[2,256]{1,0:T(2,128)S(1)} %convert_reduce_fusion.1, f32[2,256]{1,0:T(2,128)S(1)} %convert_reduce_fusion.2), channel_id=1, replica_groups=mesh['pipe'=64,'expert'=8] {'expert'}, use_global_device_ids=true, to_apply=%region_11.0 | all-reduce | flops 1024 | bytes 8192 | tf_op jit(solution)/shard_map/psum | solution.py:122
  479.8 15.3 %all-gather.2 = bf16[1,64,3584]{2,1,0:T(8,128)(2,1)S(1)} all-gather(bf16[1,8,3584]{2,1,0:T(8,128)(2,1)} %param.17), channel_id=4, replica_groups=mesh['pipe'=64,'expert'=8] {'expert'}, dimensions={1}, use_global_device_ids=true | all-gather | bytes 516096 | tf_op jit(solution)/shard_map/all_gather | solution.py:73
  495.5 17.4 %all-gather.3 = bf16[1,2,64,3584]{3,2,1,0:T(8,128)(2,1)S(1)} all-gather(bf16[1,2,8,3584]{3,2,1,0:T(8,128)(2,1)} %param.13), channel_id=5, replica_groups=mesh['pipe'=64,'expert'=8] {'expert'}, dimensions={2}, use_global_device_ids=true | all-gather | bytes 1032192 | tf_op jit(solution)/shard_map/all_gather | solution.py:128
  513.7 2.4 collective-permute-start
  516.1 10.9 %collective-permute-done = bf16[8,3584]{1,0:T(8,128)(2,1)S(1)} collective-permute-done((bf16[8,3584]{1,0:T(8,128)(2,1)S(1)}, bf16[8,3584]{1,0:T(8,128)(2,1)S(1)}, u32[]{:S(2)}, u32[]{:S(2)}) %collective-permute-start) | collective-permute-done | bytes 57376 | tf_op jit(solution)/shard_map/ppermute | solution.py:17
  527.9 14.7 %all_gather.20 = bf16[64,3584]{1,0:T(8,128)(2,1)S(1)} all-gather(bf16[8,3584]{1,0:T(8,128)(2,1)S(1)} %bitcast_select_fusion.1), channel_id=1, replica_groups=mesh['pipe'=64,'expert'=8] {'expert'}, dimensions={0}, use_global_device_ids=true | all-gather | bytes 516096 | tf_op jit(solution)/shard_map/all_gather | solution.py:73
  542.6 1.6 fusion.26
  544.2 16.9 %reshape.77 = bf16[64,1,23296]{2,1,0:T(2,128)(2,1)} reshape(bf16[64,2,11648]{2,1,0:T(2,128)(2,1)} %all-to-all-done.1) | data formatting | bytes 5963776
  561.1 3.0 copy.32
  564.1 1.6 copy-done.2
  565.7 1.6 fusion.77
  567.3 2.3 reshape.65
  569.6 2.3 reshape.52
  571.9 2.3 reshape.64
  574.2 2.3 reshape.51
  576.5 1.6 convolution_bitcast_fusion.2
  578.0 2.2 convolution_bitcast_fusion.3
  580.2 2.2 reshape.50
  582.5 1.7 convolution_bitcast_fusion.4
  584.2 1.6 fusion.57
  587.1 2.6 fusion.15
  591.3 14.0 %pmax.7 = f32[4,64]{1,0:T(4,128)S(1)} all-reduce(f32[4,64]{1,0:T(4,128)S(1)} %fusion.37), channel_id=1, replica_groups=mesh['pipe'=64,'expert'=8] {'expert'}, use_global_device_ids=true, to_apply=%region_5.0 | all-reduce | flops 256 | bytes 2048 | tf_op jit(solution)/shard_map/pmax | solution.py:55
  605.4 13.6 %all-reduce = (f32[4,64]{1,0:T(4,128)S(1)}, f32[4,64]{1,0:T(4,128)S(1)}) all-reduce(f32[4,64]{1,0:T(4,128)S(1)} %get-tuple-element.4, f32[4,64]{1,0:T(4,128)S(1)} %get-tuple-element.3), channel_id=1, replica_groups=mesh['pipe'=64,'expert'=8] {'expert'}, use_global_device_ids=true, to_apply=%region_7.0 | all-reduce | flops 512 | bytes 4096 | tf_op jit(solution)/shard_map/psum | solution.py:57
  619.5 1.9 reduce.4
  622.2 16.4 %all-to-all-start.2 = ((bf16[64,2,896]{2,1,0:T(2,128)(2,1)}), bf16[64,2,896]{2,1,0:T(2,128)(2,1)S(1)}, u32[]{:S(2)}, u32[]{:S(2)}) async-start(bf16[64,2,896]{2,1,0:T(2,128)(2,1)} %reshape.78), calls=%async_computation.6 | async-start | bytes 458752 | tf_op jit(solution)/shard_map/all_to_all | solution.py:37
  639.5 7.4 collective-permute-start.1
  647.0 2.0 fusion.1
  648.9 7.9 %all-to-all-done.2 = bf16[64,2,896]{2,1,0:T(2,128)(2,1)S(1)} async-done(((bf16[64,2,896]{2,1,0:T(2,128)(2,1)}), bf16[64,2,896]{2,1,0:T(2,128)(2,1)S(1)}, u32[]{:S(2)}, u32[]{:S(2)}) %all-to-all-start.2) | async-done | bytes 229408 | tf_op jit(solution)/shard_map/all_to_all | solution.py:37
  658.9 12.3 %all-to-all-start.3 = ((bf16[64,2,896]{2,1,0:T(2,128)(2,1)}), bf16[64,2,896]{2,1,0:T(2,128)(2,1)S(1)}, u32[]{:S(2)}, u32[]{:S(2)}) async-start(bf16[64,2,896]{2,1,0:T(2,128)(2,1)} %reshape.80), calls=%async_computation.7 | async-start | bytes 458752 | tf_op jit(solution)/shard_map/all_to_all | solution.py:40
  672.1 15.7 %all_gather.23 = bf16[64,3584]{1,0:T(8,128)(2,1)S(1)} all-gather(bf16[8,3584]{1,0:T(8,128)(2,1)S(1)} %bitcast_select_fusion), channel_id=1, replica_groups=mesh['pipe'=64,'expert'=8] {'expert'}, dimensions={0}, use_global_device_ids=true | all-gather | bytes 516096 | tf_op jit(solution)/shard_map/all_gather | solution.py:73
  687.8 1.6 fusion.78
  691.9 1.5 fusion.35
  696.1 37.2 %reduce-scatter.11.cloned.1.call-done = bf16[8,3584]{1,0:T(8,128)(2,1)} async-done(((bf16[64,3584]{1,0:T(8,128)(2,1)}), bf16[8,3584]{1,0:T(8,128)(2,1)}) %reduce-scatter.11.cloned.1.call-update) | async-done | bytes 57360 | tf_op jit(solution)/shard_map/reduce_scatter | solution.py:89
  733.3 1.5 fusion.36
  (99 shorter events, 20.6 us)
Async XLA Ops:
  7.2 3.1 copy-start.3
  7.2 4.4 copy-start.8
  294.6 11.5 %copy-start.18 = (bf16[1,8,3584]{2,1,0:T(8,128)(2,1)S(1)}, bf16[1,8,3584]{2,1,0:T(8,128)(2,1)}, u32[]{:S(2)}) copy-start(bf16[1,8,3584]{2,1,0:T(8,128)(2,1)} %param.16) | copy-start | bytes 172036
  294.6 150.9 %copy-start.19 = (bf16[1,2,8,3584]{3,2,1,0:T(8,128)(2,1)S(1)}, bf16[1,2,8,3584]{3,2,1,0:T(8,128)(2,1)}, u32[]{:S(2)}) copy-start(bf16[1,2,8,3584]{3,2,1,0:T(8,128)(2,1)} %param.12) | copy-start | bytes 344068
  294.6 167.4 %copy-start.1 = (bf16[1,3584,128]{2,1,0:T(8,128)(2,1)S(1)}, bf16[1,3584,128]{2,1,0:T(8,128)(2,1)}, u32[]{:S(2)}) copy-start(bf16[1,3584,128]{2,1,0:T(8,128)(2,1)} %param.20) | copy-start | bytes 2752516
  294.6 249.6 %all-to-all-start.1 = ((bf16[64,2,11648]{2,1,0:T(2,128)(2,1)}), bf16[64,2,11648]{2,1,0:T(2,128)(2,1)}, u32[]{:S(2)}, u32[]{:S(2)}) async-start(bf16[64,2,11648]{2,1,0:T(2,128)(2,1)} %reshape.76), calls=%async_computation.3 | async-start | bytes 5963776 | tf_op jit(solution)/shard_map/all_to_all | solution.py:24
  306.1 156.3 %copy-start = (bf16[1,3584,128]{2,1,0:T(8,128)(2,1)S(1)}, bf16[1,3584,128]{2,1,0:T(8,128)(2,1)}, u32[]{:S(2)}) copy-start(bf16[1,3584,128]{2,1,0:T(8,128)(2,1)} %param.21) | copy-start | bytes 2752516
  306.1 206.8 %reduce-scatter.5.cloned.1.call-start = ((), (), s32[]{:S(2)}) async-start(), calls=%async_computation.8 | async-start | bytes 516096 | tf_op jit(solution)/shard_map/reduce_scatter | solution.py:89
  462.4 124.6 %copy-start.9 = (f32[2,64,128]{2,1,0:T(8,128)}, f32[2,64,128]{2,1,0:T(8,128)S(1)}, u32[]{:S(2)}) copy-start(f32[2,64,128]{2,1,0:T(8,128)S(1)} %fusion.11) | copy-start | bytes 196612
  462.5 2.2 copy-start.21
  462.5 2.2 copy-start.22
  462.9 16.8 %copy-start.16 = (f32[2,64,128]{2,1,0:T(8,128)}, f32[2,64,128]{2,1,0:T(8,128)S(1)}, u32[]{:S(2)}) copy-start(f32[2,64,128]{2,1,0:T(8,128)S(1)} %fusion.17) | copy-start | bytes 196612
  464.6 174.1 %reduce-scatter.9.cloned.1.call-start = ((), (), s32[]{:S(2)}) async-start(), calls=%async_computation.10 | async-start | bytes 516096 | tf_op jit(solution)/shard_map/reduce_scatter | solution.py:89
  513.7 13.3 %collective-permute-start = (bf16[8,3584]{1,0:T(8,128)(2,1)S(1)}, bf16[8,3584]{1,0:T(8,128)(2,1)S(1)}, u32[]{:S(2)}, u32[]{:S(2)}) collective-permute-start(bf16[8,3584]{1,0:T(8,128)(2,1)S(1)} %fusion.34), channel_id=1, source_target_pairs={{8,0},{16,8},{24,16},{32,24},{40,32},{48,40},{56,48},{64,56},{72,6... | collective-permute-start | bytes 172040 | tf_op jit(solution)/shard_map/ppermute | solution.py:17
  527.9 33.2 %copy-start.12 = (bf16[8,3584]{1,0:T(8,128)(2,1)}, bf16[8,3584]{1,0:T(8,128)(2,1)S(1)}, u32[]{:S(2)}) copy-start(bf16[8,3584]{1,0:T(8,128)(2,1)S(1)} %bitcast_select_fusion.1) | copy-start | bytes 172036
  544.2 42.9 %copy-start.14 = (f32[64,128]{1,0:T(8,128)}, f32[64,128]{1,0:T(8,128)S(1)}, u32[]{:S(2)}) copy-start(f32[64,128]{1,0:T(8,128)S(1)} %fusion.26) | copy-start | bytes 98308
  564.1 1.6 copy-start.2
  578.0 7.8 %copy-start.10 = (f32[2,64,128]{2,1,0:T(8,128)}, f32[2,64,128]{2,1,0:T(8,128)S(1)}, u32[]{:S(2)}) copy-start(f32[2,64,128]{2,1,0:T(8,128)S(1)} %convolution_bitcast_fusion.2) | copy-start | bytes 196612
  582.5 3.3 copy-start.5
  582.5 4.6 copy-start.17
  589.7 57.3 %copy-start.15 = (f32[64,128]{1,0:T(8,128)S(1)}, f32[64,128]{1,0:T(8,128)}, u32[]{:S(2)}) copy-start(f32[64,128]{1,0:T(8,128)} %copy-done.14) | copy-start | bytes 98308
  619.4 27.6 %copy-start.7 = (f32[64,3584]{1,0:T(8,128)S(1)}, f32[64,3584]{1,0:T(8,128)}, u32[]{:S(2)}) copy-start(f32[64,3584]{1,0:T(8,128)} %fusion.15) | copy-start | bytes 2752516
  622.2 34.7 %all-to-all-start.2 = ((bf16[64,2,896]{2,1,0:T(2,128)(2,1)}), bf16[64,2,896]{2,1,0:T(2,128)(2,1)S(1)}, u32[]{:S(2)}, u32[]{:S(2)}) async-start(bf16[64,2,896]{2,1,0:T(2,128)(2,1)} %reshape.78), calls=%async_computation.6 | async-start | bytes 458752 | tf_op jit(solution)/shard_map/all_to_all | solution.py:37
  638.6 53.3 %reduce-scatter.7.cloned.1.call-start = ((), (), s32[]{:S(2)}) async-start(), calls=%async_computation.9 | async-start | bytes 516096 | tf_op jit(solution)/shard_map/reduce_scatter | solution.py:89
  639.5 31.7 %copy-start.20 = (bf16[1,8,3584]{2,1,0:T(8,128)(2,1)S(1)}, bf16[1,8,3584]{2,1,0:T(8,128)(2,1)}, u32[]{:S(2)}) copy-start(bf16[1,8,3584]{2,1,0:T(8,128)(2,1)} %param.19) | copy-start | bytes 172036
  639.5 31.7 %collective-permute-start.1 = (bf16[8,3584]{1,0:T(8,128)(2,1)S(1)}, bf16[8,3584]{1,0:T(8,128)(2,1)}, u32[]{:S(2)}, u32[]{:S(2)}) collective-permute-start(bf16[8,3584]{1,0:T(8,128)(2,1)S(1)} %fusion.33), channel_id=1, source_target_pairs={{0,8},{8,16},{16,24},{24,32},{32,40},{40,48},{48,56},{56,64},{64,7... | collective-permute-start | bytes 172040 | tf_op jit(solution)/shard_map/ppermute | solution.py:17
  648.9 40.5 %copy-start.4 = (bf16[3584,128]{1,0:T(8,128)(2,1)S(1)}, bf16[3584,128]{1,0:T(8,128)(2,1)}, u32[]{:S(2)}) copy-start(bf16[3584,128]{1,0:T(8,128)(2,1)} %reshape.52) | copy-start | bytes 2752516
  648.9 40.5 %copy-start.11 = (f32[2,64,128]{2,1,0:T(8,128)S(1)}, f32[2,64,128]{2,1,0:T(8,128)}, u32[]{:S(2)}) copy-start(f32[2,64,128]{2,1,0:T(8,128)} %copy-done.10) | copy-start | bytes 196612
  657.1 33.6 %copy-start.6 = (bf16[3584,128]{1,0:T(8,128)(2,1)S(1)}, bf16[3584,128]{1,0:T(8,128)(2,1)}, u32[]{:S(2)}) copy-start(bf16[3584,128]{1,0:T(8,128)(2,1)} %reshape.51) | copy-start | bytes 2752516
  658.9 34.5 %all-to-all-start.3 = ((bf16[64,2,896]{2,1,0:T(2,128)(2,1)}), bf16[64,2,896]{2,1,0:T(2,128)(2,1)S(1)}, u32[]{:S(2)}, u32[]{:S(2)}) async-start(bf16[64,2,896]{2,1,0:T(2,128)(2,1)} %reshape.80), calls=%async_computation.7 | async-start | bytes 458752 | tf_op jit(solution)/shard_map/all_to_all | solution.py:40
  671.1 62.2 %reduce-scatter.11.cloned.1.call-start = ((), (), s32[]{:S(2)}) async-start(), calls=%async_computation.11 | async-start | bytes 516096 | tf_op jit(solution)/shard_map/reduce_scatter | solution.py:89
  687.8 4.1 copy-start.13
Sparse Core Ops, SparseCore 0:
  464.7 39.8 reduce-scatter.4
  587.2 40.7 reduce-scatter.8
  649.1 41.8 reduce-scatter.6
  693.8 39.4 reduce-scatter.10
where the time goes:
time: 752 us; the launch traced here: 741 us
  blocking collectives  418 us (56%)
  local copies, waits for them, and re-layouts  155 us (21%)
  waiting for transfers between devices  56.2 us (7%)
  starting transfers between devices  50 us (7%)
  other arithmetic  24.2 us (3%)
  matrix products  23.8 us (3%)
  between operations  14.3 us (2%)
    all_gather x4, blocking collectives, expert_rows(): lax.all_gather(grads, 'expert', axis=0, tiled=True)  185 us
    all_to_all x1, blocking collectives, mirror_half(): lax.all_to_all(packed, 'pipe', split_axis=0, concat_axis=0, tiled=True)  157 us
    rev x1, local copies, waits for them, and re-layouts, mirror_half(): spread_out[::-1]  81.4 us
    unnamed x57, local copies, waits for them, and re-layouts  53.9 us
    reduce_scatter x4, waiting for transfers between devices, expert_rows(): lax.psum_scatter(terms.astype(jnp.bfloat16), 'expert', scatter_dimension=...  37.3 us
    all_gather x1, blocking collectives, shards(): lax.all_gather(stash_b, 'expert', axis=1, tiled=True)  17.4 us
    all_gather x1, blocking collectives, shards(): lax.all_gather(stash_a, 'expert', axis=1, tiled=True)  16.5 us
    all_to_all x1, starting transfers between devices, mirror_full(): lax.all_to_all(packed.astype(jnp.bfloat16), 'pipe', split_axis=0, concat_...  16.4 us
  transfers between devices with their start and end apart: 9, of which 3 were waited for; matrix products, arithmetic and copies ran while one was open for 4% of the time, Pallas kernels for 0%

commit v1 on v0

v1 whole, which is shorter than its diff:
```python
import functools

import jax
import jax.numpy as jnp
from jax import lax
from jax.experimental import pallas as pl
from jax.experimental.pallas import tpu as pltpu
from jax.sharding import PartitionSpec as P

D = 3584
HID = 128
EXPERTS = 256
OWN = 32
TOKENS = 64
TOPK = 8
ROWS = 8
CHIPS = 4
IDCOLS = 128
z_weight = 0.01
balance_weight = 1.0
F32 = jnp.float32
BF16 = jnp.bfloat16
VMEM_LIMIT = 48 * 1024 * 1024


def dot(lhs, rhs, lhs_dim, rhs_dim):
    return lax.dot_general(
        lhs, rhs, (((lhs_dim,), (rhs_dim,)), ((), ())), preferred_element_type=F32
    )


def call(body, out_shape, scratch, args, flops):
    spec = pl.BlockSpec(memory_space=pltpu.VMEM)
    total = sum(a.size * a.dtype.itemsize for a in args)
    return pl.pallas_call(
        body,
        out_shape=out_shape,
        in_specs=[spec] * len(args),
        out_specs=[spec] * len(out_shape),
        scratch_shapes=scratch,
        compiler_params=pltpu.CompilerParams(vmem_limit_bytes=VMEM_LIMIT),
        cost_estimate=pl.CostEstimate(flops=flops, bytes_accessed=total, transcendentals=0),
    )(*args)


def backward_terms(hidden, gate, up, gates, ups, outs):
    d_gate, d_up = [], []
    for h, g, u in zip(hidden, gate, up):
        q = jax.nn.sigmoid(g)
        d_gate.append((h * u * q * (1.0 + g * (1.0 - q))).astype(BF16))
        d_up.append((h * g * q).astype(BF16))
    width = 512
    for low in range(0, D, width):
        cols = pl.ds(low, width)
        total = dot(d_gate[0], gates[0][cols, :], 1, 1)
        total += dot(d_gate[1], gates[1][cols, :], 1, 1)
        total += dot(d_up[0], ups[0][cols, :], 1, 1)
        total += dot(d_up[1], ups[1][cols, :], 1, 1)
        for k in range(CHIPS):
            part = total[16 * k : 16 * k + 16]
            outs[k][:, cols] = part.astype(outs[k].dtype)


def pick(value, offset):
    return jnp.concatenate(
        [value[16 * b + offset : 16 * b + offset + 8] for b in range(2 * CHIPS)], axis=0
    )


def first_tick_kernel(*refs):
    blocks, weights, outs, held = refs[:8], refs[8:14], refs[14:18], refs[18]
    gates, ups, downs = weights[0:2], weights[2:4], weights[4:6]
    for b in range(8):
        held[pl.ds(16 * b, 16), :] = blocks[b][...]
    rows = held[...]
    gate = [pick(dot(rows, w[...], 1, 0), 0) for w in gates]
    up = [pick(dot(rows, w[...], 1, 0), 0) for w in ups]
    hidden = [pick(dot(rows, w[...], 1, 1), 8) for w in downs]
    backward_terms(hidden, gate, up, gates, ups, outs)


def second_tick_kernel(*refs):
    blocks, pre, weights, outs, held = refs[:4], refs[4:8], refs[8:14], refs[14:18], refs[18]
    gates, ups, downs = weights[0:2], weights[2:4], weights[4:6]
    for b in range(4):
        held[pl.ds(16 * b, 16), :] = blocks[b][...]
    rows = held[...]
    hidden = [dot(rows, w[...], 1, 1) for w in downs]
    gate = [pre[0][...], pre[1][...]]
    up = [pre[2][...], pre[3][...]]
    backward_terms(hidden, gate, up, gates, ups, outs)


def forward_kernel(*refs):
    first, second = refs[0:8], refs[8:12]
    gates, ups, routers = refs[12:14], refs[14:16], refs[16:18]
    base, pre = refs[18], refs[19:23]
    expo_ref, share_ref, stats_ref = refs[23:26]
    held0, held1, ids_ref = refs[26:29]
    for b in range(8):
        held0[pl.ds(16 * b, 16), :] = first[b][...]
    ids_ref[...] = jnp.full((128, IDCOLS), -1.0, F32)
    for b in range(4):
        held1[pl.ds(16 * b, 16), :] = second[b][:, 0:D]
        ids_ref[pl.ds(16 * b, 16), :] = second[b][:, D : D + IDCOLS].astype(F32)
    rows0, rows1 = held0[...], held1[...]
    for w, out in zip((*gates, *ups), pre):
        out[...] = dot(rows1, w[...], 1, 0)
    logits = jnp.concatenate(
        [
            jnp.concatenate([dot(r[...], rows, 1, 1) for r in routers], axis=0)
            for rows in (rows0, jnp.concatenate([rows1, rows1], axis=0))
        ],
        axis=1,
    )
    ids = ids_ref[...].T
    experts = base[:, 0:1]
    stream_b = (lax.broadcasted_iota(jnp.int32, (2 * OWN, 128), 1) % 16) >= 8
    scale = EXPERTS / (TOKENS * TOPK)
    shares = []
    for tick in range(2):
        hits = jnp.zeros((2 * OWN, 128), F32)
        for core in range(2):
            for j in range(TOPK):
                slot = 16 * core + 8 * tick + j
                hits += (experts == ids[slot : slot + 1, :]).astype(F32)
        count_a = jnp.sum(jnp.where(stream_b, 0.0, hits), axis=1, keepdims=True)
        count_b = jnp.sum(jnp.where(stream_b, hits, 0.0), axis=1, keepdims=True)
        shares.append((count_a * scale, count_b * scale))
    column = lax.broadcasted_iota(jnp.int32, (2 * OWN, 128), 1)
    share0 = jnp.where((column % 32) >= 16, shares[0][1], shares[0][0])
    share1 = jnp.where(stream_b, shares[1][1], shares[1][0])
    share = jnp.concatenate([share0, share1], axis=1)
    peak = jnp.max(logits, axis=0, keepdims=True)
    expo = jnp.exp(logits - peak)
    total = jnp.sum(expo, axis=0, keepdims=True)
    weighted = jnp.sum(expo * share, axis=0, keepdims=True)
    expo_ref[...] = expo
    share_ref[...] = share
    stats_ref[...] = jnp.concatenate(
        [peak, total, weighted, jnp.zeros((5, 256), F32)], axis=0
    )


def router_kernel(*refs):
    first, second = refs[0:8], refs[8:12]
    expo_ref, share_ref = refs[12:14]
    stats = refs[14:18]
    own_out, other_out = refs[18:20]
    held0, held1 = refs[20:22]
    for b in range(8):
        held0[pl.ds(16 * b, 16), :] = first[b][...]
    for b in range(4):
        held1[pl.ds(16 * b, 16), :] = second[b][:, 0:D]
    stats = [
        jnp.concatenate(
            [pltpu.roll(s[:, 0:128], 32 * k, 1), pltpu.roll(s[:, 128:256], 16 * k, 1)], axis=1
        )
        if k
        else s[...]
        for k, s in enumerate(stats)
    ]
    peaks = [s[0:1, :] for s in stats]
    peak = functools.reduce(jnp.maximum, peaks)
    factors = [jnp.exp(p - peak) for p in peaks]
    total = sum(s[1:2, :] * f for s, f in zip(stats, factors))
    weighted = sum(s[2:3, :] * f for s, f in zip(stats, factors))
    log_total = peak + jnp.log(total)
    mean_share = weighted / total
    probs = expo_ref[...] * (factors[0] / total)
    slopes = (
        2.0 * z_weight * log_total - balance_weight * mean_share + balance_weight * share_ref[...]
    ) * probs
    column = lax.broadcasted_iota(jnp.int32, (2 * OWN, 128), 1)
    slopes0 = jnp.where((column % 16) < 8, slopes[:, 0:128], 0.0).astype(BF16)
    slopes1 = slopes[:, 128:192].astype(BF16)
    width = 512
    for low in range(0, D, width):
        cols = pl.ds(low, width)
        part = dot(slopes0, held0[:, cols], 1, 0) + dot(slopes1, held1[:, cols], 1, 0)
        own_out[:, cols] = part[0:OWN]
        other_out[:, cols] = part[OWN:]


def swapped(value):
    return lax.ppermute(value, "expert", [(e, e ^ 1) for e in range(8)])


def mirrored(value):
    count = lax.axis_size("pipe")
    return lax.ppermute(value, "pipe", [(i, count - 1 - i) for i in range(count)])


def from_chip(value, k):
    return lax.ppermute(value, "expert", [((e + 2 * k) % 8, e) for e in range(8)])


def spread(value):
    return [value] + [from_chip(value, k) for k in range(1, CHIPS)]


def returned(parts):
    return [parts[0]] + [from_chip(parts[k], CHIPS - k) for k in range(1, CHIPS)]


def shards(
    stash_a, stash_b, ids_a, ids_b, arriving_a, arriving_b, head_a, head_b,
    w_gate, w_up, w_down, router,
):
    stash_a, stash_b, ids_a, ids_b = stash_a[0], stash_b[0], ids_a[0], ids_b[0]
    arriving_a, arriving_b = arriving_a[0], arriving_b[0]
    w_gate, w_up, w_down, router = w_gate[0], w_up[0], w_down[0], router[0]
    section = lax.axis_index("pipe")
    top = lax.axis_size("pipe") - 1
    member = lax.axis_index("expert")

    block_b = mirrored(jnp.concatenate([stash_b[0], arriving_b], axis=0))
    block_a = jnp.concatenate([stash_a[0], arriving_a], axis=0)
    blocks_a = spread(block_a)
    other_gate, other_up, other_down, other_router = (
        swapped(w_gate), swapped(w_up), swapped(w_down), swapped(router)
    )
    gates, ups = [w_gate, other_gate], [w_up, other_up]
    downs, routers = [w_down, other_down], [router, other_router]

    def id_rows(ids):
        return jnp.concatenate([ids[0], ids[1]], axis=1)

    ids = jnp.concatenate([id_rows(ids_a), id_rows(ids_b)], axis=0).astype(BF16)
    ids = jnp.pad(ids, ((0, 0), (0, 112)), constant_values=-1)
    ids_other = swapped(ids)
    ids = jnp.concatenate([ids[:, :16], ids_other[:, :16], ids[:, 32:]], axis=1)
    later_b = mirrored(jnp.concatenate([stash_b[1], ids[8:]], axis=1))
    later_a = jnp.concatenate([stash_a[1], ids[:8]], axis=1)
    blocks_b = spread(block_b)
    later = spread(jnp.concatenate([later_a, later_b], axis=0))
    first = [block for pair in zip(blocks_a, blocks_b) for block in pair]

    sums = [
        jax.ShapeDtypeStruct((16, D), F32 if k == 0 else BF16) for k in range(CHIPS)
    ]
    terms = call(
        first_tick_kernel, sums, [pltpu.VMEM((128, D), BF16)],
        first + gates + ups + downs, 2 * 128 * D * 128 * 10,
    )
    base = jnp.concatenate(
        [OWN * member + jnp.arange(OWN), OWN * (member ^ 1) + jnp.arange(OWN)]
    ).astype(F32)
    base = jnp.broadcast_to(base[:, None], (2 * OWN, 128))
    pre = [jax.ShapeDtypeStruct((64, HID), F32)] * 4
    *pre, expo, share, stats = call(
        forward_kernel,
        pre
        + [
            jax.ShapeDtypeStruct((2 * OWN, 256), F32),
            jax.ShapeDtypeStruct((2 * OWN, 256), F32),
            jax.ShapeDtypeStruct((8, 256), F32),
        ],
        [pltpu.VMEM((128, D), BF16), pltpu.VMEM((64, D), BF16), pltpu.VMEM((128, IDCOLS), F32)],
        first + later + gates + ups + routers + [base], 2 * 128 * D * 128 * 4,
    )

    def emitted(grads, parts):
        total = grads.astype(F32) + parts[0]
        for part in parts[1:]:
            total = total + part.astype(F32)
        return total.astype(BF16)

    grads = jnp.concatenate([block_a[8:], block_b[8:]], axis=0)
    out = emitted(grads, returned(terms))
    moved = lax.ppermute(out, "pipe", [(i, i - 1) for i in range(1, top + 1)])
    head = jnp.concatenate([head_a[0], head_b[0]], axis=0)
    grads = jnp.where(section == top, head, moved)
    terms = call(
        second_tick_kernel, sums, [pltpu.VMEM((64, D), BF16)],
        spread(grads) + pre + gates + ups + downs, 2 * 64 * D * 128 * 6,
    )
    own, other = call(
        router_kernel, [jax.ShapeDtypeStruct((OWN, D), F32)] * 2,
        [pltpu.VMEM((128, D), BF16), pltpu.VMEM((64, D), BF16)],
        first + later + [expo, share] + spread(stats), 2 * 192 * D * 64,
    )
    router_grad = own + swapped(other)
    out = emitted(grads, returned(terms))
    return out[None, :8], mirrored(out[8:])[None], router_grad[None]


def solution(mesh):
    placed = (
        P("pipe", None, "expert", None),
        P("pipe", None, "expert", None),
        P("pipe", None, "expert", None),
        P("pipe", None, "expert", None),
        P("pipe", "expert", None),
        P("pipe", "expert", None),
        P(None, "expert", None),
        P(None, "expert", None),
        P("pipe", None, "expert"),
        P("pipe", None, "expert"),
        P("pipe", "expert", None),
        P("pipe", "expert", None),
    )
    return jax.shard_map(
        shards,
        mesh=mesh,
        in_specs=placed,
        out_specs=(P("pipe", "expert", None), P("pipe", "expert", None), P("pipe", "expert", None)),
        check_vma=False,
    )
```

time: 752 us -> 168 us (0.22); the launches traced: 741 us -> 165 us
  blocking collectives: 418 us -> 0 us
  local copies, waits for them, and re-layouts: 155 us -> 5.52 us
  starting transfers between devices: 50 us -> 114 us
  waiting for transfers between devices: 56.2 us -> 31.7 us
  matrix products: 23.8 us -> 0 us
  other arithmetic: 24.2 us -> 3.7 us
  between operations: 14.3 us -> 1.14 us
  Pallas kernels: 0 us -> 9.77 us
    all_gather x6 -> x0, blocking collectives: 219 us -> none  [the longest x4 185 us: expert_rows(): lax.all_gather(grads, 'expert', axis=0, tiled=True)]
    all_to_all x1 -> x0, blocking collectives: 157 us -> none  [mirror_half(): lax.all_to_all(packed, 'pipe', split_axis=0, concat_axis=0, tiled=True)]
    ppermute x2 -> x31, starting transfers between devices: 9.79 us -> 114 us  [the longest x21 62.9 us: from_chip(): lax.ppermute(value, 'expert', [((e + 2 * k) % 8, e) for e in range(8)])]
    rev x2 -> x0, local copies, waits for them, and re-layouts: 81.8 us -> none  [the longest x1 81.4 us: mirror_half(): spread_out[::-1]]
    unnamed x57 -> x19, local copies, waits for them, and re-layouts: 53.9 us -> 3.01 us
    all_to_all x3 -> x0, starting transfers between devices: 40.1 us -> none  [the longest x1 16.4 us: mirror_full(): lax.all_to_all(packed.astype(jnp.bfloat16), 'pipe', split_axis=0, concat_...]
    reduce_scatter x4 -> x0, waiting for transfers between devices: 37.3 us -> none  [expert_rows(): lax.psum_scatter(terms.astype(jnp.bfloat16), 'expert', scatter_dimension=...]
    psum x2 -> x0, blocking collectives: 28.3 us -> none  [the longest x1 14.7 us: shards(): lax.psum((local_counts(ids_a), local_counts(ids_b)), 'expert')]
  transfers between devices with their start and end apart: 9 -> 31, of which waited for: 3 -> 10; matrix products, arithmetic and copies ran while one was open for 4% -> 3% of each run, Pallas kernels for 0% -> 4%
where the time goes in v1:
time: 168 us; the launch traced here: 165 us
  starting transfers between devices  114 us (68%)
  waiting for transfers between devices  31.7 us (19%)
  Pallas kernels  9.77 us (6%)
  local copies, waits for them, and re-layouts  5.52 us (3%)
  other arithmetic  3.7 us (2%)
    ppermute x21, starting transfers between devices, from_chip(): lax.ppermute(value, 'expert', [((e + 2 * k) % 8, e) for e in range(8)])  62.9 us
    ppermute x3, starting transfers between devices, mirrored(): lax.ppermute(value, 'pipe', [(i, count - 1 - i) for i in range(count)])  36.6 us
    ppermute x21, waiting for transfers between devices, from_chip(): lax.ppermute(value, 'expert', [((e + 2 * k) % 8, e) for e in range(8)])  21.8 us
    ppermute x6, starting transfers between devices, swapped(): return lax.ppermute(value, 'expert', [(e, e ^ 1) for e in range(8)])  12.2 us
    pallas_call x4, Pallas kernels, call(): pl.pallas_call(body, out_shape=out_shape, in_specs=[spec] * len(args), ou...  9.77 us
    ppermute x3, waiting for transfers between devices, mirrored(): lax.ppermute(value, 'pipe', [(i, count - 1 - i) for i in range(count)])  6.96 us
  transfers between devices with their start and end apart: 31, of which 10 were waited for; matrix products, arithmetic and copies ran while one was open for 3% of the time, Pallas kernels for 4%

profile of v1, /device:TPU:6, one launch (start us, length us, event | category | flops | bytes accessed | tf_op | source)
XLA Modules:
  0.0 165.5 jit_solution(16276970650181076122)
XLA Ops:
  1.5 1.9 %collective-permute-start.17 = (bf16[16,128]{1,0:T(8,128)(2,1)S(1)}, bf16[16,128]{1,0:T(8,128)(2,1)S(1)}, u32[]{:S(2)}, u32[]{:S(2)}) collective-permute-start(bf16[16,128]{1,0:T(8,128)(2,1)S(1)} %fusion.8), channel_id=1, source_target_pairs={{0,1},{1,0},{2,3},{3,2},{4,5},{5,4},{6,7},{7,6},{8,9},{9,8},{10,11... | collective-permute-start | bytes 12296 | tf_op jit(solution)/shard_map/ppermute | solution.py:186
  3.4 0.9 slice_bitcast_fusion.1
  4.3 0.8 pad_maximum_fusion.1
  5.1 15.1 %collective-permute-start = (bf16[16,3584]{1,0:T(8,128)(2,1)S(1)}, bf16[16,3584]{1,0:T(8,128)(2,1)S(1)}, u32[]{:S(2)}, u32[]{:S(2)}) collective-permute-start(bf16[16,3584]{1,0:T(8,128)(2,1)S(1)} %pad_maximum_fusion.1), channel_id=1, source_target_pairs={{0,504},{8,496},{16,488},{24,480},{32,472},{40,464},{48,456},{56,4... | collective-permute-start | bytes 344072 | tf_op jit(solution)/shard_map/ppermute | solution.py:191
  20.2 2.1 %collective-permute-start.7 = (bf16[3584,128]{1,0:T(8,128)(2,1)}, bf16[3584,128]{1,0:T(8,128)(2,1)S(1)}, u32[]{:S(2)}, u32[]{:S(2)}) collective-permute-start(bf16[3584,128]{1,0:T(8,128)(2,1)} %bitcast.30), channel_id=1, source_target_pairs={{0,1},{1,0},{2,3},{3,2},{4,5},{5,4},{6,7},{7,6},{8,9},{9,8},{10,11... | collective-permute-start | bytes 2752520 | tf_op jit(solution)/shard_map/ppermute | solution.py:186
  22.4 2.2 %collective-permute-start.8 = (bf16[3584,128]{1,0:T(8,128)(2,1)}, bf16[3584,128]{1,0:T(8,128)(2,1)S(1)}, u32[]{:S(2)}, u32[]{:S(2)}) collective-permute-start(bf16[3584,128]{1,0:T(8,128)(2,1)} %bitcast.34), channel_id=1, source_target_pairs={{0,1},{1,0},{2,3},{3,2},{4,5},{5,4},{6,7},{7,6},{8,9},{9,8},{10,11... | collective-permute-start | bytes 2752520 | tf_op jit(solution)/shard_map/ppermute | solution.py:186
  24.6 2.1 %collective-permute-start.9 = (bf16[128,3584]{1,0:T(8,128)(2,1)}, bf16[128,3584]{1,0:T(8,128)(2,1)}, u32[]{:S(2)}, u32[]{:S(2)}) collective-permute-start(bf16[128,3584]{1,0:T(8,128)(2,1)} %bitcast.38), channel_id=1, source_target_pairs={{0,1},{1,0},{2,3},{3,2},{4,5},{5,4},{6,7},{7,6},{8,9},{9,8},{10,11... | collective-permute-start | bytes 2752520 | tf_op jit(solution)/shard_map/ppermute | solution.py:186
  26.7 0.9 slice_bitcast_fusion.2
  28.4 3.8 %collective-permute-start.1 = (bf16[16,3584]{1,0:T(8,128)(2,1)S(1)}, bf16[16,3584]{1,0:T(8,128)(2,1)S(1)}, u32[]{:S(2)}, u32[]{:S(2)}) collective-permute-start(bf16[16,3584]{1,0:T(8,128)(2,1)S(1)} %pad_maximum_fusion.2.refs_0_), channel_id=1, source_target_pairs={{2,0},{3,1},{4,2},{5,3},{6,4},{7,5},{0,6},{1,7},{10,8},{11,9},{12,... | collective-permute-start | bytes 344072 | tf_op jit(solution)/shard_map/ppermute | solution.py:195
  32.3 2.5 %collective-permute-start.3 = (bf16[16,3584]{1,0:T(8,128)(2,1)S(1)}, bf16[16,3584]{1,0:T(8,128)(2,1)S(1)}, u32[]{:S(2)}, u32[]{:S(2)}) collective-permute-start(bf16[16,3584]{1,0:T(8,128)(2,1)S(1)} %pad_maximum_fusion.2.refs_0_), channel_id=1, source_target_pairs={{4,0},{5,1},{6,2},{7,3},{0,4},{1,5},{2,6},{3,7},{12,8},{13,9},{14,... | collective-permute-start | bytes 344072 | tf_op jit(solution)/shard_map/ppermute | solution.py:195
  35.6 2.9 %collective-permute-start.5 = (bf16[16,3584]{1,0:T(8,128)(2,1)S(1)}, bf16[16,3584]{1,0:T(8,128)(2,1)S(1)}, u32[]{:S(2)}, u32[]{:S(2)}) collective-permute-start(bf16[16,3584]{1,0:T(8,128)(2,1)S(1)} %pad_maximum_fusion.2.refs_0_), channel_id=1, source_target_pairs={{6,0},{7,1},{0,2},{1,3},{2,4},{3,5},{4,6},{5,7},{14,8},{15,9},{8,1... | collective-permute-start | bytes 344072 | tf_op jit(solution)/shard_map/ppermute | solution.py:195
  38.6 6.0 %collective-permute-done.3.refs_4_ = bf16[16,3584]{1,0:T(8,128)(2,1)S(1)} collective-permute-done((bf16[16,3584]{1,0:T(8,128)(2,1)S(1)}, bf16[16,3584]{1,0:T(8,128)(2,1)S(1)}, u32[]{:S(2)}, u32[]{:S(2)}) %collective-permute-start.3) | collective-permute-done | bytes 114720 | tf_op jit(solution)/shard_map/ppermute | solution.py:195
  44.6 1.9 %collective-permute-start.2 = (bf16[16,3584]{1,0:T(8,128)(2,1)S(1)}, bf16[16,3584]{1,0:T(8,128)(2,1)S(1)}, u32[]{:S(2)}, u32[]{:S(2)}) collective-permute-start(bf16[16,3584]{1,0:T(8,128)(2,1)S(1)} %collective-permute-done.refs_1_), channel_id=1, source_target_pairs={{2,0},{3,1},{4,2},{5,3},{6,4},{7,5},{0,6},{1,7},{10,8},{11,9},{12,... | collective-permute-start | bytes 344072 | tf_op jit(solution)/shard_map/ppermute | solution.py:195
  46.6 1.9 %collective-permute-start.4 = (bf16[16,3584]{1,0:T(8,128)(2,1)S(1)}, bf16[16,3584]{1,0:T(8,128)(2,1)S(1)}, u32[]{:S(2)}, u32[]{:S(2)}) collective-permute-start(bf16[16,3584]{1,0:T(8,128)(2,1)S(1)} %collective-permute-done.refs_1_), channel_id=1, source_target_pairs={{4,0},{5,1},{6,2},{7,3},{0,4},{1,5},{2,6},{3,7},{12,8},{13,9},{14,... | collective-permute-start | bytes 344072 | tf_op jit(solution)/shard_map/ppermute | solution.py:195
  48.5 3.0 %collective-permute-done.2.refs_3_ = bf16[16,3584]{1,0:T(8,128)(2,1)S(1)} collective-permute-done((bf16[16,3584]{1,0:T(8,128)(2,1)S(1)}, bf16[16,3584]{1,0:T(8,128)(2,1)S(1)}, u32[]{:S(2)}, u32[]{:S(2)}) %collective-permute-start.2) | collective-permute-done | bytes 114720 | tf_op jit(solution)/shard_map/ppermute | solution.py:195
  51.5 1.9 %collective-permute-start.6 = (bf16[16,3584]{1,0:T(8,128)(2,1)S(1)}, bf16[16,3584]{1,0:T(8,128)(2,1)S(1)}, u32[]{:S(2)}, u32[]{:S(2)}) collective-permute-start(bf16[16,3584]{1,0:T(8,128)(2,1)S(1)} %collective-permute-done.refs_1_), channel_id=1, source_target_pairs={{6,0},{7,1},{0,2},{1,3},{2,4},{3,5},{4,6},{5,7},{14,8},{15,9},{8,1... | collective-permute-start | bytes 344072 | tf_op jit(solution)/shard_map/ppermute | solution.py:195
  53.5 3.4 %collective-permute-done.4.refs_5_ = bf16[16,3584]{1,0:T(8,128)(2,1)S(1)} collective-permute-done((bf16[16,3584]{1,0:T(8,128)(2,1)S(1)}, bf16[16,3584]{1,0:T(8,128)(2,1)S(1)}, u32[]{:S(2)}, u32[]{:S(2)}) %collective-permute-start.4) | collective-permute-done | bytes 114720 | tf_op jit(solution)/shard_map/ppermute | solution.py:195
  56.9 1.9 %collective-permute-start.22 = (bf16[32,3584]{1,0:T(8,128)(2,1)}, bf16[32,3584]{1,0:T(8,128)(2,1)S(1)}, u32[]{:S(2)}, u32[]{:S(2)}) collective-permute-start(bf16[32,3584]{1,0:T(8,128)(2,1)} %bitcast.41), channel_id=1, source_target_pairs={{0,1},{1,0},{2,3},{3,2},{4,5},{5,4},{6,7},{7,6},{8,9},{9,8},{10,11... | collective-permute-start | bytes 688136 | tf_op jit(solution)/shard_map/ppermute | solution.py:186
  58.8 1.2 collective-permute-done.6.refs_7_
  60.0 1.2 copy-done.1
  61.2 1.2 copy-done.3
  62.4 4.1 %shard_map.139 = (f32[16,3584]{1,0:T(8,128)S(1)}, bf16[16,3584]{1,0:T(8,128)(2,1)S(1)}, bf16[16,3584]{1,0:T(8,128)(2,1)S(1)}, bf16[16,3584]{1,0:T(8,128)(2,1)S(1)}) custom-call(bf16[16,3584]{1,0:T(8,128)(2,1)S(1)} %pad_maximum_fusion.2.refs_0_, bf16[16,3584]{1,0:T(8,128)(2,1)S(1)} %collective-permute-done.refs_1_, ...), custom_call_target="tpu_custom_call" | custom-call | flops 1174405120 | bytes 6422528 | tf_op jit(solution)/shard_map/pallas_call | solution.py:35
  66.5 1.9 %collective-permute-start.10 = (bf16[16,3584]{1,0:T(8,128)(2,1)S(1)}, bf16[16,3584]{1,0:T(8,128)(2,1)S(1)}, u32[]{:S(2)}, u32[]{:S(2)}) collective-permute-start(bf16[16,3584]{1,0:T(8,128)(2,1)S(1)} %get-tuple-element.21), channel_id=1, source_target_pairs={{6,0},{7,1},{0,2},{1,3},{2,4},{3,5},{4,6},{5,7},{14,8},{15,9},{8,1... | collective-permute-start | bytes 344072 | tf_op jit(solution)/shard_map/ppermute | solution.py:195
  68.4 3.5 %collective-permute-start.11 = (bf16[16,3584]{1,0:T(8,128)(2,1)S(1)}, bf16[16,3584]{1,0:T(8,128)(2,1)S(1)}, u32[]{:S(2)}, u32[]{:S(2)}) collective-permute-start(bf16[16,3584]{1,0:T(8,128)(2,1)S(1)} %get-tuple-element.22), channel_id=1, source_target_pairs={{4,0},{5,1},{6,2},{7,3},{0,4},{1,5},{2,6},{3,7},{12,8},{13,9},{14,... | collective-permute-start | bytes 344072 | tf_op jit(solution)/shard_map/ppermute | solution.py:195
  71.9 4.2 %collective-permute-start.12 = (bf16[16,3584]{1,0:T(8,128)(2,1)S(1)}, bf16[16,3584]{1,0:T(8,128)(2,1)S(1)}, u32[]{:S(2)}, u32[]{:S(2)}) collective-permute-start(bf16[16,3584]{1,0:T(8,128)(2,1)S(1)} %get-tuple-element.23), channel_id=1, source_target_pairs={{2,0},{3,1},{4,2},{5,3},{6,4},{7,5},{0,6},{1,7},{10,8},{11,9},{12,... | collective-permute-start | bytes 344072 | tf_op jit(solution)/shard_map/ppermute | solution.py:195
  76.1 9.3 %collective-permute-start.18 = (bf16[8,3712]{1,0:T(8,128)(2,1)S(1)}, bf16[8,3712]{1,0:T(8,128)(2,1)S(1)}, u32[]{:S(2)}, u32[]{:S(2)}) collective-permute-start(bf16[8,3712]{1,0:T(8,128)(2,1)S(1)} %pad_maximum_fusion.3), channel_id=1, source_target_pairs={{0,504},{8,496},{16,488},{24,480},{32,472},{40,464},{48,456},{56,4... | collective-permute-start | bytes 178184 | tf_op jit(solution)/shard_map/ppermute | solution.py:191
  85.6 1.9 %collective-permute-start.13 = (bf16[16,3584]{1,0:T(8,128)(2,1)S(1)}, bf16[16,3584]{1,0:T(8,128)(2,1)S(1)}, u32[]{:S(2)}, u32[]{:S(2)}) collective-permute-start(bf16[16,3584]{1,0:T(8,128)(2,1)S(1)} %add_convert_fusion.1), channel_id=1, source_target_pairs={{8,0},{16,8},{24,16},{32,24},{40,32},{48,40},{56,48},{64,56},{72,6... | collective-permute-start | bytes 344072 | tf_op jit(solution)/shard_map/ppermute | solution.py:271
  87.5 2.9 %collective-permute-done.18 = bf16[8,3712]{1,0:T(8,128)(2,1)S(1)} collective-permute-done((bf16[8,3712]{1,0:T(8,128)(2,1)S(1)}, bf16[8,3712]{1,0:T(8,128)(2,1)S(1)}, u32[]{:S(2)}, u32[]{:S(2)}) %collective-permute-start.18) | collective-permute-done | bytes 59424 | tf_op jit(solution)/shard_map/ppermute | solution.py:191
  90.5 6.1 %collective-permute-start.19 = (bf16[16,3712]{1,0:T(8,128)(2,1)S(1)}, bf16[16,3712]{1,0:T(8,128)(2,1)S(1)}, u32[]{:S(2)}, u32[]{:S(2)}) collective-permute-start(bf16[16,3712]{1,0:T(8,128)(2,1)S(1)} %pad_maximum_fusion.refs_8_), channel_id=1, source_target_pairs={{2,0},{3,1},{4,2},{5,3},{6,4},{7,5},{0,6},{1,7},{10,8},{11,9},{12,... | collective-permute-start | bytes 356360 | tf_op jit(solution)/shard_map/ppermute | solution.py:195
  96.6 1.9 %collective-permute-start.20 = (bf16[16,3712]{1,0:T(8,128)(2,1)S(1)}, bf16[16,3712]{1,0:T(8,128)(2,1)S(1)}, u32[]{:S(2)}, u32[]{:S(2)}) collective-permute-start(bf16[16,3712]{1,0:T(8,128)(2,1)S(1)} %pad_maximum_fusion.refs_8_), channel_id=1, source_target_pairs={{4,0},{5,1},{6,2},{7,3},{0,4},{1,5},{2,6},{3,7},{12,8},{13,9},{14,... | collective-permute-start | bytes 356360 | tf_op jit(solution)/shard_map/ppermute | solution.py:195
  98.6 2.9 %collective-permute-start.21 = (bf16[16,3712]{1,0:T(8,128)(2,1)S(1)}, bf16[16,3712]{1,0:T(8,128)(2,1)S(1)}, u32[]{:S(2)}, u32[]{:S(2)}) collective-permute-start(bf16[16,3712]{1,0:T(8,128)(2,1)S(1)} %pad_maximum_fusion.refs_8_), channel_id=1, source_target_pairs={{6,0},{7,1},{0,2},{1,3},{2,4},{3,5},{4,6},{5,7},{14,8},{15,9},{8,1... | collective-permute-start | bytes 356360 | tf_op jit(solution)/shard_map/ppermute | solution.py:195
  101.5 2.9 %collective-permute-done.13 = bf16[16,3584]{1,0:T(8,128)(2,1)S(1)} collective-permute-done((bf16[16,3584]{1,0:T(8,128)(2,1)S(1)}, bf16[16,3584]{1,0:T(8,128)(2,1)S(1)}, u32[]{:S(2)}, u32[]{:S(2)}) %collective-permute-start.13) | collective-permute-done | bytes 114720 | tf_op jit(solution)/shard_map/ppermute | solution.py:271
  104.4 1.9 %collective-permute-start.14 = (bf16[16,3584]{1,0:T(8,128)(2,1)S(1)}, bf16[16,3584]{1,0:T(8,128)(2,1)S(1)}, u32[]{:S(2)}, u32[]{:S(2)}) collective-permute-start(bf16[16,3584]{1,0:T(8,128)(2,1)S(1)} %maximum_select_fusion.refs_0_), channel_id=1, source_target_pairs={{2,0},{3,1},{4,2},{5,3},{6,4},{7,5},{0,6},{1,7},{10,8},{11,9},{12,... | collective-permute-start | bytes 344072 | tf_op jit(solution)/shard_map/ppermute | solution.py:195
  106.4 3.3 %collective-permute-start.15 = (bf16[16,3584]{1,0:T(8,128)(2,1)S(1)}, bf16[16,3584]{1,0:T(8,128)(2,1)S(1)}, u32[]{:S(2)}, u32[]{:S(2)}) collective-permute-start(bf16[16,3584]{1,0:T(8,128)(2,1)S(1)} %maximum_select_fusion.refs_0_), channel_id=1, source_target_pairs={{4,0},{5,1},{6,2},{7,3},{0,4},{1,5},{2,6},{3,7},{12,8},{13,9},{14,... | collective-permute-start | bytes 344072 | tf_op jit(solution)/shard_map/ppermute | solution.py:195
  109.7 2.9 %collective-permute-start.16 = (bf16[16,3584]{1,0:T(8,128)(2,1)S(1)}, bf16[16,3584]{1,0:T(8,128)(2,1)S(1)}, u32[]{:S(2)}, u32[]{:S(2)}) collective-permute-start(bf16[16,3584]{1,0:T(8,128)(2,1)S(1)} %maximum_select_fusion.refs_0_), channel_id=1, source_target_pairs={{6,0},{7,1},{0,2},{1,3},{2,4},{3,5},{4,6},{5,7},{14,8},{15,9},{8,1... | collective-permute-start | bytes 344072 | tf_op jit(solution)/shard_map/ppermute | solution.py:195
  112.8 1.9 %shard_map.140 = (f32[64,128]{1,0:T(8,128)S(1)}, f32[64,128]{1,0:T(8,128)S(1)}, f32[64,128]{1,0:T(8,128)S(1)}, f32[64,128]{1,0:T(8,128)S(1)}, f32[64,256]{1,0:T(...) custom-call(bf16[16,3584]{1,0:T(8,128)(2,1)S(1)} %pad_maximum_fusion.2.refs_0_, ...), custom_call_target="tpu_custom_call" | custom-call | flops 469762048 | bytes 5554176 | tf_op jit(solution)/shard_map/pallas_call | solution.py:35
  114.7 3.9 %collective-permute-done.15.refs_2_ = bf16[16,3584]{1,0:T(8,128)(2,1)S(1)} collective-permute-done((bf16[16,3584]{1,0:T(8,128)(2,1)S(1)}, bf16[16,3584]{1,0:T(8,128)(2,1)S(1)}, u32[]{:S(2)}, u32[]{:S(2)}) %collective-permute-start.15) | collective-permute-done | bytes 114720 | tf_op jit(solution)/shard_map/ppermute | solution.py:195
  118.6 3.3 %shard_map.141 = (f32[16,3584]{1,0:T(8,128)S(1)}, bf16[16,3584]{1,0:T(8,128)(2,1)S(1)}, bf16[16,3584]{1,0:T(8,128)(2,1)S(1)}, bf16[16,3584]{1,0:T(8,128)(2,1)S(1)}) custom-call(bf16[16,3584]{1,0:T(8,128)(2,1)S(1)} %maximum_select_fusion.refs_0_, bf16[16,3584]{1,0:T(8,128)(2,1)S(1)} %collective-permute-done.14.refs_1_, ...), custom_call_target="tpu_custom_call" | custom-call | flops 352321536 | bytes 6094848 | tf_op jit(solution)/shard_map/pallas_call | solution.py:35
  121.9 1.9 %collective-permute-start.23 = (bf16[16,3584]{1,0:T(8,128)(2,1)S(1)}, bf16[16,3584]{1,0:T(8,128)(2,1)S(1)}, u32[]{:S(2)}, u32[]{:S(2)}) collective-permute-start(bf16[16,3584]{1,0:T(8,128)(2,1)S(1)} %get-tuple-element.29), channel_id=1, source_target_pairs={{6,0},{7,1},{0,2},{1,3},{2,4},{3,5},{4,6},{5,7},{14,8},{15,9},{8,1... | collective-permute-start | bytes 344072 | tf_op jit(solution)/shard_map/ppermute | solution.py:195
  123.8 3.8 %collective-permute-start.24 = (bf16[16,3584]{1,0:T(8,128)(2,1)S(1)}, bf16[16,3584]{1,0:T(8,128)(2,1)S(1)}, u32[]{:S(2)}, u32[]{:S(2)}) collective-permute-start(bf16[16,3584]{1,0:T(8,128)(2,1)S(1)} %get-tuple-element.30), channel_id=1, source_target_pairs={{4,0},{5,1},{6,2},{7,3},{0,4},{1,5},{2,6},{3,7},{12,8},{13,9},{14,... | collective-permute-start | bytes 344072 | tf_op jit(solution)/shard_map/ppermute | solution.py:195
  127.6 3.9 %collective-permute-start.25 = (bf16[16,3584]{1,0:T(8,128)(2,1)S(1)}, bf16[16,3584]{1,0:T(8,128)(2,1)S(1)}, u32[]{:S(2)}, u32[]{:S(2)}) collective-permute-start(bf16[16,3584]{1,0:T(8,128)(2,1)S(1)} %get-tuple-element.31), channel_id=1, source_target_pairs={{2,0},{3,1},{4,2},{5,3},{6,4},{7,5},{0,6},{1,7},{10,8},{11,9},{12,... | collective-permute-start | bytes 344072 | tf_op jit(solution)/shard_map/ppermute | solution.py:195
  131.5 2.5 %collective-permute-start.27 = (f32[8,256]{1,0:T(8,128)S(1)}, f32[8,256]{1,0:T(8,128)S(1)}, u32[]{:S(2)}, u32[]{:S(2)}) collective-permute-start(f32[8,256]{1,0:T(8,128)S(1)} %get-tuple-element.34.refs_14_), channel_id=1, source_target_pairs={{2,0},{3,1},{4,2},{5,3},{6,4},{7,5},{0,6},{1,7},{10,8},{11,9},{12,... | collective-permute-start | bytes 24584 | tf_op jit(solution)/shard_map/ppermute | solution.py:195
  134.0 3.4 %collective-permute-start.28 = (f32[8,256]{1,0:T(8,128)S(1)}, f32[8,256]{1,0:T(8,128)S(1)}, u32[]{:S(2)}, u32[]{:S(2)}) collective-permute-start(f32[8,256]{1,0:T(8,128)S(1)} %get-tuple-element.34.refs_14_), channel_id=1, source_target_pairs={{4,0},{5,1},{6,2},{7,3},{0,4},{1,5},{2,6},{3,7},{12,8},{13,9},{14,... | collective-permute-start | bytes 24584 | tf_op jit(solution)/shard_map/ppermute | solution.py:195
  137.3 3.9 %collective-permute-start.29 = (f32[8,256]{1,0:T(8,128)S(1)}, f32[8,256]{1,0:T(8,128)S(1)}, u32[]{:S(2)}, u32[]{:S(2)}) collective-permute-start(f32[8,256]{1,0:T(8,128)S(1)} %get-tuple-element.34.refs_14_), channel_id=1, source_target_pairs={{6,0},{7,1},{0,2},{1,3},{2,4},{3,5},{4,6},{5,7},{14,8},{15,9},{8,1... | collective-permute-start | bytes 24584 | tf_op jit(solution)/shard_map/ppermute | solution.py:195
  141.3 3.4 %collective-permute-done.29.refs_17_ = f32[8,256]{1,0:T(8,128)S(1)} collective-permute-done((f32[8,256]{1,0:T(8,128)S(1)}, f32[8,256]{1,0:T(8,128)S(1)}, u32[]{:S(2)}, u32[]{:S(2)}) %collective-permute-start.29) | collective-permute-done | bytes 8224 | tf_op jit(solution)/shard_map/ppermute | solution.py:195
  145.2 1.9 %collective-permute-start.30 = (f32[32,3584]{1,0:T(8,128)S(1)}, f32[32,3584]{1,0:T(8,128)S(1)}, u32[]{:S(2)}, u32[]{:S(2)}) collective-permute-start(f32[32,3584]{1,0:T(8,128)S(1)} %get-tuple-element.36), channel_id=1, source_target_pairs={{0,1},{1,0},{2,3},{3,2},{4,5},{5,4},{6,7},{7,6},{8,9},{9,8},{10,11... | collective-permute-start | bytes 1376264 | tf_op jit(solution)/shard_map/ppermute | solution.py:186
  147.8 12.2 %collective-permute-start.26 = (bf16[8,3584]{1,0:T(8,128)(2,1)S(1)}, bf16[8,3584]{1,0:T(8,128)(2,1)S(1)}, u32[]{:S(2)}, u32[]{:S(2)}) collective-permute-start(bf16[8,3584]{1,0:T(8,128)(2,1)S(1)} %get-tuple-element.37), channel_id=1, source_target_pairs={{0,504},{8,496},{16,488},{24,480},{32,472},{40,464},{48,456},{56,4... | collective-permute-start | bytes 172040 | tf_op jit(solution)/shard_map/ppermute | solution.py:191
  160.8 4.0 %collective-permute-done.26 = bf16[8,3584]{1,0:T(8,128)(2,1)S(1)} collective-permute-done((bf16[8,3584]{1,0:T(8,128)(2,1)S(1)}, bf16[8,3584]{1,0:T(8,128)(2,1)S(1)}, u32[]{:S(2)}, u32[]{:S(2)}) %collective-permute-start.26) | collective-permute-done | bytes 57376 | tf_op jit(solution)/shard_map/ppermute | solution.py:191
  (60 shorter events, 5.7 us)
Async XLA Ops:
  0.6 0.8 copy-start.8
  0.6 59.4 %copy-start = (bf16[1,3584,128]{2,1,0:T(8,128)(2,1)S(1)}, bf16[1,3584,128]{2,1,0:T(8,128)(2,1)}, u32[]{:S(2)}) copy-start(bf16[1,3584,128]{2,1,0:T(8,128)(2,1)} %param.20) | copy-start | bytes 2752516
  1.5 26.9 %collective-permute-start.17 = (bf16[16,128]{1,0:T(8,128)(2,1)S(1)}, bf16[16,128]{1,0:T(8,128)(2,1)S(1)}, u32[]{:S(2)}, u32[]{:S(2)}) collective-permute-start(bf16[16,128]{1,0:T(8,128)(2,1)S(1)} %fusion.8), channel_id=1, source_target_pairs={{0,1},{1,0},{2,3},{3,2},{4,5},{5,4},{6,7},{7,6},{8,9},{9,8},{10,11... | collective-permute-start | bytes 12296 | tf_op jit(solution)/shard_map/ppermute | solution.py:186
  5.1 27.1 %collective-permute-start = (bf16[16,3584]{1,0:T(8,128)(2,1)S(1)}, bf16[16,3584]{1,0:T(8,128)(2,1)S(1)}, u32[]{:S(2)}, u32[]{:S(2)}) collective-permute-start(bf16[16,3584]{1,0:T(8,128)(2,1)S(1)} %pad_maximum_fusion.1), channel_id=1, source_target_pairs={{0,504},{8,496},{16,488},{24,480},{32,472},{40,464},{48,456},{56,4... | collective-permute-start | bytes 344072 | tf_op jit(solution)/shard_map/ppermute | solution.py:191
  20.2 39.8 %collective-permute-start.7 = (bf16[3584,128]{1,0:T(8,128)(2,1)}, bf16[3584,128]{1,0:T(8,128)(2,1)S(1)}, u32[]{:S(2)}, u32[]{:S(2)}) collective-permute-start(bf16[3584,128]{1,0:T(8,128)(2,1)} %bitcast.30), channel_id=1, source_target_pairs={{0,1},{1,0},{2,3},{3,2},{4,5},{5,4},{6,7},{7,6},{8,9},{9,8},{10,11... | collective-permute-start | bytes 2752520 | tf_op jit(solution)/shard_map/ppermute | solution.py:186
  22.4 37.6 %collective-permute-start.8 = (bf16[3584,128]{1,0:T(8,128)(2,1)}, bf16[3584,128]{1,0:T(8,128)(2,1)S(1)}, u32[]{:S(2)}, u32[]{:S(2)}) collective-permute-start(bf16[3584,128]{1,0:T(8,128)(2,1)} %bitcast.34), channel_id=1, source_target_pairs={{0,1},{1,0},{2,3},{3,2},{4,5},{5,4},{6,7},{7,6},{8,9},{9,8},{10,11... | collective-permute-start | bytes 2752520 | tf_op jit(solution)/shard_map/ppermute | solution.py:186
  24.6 35.4 %collective-permute-start.9 = (bf16[128,3584]{1,0:T(8,128)(2,1)}, bf16[128,3584]{1,0:T(8,128)(2,1)}, u32[]{:S(2)}, u32[]{:S(2)}) collective-permute-start(bf16[128,3584]{1,0:T(8,128)(2,1)} %bitcast.38), channel_id=1, source_target_pairs={{0,1},{1,0},{2,3},{3,2},{4,5},{5,4},{6,7},{7,6},{8,9},{9,8},{10,11... | collective-permute-start | bytes 2752520 | tf_op jit(solution)/shard_map/ppermute | solution.py:186
  28.4 7.2 %collective-permute-start.1 = (bf16[16,3584]{1,0:T(8,128)(2,1)S(1)}, bf16[16,3584]{1,0:T(8,128)(2,1)S(1)}, u32[]{:S(2)}, u32[]{:S(2)}) collective-permute-start(bf16[16,3584]{1,0:T(8,128)(2,1)S(1)} %pad_maximum_fusion.2.refs_0_), channel_id=1, source_target_pairs={{2,0},{3,1},{4,2},{5,3},{6,4},{7,5},{0,6},{1,7},{10,8},{11,9},{12,... | collective-permute-start | bytes 344072 | tf_op jit(solution)/shard_map/ppermute | solution.py:195
  32.3 12.3 %collective-permute-start.3 = (bf16[16,3584]{1,0:T(8,128)(2,1)S(1)}, bf16[16,3584]{1,0:T(8,128)(2,1)S(1)}, u32[]{:S(2)}, u32[]{:S(2)}) collective-permute-start(bf16[16,3584]{1,0:T(8,128)(2,1)S(1)} %pad_maximum_fusion.2.refs_0_), channel_id=1, source_target_pairs={{4,0},{5,1},{6,2},{7,3},{0,4},{1,5},{2,6},{3,7},{12,8},{13,9},{14,... | collective-permute-start | bytes 344072 | tf_op jit(solution)/shard_map/ppermute | solution.py:195
  35.6 10.9 %collective-permute-start.5 = (bf16[16,3584]{1,0:T(8,128)(2,1)S(1)}, bf16[16,3584]{1,0:T(8,128)(2,1)S(1)}, u32[]{:S(2)}, u32[]{:S(2)}) collective-permute-start(bf16[16,3584]{1,0:T(8,128)(2,1)S(1)} %pad_maximum_fusion.2.refs_0_), channel_id=1, source_target_pairs={{6,0},{7,1},{0,2},{1,3},{2,4},{3,5},{4,6},{5,7},{14,8},{15,9},{8,1... | collective-permute-start | bytes 344072 | tf_op jit(solution)/shard_map/ppermute | solution.py:195
  44.6 7.0 %collective-permute-start.2 = (bf16[16,3584]{1,0:T(8,128)(2,1)S(1)}, bf16[16,3584]{1,0:T(8,128)(2,1)S(1)}, u32[]{:S(2)}, u32[]{:S(2)}) collective-permute-start(bf16[16,3584]{1,0:T(8,128)(2,1)S(1)} %collective-permute-done.refs_1_), channel_id=1, source_target_pairs={{2,0},{3,1},{4,2},{5,3},{6,4},{7,5},{0,6},{1,7},{10,8},{11,9},{12,... | collective-permute-start | bytes 344072 | tf_op jit(solution)/shard_map/ppermute | solution.py:195
  46.6 10.3 %collective-permute-start.4 = (bf16[16,3584]{1,0:T(8,128)(2,1)S(1)}, bf16[16,3584]{1,0:T(8,128)(2,1)S(1)}, u32[]{:S(2)}, u32[]{:S(2)}) collective-permute-start(bf16[16,3584]{1,0:T(8,128)(2,1)S(1)} %collective-permute-done.refs_1_), channel_id=1, source_target_pairs={{4,0},{5,1},{6,2},{7,3},{0,4},{1,5},{2,6},{3,7},{12,8},{13,9},{14,... | collective-permute-start | bytes 344072 | tf_op jit(solution)/shard_map/ppermute | solution.py:195
  51.5 8.5 %collective-permute-start.6 = (bf16[16,3584]{1,0:T(8,128)(2,1)S(1)}, bf16[16,3584]{1,0:T(8,128)(2,1)S(1)}, u32[]{:S(2)}, u32[]{:S(2)}) collective-permute-start(bf16[16,3584]{1,0:T(8,128)(2,1)S(1)} %collective-permute-done.refs_1_), channel_id=1, source_target_pairs={{6,0},{7,1},{0,2},{1,3},{2,4},{3,5},{4,6},{5,7},{14,8},{15,9},{8,1... | collective-permute-start | bytes 344072 | tf_op jit(solution)/shard_map/ppermute | solution.py:195
  56.9 55.8 %collective-permute-start.22 = (bf16[32,3584]{1,0:T(8,128)(2,1)}, bf16[32,3584]{1,0:T(8,128)(2,1)S(1)}, u32[]{:S(2)}, u32[]{:S(2)}) collective-permute-start(bf16[32,3584]{1,0:T(8,128)(2,1)} %bitcast.41), channel_id=1, source_target_pairs={{0,1},{1,0},{2,3},{3,2},{4,5},{5,4},{6,7},{7,6},{8,9},{9,8},{10,11... | collective-permute-start | bytes 688136 | tf_op jit(solution)/shard_map/ppermute | solution.py:186
  60.0 1.2 copy-start.1
  61.2 1.2 copy-start.3
  66.5 19.0 %collective-permute-start.10 = (bf16[16,3584]{1,0:T(8,128)(2,1)S(1)}, bf16[16,3584]{1,0:T(8,128)(2,1)S(1)}, u32[]{:S(2)}, u32[]{:S(2)}) collective-permute-start(bf16[16,3584]{1,0:T(8,128)(2,1)S(1)} %get-tuple-element.21), channel_id=1, source_target_pairs={{6,0},{7,1},{0,2},{1,3},{2,4},{3,5},{4,6},{5,7},{14,8},{15,9},{8,1... | collective-permute-start | bytes 344072 | tf_op jit(solution)/shard_map/ppermute | solution.py:195
  68.4 17.1 %collective-permute-start.11 = (bf16[16,3584]{1,0:T(8,128)(2,1)S(1)}, bf16[16,3584]{1,0:T(8,128)(2,1)S(1)}, u32[]{:S(2)}, u32[]{:S(2)}) collective-permute-start(bf16[16,3584]{1,0:T(8,128)(2,1)S(1)} %get-tuple-element.22), channel_id=1, source_target_pairs={{4,0},{5,1},{6,2},{7,3},{0,4},{1,5},{2,6},{3,7},{12,8},{13,9},{14,... | collective-permute-start | bytes 344072 | tf_op jit(solution)/shard_map/ppermute | solution.py:195
  71.9 13.6 %collective-permute-start.12 = (bf16[16,3584]{1,0:T(8,128)(2,1)S(1)}, bf16[16,3584]{1,0:T(8,128)(2,1)S(1)}, u32[]{:S(2)}, u32[]{:S(2)}) collective-permute-start(bf16[16,3584]{1,0:T(8,128)(2,1)S(1)} %get-tuple-element.23), channel_id=1, source_target_pairs={{2,0},{3,1},{4,2},{5,3},{6,4},{7,5},{0,6},{1,7},{10,8},{11,9},{12,... | collective-permute-start | bytes 344072 | tf_op jit(solution)/shard_map/ppermute | solution.py:195
  76.1 9.4 %copy-start.5 = (bf16[1,8,3584]{2,1,0:T(8,128)(2,1)S(1)}, bf16[1,8,3584]{2,1,0:T(8,128)(2,1)}, u32[]{:S(2)}) copy-start(bf16[1,8,3584]{2,1,0:T(8,128)(2,1)} %param.16) | copy-start | bytes 172036
  76.1 14.4 %collective-permute-start.18 = (bf16[8,3712]{1,0:T(8,128)(2,1)S(1)}, bf16[8,3712]{1,0:T(8,128)(2,1)S(1)}, u32[]{:S(2)}, u32[]{:S(2)}) collective-permute-start(bf16[8,3712]{1,0:T(8,128)(2,1)S(1)} %pad_maximum_fusion.3), channel_id=1, source_target_pairs={{0,504},{8,496},{16,488},{24,480},{32,472},{40,464},{48,456},{56,4... | collective-permute-start | bytes 178184 | tf_op jit(solution)/shard_map/ppermute | solution.py:191
  85.6 18.8 %collective-permute-start.13 = (bf16[16,3584]{1,0:T(8,128)(2,1)S(1)}, bf16[16,3584]{1,0:T(8,128)(2,1)S(1)}, u32[]{:S(2)}, u32[]{:S(2)}) collective-permute-start(bf16[16,3584]{1,0:T(8,128)(2,1)S(1)} %add_convert_fusion.1), channel_id=1, source_target_pairs={{8,0},{16,8},{24,16},{32,24},{40,32},{48,40},{56,48},{64,56},{72,6... | collective-permute-start | bytes 344072 | tf_op jit(solution)/shard_map/ppermute | solution.py:271
  90.5 14.0 %copy-start.6 = (bf16[1,8,3584]{2,1,0:T(8,128)(2,1)S(1)}, bf16[1,8,3584]{2,1,0:T(8,128)(2,1)}, u32[]{:S(2)}) copy-start(bf16[1,8,3584]{2,1,0:T(8,128)(2,1)} %param.19) | copy-start | bytes 172036
  90.5 14.0 %copy-start.7 = (bf16[1,8,3584]{2,1,0:T(8,128)(2,1)S(1)}, bf16[1,8,3584]{2,1,0:T(8,128)(2,1)}, u32[]{:S(2)}) copy-start(bf16[1,8,3584]{2,1,0:T(8,128)(2,1)} %param.18) | copy-start | bytes 172036
  90.5 22.3 %copy-start.4 = (bf16[1,32,3584]{2,1,0:T(8,128)(2,1)S(1)}, bf16[1,32,3584]{2,1,0:T(8,128)(2,1)}, u32[]{:S(2)}) copy-start(bf16[1,32,3584]{2,1,0:T(8,128)(2,1)} %param.23) | copy-start | bytes 688132
  90.5 15.9 %collective-permute-start.19 = (bf16[16,3712]{1,0:T(8,128)(2,1)S(1)}, bf16[16,3712]{1,0:T(8,128)(2,1)S(1)}, u32[]{:S(2)}, u32[]{:S(2)}) collective-permute-start(bf16[16,3712]{1,0:T(8,128)(2,1)S(1)} %pad_maximum_fusion.refs_8_), channel_id=1, source_target_pairs={{2,0},{3,1},{4,2},{5,3},{6,4},{7,5},{0,6},{1,7},{10,8},{11,9},{12,... | collective-permute-start | bytes 356360 | tf_op jit(solution)/shard_map/ppermute | solution.py:195
  96.6 13.1 %collective-permute-start.20 = (bf16[16,3712]{1,0:T(8,128)(2,1)S(1)}, bf16[16,3712]{1,0:T(8,128)(2,1)S(1)}, u32[]{:S(2)}, u32[]{:S(2)}) collective-permute-start(bf16[16,3712]{1,0:T(8,128)(2,1)S(1)} %pad_maximum_fusion.refs_8_), channel_id=1, source_target_pairs={{4,0},{5,1},{6,2},{7,3},{0,4},{1,5},{2,6},{3,7},{12,8},{13,9},{14,... | collective-permute-start | bytes 356360 | tf_op jit(solution)/shard_map/ppermute | solution.py:195
  98.6 14.1 %collective-permute-start.21 = (bf16[16,3712]{1,0:T(8,128)(2,1)S(1)}, bf16[16,3712]{1,0:T(8,128)(2,1)S(1)}, u32[]{:S(2)}, u32[]{:S(2)}) collective-permute-start(bf16[16,3712]{1,0:T(8,128)(2,1)S(1)} %pad_maximum_fusion.refs_8_), channel_id=1, source_target_pairs={{6,0},{7,1},{0,2},{1,3},{2,4},{3,5},{4,6},{5,7},{14,8},{15,9},{8,1... | collective-permute-start | bytes 356360 | tf_op jit(solution)/shard_map/ppermute | solution.py:195
  104.4 10.2 %collective-permute-start.14 = (bf16[16,3584]{1,0:T(8,128)(2,1)S(1)}, bf16[16,3584]{1,0:T(8,128)(2,1)S(1)}, u32[]{:S(2)}, u32[]{:S(2)}) collective-permute-start(bf16[16,3584]{1,0:T(8,128)(2,1)S(1)} %maximum_select_fusion.refs_0_), channel_id=1, source_target_pairs={{2,0},{3,1},{4,2},{5,3},{6,4},{7,5},{0,6},{1,7},{10,8},{11,9},{12,... | collective-permute-start | bytes 344072 | tf_op jit(solution)/shard_map/ppermute | solution.py:195
  106.4 12.2 %collective-permute-start.15 = (bf16[16,3584]{1,0:T(8,128)(2,1)S(1)}, bf16[16,3584]{1,0:T(8,128)(2,1)S(1)}, u32[]{:S(2)}, u32[]{:S(2)}) collective-permute-start(bf16[16,3584]{1,0:T(8,128)(2,1)S(1)} %maximum_select_fusion.refs_0_), channel_id=1, source_target_pairs={{4,0},{5,1},{6,2},{7,3},{0,4},{1,5},{2,6},{3,7},{12,8},{13,9},{14,... | collective-permute-start | bytes 344072 | tf_op jit(solution)/shard_map/ppermute | solution.py:195
  109.7 8.8 %collective-permute-start.16 = (bf16[16,3584]{1,0:T(8,128)(2,1)S(1)}, bf16[16,3584]{1,0:T(8,128)(2,1)S(1)}, u32[]{:S(2)}, u32[]{:S(2)}) collective-permute-start(bf16[16,3584]{1,0:T(8,128)(2,1)S(1)} %maximum_select_fusion.refs_0_), channel_id=1, source_target_pairs={{6,0},{7,1},{0,2},{1,3},{2,4},{3,5},{4,6},{5,7},{14,8},{15,9},{8,1... | collective-permute-start | bytes 344072 | tf_op jit(solution)/shard_map/ppermute | solution.py:195
  112.8 5.8 %copy-start.2 = (bf16[1,3584,128]{2,1,0:T(8,128)(2,1)S(1)}, bf16[1,3584,128]{2,1,0:T(8,128)(2,1)}, u32[]{:S(2)}) copy-start(bf16[1,3584,128]{2,1,0:T(8,128)(2,1)} %param.21) | copy-start | bytes 2752516
  121.9 25.2 %collective-permute-start.23 = (bf16[16,3584]{1,0:T(8,128)(2,1)S(1)}, bf16[16,3584]{1,0:T(8,128)(2,1)S(1)}, u32[]{:S(2)}, u32[]{:S(2)}) collective-permute-start(bf16[16,3584]{1,0:T(8,128)(2,1)S(1)} %get-tuple-element.29), channel_id=1, source_target_pairs={{6,0},{7,1},{0,2},{1,3},{2,4},{3,5},{4,6},{5,7},{14,8},{15,9},{8,1... | collective-permute-start | bytes 344072 | tf_op jit(solution)/shard_map/ppermute | solution.py:195
  123.8 23.3 %collective-permute-start.24 = (bf16[16,3584]{1,0:T(8,128)(2,1)S(1)}, bf16[16,3584]{1,0:T(8,128)(2,1)S(1)}, u32[]{:S(2)}, u32[]{:S(2)}) collective-permute-start(bf16[16,3584]{1,0:T(8,128)(2,1)S(1)} %get-tuple-element.30), channel_id=1, source_target_pairs={{4,0},{5,1},{6,2},{7,3},{0,4},{1,5},{2,6},{3,7},{12,8},{13,9},{14,... | collective-permute-start | bytes 344072 | tf_op jit(solution)/shard_map/ppermute | solution.py:195
  127.6 19.5 %collective-permute-start.25 = (bf16[16,3584]{1,0:T(8,128)(2,1)S(1)}, bf16[16,3584]{1,0:T(8,128)(2,1)S(1)}, u32[]{:S(2)}, u32[]{:S(2)}) collective-permute-start(bf16[16,3584]{1,0:T(8,128)(2,1)S(1)} %get-tuple-element.31), channel_id=1, source_target_pairs={{2,0},{3,1},{4,2},{5,3},{6,4},{7,5},{0,6},{1,7},{10,8},{11,9},{12,... | collective-permute-start | bytes 344072 | tf_op jit(solution)/shard_map/ppermute | solution.py:195
  131.5 5.9 %collective-permute-start.27 = (f32[8,256]{1,0:T(8,128)S(1)}, f32[8,256]{1,0:T(8,128)S(1)}, u32[]{:S(2)}, u32[]{:S(2)}) collective-permute-start(f32[8,256]{1,0:T(8,128)S(1)} %get-tuple-element.34.refs_14_), channel_id=1, source_target_pairs={{2,0},{3,1},{4,2},{5,3},{6,4},{7,5},{0,6},{1,7},{10,8},{11,9},{12,... | collective-permute-start | bytes 24584 | tf_op jit(solution)/shard_map/ppermute | solution.py:195
  134.0 7.3 %collective-permute-start.28 = (f32[8,256]{1,0:T(8,128)S(1)}, f32[8,256]{1,0:T(8,128)S(1)}, u32[]{:S(2)}, u32[]{:S(2)}) collective-permute-start(f32[8,256]{1,0:T(8,128)S(1)} %get-tuple-element.34.refs_14_), channel_id=1, source_target_pairs={{4,0},{5,1},{6,2},{7,3},{0,4},{1,5},{2,6},{3,7},{12,8},{13,9},{14,... | collective-permute-start | bytes 24584 | tf_op jit(solution)/shard_map/ppermute | solution.py:195
  137.3 7.3 %collective-permute-start.29 = (f32[8,256]{1,0:T(8,128)S(1)}, f32[8,256]{1,0:T(8,128)S(1)}, u32[]{:S(2)}, u32[]{:S(2)}) collective-permute-start(f32[8,256]{1,0:T(8,128)S(1)} %get-tuple-element.34.refs_14_), channel_id=1, source_target_pairs={{6,0},{7,1},{0,2},{1,3},{2,4},{3,5},{4,6},{5,7},{14,8},{15,9},{8,1... | collective-permute-start | bytes 24584 | tf_op jit(solution)/shard_map/ppermute | solution.py:195
  145.2 14.9 %collective-permute-start.30 = (f32[32,3584]{1,0:T(8,128)S(1)}, f32[32,3584]{1,0:T(8,128)S(1)}, u32[]{:S(2)}, u32[]{:S(2)}) collective-permute-start(f32[32,3584]{1,0:T(8,128)S(1)} %get-tuple-element.36), channel_id=1, source_target_pairs={{0,1},{1,0},{2,3},{3,2},{4,5},{5,4},{6,7},{7,6},{8,9},{9,8},{10,11... | collective-permute-start | bytes 1376264 | tf_op jit(solution)/shard_map/ppermute | solution.py:186
  147.8 17.0 %collective-permute-start.26 = (bf16[8,3584]{1,0:T(8,128)(2,1)S(1)}, bf16[8,3584]{1,0:T(8,128)(2,1)S(1)}, u32[]{:S(2)}, u32[]{:S(2)}) collective-permute-start(bf16[8,3584]{1,0:T(8,128)(2,1)S(1)} %get-tuple-element.37), channel_id=1, source_target_pairs={{0,504},{8,496},{16,488},{24,480},{32,472},{40,464},{48,456},{56,4... | collective-permute-start | bytes 172040 | tf_op jit(solution)/shard_map/ppermute | solution.py:191

commit v2 on v1

v2 whole, which is shorter than its diff:
```python
import functools

import jax
import jax.numpy as jnp
from jax import lax
from jax.experimental import pallas as pl
from jax.experimental.pallas import tpu as pltpu
from jax.sharding import PartitionSpec as P

D = 3584
HID = 128
EXPERTS = 256
OWN = 32
TOKENS = 64
TOPK = 8
ROWS = 8
CHIPS = 4
IDCOLS = 128
z_weight = 0.01
balance_weight = 1.0
F32 = jnp.float32
BF16 = jnp.bfloat16
VMEM_LIMIT = 48 * 1024 * 1024


def dot(lhs, rhs, lhs_dim, rhs_dim):
    return lax.dot_general(
        lhs, rhs, (((lhs_dim,), (rhs_dim,)), ((), ())), preferred_element_type=F32
    )


def call(body, out_shape, scratch, args, flops):
    spec = pl.BlockSpec(memory_space=pltpu.VMEM)
    total = sum(a.size * a.dtype.itemsize for a in args)
    return pl.pallas_call(
        body,
        out_shape=out_shape,
        in_specs=[spec] * len(args),
        out_specs=[spec] * len(out_shape),
        scratch_shapes=scratch,
        compiler_params=pltpu.CompilerParams(vmem_limit_bytes=VMEM_LIMIT),
        cost_estimate=pl.CostEstimate(flops=flops, bytes_accessed=total, transcendentals=0),
    )(*args)


def backward_terms(hidden, gate, up, gates, ups, out):
    d_gate, d_up = [], []
    for h, g, u in zip(hidden, gate, up):
        q = jax.nn.sigmoid(g)
        d_gate.append((h * u * q * (1.0 + g * (1.0 - q))).astype(BF16))
        d_up.append((h * g * q).astype(BF16))
    width = 512
    for low in range(0, D, width):
        cols = pl.ds(low, width)
        total = dot(d_gate[0], gates[0][cols, :], 1, 1)
        total += dot(d_gate[1], gates[1][cols, :], 1, 1)
        total += dot(d_up[0], ups[0][cols, :], 1, 1)
        total += dot(d_up[1], ups[1][cols, :], 1, 1)
        out[:, cols] = total.astype(BF16)


def first_tick_kernel(*refs):
    streams, weights, out, held = refs[:2], refs[2:8], refs[8], refs[9]
    gates, ups, downs = weights[0:2], weights[2:4], weights[4:6]
    for s in range(2):
        held[pl.ds(64 * s, 64), :] = streams[s][...]
    rows = held[...]

    def pick(value, offset):
        return jnp.concatenate(
            [
                value[64 * s + 16 * k + offset : 64 * s + 16 * k + offset + 8]
                for k in range(CHIPS)
                for s in range(2)
            ],
            axis=0,
        )

    gate = [pick(dot(rows, w[...], 1, 0), 0) for w in gates]
    up = [pick(dot(rows, w[...], 1, 0), 0) for w in ups]
    hidden = [pick(dot(rows, w[...], 1, 1), 8) for w in downs]
    backward_terms(hidden, gate, up, gates, ups, out)


def second_tick_kernel(*refs):
    grads, pre, weights, out = refs[0], refs[1:5], refs[5:11], refs[11]
    gates, ups, downs = weights[0:2], weights[2:4], weights[4:6]
    rows = grads[...]
    hidden = [dot(rows, w[...], 1, 1) for w in downs]
    gate = [pre[0][...], pre[1][...]]
    up = [pre[2][...], pre[3][...]]
    backward_terms(hidden, gate, up, gates, ups, out)


def forward_kernel(*refs):
    first_a, first_b, second = refs[0:3]
    gates, ups, routers = refs[3:5], refs[5:7], refs[7:9]
    base, pre = refs[9], refs[10:14]
    expo_ref, share_ref, stats_ref = refs[14:17]
    held0, ids_ref = refs[17:19]
    held0[0:64, :] = first_a[...]
    held0[64:128, :] = first_b[...]
    ids_ref[0:64, :] = second[:, D : D + IDCOLS].astype(F32)
    ids_ref[64:128, :] = jnp.full((64, IDCOLS), -1.0, F32)
    rows0, rows1 = held0[...], second[:, 0:D]
    for w, out in zip((*gates, *ups), pre):
        out[...] = dot(rows1, w[...], 1, 0)
    logits = jnp.concatenate(
        [
            jnp.concatenate([dot(r[...], rows, 1, 1) for r in routers], axis=0)
            for rows in (rows0, jnp.concatenate([rows1, rows1], axis=0))
        ],
        axis=1,
    )
    ids = ids_ref[...].T
    experts = base[:, 0:1]
    stream_b = (lax.broadcasted_iota(jnp.int32, (2 * OWN, 128), 1) % 16) >= 8
    scale = EXPERTS / (TOKENS * TOPK)
    shares = []
    for tick in range(2):
        hits = jnp.zeros((2 * OWN, 128), F32)
        for core in range(2):
            for j in range(TOPK):
                slot = 16 * core + 8 * tick + j
                hits += (experts == ids[slot : slot + 1, :]).astype(F32)
        count_a = jnp.sum(jnp.where(stream_b, 0.0, hits), axis=1, keepdims=True)
        count_b = jnp.sum(jnp.where(stream_b, hits, 0.0), axis=1, keepdims=True)
        shares.append((count_a * scale, count_b * scale))
    column = lax.broadcasted_iota(jnp.int32, (2 * OWN, 128), 1)
    share0 = jnp.where(column >= 64, shares[0][1], shares[0][0])
    share1 = jnp.where(stream_b, shares[1][1], shares[1][0])
    share = jnp.concatenate([share0, share1], axis=1)
    peak = jnp.max(logits, axis=0, keepdims=True)
    expo = jnp.exp(logits - peak)
    total = jnp.sum(expo, axis=0, keepdims=True)
    weighted = jnp.sum(expo * share, axis=0, keepdims=True)
    expo_ref[...] = expo
    share_ref[...] = share
    stats_ref[...] = jnp.concatenate(
        [peak, total, weighted, jnp.zeros((5, 256), F32)], axis=0
    )


def router_kernel(*refs):
    first_a, first_b, second, expo_ref, share_ref, all_stats, chip, own_out, other_out = refs
    mine = chip[...]
    stats = [all_stats[pl.ds(8 * k, 8), :] for k in range(CHIPS)]
    peaks = [s[0:1, :] for s in stats]
    peak = functools.reduce(jnp.maximum, peaks)
    factors = [jnp.exp(p - peak) for p in peaks]
    total = sum(s[1:2, :] * f for s, f in zip(stats, factors))
    weighted = sum(s[2:3, :] * f for s, f in zip(stats, factors))
    log_total = peak + jnp.log(total)
    mean_share = weighted / total
    own_factor = sum(jnp.where(mine == k, f, 0.0) for k, f in enumerate(factors))
    probs = expo_ref[...] * (own_factor / total)
    slopes = (
        2.0 * z_weight * log_total - balance_weight * mean_share + balance_weight * share_ref[...]
    ) * probs
    column = lax.broadcasted_iota(jnp.int32, (2 * OWN, 128), 1)
    slopes0 = jnp.where((column % 16) < 8, slopes[:, 0:128], 0.0).astype(BF16)
    slopes1 = slopes[:, 128:192].astype(BF16)
    width = 512
    for low in range(0, D, width):
        cols = pl.ds(low, width)
        part = dot(slopes0[:, 0:64], first_a[:, cols], 1, 0)
        part += dot(slopes0[:, 64:128], first_b[:, cols], 1, 0)
        part += dot(slopes1, second[:, cols], 1, 0)
        own_out[:, cols] = part[0:OWN]
        other_out[:, cols] = part[OWN:]


def swapped(value):
    return lax.ppermute(value, "expert", [(e, e ^ 1) for e in range(8)])


def mirrored(value):
    count = lax.axis_size("pipe")
    return lax.ppermute(value, "pipe", [(i, count - 1 - i) for i in range(count)])


def exchanged(blocks):
    return lax.all_to_all(
        blocks, "expert", split_axis=0, concat_axis=0, tiled=True,
        axis_index_groups=[[0, 2, 4, 6], [1, 3, 5, 7]],
    )


def spread(value):
    return exchanged(jnp.concatenate([value] * CHIPS, axis=0))


def shards(
    stash_a, stash_b, ids_a, ids_b, arriving_a, arriving_b, head_a, head_b,
    w_gate, w_up, w_down, router,
):
    stash_a, stash_b, ids_a, ids_b = stash_a[0], stash_b[0], ids_a[0], ids_b[0]
    arriving_a, arriving_b = arriving_a[0], arriving_b[0]
    w_gate, w_up, w_down, router = w_gate[0], w_up[0], w_down[0], router[0]
    section = lax.axis_index("pipe")
    top = lax.axis_size("pipe") - 1
    member = lax.axis_index("expert")

    block_b = mirrored(jnp.concatenate([stash_b[0], arriving_b], axis=0))
    block_a = jnp.concatenate([stash_a[0], arriving_a], axis=0)
    first_a = spread(block_a)
    other_gate, other_up, other_down, other_router = (
        swapped(w_gate), swapped(w_up), swapped(w_down), swapped(router)
    )
    gates, ups = [w_gate, other_gate], [w_up, other_up]
    downs, routers = [w_down, other_down], [router, other_router]

    def id_rows(ids):
        return jnp.concatenate([ids[0], ids[1]], axis=1)

    ids = jnp.concatenate([id_rows(ids_a), id_rows(ids_b)], axis=0).astype(BF16)
    ids = jnp.pad(ids, ((0, 0), (0, 112)), constant_values=-1)
    ids_other = swapped(ids)
    ids = jnp.concatenate([ids[:, :16], ids_other[:, :16], ids[:, 32:]], axis=1)
    later_b = mirrored(jnp.concatenate([stash_b[1], ids[8:]], axis=1))
    later_a = jnp.concatenate([stash_a[1], ids[:8]], axis=1)
    first_b = spread(block_b)
    later = jnp.concatenate([later_a, later_b], axis=0)
    sums = [jax.ShapeDtypeStruct((64, D), BF16)]
    (terms,) = call(
        first_tick_kernel, sums, [pltpu.VMEM((128, D), BF16)],
        [first_a, first_b] + gates + ups + downs, 2 * 128 * D * 128 * 10,
    )
    base = jnp.concatenate(
        [OWN * member + jnp.arange(OWN), OWN * (member ^ 1) + jnp.arange(OWN)]
    ).astype(F32)
    base = jnp.broadcast_to(base[:, None], (2 * OWN, 128))

    def emitted(grads, parts):
        total = grads.astype(F32)
        for k in range(CHIPS):
            total = total + parts[16 * k : 16 * k + 16].astype(F32)
        return total.astype(BF16)

    grads = jnp.concatenate([block_a[8:], block_b[8:]], axis=0)
    out = emitted(grads, exchanged(terms))
    out, later = lax.optimization_barrier((out, later))
    moved = lax.ppermute(out, "pipe", [(i, i - 1) for i in range(1, top + 1)])
    second = spread(later)
    head = jnp.concatenate([head_a[0], head_b[0]], axis=0)
    grads = jnp.where(section == top, head, moved)
    all_grads = spread(grads)
    pre = [jax.ShapeDtypeStruct((64, HID), F32)] * 4
    *pre, expo, share, stats = call(
        forward_kernel,
        pre
        + [
            jax.ShapeDtypeStruct((2 * OWN, 256), F32),
            jax.ShapeDtypeStruct((2 * OWN, 256), F32),
            jax.ShapeDtypeStruct((8, 256), F32),
        ],
        [pltpu.VMEM((128, D), BF16), pltpu.VMEM((128, IDCOLS), F32)],
        [first_a, first_b, second] + gates + ups + routers + [base], 2 * 128 * D * 128 * 4,
    )
    (terms,) = call(
        second_tick_kernel, sums, [],
        [all_grads] + pre + gates + ups + downs, 2 * 64 * D * 128 * 6,
    )
    terms, stats = lax.optimization_barrier((terms, stats))
    parts = exchanged(terms)
    chip = jnp.full((1, 256), member // 2, jnp.int32)
    own, other = call(
        router_kernel, [jax.ShapeDtypeStruct((OWN, D), F32)] * 2, [],
        [first_a, first_b, second, expo, share, spread(stats), chip], 2 * 192 * D * 64,
    )
    router_grad = own + swapped(other)
    out = emitted(grads, parts)
    return out[None, :8], mirrored(out[8:])[None], router_grad[None]


def solution(mesh):
    placed = (
        P("pipe", None, "expert", None),
        P("pipe", None, "expert", None),
        P("pipe", None, "expert", None),
        P("pipe", None, "expert", None),
        P("pipe", "expert", None),
        P("pipe", "expert", None),
        P(None, "expert", None),
        P(None, "expert", None),
        P("pipe", None, "expert"),
        P("pipe", None, "expert"),
        P("pipe", "expert", None),
        P("pipe", "expert", None),
    )
    return jax.shard_map(
        shards,
        mesh=mesh,
        in_specs=placed,
        out_specs=(P("pipe", "expert", None), P("pipe", "expert", None), P("pipe", "expert", None)),
        check_vma=False,
    )
```

time: 168 us -> 182 us (1.083)
  starting transfers between devices: 114 us -> 86.6 us
  local copies, waits for them, and re-layouts: 5.52 us -> 22.3 us
  waiting for transfers between devices: 31.7 us -> 42.6 us
  blocking collectives: 0 us -> 8 us
  other arithmetic: 3.7 us -> 7.53 us
  Pallas kernels: 9.77 us -> 12.5 us
    ppermute x21 -> x0, starting transfers between devices: 62.9 us -> none  [from_chip(): lax.ppermute(value, 'expert', [((e + 2 * k) % 8, e) for e in range(8)])]
    all_to_all x0 -> x6, starting transfers between devices: none -> 32.3 us  [exchanged(): lax.all_to_all(blocks, 'expert', split_axis=0, concat_axis=0, tiled=True,...]
    ppermute x21 -> x0, waiting for transfers between devices: 21.8 us -> none  [from_chip(): lax.ppermute(value, 'expert', [((e + 2 * k) % 8, e) for e in range(8)])]
    all_to_all x0 -> x6, waiting for transfers between devices: none -> 18.9 us  [exchanged(): lax.all_to_all(blocks, 'expert', split_axis=0, concat_axis=0, tiled=True,...]
    unnamed x19 -> x66, local copies, waits for them, and re-layouts: 3.01 us -> 19.6 us
    ppermute x3, waiting for transfers between devices: 6.96 us -> 17.3 us  [mirrored(): lax.ppermute(value, 'pipe', [(i, count - 1 - i) for i in range(count)])]
    all_to_all x0 -> x1, blocking collectives: none -> 8 us  [exchanged(): lax.all_to_all(blocks, 'expert', split_axis=0, concat_axis=0, tiled=True,...]
    ppermute x3, starting transfers between devices: 36.6 us -> 39.8 us  [mirrored(): lax.ppermute(value, 'pipe', [(i, count - 1 - i) for i in range(count)])]
  transfers between devices with their start and end apart: 31 -> 16, of which waited for: 10 -> 10; matrix products, arithmetic and copies ran while one was open for 3% -> 5% of each run, Pallas kernels for 4% -> 3%
where the time goes in v2:
time: 182 us; the launch traced here: 181 us
  starting transfers between devices  86.6 us (48%)
  waiting for transfers between devices  42.6 us (23%)
  local copies, waits for them, and re-layouts  22.3 us (12%)
  Pallas kernels  12.5 us (7%)
  blocking collectives  8 us (4%)
  other arithmetic  7.53 us (4%)
    ppermute x3, starting transfers between devices, mirrored(): lax.ppermute(value, 'pipe', [(i, count - 1 - i) for i in range(count)])  39.8 us
    all_to_all x6, starting transfers between devices, exchanged(): lax.all_to_all(blocks, 'expert', split_axis=0, concat_axis=0, tiled=True,...  32.3 us
    unnamed x66, local copies, waits for them, and re-layouts  19.6 us
    all_to_all x6, waiting for transfers between devices, exchanged(): lax.all_to_all(blocks, 'expert', split_axis=0, concat_axis=0, tiled=True,...  18.9 us
    ppermute x3, waiting for transfers between devices, mirrored(): lax.ppermute(value, 'pipe', [(i, count - 1 - i) for i in range(count)])  17.3 us
    ppermute x6, starting transfers between devices, swapped(): return lax.ppermute(value, 'expert', [(e, e ^ 1) for e in range(8)])  12.6 us
    pallas_call x4, Pallas kernels, call(): pl.pallas_call(body, out_shape=out_shape, in_specs=[spec] * len(args), ou...  12.5 us
    all_to_all x1, blocking collectives, exchanged(): lax.all_to_all(blocks, 'expert', split_axis=0, concat_axis=0, tiled=True,...  8 us
  transfers between devices with their start and end apart: 16, of which 10 were waited for; matrix products, arithmetic and copies ran while one was open for 5% of the time, Pallas kernels for 3%

profile of v2, /device:TPU:6, one launch (start us, length us, event | category | flops | bytes accessed | tf_op | source)
XLA Modules:
  0.0 180.6 jit_solution(14168483398428666070)
XLA Ops:
  0.6 1.5 bitcast_dynamic-update-slice_fusion.2
  6.6 6.0 %all-to-all-start = ((bf16[4,16,3584]{2,1,0:T(8,128)(2,1)}), bf16[4,16,3584]{2,1,0:T(8,128)(2,1)S(1)}, u32[]{:S(2)}, u32[]{:S(2)}) async-start(bf16[4,16,3584]{2,1,0:T(8,128)(2,1)} %bitcast.6), calls=%async_computation | async-start | bytes 917504 | tf_op jit(solution)/shard_map/all_to_all | solution.py:183
  13.2 12.8 %collective-permute-start = (bf16[16,3584]{1,0:T(8,128)(2,1)S(1)}, bf16[16,3584]{1,0:T(8,128)(2,1)S(1)}, u32[]{:S(2)}, u32[]{:S(2)}) collective-permute-start(bf16[16,3584]{1,0:T(8,128)(2,1)S(1)} %pad_maximum_fusion.4), channel_id=1, source_target_pairs={{0,504},{8,496},{16,488},{24,480},{32,472},{40,464},{48,456},{56,4... | collective-permute-start | bytes 344072 | tf_op jit(solution)/shard_map/ppermute | solution.py:179
  26.1 9.8 %collective-permute-done = bf16[16,3584]{1,0:T(8,128)(2,1)S(1)} collective-permute-done((bf16[16,3584]{1,0:T(8,128)(2,1)S(1)}, bf16[16,3584]{1,0:T(8,128)(2,1)S(1)}, u32[]{:S(2)}, u32[]{:S(2)}) %collective-permute-start) | collective-permute-done | bytes 114720 | tf_op jit(solution)/shard_map/ppermute | solution.py:179
  35.9 0.8 pad_maximum_fusion.1
  36.7 6.3 %all-to-all-start.1 = ((bf16[4,16,3584]{2,1,0:T(8,128)(2,1)}), bf16[4,16,3584]{2,1,0:T(8,128)(2,1)}, u32[]{:S(2)}, u32[]{:S(2)}) async-start(bf16[4,16,3584]{2,1,0:T(8,128)(2,1)} %bitcast.8), calls=%async_computation.1 | async-start | bytes 917504 | tf_op jit(solution)/shard_map/all_to_all | solution.py:183
  43.0 2.0 %collective-permute-start.1 = (bf16[3584,128]{1,0:T(8,128)(2,1)S(1)}, bf16[3584,128]{1,0:T(8,128)(2,1)S(1)}, u32[]{:S(2)}, u32[]{:S(2)}) collective-permute-start(bf16[3584,128]{1,0:T(8,128)(2,1)S(1)} %bitcast.90), channel_id=1, source_target_pairs={{0,1},{1,0},{2,3},{3,2},{4,5},{5,4},{6,7},{7,6},{8,9},{9,8},{10,11... | collective-permute-start | bytes 2752520 | tf_op jit(solution)/shard_map/ppermute | solution.py:174
  45.0 2.4 %collective-permute-start.2 = (bf16[3584,128]{1,0:T(8,128)(2,1)S(1)}, bf16[3584,128]{1,0:T(8,128)(2,1)S(1)}, u32[]{:S(2)}, u32[]{:S(2)}) collective-permute-start(bf16[3584,128]{1,0:T(8,128)(2,1)S(1)} %bitcast.94), channel_id=1, source_target_pairs={{0,1},{1,0},{2,3},{3,2},{4,5},{5,4},{6,7},{7,6},{8,9},{9,8},{10,11... | collective-permute-start | bytes 2752520 | tf_op jit(solution)/shard_map/ppermute | solution.py:174
  47.4 1.9 %collective-permute-start.3 = (bf16[128,3584]{1,0:T(8,128)(2,1)}, bf16[128,3584]{1,0:T(8,128)(2,1)}, u32[]{:S(2)}, u32[]{:S(2)}) collective-permute-start(bf16[128,3584]{1,0:T(8,128)(2,1)} %bitcast.101), channel_id=1, source_target_pairs={{0,1},{1,0},{2,3},{3,2},{4,5},{5,4},{6,7},{7,6},{8,9},{9,8},{10,11... | collective-permute-start | bytes 2752520 | tf_op jit(solution)/shard_map/ppermute | solution.py:174
  49.5 2.4 %collective-permute-start.4 = (bf16[16,128]{1,0:T(8,128)(2,1)S(1)}, bf16[16,128]{1,0:T(8,128)(2,1)S(1)}, u32[]{:S(2)}, u32[]{:S(2)}) collective-permute-start(bf16[16,128]{1,0:T(8,128)(2,1)S(1)} %fusion.10), channel_id=1, source_target_pairs={{0,1},{1,0},{2,3},{3,2},{4,5},{5,4},{6,7},{7,6},{8,9},{9,8},{10,11... | collective-permute-start | bytes 12296 | tf_op jit(solution)/shard_map/ppermute | solution.py:174
  52.8 0.9 copy-done.2
  53.7 1.5 all-to-all-done.1
  55.3 1.2 copy-done.3
  56.4 1.2 copy-done.6
  57.6 4.2 %shard_map.139 = bf16[64,3584]{1,0:T(8,128)(2,1)S(1)} custom-call(bf16[64,3584]{1,0:T(8,128)(2,1)S(1)} %bitcast.98, bf16[64,3584]{1,0:T(8,128)(2,1)} %bitcast.9.refs_1_, bf16[3584,128]{1,0:T(8,128)(2,1)S(1)} %bitcast.91, bf16[3584,128]{1,0:T(8,128)(2,1)S(1)} %collective-permute-done.1.refs_3_.refs_4_.refs_6_, bf16[3584,128]{1,0:T(8,128)(2,1)S(1)} %bitcast.95, ...), custom_call_target="tpu_custom_call" | custom-call | flops 1174405120 | bytes 6422528 | tf_op jit(solution)/shard_map/pallas_call | solution.py:35
  61.9 0.8 copy-done.9
  62.6 4.1 %all-to-all-start.2 = ((bf16[4,16,3584]{2,1,0:T(8,128)(2,1)}), bf16[4,16,3584]{2,1,0:T(8,128)(2,1)}, u32[]{:S(2)}, u32[]{:S(2)}) async-start(bf16[4,16,3584]{2,1,0:T(8,128)(2,1)} %bitcast.105), calls=%async_computation.2 | async-start | bytes 917504 | tf_op jit(solution)/shard_map/all_to_all | solution.py:183
  66.8 0.8 pad_maximum_fusion.5
  67.6 10.7 %collective-permute-start.5 = (bf16[8,3712]{1,0:T(8,128)(2,1)S(1)}, bf16[8,3712]{1,0:T(8,128)(2,1)S(1)}, u32[]{:S(2)}, u32[]{:S(2)}) collective-permute-start(bf16[8,3712]{1,0:T(8,128)(2,1)S(1)} %pad_maximum_fusion.5), channel_id=1, source_target_pairs={{0,504},{8,496},{16,488},{24,480},{32,472},{40,464},{48,456},{56,4... | collective-permute-start | bytes 178184 | tf_op jit(solution)/shard_map/ppermute | solution.py:179
  78.4 6.2 %collective-permute-done.5 = bf16[8,3712]{1,0:T(8,128)(2,1)S(1)} collective-permute-done((bf16[8,3712]{1,0:T(8,128)(2,1)S(1)}, bf16[8,3712]{1,0:T(8,128)(2,1)S(1)}, u32[]{:S(2)}, u32[]{:S(2)}) %collective-permute-start.5) | collective-permute-done | bytes 59424 | tf_op jit(solution)/shard_map/ppermute | solution.py:179
  85.2 1.1 fusion.1
  86.3 1.9 %collective-permute-start.6 = (bf16[16,3584]{1,0:T(8,128)(2,1)S(1)}, bf16[16,3584]{1,0:T(8,128)(2,1)}, u32[]{:S(2)}, u32[]{:S(2)}) collective-permute-start(bf16[16,3584]{1,0:T(8,128)(2,1)S(1)} %fusion.1), channel_id=1, source_target_pairs={{8,0},{16,8},{24,16},{32,24},{40,32},{48,40},{56,48},{64,56},{72,6... | collective-permute-start | bytes 344072 | tf_op jit(solution)/shard_map/ppermute | solution.py:243
  88.3 0.8 pad_maximum_fusion
  89.1 6.9 %all-to-all-start.4 = ((bf16[4,16,3712]{2,1,0:T(8,128)(2,1)}), bf16[4,16,3712]{2,1,0:T(8,128)(2,1)}, u32[]{:S(2)}, u32[]{:S(2)}) async-start(bf16[4,16,3712]{2,1,0:T(8,128)(2,1)} %bitcast.109), calls=%async_computation.4 | async-start | bytes 950272 | tf_op jit(solution)/shard_map/all_to_all | solution.py:183
  96.0 4.1 %collective-permute-done.6 = bf16[16,3584]{1,0:T(8,128)(2,1)} collective-permute-done((bf16[16,3584]{1,0:T(8,128)(2,1)S(1)}, bf16[16,3584]{1,0:T(8,128)(2,1)}, u32[]{:S(2)}, u32[]{:S(2)}) %collective-permute-start.6) | collective-permute-done | bytes 114720 | tf_op jit(solution)/shard_map/ppermute | solution.py:243
  100.1 0.9 maximum_select_fusion
  101.7 0.8 pad_maximum_fusion.2
  102.5 5.7 %all-to-all-done.4 = bf16[4,16,3712]{2,1,0:T(8,128)(2,1)} async-done(((bf16[4,16,3712]{2,1,0:T(8,128)(2,1)}), bf16[4,16,3712]{2,1,0:T(8,128)(2,1)}, u32[]{:S(2)}, u32[]{:S(2)}) %all-to-all-start.4) | async-done | bytes 475168 | tf_op jit(solution)/shard_map/all_to_all | solution.py:183
  108.2 4.7 %all-to-all-start.3 = ((bf16[4,16,3584]{2,1,0:T(8,128)(2,1)}), bf16[4,16,3584]{2,1,0:T(8,128)(2,1)}, u32[]{:S(2)}, u32[]{:S(2)}) async-start(bf16[4,16,3584]{2,1,0:T(8,128)(2,1)} %bitcast.110), calls=%async_computation.3 | async-start | bytes 917504 | tf_op jit(solution)/shard_map/all_to_all | solution.py:183
  113.0 1.9 %collective-permute-start.7 = (bf16[32,3584]{1,0:T(8,128)(2,1)S(1)}, bf16[32,3584]{1,0:T(8,128)(2,1)}, u32[]{:S(2)}, u32[]{:S(2)}) collective-permute-start(bf16[32,3584]{1,0:T(8,128)(2,1)S(1)} %bitcast.106), channel_id=1, source_target_pairs={{0,1},{1,0},{2,3},{3,2},{4,5},{5,4},{6,7},{7,6},{8,9},{9,8},{10,11... | collective-permute-start | bytes 688136 | tf_op jit(solution)/shard_map/ppermute | solution.py:174
  115.0 1.5 collective-permute-done.7.refs_8_
  116.6 1.2 copy-done.4
  117.7 3.1 %shard_map.140 = (f32[64,128]{1,0:T(8,128)S(1)}, f32[64,128]{1,0:T(8,128)S(1)}, f32[64,128]{1,0:T(8,128)S(1)}, f32[64,128]{1,0:T(8,128)S(1)}, f32[64,256]{1,0:T(...) custom-call(bf16[64,3584]{1,0:T(8,128)(2,1)S(1)} %bitcast.99, bf16[64,3584]{1,0:T(8,128)(2,1)} %bitcast.9.refs_1_, ...), custom_call_target="tpu_custom_call" | custom-call | flops 469762048 | bytes 5554176 | tf_op jit(solution)/shard_map/pallas_call | solution.py:35
  123.3 3.4 %all-to-all-done.3 = bf16[4,16,3584]{2,1,0:T(8,128)(2,1)} async-done(((bf16[4,16,3584]{2,1,0:T(8,128)(2,1)}), bf16[4,16,3584]{2,1,0:T(8,128)(2,1)}, u32[]{:S(2)}, u32[]{:S(2)}) %all-to-all-start.3) | async-done | bytes 458784 | tf_op jit(solution)/shard_map/all_to_all | solution.py:183
  126.7 1.2 copy-done.5
  127.9 1.2 copy-done.7
  129.0 0.8 copy-done.14
  131.3 3.4 %shard_map.141 = bf16[64,3584]{1,0:T(8,128)(2,1)S(1)} custom-call(bf16[64,3584]{1,0:T(8,128)(2,1)} %bitcast.25.refs_0_, f32[64,128]{1,0:T(8,128)S(1)} %get-tuple-element.18.refs_1_, f32[64,128]{1,0:T(8,128)S(1)} %copy-done.14, f32[64,128]{1,0:T(8,128)S(1)} %copy-done.16, f32[64,128]{1,0:T(8,128)S(1)} %copy-done.18, bf16[3584,128]{1,0:T(8,128)(2,1)S(1)} %bitcast.93, ...), custom_call_target="tpu_custom_call" | custom-call | flops 352321536 | bytes 6094848 | tf_op jit(solution)/shard_map/pallas_call | solution.py:35
  134.7 0.8 copy-done.8
  135.5 8.0 %all_to_all.73 = f32[4,8,256]{2,1,0:T(8,128)S(1)} all-to-all(f32[4,8,256]{2,1,0:T(8,128)S(1)} %maximum_bitcast_fusion), channel_id=1, replica_groups={{0,2,4,6},{1,3,5,7},{8,10,12,14},{9,11,13,15},{16,18,20,22},{17,19,21,2..., dimensions={0} | all-to-all | bytes 65536 | tf_op jit(solution)/shard_map/all_to_all | solution.py:183
  143.5 4.3 %all-to-all-start.5 = ((bf16[4,16,3584]{2,1,0:T(8,128)(2,1)}), bf16[4,16,3584]{2,1,0:T(8,128)(2,1)}, u32[]{:S(2)}, u32[]{:S(2)}) async-start(bf16[4,16,3584]{2,1,0:T(8,128)(2,1)} %bitcast.104), calls=%async_computation.5 | async-start | bytes 917504 | tf_op jit(solution)/shard_map/all_to_all | solution.py:183
  147.8 1.8 shard_map.142
  149.6 1.9 %collective-permute-start.9 = (f32[32,3584]{1,0:T(8,128)S(1)}, f32[32,3584]{1,0:T(8,128)S(1)}, u32[]{:S(2)}, u32[]{:S(2)}) collective-permute-start(f32[32,3584]{1,0:T(8,128)S(1)} %get-tuple-element.28), channel_id=1, source_target_pairs={{0,1},{1,0},{2,3},{3,2},{4,5},{5,4},{6,7},{7,6},{8,9},{9,8},{10,11... | collective-permute-start | bytes 1376264 | tf_op jit(solution)/shard_map/ppermute | solution.py:174
  151.5 8.3 %all-to-all-done.5 = bf16[4,16,3584]{2,1,0:T(8,128)(2,1)} async-done(((bf16[4,16,3584]{2,1,0:T(8,128)(2,1)}), bf16[4,16,3584]{2,1,0:T(8,128)(2,1)}, u32[]{:S(2)}, u32[]{:S(2)}) %all-to-all-start.5) | async-done | bytes 458784 | tf_op jit(solution)/shard_map/all_to_all | solution.py:183
  159.8 1.1 fusion
  161.6 16.2 %collective-permute-start.8 = (bf16[8,3584]{1,0:T(8,128)(2,1)S(1)}, bf16[8,3584]{1,0:T(8,128)(2,1)S(1)}, u32[]{:S(2)}, u32[]{:S(2)}) collective-permute-start(bf16[8,3584]{1,0:T(8,128)(2,1)S(1)} %get-tuple-element.29), channel_id=1, source_target_pairs={{0,504},{8,496},{16,488},{24,480},{32,472},{40,464},{48,456},{56,4... | collective-permute-start | bytes 172040 | tf_op jit(solution)/shard_map/ppermute | solution.py:179
  177.8 0.8 add_bitcast_fusion
  178.6 1.3 collective-permute-done.8
  (83 shorter events, 12.7 us)
Async XLA Ops:
  0.6 1.5 copy-start.19
  0.6 2.2 %copy-start.22 = (bf16[1,2,8,3584]{3,2,1,0:T(8,128)(2,1)S(1)}, bf16[1,2,8,3584]{3,2,1,0:T(8,128)(2,1)}, u32[]{:S(2)}) copy-start(bf16[1,2,8,3584]{3,2,1,0:T(8,128)(2,1)} %param.12) | copy-start | bytes 344068
  6.6 6.0 %copy-start.23 = (bf16[1,2,8,3584]{3,2,1,0:T(8,128)(2,1)S(1)}, bf16[1,2,8,3584]{3,2,1,0:T(8,128)(2,1)}, u32[]{:S(2)}) copy-start(bf16[1,2,8,3584]{3,2,1,0:T(8,128)(2,1)} %param.13) | copy-start | bytes 344068
  6.6 6.7 %copy-start.24 = (bf16[1,8,3584]{2,1,0:T(8,128)(2,1)S(1)}, bf16[1,8,3584]{2,1,0:T(8,128)(2,1)}, u32[]{:S(2)}) copy-start(bf16[1,8,3584]{2,1,0:T(8,128)(2,1)} %param.17) | copy-start | bytes 172036
  6.6 30.1 %all-to-all-start = ((bf16[4,16,3584]{2,1,0:T(8,128)(2,1)}), bf16[4,16,3584]{2,1,0:T(8,128)(2,1)S(1)}, u32[]{:S(2)}, u32[]{:S(2)}) async-start(bf16[4,16,3584]{2,1,0:T(8,128)(2,1)} %bitcast.6), calls=%async_computation | async-start | bytes 917504 | tf_op jit(solution)/shard_map/all_to_all | solution.py:183
  12.6 32.4 %copy-start.1 = (bf16[1,3584,128]{2,1,0:T(8,128)(2,1)S(1)}, bf16[1,3584,128]{2,1,0:T(8,128)(2,1)}, u32[]{:S(2)}) copy-start(bf16[1,3584,128]{2,1,0:T(8,128)(2,1)} %param.21) | copy-start | bytes 2752516
  13.2 29.7 %copy-start = (bf16[1,3584,128]{2,1,0:T(8,128)(2,1)S(1)}, bf16[1,3584,128]{2,1,0:T(8,128)(2,1)}, u32[]{:S(2)}) copy-start(bf16[1,3584,128]{2,1,0:T(8,128)(2,1)} %param.20) | copy-start | bytes 2752516
  13.2 22.6 %collective-permute-start = (bf16[16,3584]{1,0:T(8,128)(2,1)S(1)}, bf16[16,3584]{1,0:T(8,128)(2,1)S(1)}, u32[]{:S(2)}, u32[]{:S(2)}) collective-permute-start(bf16[16,3584]{1,0:T(8,128)(2,1)S(1)} %pad_maximum_fusion.4), channel_id=1, source_target_pairs={{0,504},{8,496},{16,488},{24,480},{32,472},{40,464},{48,456},{56,4... | collective-permute-start | bytes 344072 | tf_op jit(solution)/shard_map/ppermute | solution.py:179
  36.7 12.7 %copy-start.27 = (s32[1,2,8,8]{3,2,1,0:T(8,128)S(1)}, s32[1,2,8,8]{3,2,1,0:T(8,128)}, u32[]{:S(2)}) copy-start(s32[1,2,8,8]{3,2,1,0:T(8,128)} %param.15) | copy-start | bytes 1540
  36.7 18.6 %all-to-all-start.1 = ((bf16[4,16,3584]{2,1,0:T(8,128)(2,1)}), bf16[4,16,3584]{2,1,0:T(8,128)(2,1)}, u32[]{:S(2)}, u32[]{:S(2)}) async-start(bf16[4,16,3584]{2,1,0:T(8,128)(2,1)} %bitcast.8), calls=%async_computation.1 | async-start | bytes 917504 | tf_op jit(solution)/shard_map/all_to_all | solution.py:183
  42.9 6.4 %copy-start.28 = (s32[1,2,8,8]{3,2,1,0:T(8,128)S(1)}, s32[1,2,8,8]{3,2,1,0:T(8,128)}, u32[]{:S(2)}) copy-start(s32[1,2,8,8]{3,2,1,0:T(8,128)} %param.14) | copy-start | bytes 1540
  43.0 9.8 %collective-permute-start.1 = (bf16[3584,128]{1,0:T(8,128)(2,1)S(1)}, bf16[3584,128]{1,0:T(8,128)(2,1)S(1)}, u32[]{:S(2)}, u32[]{:S(2)}) collective-permute-start(bf16[3584,128]{1,0:T(8,128)(2,1)S(1)} %bitcast.90), channel_id=1, source_target_pairs={{0,1},{1,0},{2,3},{3,2},{4,5},{5,4},{6,7},{7,6},{8,9},{9,8},{10,11... | collective-permute-start | bytes 2752520 | tf_op jit(solution)/shard_map/ppermute | solution.py:174
  45.0 7.8 %collective-permute-start.2 = (bf16[3584,128]{1,0:T(8,128)(2,1)S(1)}, bf16[3584,128]{1,0:T(8,128)(2,1)S(1)}, u32[]{:S(2)}, u32[]{:S(2)}) collective-permute-start(bf16[3584,128]{1,0:T(8,128)(2,1)S(1)} %bitcast.94), channel_id=1, source_target_pairs={{0,1},{1,0},{2,3},{3,2},{4,5},{5,4},{6,7},{7,6},{8,9},{9,8},{10,11... | collective-permute-start | bytes 2752520 | tf_op jit(solution)/shard_map/ppermute | solution.py:174
  47.4 6.3 %collective-permute-start.3 = (bf16[128,3584]{1,0:T(8,128)(2,1)}, bf16[128,3584]{1,0:T(8,128)(2,1)}, u32[]{:S(2)}, u32[]{:S(2)}) collective-permute-start(bf16[128,3584]{1,0:T(8,128)(2,1)} %bitcast.101), channel_id=1, source_target_pairs={{0,1},{1,0},{2,3},{3,2},{4,5},{5,4},{6,7},{7,6},{8,9},{9,8},{10,11... | collective-permute-start | bytes 2752520 | tf_op jit(solution)/shard_map/ppermute | solution.py:174
  49.5 3.2 %collective-permute-start.4 = (bf16[16,128]{1,0:T(8,128)(2,1)S(1)}, bf16[16,128]{1,0:T(8,128)(2,1)S(1)}, u32[]{:S(2)}, u32[]{:S(2)}) collective-permute-start(bf16[16,128]{1,0:T(8,128)(2,1)S(1)} %fusion.10), channel_id=1, source_target_pairs={{0,1},{1,0},{2,3},{3,2},{4,5},{5,4},{6,7},{7,6},{8,9},{9,8},{10,11... | collective-permute-start | bytes 12296 | tf_op jit(solution)/shard_map/ppermute | solution.py:174
  52.8 0.9 copy-start.2
  55.3 1.2 copy-start.3
  56.4 1.2 copy-start.6
  61.9 0.8 copy-start.9
  62.6 22.6 %all-to-all-start.2 = ((bf16[4,16,3584]{2,1,0:T(8,128)(2,1)}), bf16[4,16,3584]{2,1,0:T(8,128)(2,1)}, u32[]{:S(2)}, u32[]{:S(2)}) async-start(bf16[4,16,3584]{2,1,0:T(8,128)(2,1)} %bitcast.105), calls=%async_computation.2 | async-start | bytes 917504 | tf_op jit(solution)/shard_map/all_to_all | solution.py:183
  67.6 17.0 %collective-permute-start.5 = (bf16[8,3712]{1,0:T(8,128)(2,1)S(1)}, bf16[8,3712]{1,0:T(8,128)(2,1)S(1)}, u32[]{:S(2)}, u32[]{:S(2)}) collective-permute-start(bf16[8,3712]{1,0:T(8,128)(2,1)S(1)} %pad_maximum_fusion.5), channel_id=1, source_target_pairs={{0,504},{8,496},{16,488},{24,480},{32,472},{40,464},{48,456},{56,4... | collective-permute-start | bytes 178184 | tf_op jit(solution)/shard_map/ppermute | solution.py:179
  86.3 13.8 %collective-permute-start.6 = (bf16[16,3584]{1,0:T(8,128)(2,1)S(1)}, bf16[16,3584]{1,0:T(8,128)(2,1)}, u32[]{:S(2)}, u32[]{:S(2)}) collective-permute-start(bf16[16,3584]{1,0:T(8,128)(2,1)S(1)} %fusion.1), channel_id=1, source_target_pairs={{8,0},{16,8},{24,16},{32,24},{40,32},{48,40},{56,48},{64,56},{72,6... | collective-permute-start | bytes 344072 | tf_op jit(solution)/shard_map/ppermute | solution.py:243
  89.1 11.0 %copy-start.25 = (bf16[1,8,3584]{2,1,0:T(8,128)(2,1)S(1)}, bf16[1,8,3584]{2,1,0:T(8,128)(2,1)}, u32[]{:S(2)}) copy-start(bf16[1,8,3584]{2,1,0:T(8,128)(2,1)} %param.19) | copy-start | bytes 172036
  89.1 11.0 %copy-start.26 = (bf16[1,8,3584]{2,1,0:T(8,128)(2,1)S(1)}, bf16[1,8,3584]{2,1,0:T(8,128)(2,1)}, u32[]{:S(2)}) copy-start(bf16[1,8,3584]{2,1,0:T(8,128)(2,1)} %param.18) | copy-start | bytes 172036
  89.1 19.1 %all-to-all-start.4 = ((bf16[4,16,3712]{2,1,0:T(8,128)(2,1)}), bf16[4,16,3712]{2,1,0:T(8,128)(2,1)}, u32[]{:S(2)}, u32[]{:S(2)}) async-start(bf16[4,16,3712]{2,1,0:T(8,128)(2,1)} %bitcast.109), calls=%async_computation.4 | async-start | bytes 950272 | tf_op jit(solution)/shard_map/all_to_all | solution.py:183
  101.0 0.6 copy-start.20
  108.2 4.8 %copy-start.10 = (bf16[1,32,3584]{2,1,0:T(8,128)(2,1)S(1)}, bf16[1,32,3584]{2,1,0:T(8,128)(2,1)}, u32[]{:S(2)}) copy-start(bf16[1,32,3584]{2,1,0:T(8,128)(2,1)} %param.23) | copy-start | bytes 688132
  108.2 18.4 %all-to-all-start.3 = ((bf16[4,16,3584]{2,1,0:T(8,128)(2,1)}), bf16[4,16,3584]{2,1,0:T(8,128)(2,1)}, u32[]{:S(2)}, u32[]{:S(2)}) async-start(bf16[4,16,3584]{2,1,0:T(8,128)(2,1)} %bitcast.110), calls=%async_computation.3 | async-start | bytes 917504 | tf_op jit(solution)/shard_map/all_to_all | solution.py:183
  113.0 3.5 %collective-permute-start.7 = (bf16[32,3584]{1,0:T(8,128)(2,1)S(1)}, bf16[32,3584]{1,0:T(8,128)(2,1)}, u32[]{:S(2)}, u32[]{:S(2)}) collective-permute-start(bf16[32,3584]{1,0:T(8,128)(2,1)S(1)} %bitcast.106), channel_id=1, source_target_pairs={{0,1},{1,0},{2,3},{3,2},{4,5},{5,4},{6,7},{7,6},{8,9},{9,8},{10,11... | collective-permute-start | bytes 688136 | tf_op jit(solution)/shard_map/ppermute | solution.py:174
  116.6 1.2 copy-start.4
  120.8 0.6 copy-start.11
  121.5 0.6 copy-start.13
  122.1 0.6 copy-start.15
  122.7 0.6 copy-start.17
  126.7 1.2 copy-start.5
  127.9 1.2 copy-start.7
  129.0 0.8 copy-start.14
  129.8 0.8 copy-start.16
  130.6 0.8 copy-start.18
  134.7 0.8 copy-start.8
  143.5 4.3 %copy-start.12 = (f32[64,256]{1,0:T(8,128)S(1)}, f32[64,256]{1,0:T(8,128)}, u32[]{:S(2)}) copy-start(f32[64,256]{1,0:T(8,128)} %copy-done.11) | copy-start | bytes 196612
  143.5 16.3 %all-to-all-start.5 = ((bf16[4,16,3584]{2,1,0:T(8,128)(2,1)}), bf16[4,16,3584]{2,1,0:T(8,128)(2,1)}, u32[]{:S(2)}, u32[]{:S(2)}) async-start(bf16[4,16,3584]{2,1,0:T(8,128)(2,1)} %bitcast.104), calls=%async_computation.5 | async-start | bytes 917504 | tf_op jit(solution)/shard_map/all_to_all | solution.py:183
  147.8 12.0 %copy-start.21 = (bf16[16,3584]{1,0:T(8,128)(2,1)S(1)}, bf16[16,3584]{1,0:T(8,128)(2,1)}, u32[]{:S(2)}) copy-start(bf16[16,3584]{1,0:T(8,128)(2,1)} %copy-done.20) | copy-start | bytes 344068
  149.6 28.2 %collective-permute-start.9 = (f32[32,3584]{1,0:T(8,128)S(1)}, f32[32,3584]{1,0:T(8,128)S(1)}, u32[]{:S(2)}, u32[]{:S(2)}) collective-permute-start(f32[32,3584]{1,0:T(8,128)S(1)} %get-tuple-element.28), channel_id=1, source_target_pairs={{0,1},{1,0},{2,3},{3,2},{4,5},{5,4},{6,7},{7,6},{8,9},{9,8},{10,11... | collective-permute-start | bytes 1376264 | tf_op jit(solution)/shard_map/ppermute | solution.py:174
  161.6 18.4 %collective-permute-start.8 = (bf16[8,3584]{1,0:T(8,128)(2,1)S(1)}, bf16[8,3584]{1,0:T(8,128)(2,1)S(1)}, u32[]{:S(2)}, u32[]{:S(2)}) collective-permute-start(bf16[8,3584]{1,0:T(8,128)(2,1)S(1)} %get-tuple-element.29), channel_id=1, source_target_pairs={{0,504},{8,496},{16,488},{24,480},{32,472},{40,464},{48,456},{56,4... | collective-permute-start | bytes 172040 | tf_op jit(solution)/shard_map/ppermute | solution.py:179

commit v3 on v2

--- a/solution.py
+++ b/solution.py
@@ -20,7 +20,7 @@
 balance_weight = 1.0
 F32 = jnp.float32
 BF16 = jnp.bfloat16
-VMEM_LIMIT = 48 * 1024 * 1024
+VMEM_LIMIT = 16 * 1024 * 1024
 
 
 def dot(lhs, rhs, lhs_dim, rhs_dim):
@@ -41,6 +41,26 @@
         compiler_params=pltpu.CompilerParams(vmem_limit_bytes=VMEM_LIMIT),
         cost_estimate=pl.CostEstimate(flops=flops, bytes_accessed=total, transcendentals=0),
     )(*args)
+
+
+def packed(parts):
+    return jnp.concatenate([p.astype(F32) for p in parts], axis=0).astype(BF16)
+
+
+def spread_first_kernel(inputs, grads, out):
+    block = packed([inputs[...], grads[...]])
+    for k in range(CHIPS):
+        out[16 * k : 16 * k + 16, :] = block
+
+
+def spread_kernel(block, out):
+    for k in range(CHIPS):
+        out[16 * k : 16 * k + 16, :] = block[...]
+
+
+def join_kernel(a, b, ids, out):
+    out[:, 0:D] = packed([a[...], b[...]])
+    out[:, D:] = ids[...]
 
 
 def backward_terms(hidden, gate, up, gates, ups, out):
@@ -93,16 +113,20 @@
 
 
 def forward_kernel(*refs):
-    first_a, first_b, second = refs[0:3]
-    gates, ups, routers = refs[3:5], refs[5:7], refs[7:9]
-    base, pre = refs[9], refs[10:14]
-    expo_ref, share_ref, stats_ref = refs[14:17]
-    held0, ids_ref = refs[17:19]
+    first_a, first_b, second = refs[0], refs[1], refs[2:6]
+    gates, ups, routers = refs[6:8], refs[8:10], refs[10:12]
+    base, pre = refs[12], refs[13:17]
+    expo_ref, share_ref, stats_ref, held1 = refs[17:21]
+    held0, ids_ref = refs[21:23]
+    chip = lax.axis_index("expert") // 2
     held0[0:64, :] = first_a[...]
     held0[64:128, :] = first_b[...]
-    ids_ref[0:64, :] = second[:, D : D + IDCOLS].astype(F32)
+    for k in range(CHIPS):
+        rows = pl.ds(pl.multiple_of(lax.rem(chip + k, CHIPS) * 16, 16), 16)
+        held1[rows, :] = second[k][:, 0:D]
+        ids_ref[rows, :] = second[k][:, D : D + IDCOLS].astype(F32)
     ids_ref[64:128, :] = jnp.full((64, IDCOLS), -1.0, F32)
-    rows0, rows1 = held0[...], second[:, 0:D]
+    rows0, rows1 = held0[...], held1[...]
     for w, out in zip((*gates, *ups), pre):
         out[...] = dot(rows1, w[...], 1, 0)
     logits = jnp.concatenate(
@@ -142,9 +166,8 @@
 
 
 def router_kernel(*refs):
-    first_a, first_b, second, expo_ref, share_ref, all_stats, chip, own_out, other_out = refs
-    mine = chip[...]
-    stats = [all_stats[pl.ds(8 * k, 8), :] for k in range(CHIPS)]
+    first_a, first_b, second, expo_ref, share_ref = refs[0:5]
+    stats, own_out, other_out = refs[5:9], refs[9], refs[10]
     peaks = [s[0:1, :] for s in stats]
     peak = functools.reduce(jnp.maximum, peaks)
     factors = [jnp.exp(p - peak) for p in peaks]
@@ -152,8 +175,7 @@
     weighted = sum(s[2:3, :] * f for s, f in zip(stats, factors))
     log_total = peak + jnp.log(total)
     mean_share = weighted / total
-    own_factor = sum(jnp.where(mine == k, f, 0.0) for k, f in enumerate(factors))
-    probs = expo_ref[...] * (own_factor / total)
+    probs = expo_ref[...] * (factors[0] / total)
     slopes = (
         2.0 * z_weight * log_total - balance_weight * mean_share + balance_weight * share_ref[...]
     ) * probs
@@ -187,7 +209,25 @@
 
 
 def spread(value):
-    return exchanged(jnp.concatenate([value] * CHIPS, axis=0))
+    wide = jax.ShapeDtypeStruct((CHIPS * value.shape[0], value.shape[1]), value.dtype)
+    return exchanged(call(spread_kernel, [wide], [], [value], 0)[0])
+
+
+def spread_first(inputs, grads):
+    wide = jax.ShapeDtypeStruct((64, D), BF16)
+    return exchanged(call(spread_first_kernel, [wide], [], [inputs, grads], 0)[0])
+
+
+def from_chip(value, k):
+    return lax.ppermute(value, "expert", [((e + 2 * k) % 8, e) for e in range(8)])
+
+
+def ring(value):
+    return [value] + [from_chip(value, k) for k in range(1, CHIPS)]
+
+
+def after(value, *earlier):
+    return lax.optimization_barrier((value, *earlier))[0]
 
 
 def shards(
@@ -201,26 +241,24 @@
     top = lax.axis_size("pipe") - 1
     member = lax.axis_index("expert")
 
-    block_b = mirrored(jnp.concatenate([stash_b[0], arriving_b], axis=0))
-    block_a = jnp.concatenate([stash_a[0], arriving_a], axis=0)
-    first_a = spread(block_a)
+    arrived_b = mirrored(arriving_b)
+    inputs_b = mirrored(stash_b[0])
+    first_a = spread_first(stash_a[0], arriving_a)
+    first_b = spread_first(inputs_b, arrived_b)
+
+    def id_rows(ids):
+        return jnp.concatenate([ids[0], ids[1]], axis=1)
+
+    ids = jnp.concatenate([id_rows(ids_a), id_rows(ids_b)], axis=0).astype(BF16)
+    ids = jnp.pad(ids, ((0, 0), (0, 112)), constant_values=-1)
+    other_ids = swapped(after(ids, first_a))
     other_gate, other_up, other_down, other_router = (
-        swapped(w_gate), swapped(w_up), swapped(w_down), swapped(router)
+        swapped(after(weight, first_a)) for weight in (w_gate, w_up, w_down, router)
     )
     gates, ups = [w_gate, other_gate], [w_up, other_up]
     downs, routers = [w_down, other_down], [router, other_router]
-
-    def id_rows(ids):
-        return jnp.concatenate([ids[0], ids[1]], axis=1)
-
-    ids = jnp.concatenate([id_rows(ids_a), id_rows(ids_b)], axis=0).astype(BF16)
-    ids = jnp.pad(ids, ((0, 0), (0, 112)), constant_values=-1)
-    ids_other = swapped(ids)
-    ids = jnp.concatenate([ids[:, :16], ids_other[:, :16], ids[:, 32:]], axis=1)
+    ids = jnp.concatenate([ids[:, :16], other_ids[:, :16], ids[:, 32:]], axis=1)
     later_b = mirrored(jnp.concatenate([stash_b[1], ids[8:]], axis=1))
-    later_a = jnp.concatenate([stash_a[1], ids[:8]], axis=1)
-    first_b = spread(block_b)
-    later = jnp.concatenate([later_a, later_b], axis=0)
     sums = [jax.ShapeDtypeStruct((64, D), BF16)]
     (terms,) = call(
         first_tick_kernel, sums, [pltpu.VMEM((128, D), BF16)],
@@ -237,36 +275,39 @@
             total = total + parts[16 * k : 16 * k + 16].astype(F32)
         return total.astype(BF16)
 
-    grads = jnp.concatenate([block_a[8:], block_b[8:]], axis=0)
+    grads = jnp.concatenate([arriving_a, arrived_b], axis=0)
     out = emitted(grads, exchanged(terms))
-    out, later = lax.optimization_barrier((out, later))
     moved = lax.ppermute(out, "pipe", [(i, i - 1) for i in range(1, top + 1)])
-    second = spread(later)
+    (later,) = call(
+        join_kernel, [jax.ShapeDtypeStruct((16, D + IDCOLS), BF16)], [],
+        [stash_a[1], later_b[:, :D], jnp.concatenate([ids[:8], later_b[:, D:]], axis=0)], 0,
+    )
+    second = ring(after(later, out))
     head = jnp.concatenate([head_a[0], head_b[0]], axis=0)
     grads = jnp.where(section == top, head, moved)
     all_grads = spread(grads)
     pre = [jax.ShapeDtypeStruct((64, HID), F32)] * 4
-    *pre, expo, share, stats = call(
+    *pre, expo, share, stats, rows1 = call(
         forward_kernel,
         pre
         + [
             jax.ShapeDtypeStruct((2 * OWN, 256), F32),
             jax.ShapeDtypeStruct((2 * OWN, 256), F32),
             jax.ShapeDtypeStruct((8, 256), F32),
+            jax.ShapeDtypeStruct((64, D), BF16),
         ],
         [pltpu.VMEM((128, D), BF16), pltpu.VMEM((128, IDCOLS), F32)],
-        [first_a, first_b, second] + gates + ups + routers + [base], 2 * 128 * D * 128 * 4,
+        [first_a, first_b, *second] + gates + ups + routers + [base], 2 * 128 * D * 128 * 4,
     )
     (terms,) = call(
         second_tick_kernel, sums, [],
         [all_grads] + pre + gates + ups + downs, 2 * 64 * D * 128 * 6,
     )
-    terms, stats = lax.optimization_barrier((terms, stats))
     parts = exchanged(terms)
-    chip = jnp.full((1, 256), member // 2, jnp.int32)
+    stats = ring(stats)
     own, other = call(
         router_kernel, [jax.ShapeDtypeStruct((OWN, D), F32)] * 2, [],
-        [first_a, first_b, second, expo, share, spread(stats), chip], 2 * 192 * D * 64,
+        [first_a, first_b, rows1, after(expo, terms), share, *stats], 2 * 192 * D * 64,
     )
     router_grad = own + swapped(other)
     out = emitted(grads, parts)

time: 182 us -> 194 us (1.066)
  waiting for transfers between devices: 42.6 us -> 78.4 us
  local copies, waits for them, and re-layouts: 22.3 us -> 13.2 us
  blocking collectives: 8 us -> 0 us
  other arithmetic: 7.53 us -> 2.35 us
  starting transfers between devices: 86.6 us -> 84 us
    ppermute x0 -> x6, starting transfers between devices: none -> 23.7 us  [from_chip(): lax.ppermute(value, 'expert', [((e + 2 * k) % 8, e) for e in range(8)])]
    ppermute x3 -> x4, starting transfers between devices: 39.8 us -> 20.8 us  [mirrored(): lax.ppermute(value, 'pipe', [(i, count - 1 - i) for i in range(count)])]
    ppermute x3 -> x4, waiting for transfers between devices: 17.3 us -> 32.3 us  [mirrored(): lax.ppermute(value, 'pipe', [(i, count - 1 - i) for i in range(count)])]
    ppermute x0 -> x6, waiting for transfers between devices: none -> 11.7 us  [from_chip(): lax.ppermute(value, 'expert', [((e + 2 * k) % 8, e) for e in range(8)])]
    ppermute x1, waiting for transfers between devices: 4.14 us -> 14.3 us  [shards(): moved = lax.ppermute(out, 'pipe', [(i, i - 1) for i in range(1, top + 1)])]
    unnamed x66 -> x51, local copies, waits for them, and re-layouts: 19.6 us -> 11.6 us
    all_to_all x1 -> x0, blocking collectives: 8 us -> none  [exchanged(): lax.all_to_all(blocks, 'expert', split_axis=0, concat_axis=0, tiled=True,...]
    all_to_all x6 -> x5, starting transfers between devices: 32.3 us -> 25.4 us  [exchanged(): lax.all_to_all(blocks, 'expert', split_axis=0, concat_axis=0, tiled=True,...]
  transfers between devices with their start and end apart: 16 -> 22, of which waited for: 10 -> 12; matrix products, arithmetic and copies ran while one was open for 5% -> 1% of each run, Pallas kernels for 3% -> 2%
where the time goes in v3:
time: 194 us; the launch traced here: 192 us
  starting transfers between devices  84 us (43%)
  waiting for transfers between devices  78.4 us (40%)
  Pallas kernels  13.4 us (7%)
  local copies, waits for them, and re-layouts  13.2 us (7%)
  other arithmetic  2.35 us (1%)
    ppermute x4, waiting for transfers between devices, mirrored(): lax.ppermute(value, 'pipe', [(i, count - 1 - i) for i in range(count)])  32.3 us
    all_to_all x5, starting transfers between devices, exchanged(): lax.all_to_all(blocks, 'expert', split_axis=0, concat_axis=0, tiled=True,...  25.4 us
    ppermute x6, starting transfers between devices, from_chip(): lax.ppermute(value, 'expert', [((e + 2 * k) % 8, e) for e in range(8)])  23.7 us
    ppermute x4, starting transfers between devices, mirrored(): lax.ppermute(value, 'pipe', [(i, count - 1 - i) for i in range(count)])  20.8 us
    all_to_all x5, waiting for transfers between devices, exchanged(): lax.all_to_all(blocks, 'expert', split_axis=0, concat_axis=0, tiled=True,...  19 us
    ppermute x1, waiting for transfers between devices, shards(): moved = lax.ppermute(out, 'pipe', [(i, i - 1) for i in range(1, top + 1)])  14.3 us
    pallas_call x8, Pallas kernels, call(): pl.pallas_call(body, out_shape=out_shape, in_specs=[spec] * len(args), ou...  13.4 us
    ppermute x6, starting transfers between devices, swapped(): return lax.ppermute(value, 'expert', [(e, e ^ 1) for e in range(8)])  12.1 us
  transfers between devices with their start and end apart: 22, of which 12 were waited for; matrix products, arithmetic and copies ran while one was open for 1% of the time, Pallas kernels for 2%

profile of v3, /device:TPU:6, one launch (start us, length us, event | category | flops | bytes accessed | tf_op | source)
XLA Modules:
  0.0 192.4 jit_solution(13326830628716251200)
XLA Ops:
  0.6 0.9 slice_bitcast_fusion.10
  1.5 0.8 shard_map.139
  2.3 6.0 %all-to-all-start = ((bf16[4,16,3584]{2,1,0:T(8,128)(2,1)}), bf16[4,16,3584]{2,1,0:T(8,128)(2,1)S(1)}, u32[]{:S(2)}, u32[]{:S(2)}) async-start(bf16[4,16,3584]{2,1,0:T(8,128)(2,1)} %bitcast.5), calls=%async_computation | async-start | bytes 917504 | tf_op jit(solution)/shard_map/all_to_all | solution.py:205
  8.4 12.8 %collective-permute-start.1 = (bf16[8,3584]{1,0:T(8,128)(2,1)S(1)}, bf16[8,3584]{1,0:T(8,128)(2,1)S(1)}, u32[]{:S(2)}, u32[]{:S(2)}) collective-permute-start(bf16[8,3584]{1,0:T(8,128)(2,1)S(1)} %get-tuple-element.40), channel_id=1, source_target_pairs={{0,504},{8,496},{16,488},{24,480},{32,472},{40,464},{48,456},{56,4... | collective-permute-start | bytes 172040 | tf_op jit(solution)/shard_map/ppermute | solution.py:201
  21.2 1.9 collective-permute-start
  23.2 7.4 %collective-permute-done.1.inputs = bf16[8,3584]{1,0:T(8,128)(2,1)S(1)} collective-permute-done((bf16[8,3584]{1,0:T(8,128)(2,1)S(1)}, bf16[8,3584]{1,0:T(8,128)(2,1)S(1)}, u32[]{:S(2)}, u32[]{:S(2)}) %collective-permute-start.1) | collective-permute-done | bytes 57376 | tf_op jit(solution)/shard_map/ppermute | solution.py:201
  30.5 5.0 %collective-permute-done.grads = bf16[8,3584]{1,0:T(8,128)(2,1)S(1)} collective-permute-done((bf16[8,3584]{1,0:T(8,128)(2,1)S(1)}, bf16[8,3584]{1,0:T(8,128)(2,1)S(1)}, u32[]{:S(2)}, u32[]{:S(2)}) %collective-permute-start) | collective-permute-done | bytes 57376 | tf_op jit(solution)/shard_map/ppermute | solution.py:201
  35.5 0.8 shard_map.140
  37.1 7.3 %all-to-all-start.1 = ((bf16[4,16,3584]{2,1,0:T(8,128)(2,1)}), bf16[4,16,3584]{2,1,0:T(8,128)(2,1)S(1)}, u32[]{:S(2)}, u32[]{:S(2)}) async-start(bf16[4,16,3584]{2,1,0:T(8,128)(2,1)} %bitcast.8), calls=%async_computation.1 | async-start | bytes 917504 | tf_op jit(solution)/shard_map/all_to_all | solution.py:205
  44.4 1.9 collective-permute-start.2
  46.4 2.4 %collective-permute-start.3 = (bf16[3584,128]{1,0:T(8,128)(2,1)S(1)}, bf16[3584,128]{1,0:T(8,128)(2,1)}, u32[]{:S(2)}, u32[]{:S(2)}) collective-permute-start(bf16[3584,128]{1,0:T(8,128)(2,1)S(1)} %bitcast.82), channel_id=1, source_target_pairs={{0,1},{1,0},{2,3},{3,2},{4,5},{5,4},{6,7},{7,6},{8,9},{9,8},{10,11... | collective-permute-start | bytes 2752520 | tf_op jit(solution)/shard_map/ppermute | solution.py:196
  48.8 1.9 %collective-permute-start.4 = (bf16[128,3584]{1,0:T(8,128)(2,1)}, bf16[128,3584]{1,0:T(8,128)(2,1)}, u32[]{:S(2)}, u32[]{:S(2)}) collective-permute-start(bf16[128,3584]{1,0:T(8,128)(2,1)} %bitcast.92), channel_id=1, source_target_pairs={{0,1},{1,0},{2,3},{3,2},{4,5},{5,4},{6,7},{7,6},{8,9},{9,8},{10,11... | collective-permute-start | bytes 2752520 | tf_op jit(solution)/shard_map/ppermute | solution.py:196
  50.7 7.0 %all-to-all-done.1 = bf16[4,16,3584]{2,1,0:T(8,128)(2,1)S(1)} async-done(((bf16[4,16,3584]{2,1,0:T(8,128)(2,1)}), bf16[4,16,3584]{2,1,0:T(8,128)(2,1)S(1)}, u32[]{:S(2)}, u32[]{:S(2)}) %all-to-all-start.1) | async-done | bytes 458784 | tf_op jit(solution)/shard_map/all_to_all | solution.py:205
  57.7 1.0 copy-done.3
  58.7 1.2 copy-done.6
  59.9 4.4 %shard_map.141 = bf16[64,3584]{1,0:T(8,128)(2,1)S(1)} custom-call(bf16[64,3584]{1,0:T(8,128)(2,1)S(1)} %bitcast.89, bf16[64,3584]{1,0:T(8,128)(2,1)S(1)} %bitcast.86, bf16[3584,128]{1,0:T(8,128)(2,1)S(1)} %bitcast.79, bf16[3584,128]{1,0:T(8,128)(2,1)S(1)} %collective-permute-done.2.refs_3_.refs_7_.refs_6_, bf16[3584,128]{1,0:T(8,128)(2,1)S(1)} %bitcast.83, ...), custom_call_target="tpu_custom_call" | custom-call | flops 1174405120 | bytes 6422528 | tf_op jit(solution)/shard_map/pallas_call | solution.py:35
  65.1 4.3 %all-to-all-start.2 = ((bf16[4,16,3584]{2,1,0:T(8,128)(2,1)}), bf16[4,16,3584]{2,1,0:T(8,128)(2,1)}, u32[]{:S(2)}, u32[]{:S(2)}) async-start(bf16[4,16,3584]{2,1,0:T(8,128)(2,1)} %bitcast.97), calls=%async_computation.2 | async-start | bytes 917504 | tf_op jit(solution)/shard_map/all_to_all | solution.py:205
  70.0 12.0 %all-to-all-done.2 = bf16[4,16,3584]{2,1,0:T(8,128)(2,1)} async-done(((bf16[4,16,3584]{2,1,0:T(8,128)(2,1)}), bf16[4,16,3584]{2,1,0:T(8,128)(2,1)}, u32[]{:S(2)}, u32[]{:S(2)}) %all-to-all-start.2) | async-done | bytes 458784 | tf_op jit(solution)/shard_map/all_to_all | solution.py:205
  82.0 1.1 fusion.1
  83.2 2.0 %collective-permute-start.5 = (bf16[16,3584]{1,0:T(8,128)(2,1)S(1)}, bf16[16,3584]{1,0:T(8,128)(2,1)S(1)}, u32[]{:S(2)}, u32[]{:S(2)}) collective-permute-start(bf16[16,3584]{1,0:T(8,128)(2,1)S(1)} %fusion.1), channel_id=1, source_target_pairs={{8,0},{16,8},{24,16},{32,24},{40,32},{48,40},{56,48},{64,56},{72,6... | collective-permute-start | bytes 344072 | tf_op jit(solution)/shard_map/ppermute | solution.py:280
  85.1 14.3 %collective-permute-done.5 = bf16[16,3584]{1,0:T(8,128)(2,1)S(1)} collective-permute-done((bf16[16,3584]{1,0:T(8,128)(2,1)S(1)}, bf16[16,3584]{1,0:T(8,128)(2,1)S(1)}, u32[]{:S(2)}, u32[]{:S(2)}) %collective-permute-start.5) | collective-permute-done | bytes 114720 | tf_op jit(solution)/shard_map/ppermute | solution.py:280
  99.6 0.8 copy-done.9
  100.4 4.1 %all-to-all-start.3 = ((bf16[4,16,3584]{2,1,0:T(8,128)(2,1)}), bf16[4,16,3584]{2,1,0:T(8,128)(2,1)}, u32[]{:S(2)}, u32[]{:S(2)}) async-start(bf16[4,16,3584]{2,1,0:T(8,128)(2,1)} %bitcast.96), calls=%async_computation.3 | async-start | bytes 917504 | tf_op jit(solution)/shard_map/all_to_all | solution.py:205
  104.6 1.9 collective-permute-start.6
  106.6 1.0 collective-permute-done.6
  107.7 3.2 %collective-permute-start.7 = (bf16[8,3712]{1,0:T(8,128)(2,1)S(1)}, bf16[8,3712]{1,0:T(8,128)(2,1)S(1)}, u32[]{:S(2)}, u32[]{:S(2)}) collective-permute-start(bf16[8,3712]{1,0:T(8,128)(2,1)S(1)} %pad_maximum_fusion), channel_id=1, source_target_pairs={{0,504},{8,496},{16,488},{24,480},{32,472},{40,464},{48,456},{56,4... | collective-permute-start | bytes 178184 | tf_op jit(solution)/shard_map/ppermute | solution.py:201
  110.9 2.1 %collective-permute-start.11 = (bf16[32,3584]{1,0:T(8,128)(2,1)}, bf16[32,3584]{1,0:T(8,128)(2,1)S(1)}, u32[]{:S(2)}, u32[]{:S(2)}) collective-permute-start(bf16[32,3584]{1,0:T(8,128)(2,1)} %bitcast.100), channel_id=1, source_target_pairs={{0,1},{1,0},{2,3},{3,2},{4,5},{5,4},{6,7},{7,6},{8,9},{9,8},{10,11... | collective-permute-start | bytes 688136 | tf_op jit(solution)/shard_map/ppermute | solution.py:196
  113.0 9.1 %collective-permute-done.7 = bf16[8,3712]{1,0:T(8,128)(2,1)S(1)} collective-permute-done((bf16[8,3712]{1,0:T(8,128)(2,1)S(1)}, bf16[8,3712]{1,0:T(8,128)(2,1)S(1)}, u32[]{:S(2)}, u32[]{:S(2)}) %collective-permute-start.7) | collective-permute-done | bytes 59424 | tf_op jit(solution)/shard_map/ppermute | solution.py:201
  122.2 4.5 %collective-permute-start.10 = (bf16[16,3712]{1,0:T(8,128)(2,1)S(1)}, bf16[16,3712]{1,0:T(8,128)(2,1)S(1)}, u32[]{:S(2)}, u32[]{:S(2)}) collective-permute-start(bf16[16,3712]{1,0:T(8,128)(2,1)S(1)} %shard_map.143.refs_2_), channel_id=1, source_target_pairs={{6,0},{7,1},{0,2},{1,3},{2,4},{3,5},{4,6},{5,7},{14,8},{15,9},{8,1... | collective-permute-start | bytes 356360 | tf_op jit(solution)/shard_map/ppermute | solution.py:222
  126.6 6.1 %collective-permute-start.8 = (bf16[16,3712]{1,0:T(8,128)(2,1)S(1)}, bf16[16,3712]{1,0:T(8,128)(2,1)S(1)}, u32[]{:S(2)}, u32[]{:S(2)}) collective-permute-start(bf16[16,3712]{1,0:T(8,128)(2,1)S(1)} %shard_map.143.refs_2_), channel_id=1, source_target_pairs={{2,0},{3,1},{4,2},{5,3},{6,4},{7,5},{0,6},{1,7},{10,8},{11,9},{12,... | collective-permute-start | bytes 356360 | tf_op jit(solution)/shard_map/ppermute | solution.py:222
  132.7 2.5 %collective-permute-start.9 = (bf16[16,3712]{1,0:T(8,128)(2,1)S(1)}, bf16[16,3712]{1,0:T(8,128)(2,1)S(1)}, u32[]{:S(2)}, u32[]{:S(2)}) collective-permute-start(bf16[16,3712]{1,0:T(8,128)(2,1)S(1)} %shard_map.143.refs_2_), channel_id=1, source_target_pairs={{4,0},{5,1},{6,2},{7,3},{0,4},{1,5},{2,6},{3,7},{12,8},{13,9},{14,... | collective-permute-start | bytes 356360 | tf_op jit(solution)/shard_map/ppermute | solution.py:222
  135.3 1.5 collective-permute-done.8.refs_3_
  136.8 5.7 %collective-permute-done.9.refs_4_ = bf16[16,3712]{1,0:T(8,128)(2,1)S(1)} collective-permute-done((bf16[16,3712]{1,0:T(8,128)(2,1)S(1)}, bf16[16,3712]{1,0:T(8,128)(2,1)S(1)}, u32[]{:S(2)}, u32[]{:S(2)}) %collective-permute-start.9) | collective-permute-done | bytes 118816 | tf_op jit(solution)/shard_map/ppermute | solution.py:222
  142.6 1.0 copy-done.4
  143.6 3.1 %shard_map.144 = (f32[64,128]{1,0:T(8,128)S(1)}, f32[64,128]{1,0:T(8,128)S(1)}, f32[64,128]{1,0:T(8,128)S(1)}, f32[64,128]{1,0:T(8,128)S(1)}, f32[64,256]{1,0:T(...) custom-call(bf16[64,3584]{1,0:T(8,128)(2,1)S(1)} %bitcast.90, ...), custom_call_target="tpu_custom_call" | custom-call | flops 469762048 | bytes 5554176 | tf_op jit(solution)/shard_map/pallas_call | solution.py:35
  146.7 0.8 copy-done.11
  148.7 1.2 copy-done.7
  150.6 3.7 %shard_map.145 = bf16[64,3584]{1,0:T(8,128)(2,1)S(1)} custom-call(bf16[64,3584]{1,0:T(8,128)(2,1)} %bitcast.19.refs_0_, f32[64,128]{1,0:T(8,128)S(1)} %get-tuple-element.26.refs_1_, f32[64,128]{1,0:T(8,128)S(1)} %get-tuple-element.27.refs_2_, f32[64,128]{1,0:T(8,128)S(1)} %get-tuple-element.28.refs_3_, f32[64,128]{1,0:T(8,128)S(1)} %copy-done.16, ...), custom_call_target="tpu_custom_call" | custom-call | flops 352321536 | bytes 6094848 | tf_op jit(solution)/shard_map/pallas_call | solution.py:35
  155.1 3.7 %all-to-all-start.4 = ((bf16[4,16,3584]{2,1,0:T(8,128)(2,1)}), bf16[4,16,3584]{2,1,0:T(8,128)(2,1)S(1)}, u32[]{:S(2)}, u32[]{:S(2)}) async-start(bf16[4,16,3584]{2,1,0:T(8,128)(2,1)} %bitcast.95), calls=%async_computation.4 | async-start | bytes 917504 | tf_op jit(solution)/shard_map/all_to_all | solution.py:205
  158.8 5.7 %collective-permute-start.13 = (f32[8,256]{1,0:T(8,128)}, f32[8,256]{1,0:T(8,128)S(1)}, u32[]{:S(2)}, u32[]{:S(2)}) collective-permute-start(f32[8,256]{1,0:T(8,128)} %copy-done.17), channel_id=1, source_target_pairs={{2,0},{3,1},{4,2},{5,3},{6,4},{7,5},{0,6},{1,7},{10,8},{11,9},{12,... | collective-permute-start | bytes 24584 | tf_op jit(solution)/shard_map/ppermute | solution.py:222
  164.5 1.9 collective-permute-start.14
  166.4 3.0 %collective-permute-start.15 = (f32[8,256]{1,0:T(8,128)}, f32[8,256]{1,0:T(8,128)S(1)}, u32[]{:S(2)}, u32[]{:S(2)}) collective-permute-start(f32[8,256]{1,0:T(8,128)} %copy-done.17), channel_id=1, source_target_pairs={{6,0},{7,1},{0,2},{1,3},{2,4},{3,5},{4,6},{5,7},{14,8},{15,9},{8,1... | collective-permute-start | bytes 24584 | tf_op jit(solution)/shard_map/ppermute | solution.py:222
  169.5 3.2 %collective-permute-done.14.refs_7_ = f32[8,256]{1,0:T(8,128)S(1)} collective-permute-done((f32[8,256]{1,0:T(8,128)}, f32[8,256]{1,0:T(8,128)S(1)}, u32[]{:S(2)}, u32[]{:S(2)}) %collective-permute-start.14) | collective-permute-done | bytes 8224 | tf_op jit(solution)/shard_map/ppermute | solution.py:222
  172.7 1.3 collective-permute-done.15.refs_8_
  174.6 1.9 collective-permute-start.16
  177.2 2.9 %collective-permute-start.12 = (bf16[8,3584]{1,0:T(8,128)(2,1)S(1)}, bf16[8,3584]{1,0:T(8,128)(2,1)S(1)}, u32[]{:S(2)}, u32[]{:S(2)}) collective-permute-start(bf16[8,3584]{1,0:T(8,128)(2,1)S(1)} %get-tuple-element.37), channel_id=1, source_target_pairs={{0,504},{8,496},{16,488},{24,480},{32,472},{40,464},{48,456},{56,4... | collective-permute-start | bytes 172040 | tf_op jit(solution)/shard_map/ppermute | solution.py:201
  180.2 0.8 add_bitcast_fusion
  181.0 10.7 %collective-permute-done.12 = bf16[8,3584]{1,0:T(8,128)(2,1)S(1)} collective-permute-done((bf16[8,3584]{1,0:T(8,128)(2,1)S(1)}, bf16[8,3584]{1,0:T(8,128)(2,1)S(1)}, u32[]{:S(2)}, u32[]{:S(2)}) %collective-permute-start.12) | collective-permute-done | bytes 57376 | tf_op jit(solution)/shard_map/ppermute | solution.py:201
  (77 shorter events, 7.5 us)
Async XLA Ops:
  0.6 0.9 copy-start.13
  1.5 6.8 %copy-start.19 = (bf16[1,2,8,3584]{3,2,1,0:T(8,128)(2,1)S(1)}, bf16[1,2,8,3584]{3,2,1,0:T(8,128)(2,1)}, u32[]{:S(2)}) copy-start(bf16[1,2,8,3584]{3,2,1,0:T(8,128)(2,1)} %param.13) | copy-start | bytes 344068
  2.3 18.9 %copy-start.24 = (bf16[1,8,3584]{2,1,0:T(8,128)(2,1)S(1)}, bf16[1,8,3584]{2,1,0:T(8,128)(2,1)}, u32[]{:S(2)}) copy-start(bf16[1,8,3584]{2,1,0:T(8,128)(2,1)} %param.17) | copy-start | bytes 172036
  2.3 44.0 %copy-start.1 = (bf16[1,3584,128]{2,1,0:T(8,128)(2,1)S(1)}, bf16[1,3584,128]{2,1,0:T(8,128)(2,1)}, u32[]{:S(2)}) copy-start(bf16[1,3584,128]{2,1,0:T(8,128)(2,1)} %param.21) | copy-start | bytes 2752516
  2.3 34.0 %all-to-all-start = ((bf16[4,16,3584]{2,1,0:T(8,128)(2,1)}), bf16[4,16,3584]{2,1,0:T(8,128)(2,1)S(1)}, u32[]{:S(2)}, u32[]{:S(2)}) async-start(bf16[4,16,3584]{2,1,0:T(8,128)(2,1)} %bitcast.5), calls=%async_computation | async-start | bytes 917504 | tf_op jit(solution)/shard_map/all_to_all | solution.py:205
  8.4 36.1 %copy-start = (bf16[1,3584,128]{2,1,0:T(8,128)(2,1)S(1)}, bf16[1,3584,128]{2,1,0:T(8,128)(2,1)}, u32[]{:S(2)}) copy-start(bf16[1,3584,128]{2,1,0:T(8,128)(2,1)} %param.20) | copy-start | bytes 2752516
  8.4 22.1 %collective-permute-start.1 = (bf16[8,3584]{1,0:T(8,128)(2,1)S(1)}, bf16[8,3584]{1,0:T(8,128)(2,1)S(1)}, u32[]{:S(2)}, u32[]{:S(2)}) collective-permute-start(bf16[8,3584]{1,0:T(8,128)(2,1)S(1)} %get-tuple-element.40), channel_id=1, source_target_pairs={{0,504},{8,496},{16,488},{24,480},{32,472},{40,464},{48,456},{56,4... | collective-permute-start | bytes 172040 | tf_op jit(solution)/shard_map/ppermute | solution.py:201
  21.2 14.3 %collective-permute-start = (bf16[8,3584]{1,0:T(8,128)(2,1)S(1)}, bf16[8,3584]{1,0:T(8,128)(2,1)S(1)}, u32[]{:S(2)}, u32[]{:S(2)}) collective-permute-start(bf16[8,3584]{1,0:T(8,128)(2,1)S(1)} %bitcast.106), channel_id=1, source_target_pairs={{0,504},{8,496},{16,488},{24,480},{32,472},{40,464},{48,456},{56,4... | collective-permute-start | bytes 172040 | tf_op jit(solution)/shard_map/ppermute | solution.py:201
  36.4 0.8 copy-start.2
  37.1 20.6 %all-to-all-start.1 = ((bf16[4,16,3584]{2,1,0:T(8,128)(2,1)}), bf16[4,16,3584]{2,1,0:T(8,128)(2,1)S(1)}, u32[]{:S(2)}, u32[]{:S(2)}) async-start(bf16[4,16,3584]{2,1,0:T(8,128)(2,1)} %bitcast.8), calls=%async_computation.1 | async-start | bytes 917504 | tf_op jit(solution)/shard_map/all_to_all | solution.py:205
  44.4 13.3 %collective-permute-start.2 = (bf16[3584,128]{1,0:T(8,128)(2,1)S(1)}, bf16[3584,128]{1,0:T(8,128)(2,1)S(1)}, u32[]{:S(2)}, u32[]{:S(2)}) collective-permute-start(bf16[3584,128]{1,0:T(8,128)(2,1)S(1)} %bitcast.78), channel_id=1, source_target_pairs={{0,1},{1,0},{2,3},{3,2},{4,5},{5,4},{6,7},{7,6},{8,9},{9,8},{10,11... | collective-permute-start | bytes 2752520 | tf_op jit(solution)/shard_map/ppermute | solution.py:196
  46.4 11.3 %collective-permute-start.3 = (bf16[3584,128]{1,0:T(8,128)(2,1)S(1)}, bf16[3584,128]{1,0:T(8,128)(2,1)}, u32[]{:S(2)}, u32[]{:S(2)}) collective-permute-start(bf16[3584,128]{1,0:T(8,128)(2,1)S(1)} %bitcast.82), channel_id=1, source_target_pairs={{0,1},{1,0},{2,3},{3,2},{4,5},{5,4},{6,7},{7,6},{8,9},{9,8},{10,11... | collective-permute-start | bytes 2752520 | tf_op jit(solution)/shard_map/ppermute | solution.py:196
  48.8 8.9 %collective-permute-start.4 = (bf16[128,3584]{1,0:T(8,128)(2,1)}, bf16[128,3584]{1,0:T(8,128)(2,1)}, u32[]{:S(2)}, u32[]{:S(2)}) collective-permute-start(bf16[128,3584]{1,0:T(8,128)(2,1)} %bitcast.92), channel_id=1, source_target_pairs={{0,1},{1,0},{2,3},{3,2},{4,5},{5,4},{6,7},{7,6},{8,9},{9,8},{10,11... | collective-permute-start | bytes 2752520 | tf_op jit(solution)/shard_map/ppermute | solution.py:196
  57.7 1.0 copy-start.3
  58.7 1.2 copy-start.6
  64.3 0.8 copy-start.10
  65.0 4.3 %copy-start.22 = (s32[1,2,8,8]{3,2,1,0:T(8,128)S(1)}, s32[1,2,8,8]{3,2,1,0:T(8,128)}, u32[]{:S(2)}) copy-start(s32[1,2,8,8]{3,2,1,0:T(8,128)} %param.14) | copy-start | bytes 1540
  65.1 17.0 %all-to-all-start.2 = ((bf16[4,16,3584]{2,1,0:T(8,128)(2,1)}), bf16[4,16,3584]{2,1,0:T(8,128)(2,1)}, u32[]{:S(2)}, u32[]{:S(2)}) async-start(bf16[4,16,3584]{2,1,0:T(8,128)(2,1)} %bitcast.97), calls=%async_computation.2 | async-start | bytes 917504 | tf_op jit(solution)/shard_map/all_to_all | solution.py:205
  69.3 0.7 copy-start.23
  82.0 17.5 %copy-start.20 = (bf16[1,8,3584]{2,1,0:T(8,128)(2,1)S(1)}, bf16[1,8,3584]{2,1,0:T(8,128)(2,1)}, u32[]{:S(2)}) copy-start(bf16[1,8,3584]{2,1,0:T(8,128)(2,1)} %param.19) | copy-start | bytes 172036
  82.0 17.5 %copy-start.21 = (bf16[1,8,3584]{2,1,0:T(8,128)(2,1)S(1)}, bf16[1,8,3584]{2,1,0:T(8,128)(2,1)}, u32[]{:S(2)}) copy-start(bf16[1,8,3584]{2,1,0:T(8,128)(2,1)} %param.18) | copy-start | bytes 172036
  83.2 16.3 %collective-permute-start.5 = (bf16[16,3584]{1,0:T(8,128)(2,1)S(1)}, bf16[16,3584]{1,0:T(8,128)(2,1)S(1)}, u32[]{:S(2)}, u32[]{:S(2)}) collective-permute-start(bf16[16,3584]{1,0:T(8,128)(2,1)S(1)} %fusion.1), channel_id=1, source_target_pairs={{8,0},{16,8},{24,16},{32,24},{40,32},{48,40},{56,48},{64,56},{72,6... | collective-permute-start | bytes 344072 | tf_op jit(solution)/shard_map/ppermute | solution.py:280
  99.6 0.8 copy-start.9
  100.4 48.3 %all-to-all-start.3 = ((bf16[4,16,3584]{2,1,0:T(8,128)(2,1)}), bf16[4,16,3584]{2,1,0:T(8,128)(2,1)}, u32[]{:S(2)}, u32[]{:S(2)}) async-start(bf16[4,16,3584]{2,1,0:T(8,128)(2,1)} %bitcast.96), calls=%async_computation.3 | async-start | bytes 917504 | tf_op jit(solution)/shard_map/all_to_all | solution.py:205
  104.6 3.0 %collective-permute-start.6 = (bf16[16,128]{1,0:T(8,128)(2,1)S(1)}, bf16[16,128]{1,0:T(8,128)(2,1)S(1)}, u32[]{:S(2)}, u32[]{:S(2)}) collective-permute-start(bf16[16,128]{1,0:T(8,128)(2,1)S(1)} %fusion.10), channel_id=1, source_target_pairs={{0,1},{1,0},{2,3},{3,2},{4,5},{5,4},{6,7},{7,6},{8,9},{9,8},{10,11... | collective-permute-start | bytes 12296 | tf_op jit(solution)/shard_map/ppermute | solution.py:196
  107.7 14.4 %collective-permute-start.7 = (bf16[8,3712]{1,0:T(8,128)(2,1)S(1)}, bf16[8,3712]{1,0:T(8,128)(2,1)S(1)}, u32[]{:S(2)}, u32[]{:S(2)}) collective-permute-start(bf16[8,3712]{1,0:T(8,128)(2,1)S(1)} %pad_maximum_fusion), channel_id=1, source_target_pairs={{0,504},{8,496},{16,488},{24,480},{32,472},{40,464},{48,456},{56,4... | collective-permute-start | bytes 178184 | tf_op jit(solution)/shard_map/ppermute | solution.py:201
  110.9 31.6 %copy-start.14 = (bf16[1,32,3584]{2,1,0:T(8,128)(2,1)S(1)}, bf16[1,32,3584]{2,1,0:T(8,128)(2,1)}, u32[]{:S(2)}) copy-start(bf16[1,32,3584]{2,1,0:T(8,128)(2,1)} %param.23) | copy-start | bytes 688132
  110.9 24.4 %collective-permute-start.11 = (bf16[32,3584]{1,0:T(8,128)(2,1)}, bf16[32,3584]{1,0:T(8,128)(2,1)S(1)}, u32[]{:S(2)}, u32[]{:S(2)}) collective-permute-start(bf16[32,3584]{1,0:T(8,128)(2,1)} %bitcast.100), channel_id=1, source_target_pairs={{0,1},{1,0},{2,3},{3,2},{4,5},{5,4},{6,7},{7,6},{8,9},{9,8},{10,11... | collective-permute-start | bytes 688136 | tf_op jit(solution)/shard_map/ppermute | solution.py:196
  122.2 13.1 %collective-permute-start.10 = (bf16[16,3712]{1,0:T(8,128)(2,1)S(1)}, bf16[16,3712]{1,0:T(8,128)(2,1)S(1)}, u32[]{:S(2)}, u32[]{:S(2)}) collective-permute-start(bf16[16,3712]{1,0:T(8,128)(2,1)S(1)} %shard_map.143.refs_2_), channel_id=1, source_target_pairs={{6,0},{7,1},{0,2},{1,3},{2,4},{3,5},{4,6},{5,7},{14,8},{15,9},{8,1... | collective-permute-start | bytes 356360 | tf_op jit(solution)/shard_map/ppermute | solution.py:222
  126.6 10.1 %collective-permute-start.8 = (bf16[16,3712]{1,0:T(8,128)(2,1)S(1)}, bf16[16,3712]{1,0:T(8,128)(2,1)S(1)}, u32[]{:S(2)}, u32[]{:S(2)}) collective-permute-start(bf16[16,3712]{1,0:T(8,128)(2,1)S(1)} %shard_map.143.refs_2_), channel_id=1, source_target_pairs={{2,0},{3,1},{4,2},{5,3},{6,4},{7,5},{0,6},{1,7},{10,8},{11,9},{12,... | collective-permute-start | bytes 356360 | tf_op jit(solution)/shard_map/ppermute | solution.py:222
  132.7 9.8 %collective-permute-start.9 = (bf16[16,3712]{1,0:T(8,128)(2,1)S(1)}, bf16[16,3712]{1,0:T(8,128)(2,1)S(1)}, u32[]{:S(2)}, u32[]{:S(2)}) collective-permute-start(bf16[16,3712]{1,0:T(8,128)(2,1)S(1)} %shard_map.143.refs_2_), channel_id=1, source_target_pairs={{4,0},{5,1},{6,2},{7,3},{0,4},{1,5},{2,6},{3,7},{12,8},{13,9},{14,... | collective-permute-start | bytes 356360 | tf_op jit(solution)/shard_map/ppermute | solution.py:222
  142.6 1.0 copy-start.4
  146.7 0.8 copy-start.11
  147.5 0.6 copy-start.15
  148.1 0.6 copy-start.17
  148.7 1.2 copy-start.7
  149.9 0.8 copy-start.16
  154.3 0.8 copy-start.8
  155.1 18.9 %copy-start.18 = (f32[8,256]{1,0:T(8,128)S(1)}, f32[8,256]{1,0:T(8,128)}, u32[]{:S(2)}) copy-start(f32[8,256]{1,0:T(8,128)} %copy-done.17) | copy-start | bytes 24580
  155.1 18.9 %copy-start.5 = (bf16[4,16,3584]{2,1,0:T(8,128)(2,1)S(1)}, bf16[4,16,3584]{2,1,0:T(8,128)(2,1)}, u32[]{:S(2)}) copy-start(bf16[4,16,3584]{2,1,0:T(8,128)(2,1)} %copy-done.2) | copy-start | bytes 1376260
  155.1 18.9 %copy-start.12 = (bf16[64,3584]{1,0:T(8,128)(2,1)S(1)}, bf16[64,3584]{1,0:T(8,128)(2,1)}, u32[]{:S(2)}) copy-start(bf16[64,3584]{1,0:T(8,128)(2,1)} %copy-done.11) | copy-start | bytes 1376260
  155.1 21.4 %all-to-all-start.4 = ((bf16[4,16,3584]{2,1,0:T(8,128)(2,1)}), bf16[4,16,3584]{2,1,0:T(8,128)(2,1)S(1)}, u32[]{:S(2)}, u32[]{:S(2)}) async-start(bf16[4,16,3584]{2,1,0:T(8,128)(2,1)} %bitcast.95), calls=%async_computation.4 | async-start | bytes 917504 | tf_op jit(solution)/shard_map/all_to_all | solution.py:205
  158.8 10.7 %collective-permute-start.13 = (f32[8,256]{1,0:T(8,128)}, f32[8,256]{1,0:T(8,128)S(1)}, u32[]{:S(2)}, u32[]{:S(2)}) collective-permute-start(f32[8,256]{1,0:T(8,128)} %copy-done.17), channel_id=1, source_target_pairs={{2,0},{3,1},{4,2},{5,3},{6,4},{7,5},{0,6},{1,7},{10,8},{11,9},{12,... | collective-permute-start | bytes 24584 | tf_op jit(solution)/shard_map/ppermute | solution.py:222
  164.5 8.2 %collective-permute-start.14 = (f32[8,256]{1,0:T(8,128)}, f32[8,256]{1,0:T(8,128)S(1)}, u32[]{:S(2)}, u32[]{:S(2)}) collective-permute-start(f32[8,256]{1,0:T(8,128)} %copy-done.17), channel_id=1, source_target_pairs={{4,0},{5,1},{6,2},{7,3},{0,4},{1,5},{2,6},{3,7},{12,8},{13,9},{14,... | collective-permute-start | bytes 24584 | tf_op jit(solution)/shard_map/ppermute | solution.py:222
  166.4 7.6 %collective-permute-start.15 = (f32[8,256]{1,0:T(8,128)}, f32[8,256]{1,0:T(8,128)S(1)}, u32[]{:S(2)}, u32[]{:S(2)}) collective-permute-start(f32[8,256]{1,0:T(8,128)} %copy-done.17), channel_id=1, source_target_pairs={{6,0},{7,1},{0,2},{1,3},{2,4},{3,5},{4,6},{5,7},{14,8},{15,9},{8,1... | collective-permute-start | bytes 24584 | tf_op jit(solution)/shard_map/ppermute | solution.py:222
  174.6 5.6 %collective-permute-start.16 = (f32[32,3584]{1,0:T(8,128)S(1)}, f32[32,3584]{1,0:T(8,128)S(1)}, u32[]{:S(2)}, u32[]{:S(2)}) collective-permute-start(f32[32,3584]{1,0:T(8,128)S(1)} %get-tuple-element.36), channel_id=1, source_target_pairs={{0,1},{1,0},{2,3},{3,2},{4,5},{5,4},{6,7},{7,6},{8,9},{9,8},{10,11... | collective-permute-start | bytes 1376264 | tf_op jit(solution)/shard_map/ppermute | solution.py:196
  177.2 14.5 %collective-permute-start.12 = (bf16[8,3584]{1,0:T(8,128)(2,1)S(1)}, bf16[8,3584]{1,0:T(8,128)(2,1)S(1)}, u32[]{:S(2)}, u32[]{:S(2)}) collective-permute-start(bf16[8,3584]{1,0:T(8,128)(2,1)S(1)} %get-tuple-element.37), channel_id=1, source_target_pairs={{0,504},{8,496},{16,488},{24,480},{32,472},{40,464},{48,456},{56,4... | collective-permute-start | bytes 172040 | tf_op jit(solution)/shard_map/ppermute | solution.py:201

commit v4 on v2

v4 whole, which is shorter than its diff:
```python
import functools

import jax
import jax.numpy as jnp
from jax import lax
from jax.experimental import pallas as pl
from jax.experimental.pallas import tpu as pltpu
from jax.sharding import PartitionSpec as P

D = 3584
HID = 128
EXPERTS = 256
OWN = 32
TOKENS = 64
TOPK = 8
ROWS = 8
CHIPS = 4
IDCOLS = 128
WIDE = D + IDCOLS
WIDTH = 512
z_weight = 0.01
balance_weight = 1.0
F32 = jnp.float32
BF16 = jnp.bfloat16
VMEM_LIMIT = 16 * 1024 * 1024


def dot(lhs, rhs, lhs_dim, rhs_dim):
    return lax.dot_general(
        lhs, rhs, (((lhs_dim,), (rhs_dim,)), ((), ())), preferred_element_type=F32
    )


HBM = object()


def call(body, outs, scratch, args, flops):
    vmem = pl.BlockSpec(memory_space=pltpu.VMEM)
    hbm = pl.BlockSpec(memory_space=pltpu.HBM)
    total = sum(a.size * a.dtype.itemsize for a in args)
    return pl.pallas_call(
        body,
        out_shape=[jax.ShapeDtypeStruct(o[0], o[1]) for o in outs],
        in_specs=[vmem] * len(args),
        out_specs=[hbm if o[-1] is HBM else vmem for o in outs],
        scratch_shapes=scratch,
        compiler_params=pltpu.CompilerParams(vmem_limit_bytes=VMEM_LIMIT),
        cost_estimate=pl.CostEstimate(flops=flops, bytes_accessed=total, transcendentals=0),
    )(*args)


def packed(parts):
    return jnp.concatenate([p.astype(F32) for p in parts], axis=0).astype(BF16)


def write_all(block, out, sems):
    rows = block.shape[0]
    copies = [
        pltpu.make_async_copy(block, out.at[pl.ds(rows * k, rows), :], sems.at[k])
        for k in range(CHIPS)
    ]
    for copy in copies:
        copy.start()
    for copy in copies:
        copy.wait()


def id_columns(ids):
    empty = jnp.full((ROWS, IDCOLS - 2 * TOPK), -1.0, F32)
    used = jnp.concatenate([ids[0].astype(F32), ids[1].astype(F32), empty], axis=1)
    return jnp.concatenate([used, jnp.full((ROWS, IDCOLS), -1.0, F32)], axis=0).astype(BF16)


def mirror_pack_kernel(stash, grads, ids, out):
    out[:, 0:D] = packed([stash[0], grads[...]])
    out[:, D:WIDE] = id_columns(ids)


def first_spread_kernel(stash, grads, ids, other, out, block, sems):
    block[0:16, 0:D] = packed([stash[0], grads[...]])
    block[0:16, D:WIDE] = id_columns(ids)
    block[16:32, :] = other[...]
    write_all(block, out, sems)


def second_spread_kernel(stash, other, out, block, sems):
    block[...] = packed([stash[1], other[...]])
    write_all(block, out, sems)


def grads_spread_kernel(moved, head_a, head_b, out, block, sems):
    top = lax.axis_index("pipe") == lax.axis_size("pipe") - 1
    block[...] = moved[...]

    @pl.when(top)
    def _():
        block[...] = packed([head_a[0], head_b[0]])

    write_all(block, out, sems)


def summed(parts, cols):
    total = parts[0:16, cols].astype(F32)
    for k in range(1, CHIPS):
        total += parts[16 * k : 16 * k + 16, cols].astype(F32)
    return total


def first_emit_kernel(parts, grads_a, block_b, out):
    for low in range(0, D, WIDTH):
        cols = pl.ds(low, WIDTH)
        both = jnp.concatenate(
            [grads_a[:, cols].astype(F32), block_b[:, cols].astype(F32)[8:16]], axis=0
        )
        out[:, cols] = (both + summed(parts, cols)).astype(BF16)


def second_emit_kernel(parts, grads, out_a, out_b):
    for low in range(0, D, WIDTH):
        cols = pl.ds(low, WIDTH)
        both = grads[:, cols].astype(F32) + summed(parts, cols)
        out_a[:, cols] = both[0:8].astype(BF16)
        out_b[:, cols] = both[8:16].astype(BF16)


def backward_terms(hidden, gate, up, gates, ups, out, held, sems):
    d_gate, d_up = [], []
    for h, g, u in zip(hidden, gate, up):
        q = jax.nn.sigmoid(g)
        d_gate.append((h * u * q * (1.0 + g * (1.0 - q))).astype(BF16))
        d_up.append((h * g * q).astype(BF16))
    copies = []
    for low in range(0, D, WIDTH):
        cols = pl.ds(low, WIDTH)
        total = dot(d_gate[0], gates[0][cols, :], 1, 1)
        total += dot(d_gate[1], gates[1][cols, :], 1, 1)
        total += dot(d_up[0], ups[0][cols, :], 1, 1)
        total += dot(d_up[1], ups[1][cols, :], 1, 1)
        held[:, cols] = total.astype(BF16)
        copies.append(
            pltpu.make_async_copy(held.at[:, cols], out.at[:, cols], sems.at[low // WIDTH])
        )
        copies[-1].start()
    for copy in copies:
        copy.wait()


def first_tick_kernel(*refs):
    first, weights, out, held, sems = refs[0], refs[1:7], refs[7], refs[8], refs[9]
    gates, ups, downs = weights[0:2], weights[2:4], weights[4:6]
    rows = first[:, 0:D]

    def pick(value, offset):
        return jnp.concatenate(
            [value[16 * b + offset : 16 * b + offset + 8] for b in range(2 * CHIPS)], axis=0
        )

    gate = [pick(dot(rows, w[...], 1, 0), 0) for w in gates]
    up = [pick(dot(rows, w[...], 1, 0), 0) for w in ups]
    hidden = [pick(dot(rows, w[...], 1, 1), 8) for w in downs]
    backward_terms(hidden, gate, up, gates, ups, out, held, sems)


def second_tick_kernel(*refs):
    grads, pre, weights, out, held, sems = refs[0], refs[1:5], refs[5:11], *refs[11:14]
    gates, ups, downs = weights[0:2], weights[2:4], weights[4:6]
    rows = grads[...]
    hidden = [dot(rows, w[...], 1, 1) for w in downs]
    gate = [pre[0][...], pre[1][...]]
    up = [pre[2][...], pre[3][...]]
    backward_terms(hidden, gate, up, gates, ups, out, held, sems)


def forward_kernel(*refs):
    first, second, other_ids = refs[0:3]
    gates, ups, routers = refs[3:5], refs[5:7], refs[7:9]
    pre, expo_ref, share_ref, stats_ref = refs[9:13], *refs[13:16]
    member = lax.axis_index("expert")
    rows0, rows1 = first[:, 0:D], second[...]
    for w, out in zip((*gates, *ups), pre):
        out[...] = dot(rows1, w[...], 1, 0)
    logits = jnp.concatenate(
        [
            jnp.concatenate([dot(r[...], rows, 1, 1) for r in routers], axis=0)
            for rows in (rows0, jnp.concatenate([rows1, rows1], axis=0))
        ],
        axis=1,
    )
    ids = [first[:, D:WIDE].astype(F32).T, other_ids[...].astype(F32).T]
    row = lax.broadcasted_iota(jnp.int32, (2 * OWN, 128), 0)
    column = lax.broadcasted_iota(jnp.int32, (2 * OWN, 128), 1)
    own = row + OWN * member
    other = row - OWN + OWN * (member + 1 - 2 * lax.rem(member, 2))
    experts = jnp.where(row < OWN, own, other).astype(F32)
    stream_b = (column % 32) >= 16
    scale = EXPERTS / (TOKENS * TOPK)
    shares = []
    for tick in range(2):
        hits = jnp.zeros((2 * OWN, 128), F32)
        for core in range(2):
            for j in range(TOPK):
                slot = TOPK * tick + j
                hits += (experts == ids[core][slot : slot + 1, :]).astype(F32)
        count_a = jnp.sum(jnp.where(stream_b, 0.0, hits), axis=1, keepdims=True)
        count_b = jnp.sum(jnp.where(stream_b, hits, 0.0), axis=1, keepdims=True)
        shares.append((count_a * scale, count_b * scale))
    share0 = jnp.where(stream_b, shares[0][1], shares[0][0])
    share1 = jnp.where((column % 16) >= 8, shares[1][1], shares[1][0])
    share = jnp.concatenate([share0, share1], axis=1)
    peak = jnp.max(logits, axis=0, keepdims=True)
    expo = jnp.exp(logits - peak)
    total = jnp.sum(expo, axis=0, keepdims=True)
    weighted = jnp.sum(expo * share, axis=0, keepdims=True)
    expo_ref[...] = expo
    share_ref[...] = share
    stats_ref[...] = jnp.concatenate(
        [peak, total, weighted, jnp.zeros((5, 256), F32)], axis=0
    )


def router_kernel(*refs):
    first, second, expo_ref, share_ref = refs[0:4]
    stats, own_out, other_out = refs[4:8], refs[8], refs[9]
    peaks = [s[0:1, :] for s in stats]
    peak = functools.reduce(jnp.maximum, peaks)
    factors = [jnp.exp(p - peak) for p in peaks]
    total = sum(s[1:2, :] * f for s, f in zip(stats, factors))
    weighted = sum(s[2:3, :] * f for s, f in zip(stats, factors))
    log_total = peak + jnp.log(total)
    mean_share = weighted / total
    probs = expo_ref[...] * (factors[0] / total)
    slopes = (
        2.0 * z_weight * log_total - balance_weight * mean_share + balance_weight * share_ref[...]
    ) * probs
    column = lax.broadcasted_iota(jnp.int32, (2 * OWN, 128), 1)
    slopes0 = jnp.where((column % 16) < 8, slopes[:, 0:128], 0.0).astype(BF16)
    slopes1 = slopes[:, 128:192].astype(BF16)
    for low in range(0, D, WIDTH):
        cols = pl.ds(low, WIDTH)
        part = dot(slopes0, first[:, cols], 1, 0) + dot(slopes1, second[:, cols], 1, 0)
        own_out[:, cols] = part[0:OWN]
        other_out[:, cols] = part[OWN:]


def swapped(value):
    return lax.ppermute(value, "expert", [(e, e ^ 1) for e in range(8)])


def mirrored(value):
    count = lax.axis_size("pipe")
    return lax.ppermute(value, "pipe", [(i, count - 1 - i) for i in range(count)])


def exchanged(blocks):
    return lax.all_to_all(
        blocks, "expert", split_axis=0, concat_axis=0, tiled=True,
        axis_index_groups=[[0, 2, 4, 6], [1, 3, 5, 7]],
    )


def from_chip(value, k):
    return lax.ppermute(value, "expert", [((e + 2 * k) % 8, e) for e in range(8)])


def ring(value):
    return [value] + [from_chip(value, k) for k in range(1, CHIPS)]


def after(value, *earlier):
    return lax.optimization_barrier((value, *earlier))[0]


def shards(
    stash_a, stash_b, ids_a, ids_b, arriving_a, arriving_b, head_a, head_b,
    w_gate, w_up, w_down, router,
):
    stash_a, stash_b, ids_a, ids_b = stash_a[0], stash_b[0], ids_a[0], ids_b[0]
    arriving_a, arriving_b = arriving_a[0], arriving_b[0]
    w_gate, w_up, w_down, router = w_gate[0], w_up[0], w_down[0], router[0]
    top = lax.axis_size("pipe") - 1
    weights = (w_gate, w_up, w_down)
    spread_sems = pltpu.SemaphoreType.DMA((CHIPS,))
    terms_scratch = [pltpu.VMEM((64, D), BF16), pltpu.SemaphoreType.DMA((D // WIDTH,))]

    (packed_b,) = call(mirror_pack_kernel, [((16, WIDE), BF16)], [], [stash_b, arriving_b, ids_b], 0)
    block_b = mirrored(packed_b)
    (blocks,) = call(
        first_spread_kernel, [((128, WIDE), BF16, HBM)],
        [pltpu.VMEM((32, WIDE), BF16), spread_sems], [stash_a, arriving_a, ids_a, block_b], 0,
    )
    first = exchanged(blocks)
    later_b = mirrored(after(stash_b[1], block_b))
    others = [swapped(after(weight, block_b)) for weight in weights]
    pairs = [w for pair in zip(weights, others) for w in pair]

    (terms,) = call(
        first_tick_kernel, [((64, D), BF16, HBM)], terms_scratch,
        [first] + pairs, 2 * 128 * D * 128 * 10,
    )
    parts = exchanged(after(terms, later_b))
    other_router = swapped(after(router, terms))
    other_ids = swapped(after(first[:, D:], terms))
    (out,) = call(first_emit_kernel, [((16, D), BF16)], [], [parts, arriving_a, block_b], 0)
    out = after(out, other_router, other_ids)
    moved = lax.ppermute(out, "pipe", [(i, i - 1) for i in range(1, top + 1)])

    (blocks,) = call(
        second_spread_kernel, [((64, D), BF16, HBM)],
        [pltpu.VMEM((16, D), BF16), spread_sems], [stash_a, later_b], 0,
    )
    second = exchanged(after(blocks, out))
    blocks, grads = call(
        grads_spread_kernel, [((64, D), BF16, HBM), ((16, D), BF16)], [spread_sems],
        [moved, head_a, head_b], 0,
    )
    all_grads = exchanged(after(blocks, second))
    *pre, expo, share, stats = call(
        forward_kernel,
        [((64, HID), F32)] * 4 + [((2 * OWN, 256), F32)] * 2 + [((8, 256), F32)], [],
        [first, second, other_ids] + pairs[:4] + [router, other_router], 2 * 128 * D * 128 * 4,
    )
    stats = ring(stats)
    (terms,) = call(
        second_tick_kernel, [((64, D), BF16, HBM)], terms_scratch,
        [after(all_grads, *stats)] + pre + pairs, 2 * 64 * D * 128 * 6,
    )
    parts = exchanged(terms)
    own, other = call(
        router_kernel, [((OWN, D), F32)] * 2, [],
        [first, second, after(expo, terms), share, *stats], 2 * 192 * D * 64,
    )
    router_grad = own + swapped(other)
    out_a, out_b = call(second_emit_kernel, [((ROWS, D), BF16)] * 2, [], [parts, grads], 0)
    return out_a[None], mirrored(out_b)[None], router_grad[None]


def solution(mesh):
    placed = (
        P("pipe", None, "expert", None),
        P("pipe", None, "expert", None),
        P("pipe", None, "expert", None),
        P("pipe", None, "expert", None),
        P("pipe", "expert", None),
        P("pipe", "expert", None),
        P(None, "expert", None),
        P(None, "expert", None),
        P("pipe", None, "expert"),
        P("pipe", None, "expert"),
        P("pipe", "expert", None),
        P("pipe", "expert", None),
    )
    return jax.shard_map(
        shards,
        mesh=mesh,
        in_specs=placed,
        out_specs=(P("pipe", "expert", None), P("pipe", "expert", None), P("pipe", "expert", None)),
        check_vma=False,
    )
```

time: 182 us -> 190 us (1.044)
  blocking collectives: 8 us -> 0 us
  waiting for transfers between devices: 42.6 us -> 50.1 us
  local copies, waits for them, and re-layouts: 22.3 us -> 29.7 us
  other arithmetic: 7.53 us -> 0.82 us
  starting transfers between devices: 86.6 us -> 91.9 us
    ppermute x0 -> x3, starting transfers between devices: none -> 10.7 us  [from_chip(): lax.ppermute(value, 'expert', [((e + 2 * k) % 8, e) for e in range(8)])]
    unnamed x66 -> x89, local copies, waits for them, and re-layouts: 19.6 us -> 29.1 us
    all_to_all x1 -> x0, blocking collectives: 8 us -> none  [exchanged(): lax.all_to_all(blocks, 'expert', split_axis=0, concat_axis=0, tiled=True,...]
    ppermute x3, starting transfers between devices: 39.8 us -> 31.8 us  [mirrored(): lax.ppermute(value, 'pipe', [(i, count - 1 - i) for i in range(count)])]
    ppermute x1, waiting for transfers between devices: 4.14 us -> 9.79 us  [shards(): moved = lax.ppermute(out, 'pipe', [(i, i - 1) for i in range(1, top + 1)])]
    ppermute x0 -> x3, waiting for transfers between devices: none -> 4.31 us  [from_chip(): lax.ppermute(value, 'expert', [((e + 2 * k) % 8, e) for e in range(8)])]
    concatenate x8 -> x0, other arithmetic: 3.41 us -> none  [the longest x3 2.4 us: spread(): return exchanged(jnp.concatenate([value] * CHIPS, axis=0))]
    convert_element_type x3 -> x0, other arithmetic: 2.36 us -> none  [the longest x2 2.28 us: emitted(): return total.astype(BF16)]
  transfers between devices with their start and end apart: 16 -> 18, of which waited for: 10 -> 8; matrix products, arithmetic and copies ran while one was open for 5% -> 1% of each run, Pallas kernels for 3% -> 5%
where the time goes in v4:
time: 190 us; the launch traced here: 188 us
  starting transfers between devices  91.9 us (48%)
  waiting for transfers between devices  50.1 us (26%)
  local copies, waits for them, and re-layouts  29.7 us (16%)
  Pallas kernels  14.3 us (8%)
    all_to_all x5, starting transfers between devices, exchanged(): lax.all_to_all(blocks, 'expert', split_axis=0, concat_axis=0, tiled=True,...  33.5 us
    ppermute x3, starting transfers between devices, mirrored(): lax.ppermute(value, 'pipe', [(i, count - 1 - i) for i in range(count)])  31.8 us
    unnamed x89, local copies, waits for them, and re-layouts  29.1 us
    ppermute x3, waiting for transfers between devices, mirrored(): lax.ppermute(value, 'pipe', [(i, count - 1 - i) for i in range(count)])  18.9 us
    all_to_all x5, waiting for transfers between devices, exchanged(): lax.all_to_all(blocks, 'expert', split_axis=0, concat_axis=0, tiled=True,...  17 us
    pallas_call x10, Pallas kernels, call(): pl.pallas_call(body, out_shape=[jax.ShapeDtypeStruct(o[0], o[1]) for o in...  14.3 us
    ppermute x6, starting transfers between devices, swapped(): return lax.ppermute(value, 'expert', [(e, e ^ 1) for e in range(8)])  12.6 us
    ppermute x3, starting transfers between devices, from_chip(): lax.ppermute(value, 'expert', [((e + 2 * k) % 8, e) for e in range(8)])  10.7 us
  transfers between devices with their start and end apart: 18, of which 8 were waited for; matrix products, arithmetic and copies ran while one was open for 1% of the time, Pallas kernels for 5%

profile of v4, /device:TPU:6, one launch (start us, length us, event | category | flops | bytes accessed | tf_op | source)
XLA Modules:
  0.0 187.9 jit_solution(13932399357565842664)
XLA Ops:
  0.6 0.9 copy-done.21
  1.5 0.8 copy-done.31
  3.1 15.2 %collective-permute-start = (bf16[16,3712]{1,0:T(8,128)(2,1)S(1)}, bf16[16,3712]{1,0:T(8,128)(2,1)S(1)}, u32[]{:S(2)}, u32[]{:S(2)}) collective-permute-start(bf16[16,3712]{1,0:T(8,128)(2,1)S(1)} %shard_map.139), channel_id=1, source_target_pairs={{0,504},{8,496},{16,488},{24,480},{32,472},{40,464},{48,456},{56,4... | collective-permute-start | bytes 356360 | tf_op jit(solution)/shard_map/ppermute | solution.py:251
  18.4 10.1 %collective-permute-done.other.block_b = bf16[16,3712]{1,0:T(8,128)(2,1)S(1)} collective-permute-done((bf16[16,3712]{1,0:T(8,128)(2,1)S(1)}, bf16[16,3712]{1,0:T(8,128)(2,1)S(1)}, u32[]{:S(2)}, u32[]{:S(2)}) %collective-permute-start) | collective-permute-done | bytes 118816 | tf_op jit(solution)/shard_map/ppermute | solution.py:251
  28.5 1.3 shard_map.140
  29.8 1.0 copy-done.10
  30.8 4.1 %all-to-all-start = ((bf16[4,32,3712]{2,1,0:T(8,128)(2,1)}), bf16[4,32,3712]{2,1,0:T(8,128)(2,1)S(1)}, u32[]{:S(2)}, u32[]{:S(2)}) async-start(bf16[4,32,3712]{2,1,0:T(8,128)(2,1)} %bitcast.40), calls=%async_computation | async-start | bytes 1900544 | tf_op jit(solution)/shard_map/all_to_all | solution.py:255
  34.9 1.9 %collective-permute-start.1 = (bf16[3584,128]{1,0:T(8,128)(2,1)S(1)}, bf16[3584,128]{1,0:T(8,128)(2,1)S(1)}, u32[]{:S(2)}, u32[]{:S(2)}) collective-permute-start(bf16[3584,128]{1,0:T(8,128)(2,1)S(1)} %bitcast.30), channel_id=1, source_target_pairs={{0,1},{1,0},{2,3},{3,2},{4,5},{5,4},{6,7},{7,6},{8,9},{9,8},{10,11... | collective-permute-start | bytes 2752520 | tf_op jit(solution)/shard_map/ppermute | solution.py:246
  36.8 2.4 %collective-permute-start.2 = (bf16[3584,128]{1,0:T(8,128)(2,1)S(1)}, bf16[3584,128]{1,0:T(8,128)(2,1)S(1)}, u32[]{:S(2)}, u32[]{:S(2)}) collective-permute-start(bf16[3584,128]{1,0:T(8,128)(2,1)S(1)} %bitcast.34), channel_id=1, source_target_pairs={{0,1},{1,0},{2,3},{3,2},{4,5},{5,4},{6,7},{7,6},{8,9},{9,8},{10,11... | collective-permute-start | bytes 2752520 | tf_op jit(solution)/shard_map/ppermute | solution.py:246
  39.2 1.9 %collective-permute-start.3 = (bf16[128,3584]{1,0:T(8,128)(2,1)}, bf16[128,3584]{1,0:T(8,128)(2,1)S(1)}, u32[]{:S(2)}, u32[]{:S(2)}) collective-permute-start(bf16[128,3584]{1,0:T(8,128)(2,1)} %bitcast.41), channel_id=1, source_target_pairs={{0,1},{1,0},{2,3},{3,2},{4,5},{5,4},{6,7},{7,6},{8,9},{9,8},{10,11... | collective-permute-start | bytes 2752520 | tf_op jit(solution)/shard_map/ppermute | solution.py:246
  41.2 12.1 %collective-permute-start.4 = (bf16[8,3584]{1,0:T(8,128)(2,1)S(1)}, bf16[8,3584]{1,0:T(8,128)(2,1)S(1)}, u32[]{:S(2)}, u32[]{:S(2)}) collective-permute-start(bf16[8,3584]{1,0:T(8,128)(2,1)S(1)} %slice_bitcast_fusion), channel_id=1, source_target_pairs={{0,504},{8,496},{16,488},{24,480},{32,472},{40,464},{48,456},{56,4... | collective-permute-start | bytes 172040 | tf_op jit(solution)/shard_map/ppermute | solution.py:251
  53.3 0.9 copy-done.2
  54.3 0.9 copy-done.6
  55.2 1.0 copy-done.13
  56.2 4.1 %all-to-all-done = bf16[4,32,3712]{2,1,0:T(8,128)(2,1)S(1)} async-done(((bf16[4,32,3712]{2,1,0:T(8,128)(2,1)}), bf16[4,32,3712]{2,1,0:T(8,128)(2,1)S(1)}, u32[]{:S(2)}, u32[]{:S(2)}) %all-to-all-start) | async-done | bytes 950304 | tf_op jit(solution)/shard_map/all_to_all | solution.py:255
  60.2 1.2 copy-done.3
  61.4 1.2 copy-done.7
  62.6 1.2 copy-done.11
  63.7 1.2 copy-done.14
  64.9 3.7 %shard_map.141 = bf16[64,3584]{1,0:T(8,128)(2,1)S(1)} custom-call(bf16[128,3712]{1,0:T(8,128)(2,1)S(1)} %bitcast.26, bf16[3584,128]{1,0:T(8,128)(2,1)S(1)} %bitcast.31, bf16[3584,128]{1,0:T(8,128)(2,1)S(1)} %copy-done.3, bf16[3584,128]{1,0:T(8,128)(2,1)S(1)} %bitcast.35, bf16[3584,128]{1,0:T(8,128)(2,1)S(1)} %copy-done.7, bf16[128,3584]{1,0:T(8,128)(2,1)S(1)} %bitcast.42, ...), custom_call_target="tpu_custom_call" | custom-call | flops 1174405120 | bytes 6455296 | tf_op jit(solution)/shard_map/pallas_call | solution.py:41
  70.1 3.5 %all-to-all-start.1 = ((bf16[4,16,3584]{2,1,0:T(8,128)(2,1)}), bf16[4,16,3584]{2,1,0:T(8,128)(2,1)S(1)}, u32[]{:S(2)}, u32[]{:S(2)}) async-start(bf16[4,16,3584]{2,1,0:T(8,128)(2,1)} %bitcast.48), calls=%async_computation.1 | async-start | bytes 917504 | tf_op jit(solution)/shard_map/all_to_all | solution.py:255
  73.6 2.1 %collective-permute-start.5 = (bf16[32,3584]{1,0:T(8,128)(2,1)}, bf16[32,3584]{1,0:T(8,128)(2,1)}, u32[]{:S(2)}, u32[]{:S(2)}) collective-permute-start(bf16[32,3584]{1,0:T(8,128)(2,1)} %bitcast.55), channel_id=1, source_target_pairs={{0,1},{1,0},{2,3},{3,2},{4,5},{5,4},{6,7},{7,6},{8,9},{9,8},{10,11... | collective-permute-start | bytes 688136 | tf_op jit(solution)/shard_map/ppermute | solution.py:246
  76.2 2.4 %collective-permute-start.6 = (bf16[128,128]{1,0:T(8,128)(2,1)}, bf16[128,128]{1,0:T(8,128)(2,1)}, u32[]{:S(2)}, u32[]{:S(2)}) collective-permute-start(bf16[128,128]{1,0:T(8,128)(2,1)} %slice.9), channel_id=1, source_target_pairs={{0,1},{1,0},{2,3},{3,2},{4,5},{5,4},{6,7},{7,6},{8,9},{9,8},{10,11... | collective-permute-start | bytes 98312 | tf_op jit(solution)/shard_map/ppermute | solution.py:246
  79.3 0.8 copy-done.17
  80.1 4.9 %all-to-all-done.1 = bf16[4,16,3584]{2,1,0:T(8,128)(2,1)S(1)} async-done(((bf16[4,16,3584]{2,1,0:T(8,128)(2,1)}), bf16[4,16,3584]{2,1,0:T(8,128)(2,1)S(1)}, u32[]{:S(2)}, u32[]{:S(2)}) %all-to-all-start.1) | async-done | bytes 458784 | tf_op jit(solution)/shard_map/all_to_all | solution.py:255
  85.1 3.6 %all-to-all-start.2 = ((bf16[4,16,3584]{2,1,0:T(8,128)(2,1)}), bf16[4,16,3584]{2,1,0:T(8,128)(2,1)S(1)}, u32[]{:S(2)}, u32[]{:S(2)}) async-start(bf16[4,16,3584]{2,1,0:T(8,128)(2,1)} %bitcast.45), calls=%async_computation.2 | async-start | bytes 917504 | tf_op jit(solution)/shard_map/all_to_all | solution.py:255
  88.7 3.3 %collective-permute-start.7 = (bf16[16,3584]{1,0:T(8,128)(2,1)S(1)}, bf16[16,3584]{1,0:T(8,128)(2,1)S(1)}, u32[]{:S(2)}, u32[]{:S(2)}) collective-permute-start(bf16[16,3584]{1,0:T(8,128)(2,1)S(1)} %shard_map.142), channel_id=1, source_target_pairs={{8,0},{16,8},{24,16},{32,24},{40,32},{48,40},{56,48},{64,56},{72,6... | collective-permute-start | bytes 344072 | tf_op jit(solution)/shard_map/ppermute | solution.py:305
  92.0 9.8 %collective-permute-done.7.moved = bf16[16,3584]{1,0:T(8,128)(2,1)S(1)} collective-permute-done((bf16[16,3584]{1,0:T(8,128)(2,1)S(1)}, bf16[16,3584]{1,0:T(8,128)(2,1)S(1)}, u32[]{:S(2)}, u32[]{:S(2)}) %collective-permute-start.7) | collective-permute-done | bytes 114720 | tf_op jit(solution)/shard_map/ppermute | solution.py:305
  103.8 18.8 %all-to-all-start.3 = ((bf16[4,16,3584]{2,1,0:T(8,128)(2,1)}), bf16[4,16,3584]{2,1,0:T(8,128)(2,1)}, u32[]{:S(2)}, u32[]{:S(2)}) async-start(bf16[4,16,3584]{2,1,0:T(8,128)(2,1)} %bitcast.51), calls=%async_computation.3 | async-start | bytes 917504 | tf_op jit(solution)/shard_map/all_to_all | solution.py:255
  122.6 1.2 copy-done.4
  123.8 1.2 copy-done.8
  125.0 2.8 %shard_map.145 = (f32[64,128]{1,0:T(8,128)S(1)}, f32[64,128]{1,0:T(8,128)S(1)}, f32[64,128]{1,0:T(8,128)S(1)}, f32[64,128]{1,0:T(8,128)S(1)}, f32[64,256]{1,0:T(...) custom-call(bf16[128,3712]{1,0:T(8,128)(2,1)S(1)} %bitcast.28, bf16[64,3584]{1,0:T(8,128)(2,1)S(1)} %bitcast.38, ...), custom_call_target="tpu_custom_call" | custom-call | flops 469762048 | bytes 5570560 | tf_op jit(solution)/shard_map/pallas_call | solution.py:41
  130.8 5.7 %collective-permute-start.8 = (f32[8,256]{1,0:T(8,128)S(1)}, f32[8,256]{1,0:T(8,128)S(1)}, u32[]{:S(2)}, u32[]{:S(2)}) collective-permute-start(f32[8,256]{1,0:T(8,128)S(1)} %get-tuple-element.39.refs_4_), channel_id=1, source_target_pairs={{2,0},{3,1},{4,2},{5,3},{6,4},{7,5},{0,6},{1,7},{10,8},{11,9},{12,... | collective-permute-start | bytes 24584 | tf_op jit(solution)/shard_map/ppermute | solution.py:262
  136.6 1.9 %collective-permute-start.9 = (f32[8,256]{1,0:T(8,128)S(1)}, f32[8,256]{1,0:T(8,128)S(1)}, u32[]{:S(2)}, u32[]{:S(2)}) collective-permute-start(f32[8,256]{1,0:T(8,128)S(1)} %get-tuple-element.39.refs_4_), channel_id=1, source_target_pairs={{4,0},{5,1},{6,2},{7,3},{0,4},{1,5},{2,6},{3,7},{12,8},{13,9},{14,... | collective-permute-start | bytes 24584 | tf_op jit(solution)/shard_map/ppermute | solution.py:262
  138.5 3.0 %collective-permute-start.10 = (f32[8,256]{1,0:T(8,128)S(1)}, f32[8,256]{1,0:T(8,128)S(1)}, u32[]{:S(2)}, u32[]{:S(2)}) collective-permute-start(f32[8,256]{1,0:T(8,128)S(1)} %get-tuple-element.39.refs_4_), channel_id=1, source_target_pairs={{6,0},{7,1},{0,2},{1,3},{2,4},{3,5},{4,6},{5,7},{14,8},{15,9},{8,1... | collective-permute-start | bytes 24584 | tf_op jit(solution)/shard_map/ppermute | solution.py:262
  141.5 1.5 collective-permute-done.9.refs_6_
  143.1 2.8 %collective-permute-done.10.refs_7_ = f32[8,256]{1,0:T(8,128)S(1)} collective-permute-done((f32[8,256]{1,0:T(8,128)S(1)}, f32[8,256]{1,0:T(8,128)S(1)}, u32[]{:S(2)}, u32[]{:S(2)}) %collective-permute-start.10) | collective-permute-done | bytes 8224 | tf_op jit(solution)/shard_map/ppermute | solution.py:262
  145.8 1.2 copy-done.5
  147.0 1.2 copy-done.9
  148.2 1.2 copy-done.12
  149.4 1.2 copy-done.15
  153.6 4.0 %shard_map.146 = bf16[64,3584]{1,0:T(8,128)(2,1)S(1)} custom-call(bf16[64,3584]{1,0:T(8,128)(2,1)} %bitcast.18.refs_0_, f32[64,128]{1,0:T(8,128)S(1)} %copy-done.35, f32[64,128]{1,0:T(8,128)S(1)} %copy-done.37, f32[64,128]{1,0:T(8,128)S(1)} %copy-done.39, f32[64,128]{1,0:T(8,128)S(1)} %copy-done.41, bf16[3584,128]{1,0:T(8,128)(2,1)S(1)} %bitcast.33, ...), custom_call_target="tpu_custom_call" | custom-call | flops 352321536 | bytes 6094848 | tf_op jit(solution)/shard_map/pallas_call | solution.py:41
  158.3 3.6 %all-to-all-start.4 = ((bf16[4,16,3584]{2,1,0:T(8,128)(2,1)}), bf16[4,16,3584]{2,1,0:T(8,128)(2,1)S(1)}, u32[]{:S(2)}, u32[]{:S(2)}) async-start(bf16[4,16,3584]{2,1,0:T(8,128)(2,1)} %bitcast.44), calls=%async_computation.4 | async-start | bytes 917504 | tf_op jit(solution)/shard_map/all_to_all | solution.py:255
  162.4 1.9 %collective-permute-start.12 = (f32[32,3584]{1,0:T(8,128)S(1)}, f32[32,3584]{1,0:T(8,128)S(1)}, u32[]{:S(2)}, u32[]{:S(2)}) collective-permute-start(f32[32,3584]{1,0:T(8,128)S(1)} %get-tuple-element.52), channel_id=1, source_target_pairs={{0,1},{1,0},{2,3},{3,2},{4,5},{5,4},{6,7},{7,6},{8,9},{9,8},{10,11... | collective-permute-start | bytes 1376264 | tf_op jit(solution)/shard_map/ppermute | solution.py:246
  164.3 8.1 %all-to-all-done.4 = bf16[4,16,3584]{2,1,0:T(8,128)(2,1)S(1)} async-done(((bf16[4,16,3584]{2,1,0:T(8,128)(2,1)}), bf16[4,16,3584]{2,1,0:T(8,128)(2,1)S(1)}, u32[]{:S(2)}, u32[]{:S(2)}) %all-to-all-start.4) | async-done | bytes 458784 | tf_op jit(solution)/shard_map/all_to_all | solution.py:255
  173.0 4.5 %collective-permute-start.11 = (bf16[8,3584]{1,0:T(8,128)(2,1)S(1)}, bf16[8,3584]{1,0:T(8,128)(2,1)S(1)}, u32[]{:S(2)}, u32[]{:S(2)}) collective-permute-start(bf16[8,3584]{1,0:T(8,128)(2,1)S(1)} %get-tuple-element.47), channel_id=1, source_target_pairs={{0,504},{8,496},{16,488},{24,480},{32,472},{40,464},{48,456},{56,4... | collective-permute-start | bytes 172040 | tf_op jit(solution)/shard_map/ppermute | solution.py:251
  177.6 0.8 add_bitcast_fusion
  178.4 8.8 %collective-permute-done.11 = bf16[8,3584]{1,0:T(8,128)(2,1)S(1)} collective-permute-done((bf16[8,3584]{1,0:T(8,128)(2,1)S(1)}, bf16[8,3584]{1,0:T(8,128)(2,1)S(1)}, u32[]{:S(2)}, u32[]{:S(2)}) %collective-permute-start.11) | collective-permute-done | bytes 57376 | tf_op jit(solution)/shard_map/ppermute | solution.py:251
  (90 shorter events, 14.2 us)
Async XLA Ops:
  0.6 0.9 copy-start.21
  1.5 0.8 copy-start.31
  3.0 25.4 %copy-start.19 = (bf16[1,2,8,3584]{3,2,1,0:T(8,128)(2,1)S(1)}, bf16[1,2,8,3584]{3,2,1,0:T(8,128)(2,1)}, u32[]{:S(2)}) copy-start(bf16[1,2,8,3584]{3,2,1,0:T(8,128)(2,1)} %param.12) | copy-start | bytes 344068
  3.1 25.4 %copy-start.23 = (bf16[1,8,3584]{2,1,0:T(8,128)(2,1)S(1)}, bf16[1,8,3584]{2,1,0:T(8,128)(2,1)}, u32[]{:S(2)}) copy-start(bf16[1,8,3584]{2,1,0:T(8,128)(2,1)} %param.16) | copy-start | bytes 172036
  3.1 25.4 %copy-start.42 = (s32[1,2,8,8]{3,2,1,0:T(8,128)S(1)}, s32[1,2,8,8]{3,2,1,0:T(8,128)}, u32[]{:S(2)}) copy-start(s32[1,2,8,8]{3,2,1,0:T(8,128)} %param.14) | copy-start | bytes 1540
  3.1 25.3 %collective-permute-start = (bf16[16,3712]{1,0:T(8,128)(2,1)S(1)}, bf16[16,3712]{1,0:T(8,128)(2,1)S(1)}, u32[]{:S(2)}, u32[]{:S(2)}) collective-permute-start(bf16[16,3712]{1,0:T(8,128)(2,1)S(1)} %shard_map.139), channel_id=1, source_target_pairs={{0,504},{8,496},{16,488},{24,480},{32,472},{40,464},{48,456},{56,4... | collective-permute-start | bytes 356360 | tf_op jit(solution)/shard_map/ppermute | solution.py:251
  28.5 12.7 %copy-start.22 = (bf16[1,2,8,3584]{3,2,1,0:T(8,128)(2,1)S(1)}, bf16[1,2,8,3584]{3,2,1,0:T(8,128)(2,1)}, u32[]{:S(2)}) copy-start(bf16[1,2,8,3584]{3,2,1,0:T(8,128)(2,1)} %param.13) | copy-start | bytes 344068
  29.8 1.0 copy-start.10
  30.8 4.1 %copy-start = (bf16[1,3584,128]{2,1,0:T(8,128)(2,1)S(1)}, bf16[1,3584,128]{2,1,0:T(8,128)(2,1)}, u32[]{:S(2)}) copy-start(bf16[1,3584,128]{2,1,0:T(8,128)(2,1)} %param.20) | copy-start | bytes 2752516
  30.8 6.0 %copy-start.1 = (bf16[1,3584,128]{2,1,0:T(8,128)(2,1)S(1)}, bf16[1,3584,128]{2,1,0:T(8,128)(2,1)}, u32[]{:S(2)}) copy-start(bf16[1,3584,128]{2,1,0:T(8,128)(2,1)} %param.21) | copy-start | bytes 2752516
  30.8 29.4 %all-to-all-start = ((bf16[4,32,3712]{2,1,0:T(8,128)(2,1)}), bf16[4,32,3712]{2,1,0:T(8,128)(2,1)S(1)}, u32[]{:S(2)}, u32[]{:S(2)}) async-start(bf16[4,32,3712]{2,1,0:T(8,128)(2,1)} %bitcast.40), calls=%async_computation | async-start | bytes 1900544 | tf_op jit(solution)/shard_map/all_to_all | solution.py:255
  34.9 18.4 %collective-permute-start.1 = (bf16[3584,128]{1,0:T(8,128)(2,1)S(1)}, bf16[3584,128]{1,0:T(8,128)(2,1)S(1)}, u32[]{:S(2)}, u32[]{:S(2)}) collective-permute-start(bf16[3584,128]{1,0:T(8,128)(2,1)S(1)} %bitcast.30), channel_id=1, source_target_pairs={{0,1},{1,0},{2,3},{3,2},{4,5},{5,4},{6,7},{7,6},{8,9},{9,8},{10,11... | collective-permute-start | bytes 2752520 | tf_op jit(solution)/shard_map/ppermute | solution.py:246
  36.8 17.4 %collective-permute-start.2 = (bf16[3584,128]{1,0:T(8,128)(2,1)S(1)}, bf16[3584,128]{1,0:T(8,128)(2,1)S(1)}, u32[]{:S(2)}, u32[]{:S(2)}) collective-permute-start(bf16[3584,128]{1,0:T(8,128)(2,1)S(1)} %bitcast.34), channel_id=1, source_target_pairs={{0,1},{1,0},{2,3},{3,2},{4,5},{5,4},{6,7},{7,6},{8,9},{9,8},{10,11... | collective-permute-start | bytes 2752520 | tf_op jit(solution)/shard_map/ppermute | solution.py:246
  39.2 16.0 %collective-permute-start.3 = (bf16[128,3584]{1,0:T(8,128)(2,1)}, bf16[128,3584]{1,0:T(8,128)(2,1)S(1)}, u32[]{:S(2)}, u32[]{:S(2)}) collective-permute-start(bf16[128,3584]{1,0:T(8,128)(2,1)} %bitcast.41), channel_id=1, source_target_pairs={{0,1},{1,0},{2,3},{3,2},{4,5},{5,4},{6,7},{7,6},{8,9},{9,8},{10,11... | collective-permute-start | bytes 2752520 | tf_op jit(solution)/shard_map/ppermute | solution.py:246
  41.2 28.3 %collective-permute-start.4 = (bf16[8,3584]{1,0:T(8,128)(2,1)S(1)}, bf16[8,3584]{1,0:T(8,128)(2,1)S(1)}, u32[]{:S(2)}, u32[]{:S(2)}) collective-permute-start(bf16[8,3584]{1,0:T(8,128)(2,1)S(1)} %slice_bitcast_fusion), channel_id=1, source_target_pairs={{0,504},{8,496},{16,488},{24,480},{32,472},{40,464},{48,456},{56,4... | collective-permute-start | bytes 172040 | tf_op jit(solution)/shard_map/ppermute | solution.py:251
  53.3 0.9 copy-start.2
  54.3 0.9 copy-start.6
  55.2 1.0 copy-start.13
  60.2 1.2 copy-start.3
  61.4 1.2 copy-start.7
  62.6 1.2 copy-start.11
  63.7 1.2 copy-start.14
  68.7 0.8 copy-start.18
  70.1 14.9 %all-to-all-start.1 = ((bf16[4,16,3584]{2,1,0:T(8,128)(2,1)}), bf16[4,16,3584]{2,1,0:T(8,128)(2,1)S(1)}, u32[]{:S(2)}, u32[]{:S(2)}) async-start(bf16[4,16,3584]{2,1,0:T(8,128)(2,1)} %bitcast.48), calls=%async_computation.1 | async-start | bytes 917504 | tf_op jit(solution)/shard_map/all_to_all | solution.py:255
  73.6 5.1 %copy-start.30 = (bf16[8,3584]{1,0:T(8,128)(2,1)S(1)}, bf16[8,3584]{1,0:T(8,128)(2,1)}, u32[]{:S(2)}) copy-start(bf16[8,3584]{1,0:T(8,128)(2,1)} %copy-done.29) | copy-start | bytes 172036
  73.6 11.5 %collective-permute-start.5 = (bf16[32,3584]{1,0:T(8,128)(2,1)}, bf16[32,3584]{1,0:T(8,128)(2,1)}, u32[]{:S(2)}, u32[]{:S(2)}) collective-permute-start(bf16[32,3584]{1,0:T(8,128)(2,1)} %bitcast.55), channel_id=1, source_target_pairs={{0,1},{1,0},{2,3},{3,2},{4,5},{5,4},{6,7},{7,6},{8,9},{9,8},{10,11... | collective-permute-start | bytes 688136 | tf_op jit(solution)/shard_map/ppermute | solution.py:246
  76.2 8.8 %collective-permute-start.6 = (bf16[128,128]{1,0:T(8,128)(2,1)}, bf16[128,128]{1,0:T(8,128)(2,1)}, u32[]{:S(2)}, u32[]{:S(2)}) collective-permute-start(bf16[128,128]{1,0:T(8,128)(2,1)} %slice.9), channel_id=1, source_target_pairs={{0,1},{1,0},{2,3},{3,2},{4,5},{5,4},{6,7},{7,6},{8,9},{9,8},{10,11... | collective-permute-start | bytes 98312 | tf_op jit(solution)/shard_map/ppermute | solution.py:246
  79.3 0.8 copy-start.17
  85.1 16.7 %copy-start.32 = (bf16[1,8,3584]{2,1,0:T(8,128)(2,1)S(1)}, bf16[1,8,3584]{2,1,0:T(8,128)(2,1)}, u32[]{:S(2)}) copy-start(bf16[1,8,3584]{2,1,0:T(8,128)(2,1)} %head_a.1) | copy-start | bytes 172036
  85.1 16.7 %copy-start.33 = (bf16[1,8,3584]{2,1,0:T(8,128)(2,1)S(1)}, bf16[1,8,3584]{2,1,0:T(8,128)(2,1)}, u32[]{:S(2)}) copy-start(bf16[1,8,3584]{2,1,0:T(8,128)(2,1)} %head_b.1) | copy-start | bytes 172036
  85.1 18.7 %all-to-all-start.2 = ((bf16[4,16,3584]{2,1,0:T(8,128)(2,1)}), bf16[4,16,3584]{2,1,0:T(8,128)(2,1)S(1)}, u32[]{:S(2)}, u32[]{:S(2)}) async-start(bf16[4,16,3584]{2,1,0:T(8,128)(2,1)} %bitcast.45), calls=%async_computation.2 | async-start | bytes 917504 | tf_op jit(solution)/shard_map/all_to_all | solution.py:255
  88.7 13.1 %collective-permute-start.7 = (bf16[16,3584]{1,0:T(8,128)(2,1)S(1)}, bf16[16,3584]{1,0:T(8,128)(2,1)S(1)}, u32[]{:S(2)}, u32[]{:S(2)}) collective-permute-start(bf16[16,3584]{1,0:T(8,128)(2,1)S(1)} %shard_map.142), channel_id=1, source_target_pairs={{8,0},{16,8},{24,16},{32,24},{40,32},{48,40},{56,48},{64,56},{72,6... | collective-permute-start | bytes 344072 | tf_op jit(solution)/shard_map/ppermute | solution.py:305
  103.8 18.8 %copy-start.24 = (bf16[1,32,3584]{2,1,0:T(8,128)(2,1)S(1)}, bf16[1,32,3584]{2,1,0:T(8,128)(2,1)}, u32[]{:S(2)}) copy-start(bf16[1,32,3584]{2,1,0:T(8,128)(2,1)} %param.23) | copy-start | bytes 688132
  103.8 42.0 %all-to-all-start.3 = ((bf16[4,16,3584]{2,1,0:T(8,128)(2,1)}), bf16[4,16,3584]{2,1,0:T(8,128)(2,1)}, u32[]{:S(2)}, u32[]{:S(2)}) async-start(bf16[4,16,3584]{2,1,0:T(8,128)(2,1)} %bitcast.51), calls=%async_computation.3 | async-start | bytes 917504 | tf_op jit(solution)/shard_map/all_to_all | solution.py:255
  122.6 1.2 copy-start.4
  123.8 1.2 copy-start.8
  130.8 10.7 %collective-permute-start.8 = (f32[8,256]{1,0:T(8,128)S(1)}, f32[8,256]{1,0:T(8,128)S(1)}, u32[]{:S(2)}, u32[]{:S(2)}) collective-permute-start(f32[8,256]{1,0:T(8,128)S(1)} %get-tuple-element.39.refs_4_), channel_id=1, source_target_pairs={{2,0},{3,1},{4,2},{5,3},{6,4},{7,5},{0,6},{1,7},{10,8},{11,9},{12,... | collective-permute-start | bytes 24584 | tf_op jit(solution)/shard_map/ppermute | solution.py:262
  136.6 6.5 %collective-permute-start.9 = (f32[8,256]{1,0:T(8,128)S(1)}, f32[8,256]{1,0:T(8,128)S(1)}, u32[]{:S(2)}, u32[]{:S(2)}) collective-permute-start(f32[8,256]{1,0:T(8,128)S(1)} %get-tuple-element.39.refs_4_), channel_id=1, source_target_pairs={{4,0},{5,1},{6,2},{7,3},{0,4},{1,5},{2,6},{3,7},{12,8},{13,9},{14,... | collective-permute-start | bytes 24584 | tf_op jit(solution)/shard_map/ppermute | solution.py:262
  138.5 7.3 %collective-permute-start.10 = (f32[8,256]{1,0:T(8,128)S(1)}, f32[8,256]{1,0:T(8,128)S(1)}, u32[]{:S(2)}, u32[]{:S(2)}) collective-permute-start(f32[8,256]{1,0:T(8,128)S(1)} %get-tuple-element.39.refs_4_), channel_id=1, source_target_pairs={{6,0},{7,1},{0,2},{1,3},{2,4},{3,5},{4,6},{5,7},{14,8},{15,9},{8,1... | collective-permute-start | bytes 24584 | tf_op jit(solution)/shard_map/ppermute | solution.py:262
  145.8 1.2 copy-start.5
  147.0 1.2 copy-start.9
  148.2 1.2 copy-start.12
  149.4 1.2 copy-start.15
  158.3 3.6 %copy-start.28 = (f32[64,256]{1,0:T(8,128)S(1)}, f32[64,256]{1,0:T(8,128)}, u32[]{:S(2)}) copy-start(f32[64,256]{1,0:T(8,128)} %copy-done.27) | copy-start | bytes 196612
  158.3 14.1 %all-to-all-start.4 = ((bf16[4,16,3584]{2,1,0:T(8,128)(2,1)}), bf16[4,16,3584]{2,1,0:T(8,128)(2,1)S(1)}, u32[]{:S(2)}, u32[]{:S(2)}) async-start(bf16[4,16,3584]{2,1,0:T(8,128)(2,1)} %bitcast.44), calls=%async_computation.4 | async-start | bytes 917504 | tf_op jit(solution)/shard_map/all_to_all | solution.py:255
  161.9 10.4 %copy-start.26 = (bf16[16,3584]{1,0:T(8,128)(2,1)S(1)}, bf16[16,3584]{1,0:T(8,128)(2,1)}, u32[]{:S(2)}) copy-start(bf16[16,3584]{1,0:T(8,128)(2,1)} %copy-done.25) | copy-start | bytes 344068
  162.4 15.2 %collective-permute-start.12 = (f32[32,3584]{1,0:T(8,128)S(1)}, f32[32,3584]{1,0:T(8,128)S(1)}, u32[]{:S(2)}, u32[]{:S(2)}) collective-permute-start(f32[32,3584]{1,0:T(8,128)S(1)} %get-tuple-element.52), channel_id=1, source_target_pairs={{0,1},{1,0},{2,3},{3,2},{4,5},{5,4},{6,7},{7,6},{8,9},{9,8},{10,11... | collective-permute-start | bytes 1376264 | tf_op jit(solution)/shard_map/ppermute | solution.py:246
  173.0 14.2 %collective-permute-start.11 = (bf16[8,3584]{1,0:T(8,128)(2,1)S(1)}, bf16[8,3584]{1,0:T(8,128)(2,1)S(1)}, u32[]{:S(2)}, u32[]{:S(2)}) collective-permute-start(bf16[8,3584]{1,0:T(8,128)(2,1)S(1)} %get-tuple-element.47), channel_id=1, source_target_pairs={{0,504},{8,496},{16,488},{24,480},{32,472},{40,464},{48,456},{56,4... | collective-permute-start | bytes 172040 | tf_op jit(solution)/shard_map/ppermute | solution.py:251
  (14 other events, 9.6 us)

commit v5 on v4

v5 whole, which is shorter than its diff:
```python
import functools

import jax
import jax.numpy as jnp
from jax import lax
from jax.experimental import pallas as pl
from jax.experimental.pallas import tpu as pltpu
from jax.sharding import PartitionSpec as P

D = 3584
HID = 128
EXPERTS = 256
OWN = 32
TOKENS = 64
TOPK = 8
ROWS = 8
CHIPS = 4
IDCOLS = 128
WIDE = D + IDCOLS
WIDTH = 512
z_weight = 0.01
balance_weight = 1.0
F32 = jnp.float32
BF16 = jnp.bfloat16


def dot(lhs, rhs, lhs_dim, rhs_dim):
    return lax.dot_general(
        lhs, rhs, (((lhs_dim,), (rhs_dim,)), ((), ())), preferred_element_type=F32
    )


class Fetched:
    def __init__(self, copies, held):
        self.copies, self.held = copies, held

    def ref(self):
        for copy in self.copies:
            copy.wait()
        self.copies = []
        return self.held


def call(body, outs, args, scratch=(), flops=0):
    n, m = len(args), len(outs)

    def kernel(*refs):
        ins, results, held, made = refs[:n], refs[n : n + m], refs[n + m : 2 * n + m], refs[2 * n + m :]
        made, in_sems, out_sems, rest = made[:m], made[m], made[m + 1], made[m + 2 :]
        fetched = []
        for i, (src, dst) in enumerate(zip(ins, held)):
            copy = pltpu.make_async_copy(src, dst, in_sems.at[i])
            copy.start()
            fetched.append(Fetched([copy], dst))
        pending = body(fetched, made, results, out_sems, *rest) or []
        done = set()
        for index, copies in pending:
            done.add(index)
        for j in range(m):
            if j not in done:
                copy = pltpu.make_async_copy(made[j], results[j], out_sems.at[j, 0])
                copy.start()
                pending.append((j, [copy]))
        for _, copies in pending:
            for copy in copies:
                copy.wait()
        for operand in fetched:
            operand.ref()

    hbm = pl.BlockSpec(memory_space=pltpu.HBM)
    total = sum(a.size * a.dtype.itemsize for a in args)
    return pl.pallas_call(
        kernel,
        out_shape=[jax.ShapeDtypeStruct(o[0], o[1]) for o in outs],
        in_specs=[hbm] * n,
        out_specs=[hbm] * m,
        scratch_shapes=[pltpu.VMEM(a.shape, a.dtype) for a in args]
        + [pltpu.VMEM(o[-1] if len(o) > 2 else o[0], o[1]) for o in outs]
        + [pltpu.SemaphoreType.DMA((n,)), pltpu.SemaphoreType.DMA((m, D // WIDTH + 1))]
        + list(scratch),
        cost_estimate=pl.CostEstimate(flops=flops, bytes_accessed=total, transcendentals=0),
    )(*args)


def packed(parts):
    return jnp.concatenate([p.astype(F32) for p in parts], axis=0).astype(BF16)


def write_all(block, out, sems, j):
    rows = block.shape[0]
    copies = [
        pltpu.make_async_copy(block, out.at[pl.ds(rows * k, rows), :], sems.at[j, k])
        for k in range(CHIPS)
    ]
    for copy in copies:
        copy.start()
    return (j, copies)


def id_columns(ids):
    empty = jnp.full((ROWS, IDCOLS - 2 * TOPK), -1.0, F32)
    used = jnp.concatenate([ids[0].astype(F32), ids[1].astype(F32), empty], axis=1)
    return jnp.concatenate([used, jnp.full((ROWS, IDCOLS), -1.0, F32)], axis=0).astype(BF16)


def mirror_pack_kernel(args, made, results, sems):
    stash, grads, ids = [a.ref() for a in args]
    made[0][:, 0:D] = packed([stash[0], grads[...]])
    made[0][:, D:WIDE] = id_columns(ids)


def first_spread_kernel(args, made, results, sems):
    stash, grads, ids, other = [a.ref() for a in args]
    block = made[0]
    block[0:16, 0:D] = packed([stash[0], grads[...]])
    block[0:16, D:WIDE] = id_columns(ids)
    block[16:32, :] = other[...]
    return [write_all(block, results[0], sems, 0)]


def later_join_kernel(args, made, results, sems):
    stash, other = [a.ref() for a in args]
    made[0][...] = packed([stash[1], other[...]])


def grads_spread_kernel(args, made, results, sems):
    moved, head_a, head_b = [a.ref() for a in args]
    top = lax.axis_index("pipe") == lax.axis_size("pipe") - 1
    heads = packed([head_a[0], head_b[0]]).astype(F32)
    made[1][...] = jnp.where(top, heads, moved[...].astype(F32)).astype(BF16)
    made[0][...] = made[1][...]
    return [write_all(made[0], results[0], sems, 0)]


def summed(parts, cols):
    total = parts[0:16, cols].astype(F32)
    for k in range(1, CHIPS):
        total += parts[16 * k : 16 * k + 16, cols].astype(F32)
    return total


def first_emit_kernel(args, made, results, sems):
    parts, grads_a, block_b = [a.ref() for a in args]
    for low in range(0, D, WIDTH):
        cols = pl.ds(low, WIDTH)
        both = jnp.concatenate(
            [grads_a[:, cols].astype(F32), block_b[:, cols].astype(F32)[8:16]], axis=0
        )
        made[0][:, cols] = (both + summed(parts, cols)).astype(BF16)


def second_emit_kernel(args, made, results, sems):
    parts, grads = [a.ref() for a in args]
    for low in range(0, D, WIDTH):
        cols = pl.ds(low, WIDTH)
        both = grads[:, cols].astype(F32) + summed(parts, cols)
        made[0][:, cols] = both[0:8].astype(BF16)
        made[1][:, cols] = both[8:16].astype(BF16)


def backward_terms(hidden, gate, up, gates, ups, made, results, sems):
    d_gate, d_up = [], []
    for h, g, u in zip(hidden, gate, up):
        q = jax.nn.sigmoid(g)
        d_gate.append((h * u * q * (1.0 + g * (1.0 - q))).astype(BF16))
        d_up.append((h * g * q).astype(BF16))
    copies = []
    for low in range(0, D, WIDTH):
        cols = pl.ds(low, WIDTH)
        total = dot(d_gate[0], gates[0][cols, :], 1, 1)
        total += dot(d_gate[1], gates[1][cols, :], 1, 1)
        total += dot(d_up[0], ups[0][cols, :], 1, 1)
        total += dot(d_up[1], ups[1][cols, :], 1, 1)
        made[0][:, cols] = total.astype(BF16)
        copies.append(
            pltpu.make_async_copy(
                made[0].at[:, cols], results[0].at[:, cols], sems.at[0, low // WIDTH]
            )
        )
        copies[-1].start()
    return copies


def first_tick_kernel(args, made, results, sems):
    first = args[0].ref()
    rows = first[:, 0:D]
    made[1][...] = first[:, D:WIDE]

    def pick(value, offset):
        return jnp.concatenate(
            [value[16 * b + offset : 16 * b + offset + 8] for b in range(2 * CHIPS)], axis=0
        )

    gate = [pick(dot(rows, w.ref()[...], 1, 0), 0) for w in args[1:3]]
    up = [pick(dot(rows, w.ref()[...], 1, 0), 0) for w in args[3:5]]
    hidden = [pick(dot(rows, w.ref()[...], 1, 1), 8) for w in args[5:7]]
    gates, ups = [w.ref() for w in args[1:3]], [w.ref() for w in args[3:5]]
    return [(0, backward_terms(hidden, gate, up, gates, ups, made, results, sems))]


def second_tick_kernel(args, made, results, sems):
    rows = args[0].ref()[...]
    hidden = [dot(rows, w.ref()[...], 1, 1) for w in args[1:3]]
    pre = args[3].ref()
    gate = [pre[:, 0:HID], pre[:, HID : 2 * HID]]
    up = [pre[:, 2 * HID : 3 * HID], pre[:, 3 * HID : 4 * HID]]
    gates, ups = [w.ref() for w in args[4:6]], [w.ref() for w in args[6:8]]
    copies = backward_terms(hidden, gate, up, gates, ups, made, results, sems)
    stats = args[8].ref()
    for k in range(CHIPS):
        made[0][16 * k : 16 * k + 16, D:WIDE] = stats[...]
    last = pltpu.make_async_copy(
        made[0].at[:, pl.ds(D, IDCOLS)], results[0].at[:, pl.ds(D, IDCOLS)], sems.at[0, D // WIDTH]
    )
    last.start()
    return [(0, copies + [last])]


def later_rows(blocks, held1):
    chip = lax.axis_index("expert") // 2
    for k, block in enumerate(blocks):
        rows = pl.ds(pl.multiple_of(lax.rem(chip + k, CHIPS) * 16, 16), 16)
        held1[rows, :] = block.ref()[...]


def forward_kernel(args, made, results, sems, held1):
    pre, expo_ref, share_ref, stats_ref = made
    member = lax.axis_index("expert")
    later_rows(args[2:6], held1)
    rows1 = held1[...]
    for i, w in enumerate(args[6:10]):
        pre[:, HID * i : HID * i + HID] = dot(rows1, w.ref()[...], 1, 0)
    first, other_ids, routers = args[0].ref(), args[1].ref(), [r.ref() for r in args[10:12]]
    rows0 = first[:, 0:D]
    logits = jnp.concatenate(
        [
            jnp.concatenate([dot(r[...], rows, 1, 1) for r in routers], axis=0)
            for rows in (rows0, jnp.concatenate([rows1, rows1], axis=0))
        ],
        axis=1,
    )
    ids = [first[:, D:WIDE].astype(F32).T, other_ids[...].astype(F32).T]
    row = lax.broadcasted_iota(jnp.int32, (2 * OWN, 128), 0)
    column = lax.broadcasted_iota(jnp.int32, (2 * OWN, 128), 1)
    own = row + OWN * member
    other = row - OWN + OWN * (member + 1 - 2 * lax.rem(member, 2))
    experts = jnp.where(row < OWN, own, other).astype(F32)
    stream_b = (column % 32) >= 16
    scale = EXPERTS / (TOKENS * TOPK)
    shares = []
    for tick in range(2):
        hits = jnp.zeros((2 * OWN, 128), F32)
        for core in range(2):
            for j in range(TOPK):
                slot = TOPK * tick + j
                hits += (experts == ids[core][slot : slot + 1, :]).astype(F32)
        count_a = jnp.sum(jnp.where(stream_b, 0.0, hits), axis=1, keepdims=True)
        count_b = jnp.sum(jnp.where(stream_b, hits, 0.0), axis=1, keepdims=True)
        shares.append((count_a * scale, count_b * scale))
    share0 = jnp.where(stream_b, shares[0][1], shares[0][0])
    share1 = jnp.where((column % 16) >= 8, shares[1][1], shares[1][0])
    share = jnp.concatenate([share0, share1], axis=1)
    peak = jnp.max(logits, axis=0, keepdims=True)
    expo = jnp.exp(logits - peak)
    total = jnp.sum(expo, axis=0, keepdims=True)
    weighted = jnp.sum(expo * share, axis=0, keepdims=True)
    expo_ref[...] = expo
    share_ref[...] = share
    figures = []
    for value, count in ((peak, 3), (total, 2), (weighted, 2)):
        for _ in range(count):
            figures.append(value.astype(BF16).astype(F32))
            value = value - figures[-1]
    rows = [f[:, low : low + 128] for low in (0, 128) for f in figures]
    stats_ref[...] = jnp.concatenate(rows + [jnp.zeros((2, 128), F32)], axis=0).astype(BF16)


def router_kernel(args, made, results, sems, held1):
    first, expo_ref, share_ref, parts, own = [a.ref() for a in args[0:5]]
    later_rows(args[5:9], held1)
    stats = []
    for value in [own[...]] + [parts[16 * k : 16 * k + 16, D:WIDE] for k in range(CHIPS)]:
        value = value.astype(F32)
        wide = [jnp.concatenate([value[i : i + 1], value[i + 7 : i + 8]], axis=1) for i in range(7)]
        stats.append((wide[0] + wide[1] + wide[2], wide[3] + wide[4], wide[5] + wide[6]))
    mine, stats = stats[0], stats[1:]
    peaks = [s[0] for s in stats]
    peak = functools.reduce(jnp.maximum, peaks)
    factors = [jnp.exp(p - peak) for p in peaks]
    total = sum(s[1] * f for s, f in zip(stats, factors))
    weighted = sum(s[2] * f for s, f in zip(stats, factors))
    log_total = peak + jnp.log(total)
    mean_share = weighted / total
    probs = expo_ref[...] * (jnp.exp(mine[0] - peak) / total)
    slopes = (
        2.0 * z_weight * log_total - balance_weight * mean_share + balance_weight * share_ref[...]
    ) * probs
    column = lax.broadcasted_iota(jnp.int32, (2 * OWN, 128), 1)
    slopes0 = jnp.where((column % 16) < 8, slopes[:, 0:128], 0.0).astype(BF16)
    slopes1 = slopes[:, 128:192].astype(BF16)
    for low in range(0, D, WIDTH):
        cols = pl.ds(low, WIDTH)
        part = dot(slopes0, first[:, cols], 1, 0) + dot(slopes1, held1[:, cols], 1, 0)
        made[0][:, cols] = part[0:OWN]
        made[1][:, cols] = part[OWN:]


def swapped(value):
    return lax.ppermute(value, "expert", [(e, e ^ 1) for e in range(8)])


def mirrored(value):
    count = lax.axis_size("pipe")
    return lax.ppermute(value, "pipe", [(i, count - 1 - i) for i in range(count)])


def exchanged(blocks):
    return lax.all_to_all(
        blocks, "expert", split_axis=0, concat_axis=0, tiled=True,
        axis_index_groups=[[0, 2, 4, 6], [1, 3, 5, 7]],
    )


def from_chip(value, k):
    return lax.ppermute(value, "expert", [((e + 2 * k) % 8, e) for e in range(8)])


def ring(value):
    return [value] + [from_chip(value, k) for k in range(1, CHIPS)]


def after(value, *earlier):
    return lax.optimization_barrier((value, *earlier))[0]


def shards(
    stash_a, stash_b, ids_a, ids_b, arriving_a, arriving_b, head_a, head_b,
    w_gate, w_up, w_down, router,
):
    stash_a, stash_b, ids_a, ids_b = stash_a[0], stash_b[0], ids_a[0], ids_b[0]
    arriving_a, arriving_b = arriving_a[0], arriving_b[0]
    w_gate, w_up, w_down, router = w_gate[0], w_up[0], w_down[0], router[0]
    top = lax.axis_size("pipe") - 1
    rows_scratch = [pltpu.VMEM((64, D), BF16)]

    (packed_b,) = call(mirror_pack_kernel, [((16, WIDE), BF16)], [stash_b, arriving_b, ids_b])
    block_b = mirrored(packed_b)
    (blocks,) = call(
        first_spread_kernel, [((128, WIDE), BF16, (32, WIDE))],
        [stash_a, arriving_a, ids_a, block_b],
    )
    first = exchanged(blocks)
    gates, ups, downs = (
        [weight, swapped(after(weight, block_b))] for weight in (w_gate, w_up, w_down)
    )
    later_b = mirrored(after(stash_b[1], first))

    terms, ids = call(
        first_tick_kernel, [((64, D), BF16), ((128, IDCOLS), BF16)],
        [first] + gates + ups + downs, (), 2 * 128 * D * 128 * 10,
    )
    parts = exchanged(after(terms, later_b))
    other_router = swapped(after(router, terms))
    other_ids = swapped(ids)
    (later,) = call(later_join_kernel, [((16, D), BF16)], [stash_a, later_b])
    (out,) = call(first_emit_kernel, [((16, D), BF16)], [parts, arriving_a, block_b])
    out = after(out, other_router, other_ids, later)
    moved = lax.ppermute(out, "pipe", [(i, i - 1) for i in range(1, top + 1)])

    second = ring(after(later, out))
    blocks, grads = call(
        grads_spread_kernel, [((64, D), BF16, (16, D)), ((16, D), BF16)], [moved, head_a, head_b]
    )
    all_grads = exchanged(after(blocks, *second))
    pre, expo, share, stats = call(
        forward_kernel,
        [((64, 4 * HID), F32), ((2 * OWN, 256), F32), ((2 * OWN, 256), F32), ((16, IDCOLS), BF16)],
        [first, other_ids] + second + gates + ups + [router, other_router], rows_scratch,
        2 * 128 * D * 128 * 4,
    )
    (terms,) = call(
        second_tick_kernel, [((64, WIDE), BF16)],
        [all_grads] + downs + [pre] + gates + ups + [stats], (), 2 * 64 * D * 128 * 6,
    )
    parts = exchanged(terms)
    out_a, out_b = call(second_emit_kernel, [((ROWS, D), BF16)] * 2, [parts, grads])
    out_b = mirrored(out_b)
    own, other = call(
        router_kernel, [((OWN, D), F32)] * 2, [first, expo, share, parts, stats] + second,
        rows_scratch, 2 * 192 * D * 64,
    )
    return out_a[None], out_b[None], (own + swapped(other))[None]


def solution(mesh):
    placed = (
        P("pipe", None, "expert", None),
        P("pipe", None, "expert", None),
        P("pipe", None, "expert", None),
        P("pipe", None, "expert", None),
        P("pipe", "expert", None),
        P("pipe", "expert", None),
        P(None, "expert", None),
        P(None, "expert", None),
        P("pipe", None, "expert"),
        P("pipe", None, "expert"),
        P("pipe", "expert", None),
        P("pipe", "expert", None),
    )
    return jax.shard_map(
        shards,
        mesh=mesh,
        in_specs=placed,
        out_specs=(P("pipe", "expert", None), P("pipe", "expert", None), P("pipe", "expert", None)),
        check_vma=False,
    )
```

time: 190 us -> 184 us (0.968)
  local copies, waits for them, and re-layouts: 29.7 us -> 4.8 us
  blocking collectives: 0 us -> 17.1 us
  Pallas kernels: 14.3 us -> 30.7 us
  starting transfers between devices: 91.9 us -> 76 us
    unnamed x89 -> x37, local copies, waits for them, and re-layouts: 29.1 us -> 4.79 us
    all_to_all x5 -> x3, starting transfers between devices: 33.5 us -> 14.3 us  [exchanged(): lax.all_to_all(blocks, 'expert', split_axis=0, concat_axis=0, tiled=True,...]
    all_to_all x0 -> x1, blocking collectives: none -> 17.1 us  [exchanged(): lax.all_to_all(blocks, 'expert', split_axis=0, concat_axis=0, tiled=True,...]
    pallas_call x10, Pallas kernels: 14.3 us -> 30.7 us  [call(): pl.pallas_call(kernel, out_shape=[jax.ShapeDtypeStruct(o[0], o[1]) for o...]
    all_to_all x5 -> x3, waiting for transfers between devices: 17 us -> 31.3 us  [exchanged(): lax.all_to_all(blocks, 'expert', split_axis=0, concat_axis=0, tiled=True,...]
    ppermute x1, waiting for transfers between devices: 9.79 us -> 3.47 us  [shards(): moved = lax.ppermute(out, 'pipe', [(i, i - 1) for i in range(1, top + 1)])]
    ppermute x3, starting transfers between devices: 31.8 us -> 37.6 us  [mirrored(): lax.ppermute(value, 'pipe', [(i, count - 1 - i) for i in range(count)])]
    ppermute x3, waiting for transfers between devices: 4.31 us -> 0.01 us  [from_chip(): lax.ppermute(value, 'expert', [((e + 2 * k) % 8, e) for e in range(8)])]
  transfers between devices with their start and end apart: 18 -> 16, of which waited for: 8 -> 6; matrix products, arithmetic and copies ran while one was open for 1% -> 0% of each run, Pallas kernels for 5% -> 10%
where the time goes in v5:
time: 184 us; the launch traced here: 181 us
  starting transfers between devices  76 us (41%)
  waiting for transfers between devices  50.8 us (28%)
  Pallas kernels  30.7 us (17%)
  blocking collectives  17.1 us (9%)
  local copies, waits for them, and re-layouts  4.8 us (3%)
    ppermute x3, starting transfers between devices, mirrored(): lax.ppermute(value, 'pipe', [(i, count - 1 - i) for i in range(count)])  37.6 us
    all_to_all x3, waiting for transfers between devices, exchanged(): lax.all_to_all(blocks, 'expert', split_axis=0, concat_axis=0, tiled=True,...  31.3 us
    pallas_call x10, Pallas kernels, call(): pl.pallas_call(kernel, out_shape=[jax.ShapeDtypeStruct(o[0], o[1]) for o...  30.7 us
    all_to_all x1, blocking collectives, exchanged(): lax.all_to_all(blocks, 'expert', split_axis=0, concat_axis=0, tiled=True,...  17.1 us
    ppermute x3, waiting for transfers between devices, mirrored(): lax.ppermute(value, 'pipe', [(i, count - 1 - i) for i in range(count)])  16 us
    all_to_all x3, starting transfers between devices, exchanged(): lax.all_to_all(blocks, 'expert', split_axis=0, concat_axis=0, tiled=True,...  14.3 us
    ppermute x6, starting transfers between devices, swapped(): return lax.ppermute(value, 'expert', [(e, e ^ 1) for e in range(8)])  12.6 us
    ppermute x3, starting transfers between devices, from_chip(): lax.ppermute(value, 'expert', [((e + 2 * k) % 8, e) for e in range(8)])  9.56 us
  transfers between devices with their start and end apart: 16, of which 6 were waited for; matrix products, arithmetic and copies ran while one was open for 0% of the time, Pallas kernels for 10%

profile of v5, /device:TPU:6, one launch (start us, length us, event | category | flops | bytes accessed | tf_op | source)
XLA Modules:
  0.0 181.3 jit_solution(2589902800320254166)
XLA Ops:
  0.6 1.7 shard_map.139
  2.4 15.1 %collective-permute-start = (bf16[16,3712]{1,0:T(8,128)(2,1)}, bf16[16,3712]{1,0:T(8,128)(2,1)S(1)}, u32[]{:S(2)}, u32[]{:S(2)}) collective-permute-start(bf16[16,3712]{1,0:T(8,128)(2,1)} %shard_map.139), channel_id=1, source_target_pairs={{0,504},{8,496},{16,488},{24,480},{32,472},{40,464},{48,456},{56,4... | collective-permute-start | bytes 356360 | tf_op jit(solution)/shard_map/ppermute | solution.py:314
  17.5 10.4 %collective-permute-done.refs_3_.refs_2_ = bf16[16,3712]{1,0:T(8,128)(2,1)S(1)} collective-permute-done((bf16[16,3712]{1,0:T(8,128)(2,1)}, bf16[16,3712]{1,0:T(8,128)(2,1)S(1)}, u32[]{:S(2)}, u32[]{:S(2)}) %collective-permute-start) | collective-permute-done | bytes 118816 | tf_op jit(solution)/shard_map/ppermute | solution.py:314
  27.9 0.6 copy-done.6
  28.5 2.2 %shard_map.140 = bf16[128,3712]{1,0:T(8,128)(2,1)} custom-call(bf16[2,8,3584]{2,1,0:T(8,128)(2,1)} %bitcast.44, bf16[8,3584]{1,0:T(8,128)(2,1)} %bitcast.49, s32[2,8,8]{2,1,0:T(8,128)} %bitcast.55, bf16[16,3712]{1,0:T(8,128)(2,1)} %copy-done.6), custom_call_target="tpu_custom_call" | custom-call | bytes 291328 | tf_op jit(solution)/shard_map/pallas_call | solution.py:72
  30.7 0.0 copy-start.2
  30.7 4.0 %all-to-all-start = ((bf16[4,32,3712]{2,1,0:T(8,128)(2,1)}), bf16[4,32,3712]{2,1,0:T(8,128)(2,1)S(1)}, u32[]{:S(2)}, u32[]{:S(2)}) async-start(bf16[4,32,3712]{2,1,0:T(8,128)(2,1)} %bitcast.37), calls=%async_computation | async-start | bytes 1900544 | tf_op jit(solution)/shard_map/all_to_all | solution.py:318
  34.7 1.9 %collective-permute-start.1 = (bf16[3584,128]{1,0:T(8,128)(2,1)S(1)}, bf16[3584,128]{1,0:T(8,128)(2,1)}, u32[]{:S(2)}, u32[]{:S(2)}) collective-permute-start(bf16[3584,128]{1,0:T(8,128)(2,1)S(1)} %bitcast.30), channel_id=1, source_target_pairs={{0,1},{1,0},{2,3},{3,2},{4,5},{5,4},{6,7},{7,6},{8,9},{9,8},{10,11... | collective-permute-start | bytes 2752520 | tf_op jit(solution)/shard_map/ppermute | solution.py:309
  36.6 2.4 %collective-permute-start.2 = (bf16[3584,128]{1,0:T(8,128)(2,1)S(1)}, bf16[3584,128]{1,0:T(8,128)(2,1)}, u32[]{:S(2)}, u32[]{:S(2)}) collective-permute-start(bf16[3584,128]{1,0:T(8,128)(2,1)S(1)} %bitcast.34), channel_id=1, source_target_pairs={{0,1},{1,0},{2,3},{3,2},{4,5},{5,4},{6,7},{7,6},{8,9},{9,8},{10,11... | collective-permute-start | bytes 2752520 | tf_op jit(solution)/shard_map/ppermute | solution.py:309
  39.1 1.9 %collective-permute-start.3 = (bf16[128,3584]{1,0:T(8,128)(2,1)}, bf16[128,3584]{1,0:T(8,128)(2,1)}, u32[]{:S(2)}, u32[]{:S(2)}) collective-permute-start(bf16[128,3584]{1,0:T(8,128)(2,1)} %bitcast.38), channel_id=1, source_target_pairs={{0,1},{1,0},{2,3},{3,2},{4,5},{5,4},{6,7},{7,6},{8,9},{9,8},{10,11... | collective-permute-start | bytes 2752520 | tf_op jit(solution)/shard_map/ppermute | solution.py:309
  41.0 17.1 %all-to-all-done = bf16[4,32,3712]{2,1,0:T(8,128)(2,1)S(1)} async-done(((bf16[4,32,3712]{2,1,0:T(8,128)(2,1)}), bf16[4,32,3712]{2,1,0:T(8,128)(2,1)S(1)}, u32[]{:S(2)}, u32[]{:S(2)}) %all-to-all-start) | async-done | bytes 950304 | tf_op jit(solution)/shard_map/all_to_all | solution.py:318
  58.1 12.3 %collective-permute-start.4 = (bf16[8,3584]{1,0:T(8,128)(2,1)S(1)}, bf16[8,3584]{1,0:T(8,128)(2,1)S(1)}, u32[]{:S(2)}, u32[]{:S(2)}) collective-permute-start(bf16[8,3584]{1,0:T(8,128)(2,1)S(1)} %slice_bitcast_fusion), channel_id=1, source_target_pairs={{0,504},{8,496},{16,488},{24,480},{32,472},{40,464},{48,456},{56,4... | collective-permute-start | bytes 172040 | tf_op jit(solution)/shard_map/ppermute | solution.py:314
  70.4 6.4 %shard_map.141 = (bf16[64,3584]{1,0:T(8,128)(2,1)}, bf16[128,128]{1,0:T(8,128)(2,1)}) custom-call(bf16[128,3712]{1,0:T(8,128)(2,1)} %bitcast.24, bf16[3584,128]{1,0:T(8,128)(2,1)} %bitcast.27, bf16[3584,128]{1,0:T(8,128)(2,1)} %collective-permute-done.1.refs_2_.refs_7_.refs_5_, bf16[3584,128]{1,0:T(8,128)(2,1)} %bitcast.31, ...), custom_call_target="tpu_custom_call" | custom-call | flops 1174405120 | bytes 6455296 | tf_op jit(solution)/shard_map/pallas_call | solution.py:72
  76.8 0.0 copy-start.15
  76.8 0.0 copy-start.12
  76.9 0.6 copy-done.15
  77.5 3.5 %all-to-all-start.1 = ((bf16[4,16,3584]{2,1,0:T(8,128)(2,1)}), bf16[4,16,3584]{2,1,0:T(8,128)(2,1)S(1)}, u32[]{:S(2)}, u32[]{:S(2)}) async-start(bf16[4,16,3584]{2,1,0:T(8,128)(2,1)} %bitcast.47), calls=%async_computation.1 | async-start | bytes 917504 | tf_op jit(solution)/shard_map/all_to_all | solution.py:318
  80.9 1.9 %collective-permute-start.5 = (bf16[32,3584]{1,0:T(8,128)(2,1)S(1)}, bf16[32,3584]{1,0:T(8,128)(2,1)S(1)}, u32[]{:S(2)}, u32[]{:S(2)}) collective-permute-start(bf16[32,3584]{1,0:T(8,128)(2,1)S(1)} %bitcast.52), channel_id=1, source_target_pairs={{0,1},{1,0},{2,3},{3,2},{4,5},{5,4},{6,7},{7,6},{8,9},{9,8},{10,11... | collective-permute-start | bytes 688136 | tf_op jit(solution)/shard_map/ppermute | solution.py:309
  82.9 2.4 %collective-permute-start.6 = (bf16[128,128]{1,0:T(8,128)(2,1)S(1)}, bf16[128,128]{1,0:T(8,128)(2,1)S(1)}, u32[]{:S(2)}, u32[]{:S(2)}) collective-permute-start(bf16[128,128]{1,0:T(8,128)(2,1)S(1)} %copy-done.17), channel_id=1, source_target_pairs={{0,1},{1,0},{2,3},{3,2},{4,5},{5,4},{6,7},{7,6},{8,9},{9,8},{10,11... | collective-permute-start | bytes 98312 | tf_op jit(solution)/shard_map/ppermute | solution.py:309
  85.3 1.6 shard_map.143.refs_2_.refs_5_
  86.9 6.3 %all-to-all-done.1 = bf16[4,16,3584]{2,1,0:T(8,128)(2,1)S(1)} async-done(((bf16[4,16,3584]{2,1,0:T(8,128)(2,1)}), bf16[4,16,3584]{2,1,0:T(8,128)(2,1)S(1)}, u32[]{:S(2)}, u32[]{:S(2)}) %all-to-all-start.1) | async-done | bytes 458784 | tf_op jit(solution)/shard_map/all_to_all | solution.py:318
  93.2 0.8 copy-done.4
  94.0 1.9 %shard_map.142 = bf16[16,3584]{1,0:T(8,128)(2,1)} custom-call(bf16[64,3584]{1,0:T(8,128)(2,1)} %bitcast.43, bf16[8,3584]{1,0:T(8,128)(2,1)} %bitcast.50, bf16[16,3712]{1,0:T(8,128)(2,1)} %copy-done.6), custom_call_target="tpu_custom_call" | custom-call | bytes 634880 | tf_op jit(solution)/shard_map/pallas_call | solution.py:72
  95.9 0.0 copy-start.16
  95.9 1.9 %collective-permute-start.7 = (bf16[16,3584]{1,0:T(8,128)(2,1)}, bf16[16,3584]{1,0:T(8,128)(2,1)S(1)}, u32[]{:S(2)}, u32[]{:S(2)}) collective-permute-start(bf16[16,3584]{1,0:T(8,128)(2,1)} %shard_map.142), channel_id=1, source_target_pairs={{8,0},{16,8},{24,16},{32,24},{40,32},{48,40},{56,48},{64,56},{72,6... | collective-permute-start | bytes 344072 | tf_op jit(solution)/shard_map/ppermute | solution.py:368
  97.9 1.9 %collective-permute-start.10 = (bf16[16,3584]{1,0:T(8,128)(2,1)S(1)}, bf16[16,3584]{1,0:T(8,128)(2,1)S(1)}, u32[]{:S(2)}, u32[]{:S(2)}) collective-permute-start(bf16[16,3584]{1,0:T(8,128)(2,1)S(1)} %copy-done.5), channel_id=1, source_target_pairs={{6,0},{7,1},{0,2},{1,3},{2,4},{3,5},{4,6},{5,7},{14,8},{15,9},{8,1... | collective-permute-start | bytes 344072 | tf_op jit(solution)/shard_map/ppermute | solution.py:325
  99.8 3.9 %collective-permute-start.9 = (bf16[16,3584]{1,0:T(8,128)(2,1)S(1)}, bf16[16,3584]{1,0:T(8,128)(2,1)S(1)}, u32[]{:S(2)}, u32[]{:S(2)}) collective-permute-start(bf16[16,3584]{1,0:T(8,128)(2,1)S(1)} %copy-done.5), channel_id=1, source_target_pairs={{4,0},{5,1},{6,2},{7,3},{0,4},{1,5},{2,6},{3,7},{12,8},{13,9},{14,... | collective-permute-start | bytes 344072 | tf_op jit(solution)/shard_map/ppermute | solution.py:325
  103.7 3.7 %collective-permute-start.8 = (bf16[16,3584]{1,0:T(8,128)(2,1)S(1)}, bf16[16,3584]{1,0:T(8,128)(2,1)S(1)}, u32[]{:S(2)}, u32[]{:S(2)}) collective-permute-start(bf16[16,3584]{1,0:T(8,128)(2,1)S(1)} %copy-done.5), channel_id=1, source_target_pairs={{2,0},{3,1},{4,2},{5,3},{6,4},{7,5},{0,6},{1,7},{10,8},{11,9},{12,... | collective-permute-start | bytes 344072 | tf_op jit(solution)/shard_map/ppermute | solution.py:325
  107.5 3.5 %collective-permute-done.7.refs_0_ = bf16[16,3584]{1,0:T(8,128)(2,1)S(1)} collective-permute-done((bf16[16,3584]{1,0:T(8,128)(2,1)}, bf16[16,3584]{1,0:T(8,128)(2,1)S(1)}, u32[]{:S(2)}, u32[]{:S(2)}) %collective-permute-start.7) | collective-permute-done | bytes 114720 | tf_op jit(solution)/shard_map/ppermute | solution.py:368
  110.9 0.6 copy-done.14
  111.6 1.9 %shard_map.144 = (bf16[64,3584]{1,0:T(8,128)(2,1)}, bf16[16,3584]{1,0:T(8,128)(2,1)}) custom-call(bf16[16,3584]{1,0:T(8,128)(2,1)} %copy-done.14, bf16[1,8,3584]{2,1,0:T(8,128)(2,1)} %refs_1_.1, bf16[1,8,3584]{2,1,0:T(8,128)(2,1)} %refs_2_.1), custom_call_target="tpu_custom_call" | custom-call | bytes 229376 | tf_op jit(solution)/shard_map/pallas_call | solution.py:72
  113.6 0.6 copy-done.8
  114.2 0.0 copy-done.9
  114.2 0.1 copy-done.10
  114.3 6.9 %all-to-all-start.2 = ((bf16[4,16,3584]{2,1,0:T(8,128)(2,1)}), bf16[4,16,3584]{2,1,0:T(8,128)(2,1)S(1)}, u32[]{:S(2)}, u32[]{:S(2)}) async-start(bf16[4,16,3584]{2,1,0:T(8,128)(2,1)} %bitcast.46), calls=%async_computation.2 | async-start | bytes 917504 | tf_op jit(solution)/shard_map/all_to_all | solution.py:318
  121.2 5.1 %shard_map.145 = (f32[64,512]{1,0:T(8,128)}, f32[64,256]{1,0:T(8,128)}, f32[64,256]{1,0:T(8,128)}, bf16[16,128]{1,0:T(8,128)(2,1)}) custom-call(bf16[128,3712]{1,0:T(8,128)(2,1)} %bitcast.25, bf16[128,128]{1,0:T(8,128)(2,1)} %copy-done.16, bf16[16,3584]{1,0:T(8,128)(2,1)} %shard_map.143.refs_2_.refs_5_, bf16[16,3584]{1,0:T(8,128)(2,1)} %copy-done.10, ...), custom_call_target="tpu_custom_call" | custom-call | flops 469762048 | bytes 5570560 | tf_op jit(solution)/shard_map/pallas_call | solution.py:72
  126.3 7.9 %all-to-all-done.2 = bf16[4,16,3584]{2,1,0:T(8,128)(2,1)S(1)} async-done(((bf16[4,16,3584]{2,1,0:T(8,128)(2,1)}), bf16[4,16,3584]{2,1,0:T(8,128)(2,1)S(1)}, u32[]{:S(2)}, u32[]{:S(2)}) %all-to-all-start.2) | async-done | bytes 458784 | tf_op jit(solution)/shard_map/all_to_all | solution.py:318
  134.2 0.8 copy-done.3
  135.0 4.9 %shard_map.146 = bf16[64,3712]{1,0:T(8,128)(2,1)} custom-call(bf16[64,3584]{1,0:T(8,128)(2,1)} %bitcast.42, bf16[128,3584]{1,0:T(8,128)(2,1)} %bitcast.40, bf16[128,3584]{1,0:T(8,128)(2,1)} %collective-permute-done.3.refs_6_.refs_2_, f32[64,512]{1,0:T(8,128)} %get-tuple-element.36.refs_3_, bf16[3584,128]{1,0:T(8,128)(2,1)} %bitcast.29, ...), custom_call_target="tpu_custom_call" | custom-call | flops 352321536 | bytes 6098944 | tf_op jit(solution)/shard_map/pallas_call | solution.py:72
  139.9 17.1 %all_to_all.44 = bf16[4,16,3712]{2,1,0:T(8,128)(2,1)} all-to-all(bf16[4,16,3712]{2,1,0:T(8,128)(2,1)} %bitcast.41), channel_id=1, replica_groups={{0,2,4,6},{1,3,5,7},{8,10,12,14},{9,11,13,15},{16,18,20,22},{17,19,21,2..., dimensions={0} | all-to-all | bytes 950272 | tf_op jit(solution)/shard_map/all_to_all | solution.py:318
  157.0 3.0 %shard_map.148 = (f32[32,3584]{1,0:T(8,128)}, f32[32,3584]{1,0:T(8,128)}) custom-call(bf16[128,3712]{1,0:T(8,128)(2,1)} %bitcast.26, f32[64,256]{1,0:T(8,128)} %get-tuple-element.41.refs_1_, f32[64,256]{1,0:T(8,128)} %get-tuple-element.42.refs_2_, bf16[64,3712]{1,0:T(8,128)(2,1)} %bitcast.35, bf16[16,128]{1,0:T(8,128)(2,1)} %get-tuple-element.37.refs_8_.refs_4_, ...), custom_call_target="tpu_custom_call" | custom-call | flops 88080384 | bytes 2019328 | tf_op jit(solution)/shard_map/pallas_call | solution.py:72
  160.0 0.0 copy-start.7
  160.0 2.1 %collective-permute-start.12 = (f32[32,3584]{1,0:T(8,128)}, f32[32,3584]{1,0:T(8,128)S(1)}, u32[]{:S(2)}, u32[]{:S(2)}) collective-permute-start(f32[32,3584]{1,0:T(8,128)} %get-tuple-element.44), channel_id=1, source_target_pairs={{0,1},{1,0},{2,3},{3,2},{4,5},{5,4},{6,7},{7,6},{8,9},{9,8},{10,11... | collective-permute-start | bytes 1376264 | tf_op jit(solution)/shard_map/ppermute | solution.py:309
  162.1 1.9 %shard_map.147 = (bf16[8,3584]{1,0:T(8,128)(2,1)}, bf16[8,3584]{1,0:T(8,128)(2,1)}) custom-call(bf16[64,3712]{1,0:T(8,128)(2,1)} %bitcast.36, bf16[16,3584]{1,0:T(8,128)(2,1)} %get-tuple-element.38.refs_1_), custom_call_target="tpu_custom_call" | custom-call | bytes 589824 | tf_op jit(solution)/shard_map/pallas_call | solution.py:72
  164.0 10.2 %collective-permute-start.11 = (bf16[8,3584]{1,0:T(8,128)(2,1)}, bf16[8,3584]{1,0:T(8,128)(2,1)S(1)}, u32[]{:S(2)}, u32[]{:S(2)}) collective-permute-start(bf16[8,3584]{1,0:T(8,128)(2,1)} %get-tuple-element.40), channel_id=1, source_target_pairs={{0,504},{8,496},{16,488},{24,480},{32,472},{40,464},{48,456},{56,4... | collective-permute-start | bytes 172040 | tf_op jit(solution)/shard_map/ppermute | solution.py:314
  174.2 5.6 %collective-permute-done.11 = bf16[8,3584]{1,0:T(8,128)(2,1)S(1)} collective-permute-done((bf16[8,3584]{1,0:T(8,128)(2,1)}, bf16[8,3584]{1,0:T(8,128)(2,1)S(1)}, u32[]{:S(2)}, u32[]{:S(2)}) %collective-permute-start.11) | collective-permute-done | bytes 57376 | tf_op jit(solution)/shard_map/ppermute | solution.py:314
  179.9 0.8 add_bitcast_fusion
  180.7 0.6 copy.16
  (34 shorter events, 0.1 us)
Async XLA Ops:
  2.4 25.5 %collective-permute-start = (bf16[16,3712]{1,0:T(8,128)(2,1)}, bf16[16,3712]{1,0:T(8,128)(2,1)S(1)}, u32[]{:S(2)}, u32[]{:S(2)}) collective-permute-start(bf16[16,3712]{1,0:T(8,128)(2,1)} %shard_map.139), channel_id=1, source_target_pairs={{0,504},{8,496},{16,488},{24,480},{32,472},{40,464},{48,456},{56,4... | collective-permute-start | bytes 356360 | tf_op jit(solution)/shard_map/ppermute | solution.py:314
  27.9 0.7 copy-start.6
  28.5 12.5 %copy-start.11 = (bf16[1,2,8,3584]{3,2,1,0:T(8,128)(2,1)S(1)}, bf16[1,2,8,3584]{3,2,1,0:T(8,128)(2,1)}, u32[]{:S(2)}) copy-start(bf16[1,2,8,3584]{3,2,1,0:T(8,128)(2,1)} %param.13) | copy-start | bytes 344068
  30.7 4.0 %copy-start.1 = (bf16[1,3584,128]{2,1,0:T(8,128)(2,1)S(1)}, bf16[1,3584,128]{2,1,0:T(8,128)(2,1)}, u32[]{:S(2)}) copy-start(bf16[1,3584,128]{2,1,0:T(8,128)(2,1)} %param.20) | copy-start | bytes 2752516
  30.7 5.9 %copy-start.2 = (bf16[1,3584,128]{2,1,0:T(8,128)(2,1)S(1)}, bf16[1,3584,128]{2,1,0:T(8,128)(2,1)}, u32[]{:S(2)}) copy-start(bf16[1,3584,128]{2,1,0:T(8,128)(2,1)} %param.21) | copy-start | bytes 2752516
  30.7 27.4 %all-to-all-start = ((bf16[4,32,3712]{2,1,0:T(8,128)(2,1)}), bf16[4,32,3712]{2,1,0:T(8,128)(2,1)S(1)}, u32[]{:S(2)}, u32[]{:S(2)}) async-start(bf16[4,32,3712]{2,1,0:T(8,128)(2,1)} %bitcast.37), calls=%async_computation | async-start | bytes 1900544 | tf_op jit(solution)/shard_map/all_to_all | solution.py:318
  34.7 35.7 %collective-permute-start.1 = (bf16[3584,128]{1,0:T(8,128)(2,1)S(1)}, bf16[3584,128]{1,0:T(8,128)(2,1)}, u32[]{:S(2)}, u32[]{:S(2)}) collective-permute-start(bf16[3584,128]{1,0:T(8,128)(2,1)S(1)} %bitcast.30), channel_id=1, source_target_pairs={{0,1},{1,0},{2,3},{3,2},{4,5},{5,4},{6,7},{7,6},{8,9},{9,8},{10,11... | collective-permute-start | bytes 2752520 | tf_op jit(solution)/shard_map/ppermute | solution.py:309
  36.6 33.7 %collective-permute-start.2 = (bf16[3584,128]{1,0:T(8,128)(2,1)S(1)}, bf16[3584,128]{1,0:T(8,128)(2,1)}, u32[]{:S(2)}, u32[]{:S(2)}) collective-permute-start(bf16[3584,128]{1,0:T(8,128)(2,1)S(1)} %bitcast.34), channel_id=1, source_target_pairs={{0,1},{1,0},{2,3},{3,2},{4,5},{5,4},{6,7},{7,6},{8,9},{9,8},{10,11... | collective-permute-start | bytes 2752520 | tf_op jit(solution)/shard_map/ppermute | solution.py:309
  39.1 31.3 %collective-permute-start.3 = (bf16[128,3584]{1,0:T(8,128)(2,1)}, bf16[128,3584]{1,0:T(8,128)(2,1)}, u32[]{:S(2)}, u32[]{:S(2)}) collective-permute-start(bf16[128,3584]{1,0:T(8,128)(2,1)} %bitcast.38), channel_id=1, source_target_pairs={{0,1},{1,0},{2,3},{3,2},{4,5},{5,4},{6,7},{7,6},{8,9},{9,8},{10,11... | collective-permute-start | bytes 2752520 | tf_op jit(solution)/shard_map/ppermute | solution.py:309
  58.1 12.3 %copy-start = (bf16[4,32,3712]{2,1,0:T(8,128)(2,1)}, bf16[4,32,3712]{2,1,0:T(8,128)(2,1)S(1)}, u32[]{:S(2)}) copy-start(bf16[4,32,3712]{2,1,0:T(8,128)(2,1)S(1)} %all-to-all-done) | copy-start | bytes 2850820
  58.1 18.7 %collective-permute-start.4 = (bf16[8,3584]{1,0:T(8,128)(2,1)S(1)}, bf16[8,3584]{1,0:T(8,128)(2,1)S(1)}, u32[]{:S(2)}, u32[]{:S(2)}) collective-permute-start(bf16[8,3584]{1,0:T(8,128)(2,1)S(1)} %slice_bitcast_fusion), channel_id=1, source_target_pairs={{0,504},{8,496},{16,488},{24,480},{32,472},{40,464},{48,456},{56,4... | collective-permute-start | bytes 172040 | tf_op jit(solution)/shard_map/ppermute | solution.py:314
  76.8 0.6 copy-start.15
  76.8 4.1 %copy-start.12 = (bf16[1,32,3584]{2,1,0:T(8,128)(2,1)S(1)}, bf16[1,32,3584]{2,1,0:T(8,128)(2,1)}, u32[]{:S(2)}) copy-start(bf16[1,32,3584]{2,1,0:T(8,128)(2,1)} %param.23) | copy-start | bytes 688132
  76.9 6.0 %copy-start.17 = (bf16[128,128]{1,0:T(8,128)(2,1)S(1)}, bf16[128,128]{1,0:T(8,128)(2,1)}, u32[]{:S(2)}) copy-start(bf16[128,128]{1,0:T(8,128)(2,1)} %get-tuple-element.31) | copy-start | bytes 98308
  77.5 15.7 %all-to-all-start.1 = ((bf16[4,16,3584]{2,1,0:T(8,128)(2,1)}), bf16[4,16,3584]{2,1,0:T(8,128)(2,1)S(1)}, u32[]{:S(2)}, u32[]{:S(2)}) async-start(bf16[4,16,3584]{2,1,0:T(8,128)(2,1)} %bitcast.47), calls=%async_computation.1 | async-start | bytes 917504 | tf_op jit(solution)/shard_map/all_to_all | solution.py:318
  80.9 15.0 %collective-permute-start.5 = (bf16[32,3584]{1,0:T(8,128)(2,1)S(1)}, bf16[32,3584]{1,0:T(8,128)(2,1)S(1)}, u32[]{:S(2)}, u32[]{:S(2)}) collective-permute-start(bf16[32,3584]{1,0:T(8,128)(2,1)S(1)} %bitcast.52), channel_id=1, source_target_pairs={{0,1},{1,0},{2,3},{3,2},{4,5},{5,4},{6,7},{7,6},{8,9},{9,8},{10,11... | collective-permute-start | bytes 688136 | tf_op jit(solution)/shard_map/ppermute | solution.py:309
  82.9 13.0 %collective-permute-start.6 = (bf16[128,128]{1,0:T(8,128)(2,1)S(1)}, bf16[128,128]{1,0:T(8,128)(2,1)S(1)}, u32[]{:S(2)}, u32[]{:S(2)}) collective-permute-start(bf16[128,128]{1,0:T(8,128)(2,1)S(1)} %copy-done.17), channel_id=1, source_target_pairs={{0,1},{1,0},{2,3},{3,2},{4,5},{5,4},{6,7},{7,6},{8,9},{9,8},{10,11... | collective-permute-start | bytes 98312 | tf_op jit(solution)/shard_map/ppermute | solution.py:309
  93.2 0.8 copy-start.4
  94.0 3.9 %copy-start.5 = (bf16[16,3584]{1,0:T(8,128)(2,1)S(1)}, bf16[16,3584]{1,0:T(8,128)(2,1)}, u32[]{:S(2)}) copy-start(bf16[16,3584]{1,0:T(8,128)(2,1)} %shard_map.143.refs_2_.refs_5_) | copy-start | bytes 344068
  95.9 17.6 %copy-start.16 = (bf16[128,128]{1,0:T(8,128)(2,1)}, bf16[128,128]{1,0:T(8,128)(2,1)S(1)}, u32[]{:S(2)}) copy-start(bf16[128,128]{1,0:T(8,128)(2,1)S(1)} %collective-permute-done.6.refs_1_) | copy-start | bytes 98308
  95.9 17.6 %copy-start.13 = (bf16[32,3584]{1,0:T(8,128)(2,1)}, bf16[32,3584]{1,0:T(8,128)(2,1)S(1)}, u32[]{:S(2)}) copy-start(bf16[32,3584]{1,0:T(8,128)(2,1)S(1)} %collective-permute-done.5.refs_11_) | copy-start | bytes 688132
  95.9 15.0 %collective-permute-start.7 = (bf16[16,3584]{1,0:T(8,128)(2,1)}, bf16[16,3584]{1,0:T(8,128)(2,1)S(1)}, u32[]{:S(2)}, u32[]{:S(2)}) collective-permute-start(bf16[16,3584]{1,0:T(8,128)(2,1)} %shard_map.142), channel_id=1, source_target_pairs={{8,0},{16,8},{24,16},{32,24},{40,32},{48,40},{56,48},{64,56},{72,6... | collective-permute-start | bytes 344072 | tf_op jit(solution)/shard_map/ppermute | solution.py:368
  97.9 15.6 %collective-permute-start.10 = (bf16[16,3584]{1,0:T(8,128)(2,1)S(1)}, bf16[16,3584]{1,0:T(8,128)(2,1)S(1)}, u32[]{:S(2)}, u32[]{:S(2)}) collective-permute-start(bf16[16,3584]{1,0:T(8,128)(2,1)S(1)} %copy-done.5), channel_id=1, source_target_pairs={{6,0},{7,1},{0,2},{1,3},{2,4},{3,5},{4,6},{5,7},{14,8},{15,9},{8,1... | collective-permute-start | bytes 344072 | tf_op jit(solution)/shard_map/ppermute | solution.py:325
  99.8 13.7 %collective-permute-start.9 = (bf16[16,3584]{1,0:T(8,128)(2,1)S(1)}, bf16[16,3584]{1,0:T(8,128)(2,1)S(1)}, u32[]{:S(2)}, u32[]{:S(2)}) collective-permute-start(bf16[16,3584]{1,0:T(8,128)(2,1)S(1)} %copy-done.5), channel_id=1, source_target_pairs={{4,0},{5,1},{6,2},{7,3},{0,4},{1,5},{2,6},{3,7},{12,8},{13,9},{14,... | collective-permute-start | bytes 344072 | tf_op jit(solution)/shard_map/ppermute | solution.py:325
  103.7 9.8 %collective-permute-start.8 = (bf16[16,3584]{1,0:T(8,128)(2,1)S(1)}, bf16[16,3584]{1,0:T(8,128)(2,1)S(1)}, u32[]{:S(2)}, u32[]{:S(2)}) collective-permute-start(bf16[16,3584]{1,0:T(8,128)(2,1)S(1)} %copy-done.5), channel_id=1, source_target_pairs={{2,0},{3,1},{4,2},{5,3},{6,4},{7,5},{0,6},{1,7},{10,8},{11,9},{12,... | collective-permute-start | bytes 344072 | tf_op jit(solution)/shard_map/ppermute | solution.py:325
  110.9 0.6 copy-start.14
  113.5 0.6 copy-start.8
  113.6 0.7 copy-start.9
  113.6 0.7 copy-start.10
  114.3 19.9 %all-to-all-start.2 = ((bf16[4,16,3584]{2,1,0:T(8,128)(2,1)}), bf16[4,16,3584]{2,1,0:T(8,128)(2,1)S(1)}, u32[]{:S(2)}, u32[]{:S(2)}) async-start(bf16[4,16,3584]{2,1,0:T(8,128)(2,1)} %bitcast.46), calls=%async_computation.2 | async-start | bytes 917504 | tf_op jit(solution)/shard_map/all_to_all | solution.py:318
  134.2 0.8 copy-start.3
  160.0 19.8 %copy-start.7 = (f32[32,3584]{1,0:T(8,128)S(1)}, f32[32,3584]{1,0:T(8,128)}, u32[]{:S(2)}) copy-start(f32[32,3584]{1,0:T(8,128)} %get-tuple-element.43) | copy-start | bytes 1376260
  160.0 19.8 %collective-permute-start.12 = (f32[32,3584]{1,0:T(8,128)}, f32[32,3584]{1,0:T(8,128)S(1)}, u32[]{:S(2)}, u32[]{:S(2)}) collective-permute-start(f32[32,3584]{1,0:T(8,128)} %get-tuple-element.44), channel_id=1, source_target_pairs={{0,1},{1,0},{2,3},{3,2},{4,5},{5,4},{6,7},{7,6},{8,9},{9,8},{10,11... | collective-permute-start | bytes 1376264 | tf_op jit(solution)/shard_map/ppermute | solution.py:309
  164.0 15.8 %collective-permute-start.11 = (bf16[8,3584]{1,0:T(8,128)(2,1)}, bf16[8,3584]{1,0:T(8,128)(2,1)S(1)}, u32[]{:S(2)}, u32[]{:S(2)}) collective-permute-start(bf16[8,3584]{1,0:T(8,128)(2,1)} %get-tuple-element.40), channel_id=1, source_target_pairs={{0,504},{8,496},{16,488},{24,480},{32,472},{40,464},{48,456},{56,4... | collective-permute-start | bytes 172040 | tf_op jit(solution)/shard_map/ppermute | solution.py:314

commit v6 on v4

v6 whole, which is shorter than its diff:
```python
import functools

import jax
import jax.numpy as jnp
from jax import lax
from jax.experimental import pallas as pl
from jax.experimental.pallas import tpu as pltpu
from jax.sharding import PartitionSpec as P

D = 3584
HID = 128
EXPERTS = 256
OWN = 32
TOKENS = 64
TOPK = 8
ROWS = 8
CHIPS = 4
IDCOLS = 128
WIDE = D + IDCOLS
WIDTH = 512
VMEM_LIMIT = 16 * 1024 * 1024
z_weight = 0.01
balance_weight = 1.0
F32 = jnp.float32
BF16 = jnp.bfloat16


def dot(lhs, rhs, lhs_dim, rhs_dim):
    return lax.dot_general(
        lhs, rhs, (((lhs_dim,), (rhs_dim,)), ((), ())), preferred_element_type=F32
    )


def call(body, outs, args, scratch=(), flops=0):
    spec = pl.BlockSpec(memory_space=pltpu.VMEM)
    total = sum(a.size * a.dtype.itemsize for a in args)
    return pl.pallas_call(
        body,
        out_shape=[jax.ShapeDtypeStruct(shape, dtype) for shape, dtype in outs],
        in_specs=[spec] * len(args),
        out_specs=[spec] * len(outs),
        scratch_shapes=list(scratch),
        compiler_params=pltpu.CompilerParams(vmem_limit_bytes=VMEM_LIMIT),
        cost_estimate=pl.CostEstimate(flops=flops, bytes_accessed=total, transcendentals=0),
    )(*args)


def packed(parts):
    return jnp.concatenate([p.astype(F32) for p in parts], axis=0).astype(BF16)


def id_columns(ids):
    empty = jnp.full((ROWS, IDCOLS - 2 * TOPK), -1.0, F32)
    used = jnp.concatenate([ids[0].astype(F32), ids[1].astype(F32), empty], axis=1)
    return jnp.concatenate([used, jnp.full((ROWS, IDCOLS), -1.0, F32)], axis=0).astype(BF16)


def pack_kernel(stash, grads, ids, out):
    out[:, 0:D] = packed([stash[0], grads[...]])
    out[:, D:WIDE] = id_columns(ids)


def join_kernel(stash, other, out):
    out[...] = packed([stash[1], other[...]])


def backward_terms(hidden, gate, up, gates, ups, outs):
    d_gate, d_up = [], []
    for h, g, u in zip(hidden, gate, up):
        q = jax.nn.sigmoid(g)
        d_gate.append((h * u * q * (1.0 + g * (1.0 - q))).astype(BF16))
        d_up.append((h * g * q).astype(BF16))
    for low in range(0, D, WIDTH):
        cols = pl.ds(low, WIDTH)
        total = dot(d_gate[0], gates[0][cols, :], 1, 1)
        total += dot(d_gate[1], gates[1][cols, :], 1, 1)
        total += dot(d_up[0], ups[0][cols, :], 1, 1)
        total += dot(d_up[1], ups[1][cols, :], 1, 1)
        for k in range(CHIPS):
            outs[k][:, cols] = total[16 * k : 16 * k + 16].astype(outs[k].dtype)


def first_rows(blocks, held):
    for b, block in enumerate(blocks):
        held[16 * b : 16 * b + 16, :] = block[:, 0:D]


def first_tick_kernel(*refs):
    blocks, weights, outs, ids, held = refs[:8], refs[8:14], refs[14:18], refs[18], refs[19]
    gates, ups, downs = weights[0:2], weights[2:4], weights[4:6]
    first_rows(blocks, held)
    for b, block in enumerate(blocks):
        ids[16 * b : 16 * b + 16, :] = block[:, D:WIDE]
    rows = held[...]

    def pick(value, offset):
        return jnp.concatenate(
            [value[16 * b + offset : 16 * b + offset + 8] for b in range(2 * CHIPS)], axis=0
        )

    gate = [pick(dot(rows, w[...], 1, 0), 0) for w in gates]
    up = [pick(dot(rows, w[...], 1, 0), 0) for w in ups]
    hidden = [pick(dot(rows, w[...], 1, 1), 8) for w in downs]
    backward_terms(hidden, gate, up, gates, ups, outs)


def second_tick_kernel(*refs):
    blocks, pre, stats, weights = refs[:4], refs[4], refs[5], refs[6:12]
    outs, held = refs[12:16], refs[16]
    gates, ups, downs = weights[0:2], weights[2:4], weights[4:6]
    for k in range(CHIPS):
        held[16 * k : 16 * k + 16, :] = blocks[k][...]
    rows = held[...]
    hidden = [dot(rows, w[...], 1, 1) for w in downs]
    gate = [pre[:, 0:HID], pre[:, HID : 2 * HID]]
    up = [pre[:, 2 * HID : 3 * HID], pre[:, 3 * HID : 4 * HID]]
    backward_terms(hidden, gate, up, gates, ups, outs)
    for k in range(1, CHIPS):
        outs[k][:, D:WIDE] = stats[...]


def forward_kernel(*refs):
    blocks, second, other_ids = refs[0:8], refs[8:12], refs[12]
    weights, routers = refs[13:17], refs[17:19]
    pre, expo_ref, share_ref, stats_ref = refs[19:23]
    held0, held1, ids_ref = refs[23:26]
    member = lax.axis_index("expert")
    first_rows(blocks, held0)
    for b, block in enumerate(blocks):
        ids_ref[16 * b : 16 * b + 16, :] = block[:, D:WIDE].astype(F32)
    for k in range(CHIPS):
        held1[16 * k : 16 * k + 16, :] = second[k][...]
    rows0, rows1 = held0[...], held1[...]
    for i, w in enumerate(weights):
        pre[:, HID * i : HID * i + HID] = dot(rows1, w[...], 1, 0)
    logits = jnp.concatenate(
        [
            jnp.concatenate([dot(r[...], rows, 1, 1) for r in routers], axis=0)
            for rows in (rows0, jnp.concatenate([rows1, rows1], axis=0))
        ],
        axis=1,
    )
    ids = [ids_ref[...].T, other_ids[...].astype(F32).T]
    row = lax.broadcasted_iota(jnp.int32, (2 * OWN, 128), 0)
    column = lax.broadcasted_iota(jnp.int32, (2 * OWN, 128), 1)
    own = row + OWN * member
    other = row - OWN + OWN * (member + 1 - 2 * lax.rem(member, 2))
    experts = jnp.where(row < OWN, own, other).astype(F32)
    stream_b = (column % 32) >= 16
    scale = EXPERTS / (TOKENS * TOPK)
    shares = []
    for tick in range(2):
        hits = jnp.zeros((2 * OWN, 128), F32)
        for core in range(2):
            for j in range(TOPK):
                slot = TOPK * tick + j
                hits += (experts == ids[core][slot : slot + 1, :]).astype(F32)
        count_a = jnp.sum(jnp.where(stream_b, 0.0, hits), axis=1, keepdims=True)
        count_b = jnp.sum(jnp.where(stream_b, hits, 0.0), axis=1, keepdims=True)
        shares.append((count_a * scale, count_b * scale))
    share0 = jnp.where(stream_b, shares[0][1], shares[0][0])
    share1 = jnp.where((column % 16) >= 8, shares[1][1], shares[1][0])
    share = jnp.concatenate([share0, share1], axis=1)
    peak = jnp.max(logits, axis=0, keepdims=True)
    expo = jnp.exp(logits - peak)
    total = jnp.sum(expo, axis=0, keepdims=True)
    weighted = jnp.sum(expo * share, axis=0, keepdims=True)
    expo_ref[...] = expo
    share_ref[...] = share
    figures = []
    for value, count in ((peak, 3), (total, 2), (weighted, 2)):
        for _ in range(count):
            figures.append(value.astype(BF16).astype(F32))
            value = value - figures[-1]
    rows = [f[:, low : low + 128] for low in (0, 128) for f in figures]
    stats_ref[...] = jnp.concatenate(rows + [jnp.zeros((2, 128), F32)], axis=0).astype(BF16)


def router_kernel(*refs):
    blocks, second, expo_ref, share_ref, parts = refs[0:8], refs[8:12], refs[12], refs[13], refs[14:18]
    own_out, other_out, held0, held1 = refs[18:22]
    first_rows(blocks, held0)
    for k in range(CHIPS):
        held1[16 * k : 16 * k + 16, :] = second[k][...]
    stats = []
    for k, part in enumerate(parts):
        value = (part[...] if k == 0 else part[:, D:WIDE]).astype(F32)
        wide = [
            jnp.concatenate(
                [pltpu.roll(value, 32 * k, 1)[i : i + 1], pltpu.roll(value, 16 * k, 1)[i + 7 : i + 8]],
                axis=1,
            )
            if k
            else jnp.concatenate([value[i : i + 1], value[i + 7 : i + 8]], axis=1)
            for i in range(7)
        ]
        stats.append((wide[0] + wide[1] + wide[2], wide[3] + wide[4], wide[5] + wide[6]))
    mine = stats[0]
    peaks = [s[0] for s in stats]
    peak = functools.reduce(jnp.maximum, peaks)
    factors = [jnp.exp(p - peak) for p in peaks]
    total = sum(s[1] * f for s, f in zip(stats, factors))
    weighted = sum(s[2] * f for s, f in zip(stats, factors))
    log_total = peak + jnp.log(total)
    mean_share = weighted / total
    probs = expo_ref[...] * (jnp.exp(mine[0] - peak) / total)
    slopes = (
        2.0 * z_weight * log_total - balance_weight * mean_share + balance_weight * share_ref[...]
    ) * probs
    column = lax.broadcasted_iota(jnp.int32, (2 * OWN, 128), 1)
    slopes0 = jnp.where((column % 16) < 8, slopes[:, 0:128], 0.0).astype(BF16)
    slopes1 = slopes[:, 128:192].astype(BF16)
    for low in range(0, D, WIDTH):
        cols = pl.ds(low, WIDTH)
        part = dot(slopes0, held0[:, cols], 1, 0) + dot(slopes1, held1[:, cols], 1, 0)
        own_out[:, cols] = part[0:OWN]
        other_out[:, cols] = part[OWN:]


def swapped(value):
    return lax.ppermute(value, "expert", [(e, e ^ 1) for e in range(8)])


def mirrored(value):
    count = lax.axis_size("pipe")
    return lax.ppermute(value, "pipe", [(i, count - 1 - i) for i in range(count)])


def from_chip(value, k):
    return lax.ppermute(value, "expert", [((e + 2 * k) % 8, e) for e in range(8)])


def ring(value):
    return [value] + [from_chip(value, k) for k in range(1, CHIPS)]


def returned(parts):
    return [parts[0]] + [from_chip(parts[CHIPS - k], k) for k in range(1, CHIPS)]


def emitted(grads, parts):
    total = grads.astype(F32)
    for part in parts:
        total = total + part[:, :D].astype(F32)
    return total.astype(BF16)


def after(value, *earlier):
    return lax.optimization_barrier((value, *earlier))[0]


def shards(
    stash_a, stash_b, ids_a, ids_b, arriving_a, arriving_b, head_a, head_b,
    w_gate, w_up, w_down, router,
):
    stash_a, stash_b, ids_a, ids_b = stash_a[0], stash_b[0], ids_a[0], ids_b[0]
    arriving_a, arriving_b = arriving_a[0], arriving_b[0]
    w_gate, w_up, w_down, router = w_gate[0], w_up[0], w_down[0], router[0]
    section = lax.axis_index("pipe")
    top = lax.axis_size("pipe") - 1
    rows0, rows1 = pltpu.VMEM((128, D), BF16), pltpu.VMEM((64, D), BF16)

    (packed_b,) = call(pack_kernel, [((16, WIDE), BF16)], [stash_b, arriving_b, ids_b])
    block_b = mirrored(packed_b)
    (block_a,) = call(pack_kernel, [((16, WIDE), BF16)], [stash_a, arriving_a, ids_a])
    blocks_a = ring(block_a)
    blocks_b = ring(block_b)
    first = [block for pair in zip(blocks_a, blocks_b) for block in pair]
    other_gate, other_up, other_down, other_router = lax.optimization_barrier(
        tuple(swapped(weight) for weight in (w_gate, w_up, w_down, router))
    )
    gates, ups, downs = [w_gate, other_gate], [w_up, other_up], [w_down, other_down]
    later_b = mirrored(after(stash_b[1], block_b))
    (later,) = call(join_kernel, [((16, D), BF16)], [stash_a, later_b])
    second = ring(later)

    own_terms = ((16, D), F32)
    *terms, ids = call(
        first_tick_kernel, [own_terms] + [((16, D), BF16)] * 3 + [((128, IDCOLS), BF16)],
        first + gates + ups + downs, [rows0], 2 * 128 * D * 128 * 10,
    )
    terms = lax.optimization_barrier((*terms, *second))[:CHIPS]
    grads = jnp.concatenate([arriving_a, block_b[8:, :D]], axis=0)
    out = emitted(grads, returned(terms))
    moved = lax.ppermute(out, "pipe", [(i, i - 1) for i in range(1, top + 1)])
    head = jnp.concatenate([head_a[0], head_b[0]], axis=0)
    grads = jnp.where(section == top, head, moved)
    all_grads = ring(grads)
    other_ids = swapped(after(ids, out))
    pre, expo, share, stats = call(
        forward_kernel,
        [((64, 4 * HID), F32), ((2 * OWN, 256), F32), ((2 * OWN, 256), F32), ((16, IDCOLS), BF16)],
        first + second + [other_ids] + gates + ups + [router, other_router],
        [rows0, rows1, pltpu.VMEM((128, IDCOLS), F32)], 2 * 128 * D * 128 * 4,
    )
    terms = call(
        second_tick_kernel, [own_terms] + [((16, WIDE), BF16)] * 3,
        all_grads + [pre, stats] + gates + ups + downs, [rows1], 2 * 64 * D * 128 * 6,
    )
    parts = returned(terms)
    out = emitted(grads, parts)
    own, other = call(
        router_kernel, [((OWN, D), F32)] * 2,
        first + second + [after(expo, out), share, stats] + parts[1:], [rows0, rows1],
        2 * 192 * D * 64,
    )
    return out[None, :8], mirrored(out[8:])[None], (own + swapped(other))[None]


def solution(mesh):
    placed = (
        P("pipe", None, "expert", None),
        P("pipe", None, "expert", None),
        P("pipe", None, "expert", None),
        P("pipe", None, "expert", None),
        P("pipe", "expert", None),
        P("pipe", "expert", None),
        P(None, "expert", None),
        P(None, "expert", None),
        P("pipe", None, "expert"),
        P("pipe", None, "expert"),
        P("pipe", "expert", None),
        P("pipe", "expert", None),
    )
    return jax.shard_map(
        shards,
        mesh=mesh,
        in_specs=placed,
        out_specs=(P("pipe", "expert", None), P("pipe", "expert", None), P("pipe", "expert", None)),
        check_vma=False,
    )
```

time: 190 us -> 180 us (0.947)
  local copies, waits for them, and re-layouts: 29.7 us -> 18.5 us
  starting transfers between devices: 91.9 us -> 100 us
  Pallas kernels: 14.3 us -> 7.63 us
  waiting for transfers between devices: 50.1 us -> 47.5 us
    ppermute x3 -> x18, starting transfers between devices: 10.7 us -> 61.8 us  [from_chip(): lax.ppermute(value, 'expert', [((e + 2 * k) % 8, e) for e in range(8)])]
    all_to_all x5 -> x0, starting transfers between devices: 33.5 us -> none  [exchanged(): lax.all_to_all(blocks, 'expert', split_axis=0, concat_axis=0, tiled=True,...]
    all_to_all x5 -> x0, waiting for transfers between devices: 17 us -> none  [exchanged(): lax.all_to_all(blocks, 'expert', split_axis=0, concat_axis=0, tiled=True,...]
    unnamed x89 -> x67, local copies, waits for them, and re-layouts: 29.1 us -> 17 us
    ppermute x3, starting transfers between devices: 31.8 us -> 24.2 us  [mirrored(): lax.ppermute(value, 'pipe', [(i, count - 1 - i) for i in range(count)])]
    ppermute x1, waiting for transfers between devices: 9.79 us -> 16.5 us  [shards(): moved = lax.ppermute(out, 'pipe', [(i, i - 1) for i in range(1, top + 1)])]
    pallas_call x10 -> x7, Pallas kernels: 14.3 us -> 7.63 us  [call(): pl.pallas_call(body, out_shape=[jax.ShapeDtypeStruct(shape, dtype) for sh...]
    ppermute x3 -> x18, waiting for transfers between devices: 4.31 us -> 10.2 us  [from_chip(): lax.ppermute(value, 'expert', [((e + 2 * k) % 8, e) for e in range(8)])]
  transfers between devices with their start and end apart: 18 -> 28, of which waited for: 8 -> 7; matrix products, arithmetic and copies ran while one was open for 1% -> 1% of each run, Pallas kernels for 5% -> 3%
where the time goes in v6:
time: 180 us; the launch traced here: 178 us
  starting transfers between devices  100 us (56%)
  waiting for transfers between devices  47.5 us (26%)
  local copies, waits for them, and re-layouts  18.5 us (10%)
  Pallas kernels  7.63 us (4%)
  other arithmetic  2.59 us (1%)
    ppermute x18, starting transfers between devices, from_chip(): lax.ppermute(value, 'expert', [((e + 2 * k) % 8, e) for e in range(8)])  61.8 us
    ppermute x3, starting transfers between devices, mirrored(): lax.ppermute(value, 'pipe', [(i, count - 1 - i) for i in range(count)])  24.2 us
    ppermute x3, waiting for transfers between devices, mirrored(): lax.ppermute(value, 'pipe', [(i, count - 1 - i) for i in range(count)])  19.6 us
    unnamed x67, local copies, waits for them, and re-layouts  17 us
    ppermute x1, waiting for transfers between devices, shards(): moved = lax.ppermute(out, 'pipe', [(i, i - 1) for i in range(1, top + 1)])  16.5 us
    ppermute x6, starting transfers between devices, swapped(): return lax.ppermute(value, 'expert', [(e, e ^ 1) for e in range(8)])  12.5 us
    ppermute x18, waiting for transfers between devices, from_chip(): lax.ppermute(value, 'expert', [((e + 2 * k) % 8, e) for e in range(8)])  10.2 us
    pallas_call x7, Pallas kernels, call(): pl.pallas_call(body, out_shape=[jax.ShapeDtypeStruct(shape, dtype) for sh...  7.63 us
  transfers between devices with their start and end apart: 28, of which 7 were waited for; matrix products, arithmetic and copies ran while one was open for 1% of the time, Pallas kernels for 3%

profile of v6, /device:TPU:6, one launch (start us, length us, event | category | flops | bytes accessed | tf_op | source)
XLA Modules:
  0.0 177.9 jit_solution(16286770220480681638)
XLA Ops:
  0.7 1.0 copy-done.23
  3.2 15.1 %collective-permute-start = (bf16[16,3712]{1,0:T(8,128)(2,1)S(1)}, bf16[16,3712]{1,0:T(8,128)(2,1)S(1)}, u32[]{:S(2)}, u32[]{:S(2)}) collective-permute-start(bf16[16,3712]{1,0:T(8,128)(2,1)S(1)} %shard_map.139), channel_id=1, source_target_pairs={{0,504},{8,496},{16,488},{24,480},{32,472},{40,464},{48,456},{56,4... | collective-permute-start | bytes 356360 | tf_op jit(solution)/shard_map/ppermute | solution.py:226
  20.8 2.9 %collective-permute-start.5 = (bf16[16,3712]{1,0:T(8,128)(2,1)S(1)}, bf16[16,3712]{1,0:T(8,128)(2,1)S(1)}, u32[]{:S(2)}, u32[]{:S(2)}) collective-permute-start(bf16[16,3712]{1,0:T(8,128)(2,1)S(1)} %shard_map.140.refs_0_), channel_id=1, source_target_pairs={{6,0},{7,1},{0,2},{1,3},{2,4},{3,5},{4,6},{5,7},{14,8},{15,9},{8,1... | collective-permute-start | bytes 356360 | tf_op jit(solution)/shard_map/ppermute | solution.py:230
  23.7 3.4 %collective-permute-start.3 = (bf16[16,3712]{1,0:T(8,128)(2,1)S(1)}, bf16[16,3712]{1,0:T(8,128)(2,1)S(1)}, u32[]{:S(2)}, u32[]{:S(2)}) collective-permute-start(bf16[16,3712]{1,0:T(8,128)(2,1)S(1)} %shard_map.140.refs_0_), channel_id=1, source_target_pairs={{4,0},{5,1},{6,2},{7,3},{0,4},{1,5},{2,6},{3,7},{12,8},{13,9},{14,... | collective-permute-start | bytes 356360 | tf_op jit(solution)/shard_map/ppermute | solution.py:230
  27.1 3.8 %collective-permute-start.1 = (bf16[16,3712]{1,0:T(8,128)(2,1)S(1)}, bf16[16,3712]{1,0:T(8,128)(2,1)S(1)}, u32[]{:S(2)}, u32[]{:S(2)}) collective-permute-start(bf16[16,3712]{1,0:T(8,128)(2,1)S(1)} %shard_map.140.refs_0_), channel_id=1, source_target_pairs={{2,0},{3,1},{4,2},{5,3},{6,4},{7,5},{0,6},{1,7},{10,8},{11,9},{12,... | collective-permute-start | bytes 356360 | tf_op jit(solution)/shard_map/ppermute | solution.py:230
  30.9 1.9 %collective-permute-start.10 = (bf16[32,3584]{1,0:T(8,128)(2,1)}, bf16[32,3584]{1,0:T(8,128)(2,1)S(1)}, u32[]{:S(2)}, u32[]{:S(2)}) collective-permute-start(bf16[32,3584]{1,0:T(8,128)(2,1)} %bitcast.35), channel_id=1, source_target_pairs={{0,1},{1,0},{2,3},{3,2},{4,5},{5,4},{6,7},{7,6},{8,9},{9,8},{10,11... | collective-permute-start | bytes 688136 | tf_op jit(solution)/shard_map/ppermute | solution.py:221
  32.9 2.4 %collective-permute-start.7 = (bf16[3584,128]{1,0:T(8,128)(2,1)}, bf16[3584,128]{1,0:T(8,128)(2,1)S(1)}, u32[]{:S(2)}, u32[]{:S(2)}) collective-permute-start(bf16[3584,128]{1,0:T(8,128)(2,1)} %bitcast.19), channel_id=1, source_target_pairs={{0,1},{1,0},{2,3},{3,2},{4,5},{5,4},{6,7},{7,6},{8,9},{9,8},{10,11... | collective-permute-start | bytes 2752520 | tf_op jit(solution)/shard_map/ppermute | solution.py:221
  35.3 1.9 %collective-permute-start.8 = (bf16[3584,128]{1,0:T(8,128)(2,1)}, bf16[3584,128]{1,0:T(8,128)(2,1)S(1)}, u32[]{:S(2)}, u32[]{:S(2)}) collective-permute-start(bf16[3584,128]{1,0:T(8,128)(2,1)} %bitcast.23), channel_id=1, source_target_pairs={{0,1},{1,0},{2,3},{3,2},{4,5},{5,4},{6,7},{7,6},{8,9},{9,8},{10,11... | collective-permute-start | bytes 2752520 | tf_op jit(solution)/shard_map/ppermute | solution.py:221
  37.2 2.4 %collective-permute-start.9 = (bf16[128,3584]{1,0:T(8,128)(2,1)}, bf16[128,3584]{1,0:T(8,128)(2,1)S(1)}, u32[]{:S(2)}, u32[]{:S(2)}) collective-permute-start(bf16[128,3584]{1,0:T(8,128)(2,1)} %bitcast.27), channel_id=1, source_target_pairs={{0,1},{1,0},{2,3},{3,2},{4,5},{5,4},{6,7},{7,6},{8,9},{9,8},{10,11... | collective-permute-start | bytes 2752520 | tf_op jit(solution)/shard_map/ppermute | solution.py:221
  40.5 7.2 %collective-permute-start.11 = (bf16[8,3584]{1,0:T(8,128)(2,1)S(1)}, bf16[8,3584]{1,0:T(8,128)(2,1)S(1)}, u32[]{:S(2)}, u32[]{:S(2)}) collective-permute-start(bf16[8,3584]{1,0:T(8,128)(2,1)S(1)} %slice_bitcast_fusion.1), channel_id=1, source_target_pairs={{0,504},{8,496},{16,488},{24,480},{32,472},{40,464},{48,456},{56,4... | collective-permute-start | bytes 172040 | tf_op jit(solution)/shard_map/ppermute | solution.py:226
  47.7 7.0 %collective-permute-done.11.other = bf16[8,3584]{1,0:T(8,128)(2,1)S(1)} collective-permute-done((bf16[8,3584]{1,0:T(8,128)(2,1)S(1)}, bf16[8,3584]{1,0:T(8,128)(2,1)S(1)}, u32[]{:S(2)}, u32[]{:S(2)}) %collective-permute-start.11) | collective-permute-done | bytes 57376 | tf_op jit(solution)/shard_map/ppermute | solution.py:226
  54.7 2.7 %collective-permute-start.6 = (bf16[16,3712]{1,0:T(8,128)(2,1)S(1)}, bf16[16,3712]{1,0:T(8,128)(2,1)S(1)}, u32[]{:S(2)}, u32[]{:S(2)}) collective-permute-start(bf16[16,3712]{1,0:T(8,128)(2,1)S(1)} %collective-permute-done.refs_1_), channel_id=1, source_target_pairs={{6,0},{7,1},{0,2},{1,3},{2,4},{3,5},{4,6},{5,7},{14,8},{15,9},{8,1... | collective-permute-start | bytes 356360 | tf_op jit(solution)/shard_map/ppermute | solution.py:230
  58.1 6.6 %collective-permute-start.4 = (bf16[16,3712]{1,0:T(8,128)(2,1)S(1)}, bf16[16,3712]{1,0:T(8,128)(2,1)S(1)}, u32[]{:S(2)}, u32[]{:S(2)}) collective-permute-start(bf16[16,3712]{1,0:T(8,128)(2,1)S(1)} %collective-permute-done.refs_1_), channel_id=1, source_target_pairs={{4,0},{5,1},{6,2},{7,3},{0,4},{1,5},{2,6},{3,7},{12,8},{13,9},{14,... | collective-permute-start | bytes 356360 | tf_op jit(solution)/shard_map/ppermute | solution.py:230
  64.8 3.6 %collective-permute-start.2 = (bf16[16,3712]{1,0:T(8,128)(2,1)S(1)}, bf16[16,3712]{1,0:T(8,128)(2,1)S(1)}, u32[]{:S(2)}, u32[]{:S(2)}) collective-permute-start(bf16[16,3712]{1,0:T(8,128)(2,1)S(1)} %collective-permute-done.refs_1_), channel_id=1, source_target_pairs={{2,0},{3,1},{4,2},{5,3},{6,4},{7,5},{0,6},{1,7},{10,8},{11,9},{12,... | collective-permute-start | bytes 356360 | tf_op jit(solution)/shard_map/ppermute | solution.py:230
  68.5 2.2 %collective-permute-start.14 = (bf16[16,3584]{1,0:T(8,128)(2,1)S(1)}, bf16[16,3584]{1,0:T(8,128)(2,1)S(1)}, u32[]{:S(2)}, u32[]{:S(2)}) collective-permute-start(bf16[16,3584]{1,0:T(8,128)(2,1)S(1)} %shard_map.142.refs_8_), channel_id=1, source_target_pairs={{6,0},{7,1},{0,2},{1,3},{2,4},{3,5},{4,6},{5,7},{14,8},{15,9},{8,1... | collective-permute-start | bytes 344072 | tf_op jit(solution)/shard_map/ppermute | solution.py:230
  70.7 2.2 %collective-permute-start.13 = (bf16[16,3584]{1,0:T(8,128)(2,1)S(1)}, bf16[16,3584]{1,0:T(8,128)(2,1)S(1)}, u32[]{:S(2)}, u32[]{:S(2)}) collective-permute-start(bf16[16,3584]{1,0:T(8,128)(2,1)S(1)} %shard_map.142.refs_8_), channel_id=1, source_target_pairs={{4,0},{5,1},{6,2},{7,3},{0,4},{1,5},{2,6},{3,7},{12,8},{13,9},{14,... | collective-permute-start | bytes 344072 | tf_op jit(solution)/shard_map/ppermute | solution.py:230
  72.9 5.2 %collective-permute-start.12 = (bf16[16,3584]{1,0:T(8,128)(2,1)S(1)}, bf16[16,3584]{1,0:T(8,128)(2,1)S(1)}, u32[]{:S(2)}, u32[]{:S(2)}) collective-permute-start(bf16[16,3584]{1,0:T(8,128)(2,1)S(1)} %shard_map.142.refs_8_), channel_id=1, source_target_pairs={{2,0},{3,1},{4,2},{5,3},{6,4},{7,5},{0,6},{1,7},{10,8},{11,9},{12,... | collective-permute-start | bytes 344072 | tf_op jit(solution)/shard_map/ppermute | solution.py:230
  78.1 1.2 copy-done.1
  79.3 1.2 copy-done.5
  80.5 3.0 %shard_map.141 = (f32[16,3584]{1,0:T(8,128)S(1)}, bf16[16,3584]{1,0:T(8,128)(2,1)S(1)}, bf16[16,3584]{1,0:T(8,128)(2,1)S(1)}, bf16[16,3584]{1,0:T(8,128)(2,1)S(1)}, bf16[128,128]{1,0:T(8,128)(2,1)S(1)}) custom-call(bf16[16,3712]{1,0:T(8,128)(2,1)S(1)} %shard_map.140.refs_0_, bf16[16,3712]{1,0:T(8,128)(2,1)S(1)} %collective-permute-done.refs_1_, ...), custom_call_target="tpu_custom_call" | custom-call | flops 1174405120 | bytes 6455296 | tf_op jit(solution)/shard_map/pallas_call | solution.py:37
  83.6 0.9 copy-done.3
  84.6 2.9 %collective-permute-start.15 = (bf16[16,3584]{1,0:T(8,128)(2,1)S(1)}, bf16[16,3584]{1,0:T(8,128)(2,1)S(1)}, u32[]{:S(2)}, u32[]{:S(2)}) collective-permute-start(bf16[16,3584]{1,0:T(8,128)(2,1)S(1)} %get-tuple-element.38), channel_id=1, source_target_pairs={{2,0},{3,1},{4,2},{5,3},{6,4},{7,5},{0,6},{1,7},{10,8},{11,9},{12,... | collective-permute-start | bytes 344072 | tf_op jit(solution)/shard_map/ppermute | solution.py:230
  87.5 3.1 %collective-permute-start.16 = (bf16[16,3584]{1,0:T(8,128)(2,1)S(1)}, bf16[16,3584]{1,0:T(8,128)(2,1)S(1)}, u32[]{:S(2)}, u32[]{:S(2)}) collective-permute-start(bf16[16,3584]{1,0:T(8,128)(2,1)S(1)} %get-tuple-element.39), channel_id=1, source_target_pairs={{4,0},{5,1},{6,2},{7,3},{0,4},{1,5},{2,6},{3,7},{12,8},{13,9},{14,... | collective-permute-start | bytes 344072 | tf_op jit(solution)/shard_map/ppermute | solution.py:230
  90.6 3.9 %collective-permute-start.17 = (bf16[16,3584]{1,0:T(8,128)(2,1)S(1)}, bf16[16,3584]{1,0:T(8,128)(2,1)S(1)}, u32[]{:S(2)}, u32[]{:S(2)}) collective-permute-start(bf16[16,3584]{1,0:T(8,128)(2,1)S(1)} %get-tuple-element.40), channel_id=1, source_target_pairs={{6,0},{7,1},{0,2},{1,3},{2,4},{3,5},{4,6},{5,7},{14,8},{15,9},{8,1... | collective-permute-start | bytes 344072 | tf_op jit(solution)/shard_map/ppermute | solution.py:230
  94.5 3.0 %collective-permute-done.16 = bf16[16,3584]{1,0:T(8,128)(2,1)S(1)} collective-permute-done((bf16[16,3584]{1,0:T(8,128)(2,1)S(1)}, bf16[16,3584]{1,0:T(8,128)(2,1)S(1)}, u32[]{:S(2)}, u32[]{:S(2)}) %collective-permute-start.16) | collective-permute-done | bytes 114720 | tf_op jit(solution)/shard_map/ppermute | solution.py:230
  97.6 1.5 collective-permute-done.17
  99.8 1.9 %collective-permute-start.18 = (bf16[16,3584]{1,0:T(8,128)(2,1)}, bf16[16,3584]{1,0:T(8,128)(2,1)}, u32[]{:S(2)}, u32[]{:S(2)}) collective-permute-start(bf16[16,3584]{1,0:T(8,128)(2,1)} %add_convert_fusion.1), channel_id=1, source_target_pairs={{8,0},{16,8},{24,16},{32,24},{40,32},{48,40},{56,48},{64,56},{72,6... | collective-permute-start | bytes 344072 | tf_op jit(solution)/shard_map/ppermute | solution.py:285
  101.7 16.5 %collective-permute-done.18 = bf16[16,3584]{1,0:T(8,128)(2,1)} collective-permute-done((bf16[16,3584]{1,0:T(8,128)(2,1)}, bf16[16,3584]{1,0:T(8,128)(2,1)}, u32[]{:S(2)}, u32[]{:S(2)}) %collective-permute-start.18) | collective-permute-done | bytes 114720 | tf_op jit(solution)/shard_map/ppermute | solution.py:285
  118.3 1.0 maximum_select_fusion.refs_0_
  119.3 1.9 %collective-permute-start.21 = (bf16[16,3584]{1,0:T(8,128)(2,1)S(1)}, bf16[16,3584]{1,0:T(8,128)(2,1)S(1)}, u32[]{:S(2)}, u32[]{:S(2)}) collective-permute-start(bf16[16,3584]{1,0:T(8,128)(2,1)S(1)} %maximum_select_fusion.refs_0_), channel_id=1, source_target_pairs={{6,0},{7,1},{0,2},{1,3},{2,4},{3,5},{4,6},{5,7},{14,8},{15,9},{8,1... | collective-permute-start | bytes 344072 | tf_op jit(solution)/shard_map/ppermute | solution.py:230
  121.2 1.9 %collective-permute-start.20 = (bf16[16,3584]{1,0:T(8,128)(2,1)S(1)}, bf16[16,3584]{1,0:T(8,128)(2,1)S(1)}, u32[]{:S(2)}, u32[]{:S(2)}) collective-permute-start(bf16[16,3584]{1,0:T(8,128)(2,1)S(1)} %maximum_select_fusion.refs_0_), channel_id=1, source_target_pairs={{4,0},{5,1},{6,2},{7,3},{0,4},{1,5},{2,6},{3,7},{12,8},{13,9},{14,... | collective-permute-start | bytes 344072 | tf_op jit(solution)/shard_map/ppermute | solution.py:230
  123.1 5.7 %collective-permute-start.19 = (bf16[16,3584]{1,0:T(8,128)(2,1)S(1)}, bf16[16,3584]{1,0:T(8,128)(2,1)S(1)}, u32[]{:S(2)}, u32[]{:S(2)}) collective-permute-start(bf16[16,3584]{1,0:T(8,128)(2,1)S(1)} %maximum_select_fusion.refs_0_), channel_id=1, source_target_pairs={{2,0},{3,1},{4,2},{5,3},{6,4},{7,5},{0,6},{1,7},{10,8},{11,9},{12,... | collective-permute-start | bytes 344072 | tf_op jit(solution)/shard_map/ppermute | solution.py:230
  128.9 1.9 %collective-permute-start.22 = (bf16[128,128]{1,0:T(8,128)(2,1)S(1)}, bf16[128,128]{1,0:T(8,128)(2,1)S(1)}, u32[]{:S(2)}, u32[]{:S(2)}) collective-permute-start(bf16[128,128]{1,0:T(8,128)(2,1)S(1)} %get-tuple-element.42), channel_id=1, source_target_pairs={{0,1},{1,0},{2,3},{3,2},{4,5},{5,4},{6,7},{7,6},{8,9},{9,8},{10,11... | collective-permute-start | bytes 98312 | tf_op jit(solution)/shard_map/ppermute | solution.py:221
  130.8 1.2 collective-permute-done.22.refs_12_
  132.0 1.2 copy-done.4
  133.2 0.9 copy-done.14
  134.1 0.9 copy-done.17
  136.8 0.9 copy-done.26
  137.7 0.9 copy-done.28
  138.6 1.9 %shard_map.143 = (f32[64,512]{1,0:T(8,128)S(1)}, f32[64,256]{1,0:T(8,128)S(1)}, f32[64,256]{1,0:T(8,128)S(1)}, bf16[16,128]{1,0:T(8,128)(2,1)S(1)}) custom-call(bf16[16,3712]{1,0:T(8,128)(2,1)S(1)} %shard_map.140.refs_0_, bf16[16,3712]{1,0:T(8,128)(2,1)S(1)} %collective-permute-done.refs_1_, bf16[16,3712]{1,0:T(8,128)(2,1)S(1)} %collective-permute-done.1.refs_2_, ...), custom_call_target="tpu_custom_call" | custom-call | flops 469762048 | bytes 5570560 | tf_op jit(solution)/shard_map/pallas_call | solution.py:37
  140.6 2.1 %shard_map.144 = (f32[16,3584]{1,0:T(8,128)S(1)}, bf16[16,3712]{1,0:T(8,128)(2,1)S(1)}, bf16[16,3712]{1,0:T(8,128)(2,1)S(1)}, bf16[16,3712]{1,0:T(8,128)(2,1)S(1)}) custom-call(bf16[16,3584]{1,0:T(8,128)(2,1)S(1)} %maximum_select_fusion.refs_0_, bf16[16,3584]{1,0:T(8,128)(2,1)S(1)} %collective-permute-done.19.refs_1_, ...), custom_call_target="tpu_custom_call" | custom-call | flops 352321536 | bytes 6098944 | tf_op jit(solution)/shard_map/pallas_call | solution.py:37
  142.7 2.5 %collective-permute-start.23 = (bf16[16,3712]{1,0:T(8,128)(2,1)S(1)}, bf16[16,3712]{1,0:T(8,128)(2,1)S(1)}, u32[]{:S(2)}, u32[]{:S(2)}) collective-permute-start(bf16[16,3712]{1,0:T(8,128)(2,1)S(1)} %get-tuple-element.47), channel_id=1, source_target_pairs={{2,0},{3,1},{4,2},{5,3},{6,4},{7,5},{0,6},{1,7},{10,8},{11,9},{12,... | collective-permute-start | bytes 356360 | tf_op jit(solution)/shard_map/ppermute | solution.py:230
  145.1 3.4 %collective-permute-start.24 = (bf16[16,3712]{1,0:T(8,128)(2,1)S(1)}, bf16[16,3712]{1,0:T(8,128)(2,1)S(1)}, u32[]{:S(2)}, u32[]{:S(2)}) collective-permute-start(bf16[16,3712]{1,0:T(8,128)(2,1)S(1)} %get-tuple-element.48), channel_id=1, source_target_pairs={{4,0},{5,1},{6,2},{7,3},{0,4},{1,5},{2,6},{3,7},{12,8},{13,9},{14,... | collective-permute-start | bytes 356360 | tf_op jit(solution)/shard_map/ppermute | solution.py:230
  148.5 3.9 %collective-permute-start.25 = (bf16[16,3712]{1,0:T(8,128)(2,1)S(1)}, bf16[16,3712]{1,0:T(8,128)(2,1)S(1)}, u32[]{:S(2)}, u32[]{:S(2)}) collective-permute-start(bf16[16,3712]{1,0:T(8,128)(2,1)S(1)} %get-tuple-element.49), channel_id=1, source_target_pairs={{6,0},{7,1},{0,2},{1,3},{2,4},{3,5},{4,6},{5,7},{14,8},{15,9},{8,1... | collective-permute-start | bytes 356360 | tf_op jit(solution)/shard_map/ppermute | solution.py:230
  152.4 5.6 %collective-permute-done.24.refs_16_ = bf16[16,3712]{1,0:T(8,128)(2,1)S(1)} collective-permute-done((bf16[16,3712]{1,0:T(8,128)(2,1)S(1)}, bf16[16,3712]{1,0:T(8,128)(2,1)S(1)}, u32[]{:S(2)}, u32[]{:S(2)}) %collective-permute-start.24) | collective-permute-done | bytes 118816 | tf_op jit(solution)/shard_map/ppermute | solution.py:230
  159.4 1.9 %collective-permute-start.27 = (f32[32,3584]{1,0:T(8,128)S(1)}, f32[32,3584]{1,0:T(8,128)S(1)}, u32[]{:S(2)}, u32[]{:S(2)}) collective-permute-start(f32[32,3584]{1,0:T(8,128)S(1)} %get-tuple-element.54), channel_id=1, source_target_pairs={{0,1},{1,0},{2,3},{3,2},{4,5},{5,4},{6,7},{7,6},{8,9},{9,8},{10,11... | collective-permute-start | bytes 1376264 | tf_op jit(solution)/shard_map/ppermute | solution.py:221
  162.0 1.9 %collective-permute-start.26 = (bf16[8,3584]{1,0:T(8,128)(2,1)S(1)}, bf16[8,3584]{1,0:T(8,128)(2,1)S(1)}, u32[]{:S(2)}, u32[]{:S(2)}) collective-permute-start(bf16[8,3584]{1,0:T(8,128)(2,1)S(1)} %get-tuple-element.55), channel_id=1, source_target_pairs={{0,504},{8,496},{16,488},{24,480},{32,472},{40,464},{48,456},{56,4... | collective-permute-start | bytes 172040 | tf_op jit(solution)/shard_map/ppermute | solution.py:226
  163.9 12.5 %collective-permute-done.26 = bf16[8,3584]{1,0:T(8,128)(2,1)S(1)} collective-permute-done((bf16[8,3584]{1,0:T(8,128)(2,1)S(1)}, bf16[8,3584]{1,0:T(8,128)(2,1)S(1)}, u32[]{:S(2)}, u32[]{:S(2)}) %collective-permute-start.26) | collective-permute-done | bytes 57376 | tf_op jit(solution)/shard_map/ppermute | solution.py:226
  (89 shorter events, 11.7 us)
Async XLA Ops:
  0.6 77.5 %copy-start = (bf16[1,3584,128]{2,1,0:T(8,128)(2,1)S(1)}, bf16[1,3584,128]{2,1,0:T(8,128)(2,1)}, u32[]{:S(2)}) copy-start(bf16[1,3584,128]{2,1,0:T(8,128)(2,1)} %param.20) | copy-start | bytes 2752516
  0.6 1.0 copy-start.23
  3.2 29.7 %collective-permute-start = (bf16[16,3712]{1,0:T(8,128)(2,1)S(1)}, bf16[16,3712]{1,0:T(8,128)(2,1)S(1)}, u32[]{:S(2)}, u32[]{:S(2)}) collective-permute-start(bf16[16,3712]{1,0:T(8,128)(2,1)S(1)} %shard_map.139), channel_id=1, source_target_pairs={{0,504},{8,496},{16,488},{24,480},{32,472},{40,464},{48,456},{56,4... | collective-permute-start | bytes 356360 | tf_op jit(solution)/shard_map/ppermute | solution.py:226
  20.8 14.5 %collective-permute-start.5 = (bf16[16,3712]{1,0:T(8,128)(2,1)S(1)}, bf16[16,3712]{1,0:T(8,128)(2,1)S(1)}, u32[]{:S(2)}, u32[]{:S(2)}) collective-permute-start(bf16[16,3712]{1,0:T(8,128)(2,1)S(1)} %shard_map.140.refs_0_), channel_id=1, source_target_pairs={{6,0},{7,1},{0,2},{1,3},{2,4},{3,5},{4,6},{5,7},{14,8},{15,9},{8,1... | collective-permute-start | bytes 356360 | tf_op jit(solution)/shard_map/ppermute | solution.py:230
  23.7 13.5 %collective-permute-start.3 = (bf16[16,3712]{1,0:T(8,128)(2,1)S(1)}, bf16[16,3712]{1,0:T(8,128)(2,1)S(1)}, u32[]{:S(2)}, u32[]{:S(2)}) collective-permute-start(bf16[16,3712]{1,0:T(8,128)(2,1)S(1)} %shard_map.140.refs_0_), channel_id=1, source_target_pairs={{4,0},{5,1},{6,2},{7,3},{0,4},{1,5},{2,6},{3,7},{12,8},{13,9},{14,... | collective-permute-start | bytes 356360 | tf_op jit(solution)/shard_map/ppermute | solution.py:230
  27.1 13.4 %collective-permute-start.1 = (bf16[16,3712]{1,0:T(8,128)(2,1)S(1)}, bf16[16,3712]{1,0:T(8,128)(2,1)S(1)}, u32[]{:S(2)}, u32[]{:S(2)}) collective-permute-start(bf16[16,3712]{1,0:T(8,128)(2,1)S(1)} %shard_map.140.refs_0_), channel_id=1, source_target_pairs={{2,0},{3,1},{4,2},{5,3},{6,4},{7,5},{0,6},{1,7},{10,8},{11,9},{12,... | collective-permute-start | bytes 356360 | tf_op jit(solution)/shard_map/ppermute | solution.py:230
  30.9 26.5 %collective-permute-start.10 = (bf16[32,3584]{1,0:T(8,128)(2,1)}, bf16[32,3584]{1,0:T(8,128)(2,1)S(1)}, u32[]{:S(2)}, u32[]{:S(2)}) collective-permute-start(bf16[32,3584]{1,0:T(8,128)(2,1)} %bitcast.35), channel_id=1, source_target_pairs={{0,1},{1,0},{2,3},{3,2},{4,5},{5,4},{6,7},{7,6},{8,9},{9,8},{10,11... | collective-permute-start | bytes 688136 | tf_op jit(solution)/shard_map/ppermute | solution.py:221
  32.9 35.6 %collective-permute-start.7 = (bf16[3584,128]{1,0:T(8,128)(2,1)}, bf16[3584,128]{1,0:T(8,128)(2,1)S(1)}, u32[]{:S(2)}, u32[]{:S(2)}) collective-permute-start(bf16[3584,128]{1,0:T(8,128)(2,1)} %bitcast.19), channel_id=1, source_target_pairs={{0,1},{1,0},{2,3},{3,2},{4,5},{5,4},{6,7},{7,6},{8,9},{9,8},{10,11... | collective-permute-start | bytes 2752520 | tf_op jit(solution)/shard_map/ppermute | solution.py:221
  35.3 35.4 %collective-permute-start.8 = (bf16[3584,128]{1,0:T(8,128)(2,1)}, bf16[3584,128]{1,0:T(8,128)(2,1)S(1)}, u32[]{:S(2)}, u32[]{:S(2)}) collective-permute-start(bf16[3584,128]{1,0:T(8,128)(2,1)} %bitcast.23), channel_id=1, source_target_pairs={{0,1},{1,0},{2,3},{3,2},{4,5},{5,4},{6,7},{7,6},{8,9},{9,8},{10,11... | collective-permute-start | bytes 2752520 | tf_op jit(solution)/shard_map/ppermute | solution.py:221
  37.2 35.6 %collective-permute-start.9 = (bf16[128,3584]{1,0:T(8,128)(2,1)}, bf16[128,3584]{1,0:T(8,128)(2,1)S(1)}, u32[]{:S(2)}, u32[]{:S(2)}) collective-permute-start(bf16[128,3584]{1,0:T(8,128)(2,1)} %bitcast.27), channel_id=1, source_target_pairs={{0,1},{1,0},{2,3},{3,2},{4,5},{5,4},{6,7},{7,6},{8,9},{9,8},{10,11... | collective-permute-start | bytes 2752520 | tf_op jit(solution)/shard_map/ppermute | solution.py:221
  40.5 14.2 %collective-permute-start.11 = (bf16[8,3584]{1,0:T(8,128)(2,1)S(1)}, bf16[8,3584]{1,0:T(8,128)(2,1)S(1)}, u32[]{:S(2)}, u32[]{:S(2)}) collective-permute-start(bf16[8,3584]{1,0:T(8,128)(2,1)S(1)} %slice_bitcast_fusion.1), channel_id=1, source_target_pairs={{0,504},{8,496},{16,488},{24,480},{32,472},{40,464},{48,456},{56,4... | collective-permute-start | bytes 172040 | tf_op jit(solution)/shard_map/ppermute | solution.py:226
  54.7 10.0 %collective-permute-start.6 = (bf16[16,3712]{1,0:T(8,128)(2,1)S(1)}, bf16[16,3712]{1,0:T(8,128)(2,1)S(1)}, u32[]{:S(2)}, u32[]{:S(2)}) collective-permute-start(bf16[16,3712]{1,0:T(8,128)(2,1)S(1)} %collective-permute-done.refs_1_), channel_id=1, source_target_pairs={{6,0},{7,1},{0,2},{1,3},{2,4},{3,5},{4,6},{5,7},{14,8},{15,9},{8,1... | collective-permute-start | bytes 356360 | tf_op jit(solution)/shard_map/ppermute | solution.py:230
  58.1 20.0 %collective-permute-start.4 = (bf16[16,3712]{1,0:T(8,128)(2,1)S(1)}, bf16[16,3712]{1,0:T(8,128)(2,1)S(1)}, u32[]{:S(2)}, u32[]{:S(2)}) collective-permute-start(bf16[16,3712]{1,0:T(8,128)(2,1)S(1)} %collective-permute-done.refs_1_), channel_id=1, source_target_pairs={{4,0},{5,1},{6,2},{7,3},{0,4},{1,5},{2,6},{3,7},{12,8},{13,9},{14,... | collective-permute-start | bytes 356360 | tf_op jit(solution)/shard_map/ppermute | solution.py:230
  64.8 13.3 %collective-permute-start.2 = (bf16[16,3712]{1,0:T(8,128)(2,1)S(1)}, bf16[16,3712]{1,0:T(8,128)(2,1)S(1)}, u32[]{:S(2)}, u32[]{:S(2)}) collective-permute-start(bf16[16,3712]{1,0:T(8,128)(2,1)S(1)} %collective-permute-done.refs_1_), channel_id=1, source_target_pairs={{2,0},{3,1},{4,2},{5,3},{6,4},{7,5},{0,6},{1,7},{10,8},{11,9},{12,... | collective-permute-start | bytes 356360 | tf_op jit(solution)/shard_map/ppermute | solution.py:230
  68.4 15.1 %copy-start.13 = (bf16[16,3584]{1,0:T(8,128)(2,1)}, bf16[16,3584]{1,0:T(8,128)(2,1)S(1)}, u32[]{:S(2)}) copy-start(bf16[16,3584]{1,0:T(8,128)(2,1)S(1)} %shard_map.142.refs_8_) | copy-start | bytes 344068
  68.5 16.1 %collective-permute-start.14 = (bf16[16,3584]{1,0:T(8,128)(2,1)S(1)}, bf16[16,3584]{1,0:T(8,128)(2,1)S(1)}, u32[]{:S(2)}, u32[]{:S(2)}) collective-permute-start(bf16[16,3584]{1,0:T(8,128)(2,1)S(1)} %shard_map.142.refs_8_), channel_id=1, source_target_pairs={{6,0},{7,1},{0,2},{1,3},{2,4},{3,5},{4,6},{5,7},{14,8},{15,9},{8,1... | collective-permute-start | bytes 344072 | tf_op jit(solution)/shard_map/ppermute | solution.py:230
  70.7 13.9 %collective-permute-start.13 = (bf16[16,3584]{1,0:T(8,128)(2,1)S(1)}, bf16[16,3584]{1,0:T(8,128)(2,1)S(1)}, u32[]{:S(2)}, u32[]{:S(2)}) collective-permute-start(bf16[16,3584]{1,0:T(8,128)(2,1)S(1)} %shard_map.142.refs_8_), channel_id=1, source_target_pairs={{4,0},{5,1},{6,2},{7,3},{0,4},{1,5},{2,6},{3,7},{12,8},{13,9},{14,... | collective-permute-start | bytes 344072 | tf_op jit(solution)/shard_map/ppermute | solution.py:230
  72.9 10.7 %copy-start.7 = (bf16[128,3584]{1,0:T(8,128)(2,1)}, bf16[128,3584]{1,0:T(8,128)(2,1)S(1)}, u32[]{:S(2)}) copy-start(bf16[128,3584]{1,0:T(8,128)(2,1)S(1)} %collective-permute-done.9.refs_13_.refs_11_) | copy-start | bytes 2752516
  72.9 11.7 %collective-permute-start.12 = (bf16[16,3584]{1,0:T(8,128)(2,1)S(1)}, bf16[16,3584]{1,0:T(8,128)(2,1)S(1)}, u32[]{:S(2)}, u32[]{:S(2)}) collective-permute-start(bf16[16,3584]{1,0:T(8,128)(2,1)S(1)} %shard_map.142.refs_8_), channel_id=1, source_target_pairs={{2,0},{3,1},{4,2},{5,3},{6,4},{7,5},{0,6},{1,7},{10,8},{11,9},{12,... | collective-permute-start | bytes 344072 | tf_op jit(solution)/shard_map/ppermute | solution.py:230
  78.1 5.5 %copy-start.9 = (bf16[16,3712]{1,0:T(8,128)(2,1)}, bf16[16,3712]{1,0:T(8,128)(2,1)S(1)}, u32[]{:S(2)}) copy-start(bf16[16,3712]{1,0:T(8,128)(2,1)S(1)} %collective-permute-done.4.refs_5_) | copy-start | bytes 356356
  78.1 1.2 copy-start.1
  79.3 1.2 copy-start.5
  80.5 3.1 %copy-start.11 = (bf16[16,3712]{1,0:T(8,128)(2,1)}, bf16[16,3712]{1,0:T(8,128)(2,1)S(1)}, u32[]{:S(2)}) copy-start(bf16[16,3712]{1,0:T(8,128)(2,1)S(1)} %collective-permute-done.2.refs_3_) | copy-start | bytes 356356
  80.5 18.6 %copy-start.25 = (bf16[1,8,3584]{2,1,0:T(8,128)(2,1)S(1)}, bf16[1,8,3584]{2,1,0:T(8,128)(2,1)}, u32[]{:S(2)}) copy-start(bf16[1,8,3584]{2,1,0:T(8,128)(2,1)} %param.16) | copy-start | bytes 172036
  80.5 37.8 %copy-start.32 = (bf16[1,8,3584]{2,1,0:T(8,128)(2,1)S(1)}, bf16[1,8,3584]{2,1,0:T(8,128)(2,1)}, u32[]{:S(2)}) copy-start(bf16[1,8,3584]{2,1,0:T(8,128)(2,1)} %param.19) | copy-start | bytes 172036
  83.6 1.0 copy-start.3
  84.6 47.4 %copy-start.2 = (bf16[1,3584,128]{2,1,0:T(8,128)(2,1)S(1)}, bf16[1,3584,128]{2,1,0:T(8,128)(2,1)}, u32[]{:S(2)}) copy-start(bf16[1,3584,128]{2,1,0:T(8,128)(2,1)} %param.21) | copy-start | bytes 2752516
  84.6 15.2 %copy-start.16 = (bf16[16,3584]{1,0:T(8,128)(2,1)}, bf16[16,3584]{1,0:T(8,128)(2,1)S(1)}, u32[]{:S(2)}) copy-start(bf16[16,3584]{1,0:T(8,128)(2,1)S(1)} %collective-permute-done.14.refs_11_) | copy-start | bytes 344068
  84.6 15.2 %copy-start.18 = (bf16[16,3584]{1,0:T(8,128)(2,1)}, bf16[16,3584]{1,0:T(8,128)(2,1)S(1)}, u32[]{:S(2)}) copy-start(bf16[16,3584]{1,0:T(8,128)(2,1)S(1)} %collective-permute-done.13.refs_10_) | copy-start | bytes 344068
  84.6 15.2 %copy-start.20 = (bf16[16,3584]{1,0:T(8,128)(2,1)}, bf16[16,3584]{1,0:T(8,128)(2,1)S(1)}, u32[]{:S(2)}) copy-start(bf16[16,3584]{1,0:T(8,128)(2,1)S(1)} %collective-permute-done.12.refs_9_) | copy-start | bytes 344068
  84.6 9.9 %collective-permute-start.15 = (bf16[16,3584]{1,0:T(8,128)(2,1)S(1)}, bf16[16,3584]{1,0:T(8,128)(2,1)S(1)}, u32[]{:S(2)}, u32[]{:S(2)}) collective-permute-start(bf16[16,3584]{1,0:T(8,128)(2,1)S(1)} %get-tuple-element.38), channel_id=1, source_target_pairs={{2,0},{3,1},{4,2},{5,3},{6,4},{7,5},{0,6},{1,7},{10,8},{11,9},{12,... | collective-permute-start | bytes 344072 | tf_op jit(solution)/shard_map/ppermute | solution.py:230
  87.5 10.1 %collective-permute-start.16 = (bf16[16,3584]{1,0:T(8,128)(2,1)S(1)}, bf16[16,3584]{1,0:T(8,128)(2,1)S(1)}, u32[]{:S(2)}, u32[]{:S(2)}) collective-permute-start(bf16[16,3584]{1,0:T(8,128)(2,1)S(1)} %get-tuple-element.39), channel_id=1, source_target_pairs={{4,0},{5,1},{6,2},{7,3},{0,4},{1,5},{2,6},{3,7},{12,8},{13,9},{14,... | collective-permute-start | bytes 344072 | tf_op jit(solution)/shard_map/ppermute | solution.py:230
  90.6 8.5 %collective-permute-start.17 = (bf16[16,3584]{1,0:T(8,128)(2,1)S(1)}, bf16[16,3584]{1,0:T(8,128)(2,1)S(1)}, u32[]{:S(2)}, u32[]{:S(2)}) collective-permute-start(bf16[16,3584]{1,0:T(8,128)(2,1)S(1)} %get-tuple-element.40), channel_id=1, source_target_pairs={{6,0},{7,1},{0,2},{1,3},{2,4},{3,5},{4,6},{5,7},{14,8},{15,9},{8,1... | collective-permute-start | bytes 344072 | tf_op jit(solution)/shard_map/ppermute | solution.py:230
  99.8 18.5 %collective-permute-start.18 = (bf16[16,3584]{1,0:T(8,128)(2,1)}, bf16[16,3584]{1,0:T(8,128)(2,1)}, u32[]{:S(2)}, u32[]{:S(2)}) collective-permute-start(bf16[16,3584]{1,0:T(8,128)(2,1)} %add_convert_fusion.1), channel_id=1, source_target_pairs={{8,0},{16,8},{24,16},{32,24},{40,32},{48,40},{56,48},{64,56},{72,6... | collective-permute-start | bytes 344072 | tf_op jit(solution)/shard_map/ppermute | solution.py:285
  118.3 13.7 %copy-start.10 = (bf16[16,3712]{1,0:T(8,128)(2,1)S(1)}, bf16[16,3712]{1,0:T(8,128)(2,1)}, u32[]{:S(2)}) copy-start(bf16[16,3712]{1,0:T(8,128)(2,1)} %copy-done.9) | copy-start | bytes 356356
  118.3 13.7 %copy-start.12 = (bf16[16,3712]{1,0:T(8,128)(2,1)S(1)}, bf16[16,3712]{1,0:T(8,128)(2,1)}, u32[]{:S(2)}) copy-start(bf16[16,3712]{1,0:T(8,128)(2,1)} %copy-done.11) | copy-start | bytes 356356
  119.3 21.2 %collective-permute-start.21 = (bf16[16,3584]{1,0:T(8,128)(2,1)S(1)}, bf16[16,3584]{1,0:T(8,128)(2,1)S(1)}, u32[]{:S(2)}, u32[]{:S(2)}) collective-permute-start(bf16[16,3584]{1,0:T(8,128)(2,1)S(1)} %maximum_select_fusion.refs_0_), channel_id=1, source_target_pairs={{6,0},{7,1},{0,2},{1,3},{2,4},{3,5},{4,6},{5,7},{14,8},{15,9},{8,1... | collective-permute-start | bytes 344072 | tf_op jit(solution)/shard_map/ppermute | solution.py:230
  121.2 19.3 %collective-permute-start.20 = (bf16[16,3584]{1,0:T(8,128)(2,1)S(1)}, bf16[16,3584]{1,0:T(8,128)(2,1)S(1)}, u32[]{:S(2)}, u32[]{:S(2)}) collective-permute-start(bf16[16,3584]{1,0:T(8,128)(2,1)S(1)} %maximum_select_fusion.refs_0_), channel_id=1, source_target_pairs={{4,0},{5,1},{6,2},{7,3},{0,4},{1,5},{2,6},{3,7},{12,8},{13,9},{14,... | collective-permute-start | bytes 344072 | tf_op jit(solution)/shard_map/ppermute | solution.py:230
  123.1 17.4 %collective-permute-start.19 = (bf16[16,3584]{1,0:T(8,128)(2,1)S(1)}, bf16[16,3584]{1,0:T(8,128)(2,1)S(1)}, u32[]{:S(2)}, u32[]{:S(2)}) collective-permute-start(bf16[16,3584]{1,0:T(8,128)(2,1)S(1)} %maximum_select_fusion.refs_0_), channel_id=1, source_target_pairs={{2,0},{3,1},{4,2},{5,3},{6,4},{7,5},{0,6},{1,7},{10,8},{11,9},{12,... | collective-permute-start | bytes 344072 | tf_op jit(solution)/shard_map/ppermute | solution.py:230
  128.9 3.1 %collective-permute-start.22 = (bf16[128,128]{1,0:T(8,128)(2,1)S(1)}, bf16[128,128]{1,0:T(8,128)(2,1)S(1)}, u32[]{:S(2)}, u32[]{:S(2)}) collective-permute-start(bf16[128,128]{1,0:T(8,128)(2,1)S(1)} %get-tuple-element.42), channel_id=1, source_target_pairs={{0,1},{1,0},{2,3},{3,2},{4,5},{5,4},{6,7},{7,6},{8,9},{9,8},{10,11... | collective-permute-start | bytes 98312 | tf_op jit(solution)/shard_map/ppermute | solution.py:221
  132.0 1.2 copy-start.4
  138.6 1.9 %copy-start.6 = (bf16[1,128,3584]{2,1,0:T(8,128)(2,1)S(1)}, bf16[1,128,3584]{2,1,0:T(8,128)(2,1)}, u32[]{:S(2)}) copy-start(bf16[1,128,3584]{2,1,0:T(8,128)(2,1)} %param.22) | copy-start | bytes 2752516
  138.6 1.9 %copy-start.8 = (bf16[128,3584]{1,0:T(8,128)(2,1)S(1)}, bf16[128,3584]{1,0:T(8,128)(2,1)}, u32[]{:S(2)}) copy-start(bf16[128,3584]{1,0:T(8,128)(2,1)} %copy-done.7) | copy-start | bytes 2752516
  142.7 9.8 %collective-permute-start.23 = (bf16[16,3712]{1,0:T(8,128)(2,1)S(1)}, bf16[16,3712]{1,0:T(8,128)(2,1)S(1)}, u32[]{:S(2)}, u32[]{:S(2)}) collective-permute-start(bf16[16,3712]{1,0:T(8,128)(2,1)S(1)} %get-tuple-element.47), channel_id=1, source_target_pairs={{2,0},{3,1},{4,2},{5,3},{6,4},{7,5},{0,6},{1,7},{10,8},{11,9},{12,... | collective-permute-start | bytes 356360 | tf_op jit(solution)/shard_map/ppermute | solution.py:230
  145.1 12.9 %collective-permute-start.24 = (bf16[16,3712]{1,0:T(8,128)(2,1)S(1)}, bf16[16,3712]{1,0:T(8,128)(2,1)S(1)}, u32[]{:S(2)}, u32[]{:S(2)}) collective-permute-start(bf16[16,3712]{1,0:T(8,128)(2,1)S(1)} %get-tuple-element.48), channel_id=1, source_target_pairs={{4,0},{5,1},{6,2},{7,3},{0,4},{1,5},{2,6},{3,7},{12,8},{13,9},{14,... | collective-permute-start | bytes 356360 | tf_op jit(solution)/shard_map/ppermute | solution.py:230
  148.5 9.5 %collective-permute-start.25 = (bf16[16,3712]{1,0:T(8,128)(2,1)S(1)}, bf16[16,3712]{1,0:T(8,128)(2,1)S(1)}, u32[]{:S(2)}, u32[]{:S(2)}) collective-permute-start(bf16[16,3712]{1,0:T(8,128)(2,1)S(1)} %get-tuple-element.49), channel_id=1, source_target_pairs={{6,0},{7,1},{0,2},{1,3},{2,4},{3,5},{4,6},{5,7},{14,8},{15,9},{8,1... | collective-permute-start | bytes 356360 | tf_op jit(solution)/shard_map/ppermute | solution.py:230
  159.4 17.0 %collective-permute-start.27 = (f32[32,3584]{1,0:T(8,128)S(1)}, f32[32,3584]{1,0:T(8,128)S(1)}, u32[]{:S(2)}, u32[]{:S(2)}) collective-permute-start(f32[32,3584]{1,0:T(8,128)S(1)} %get-tuple-element.54), channel_id=1, source_target_pairs={{0,1},{1,0},{2,3},{3,2},{4,5},{5,4},{6,7},{7,6},{8,9},{9,8},{10,11... | collective-permute-start | bytes 1376264 | tf_op jit(solution)/shard_map/ppermute | solution.py:221
  162.0 14.4 %collective-permute-start.26 = (bf16[8,3584]{1,0:T(8,128)(2,1)S(1)}, bf16[8,3584]{1,0:T(8,128)(2,1)S(1)}, u32[]{:S(2)}, u32[]{:S(2)}) collective-permute-start(bf16[8,3584]{1,0:T(8,128)(2,1)S(1)} %get-tuple-element.55), channel_id=1, source_target_pairs={{0,504},{8,496},{16,488},{24,480},{32,472},{40,464},{48,456},{56,4... | collective-permute-start | bytes 172040 | tf_op jit(solution)/shard_map/ppermute | solution.py:226
  (13 other events, 11.0 us)

commit v7 on v6

--- a/solution.py
+++ b/solution.py
@@ -18,7 +18,7 @@
 IDCOLS = 128
 WIDE = D + IDCOLS
 WIDTH = 512
-VMEM_LIMIT = 16 * 1024 * 1024
+VMEM_LIMIT = 48 * 1024 * 1024
 z_weight = 0.01
 balance_weight = 1.0
 F32 = jnp.float32
@@ -49,19 +49,35 @@
     return jnp.concatenate([p.astype(F32) for p in parts], axis=0).astype(BF16)
 
 
-def id_columns(ids):
+def pack_kernel(stash, grads, ids, out, held_stash, held_grads, held_ids, sems):
+    copies = [
+        pltpu.make_async_copy(src, dst, sems.at[i])
+        for i, (src, dst) in enumerate(
+            ((ids, held_ids), (stash, held_stash), (grads, held_grads))
+        )
+    ]
+    for copy in copies:
+        copy.start()
+    for copy in copies:
+        copy.wait()
     empty = jnp.full((ROWS, IDCOLS - 2 * TOPK), -1.0, F32)
-    used = jnp.concatenate([ids[0].astype(F32), ids[1].astype(F32), empty], axis=1)
-    return jnp.concatenate([used, jnp.full((ROWS, IDCOLS), -1.0, F32)], axis=0).astype(BF16)
-
-
-def pack_kernel(stash, grads, ids, out):
-    out[:, 0:D] = packed([stash[0], grads[...]])
-    out[:, D:WIDE] = id_columns(ids)
-
-
-def join_kernel(stash, other, out):
-    out[...] = packed([stash[1], other[...]])
+    used = [held_ids[0].astype(F32), held_ids[1].astype(F32), empty]
+    for i, rows in enumerate((held_stash[0], held_grads[...], held_stash[1])):
+        out[i, :, 0:D] = rows
+        out[i, :, D:WIDE] = jnp.full((ROWS, IDCOLS), -1.0, F32).astype(BF16)
+    out[0, :, D:WIDE] = jnp.concatenate(used, axis=1).astype(BF16)
+
+
+def payload(stash, grads, ids):
+    hbm = pl.BlockSpec(memory_space=pltpu.HBM)
+    return pl.pallas_call(
+        pack_kernel,
+        out_shape=jax.ShapeDtypeStruct((3, ROWS, WIDE), BF16),
+        in_specs=[hbm] * 3,
+        out_specs=pl.BlockSpec(memory_space=pltpu.VMEM),
+        scratch_shapes=[pltpu.VMEM(a.shape, a.dtype) for a in (stash, grads, ids)]
+        + [pltpu.SemaphoreType.DMA((3,))],
+    )(stash, grads, ids)
 
 
 def backward_terms(hidden, gate, up, gates, ups, outs):
@@ -82,7 +98,13 @@
 
 def first_rows(blocks, held):
     for b, block in enumerate(blocks):
-        held[16 * b : 16 * b + 16, :] = block[:, 0:D]
+        held[16 * b : 16 * b + 16, :] = packed([block[0, :, 0:D], block[1, :, 0:D]])
+
+
+def later_rows(blocks, held):
+    for k in range(CHIPS):
+        pair = [blocks[2 * k][2, :, 0:D], blocks[2 * k + 1][2, :, 0:D]]
+        held[16 * k : 16 * k + 16, :] = packed(pair)
 
 
 def first_tick_kernel(*refs):
@@ -90,7 +112,7 @@
     gates, ups, downs = weights[0:2], weights[2:4], weights[4:6]
     first_rows(blocks, held)
     for b, block in enumerate(blocks):
-        ids[16 * b : 16 * b + 16, :] = block[:, D:WIDE]
+        ids[16 * b : 16 * b + 16, :] = packed([block[0, :, D:WIDE], block[1, :, D:WIDE]])
     rows = held[...]
 
     def pick(value, offset):
@@ -105,31 +127,26 @@
 
 
 def second_tick_kernel(*refs):
-    blocks, pre, stats, weights = refs[:4], refs[4], refs[5], refs[6:12]
-    outs, held = refs[12:16], refs[16]
+    blocks, pre, weights = refs[:4], refs[4], refs[5:11]
+    outs, held = refs[11:15], refs[15]
     gates, ups, downs = weights[0:2], weights[2:4], weights[4:6]
     for k in range(CHIPS):
-        held[16 * k : 16 * k + 16, :] = blocks[k][...]
+        held[16 * k : 16 * k + 16, :] = blocks[k][:, 0:D]
     rows = held[...]
     hidden = [dot(rows, w[...], 1, 1) for w in downs]
     gate = [pre[:, 0:HID], pre[:, HID : 2 * HID]]
     up = [pre[:, 2 * HID : 3 * HID], pre[:, 3 * HID : 4 * HID]]
     backward_terms(hidden, gate, up, gates, ups, outs)
-    for k in range(1, CHIPS):
-        outs[k][:, D:WIDE] = stats[...]
 
 
 def forward_kernel(*refs):
-    blocks, second, other_ids = refs[0:8], refs[8:12], refs[12]
-    weights, routers = refs[13:17], refs[17:19]
-    pre, expo_ref, share_ref, stats_ref = refs[19:23]
-    held0, held1, ids_ref = refs[23:26]
+    blocks, own_ids, other_ids = refs[0:8], refs[8], refs[9]
+    weights, routers = refs[10:14], refs[14:16]
+    pre, expo_ref, share_ref, stats_ref = refs[16:20]
+    held0, held1 = refs[20:22]
     member = lax.axis_index("expert")
     first_rows(blocks, held0)
-    for b, block in enumerate(blocks):
-        ids_ref[16 * b : 16 * b + 16, :] = block[:, D:WIDE].astype(F32)
-    for k in range(CHIPS):
-        held1[16 * k : 16 * k + 16, :] = second[k][...]
+    later_rows(blocks, held1)
     rows0, rows1 = held0[...], held1[...]
     for i, w in enumerate(weights):
         pre[:, HID * i : HID * i + HID] = dot(rows1, w[...], 1, 0)
@@ -140,7 +157,7 @@
         ],
         axis=1,
     )
-    ids = [ids_ref[...].T, other_ids[...].astype(F32).T]
+    ids = [own_ids[...].astype(F32).T, other_ids[...].astype(F32).T]
     row = lax.broadcasted_iota(jnp.int32, (2 * OWN, 128), 0)
     column = lax.broadcasted_iota(jnp.int32, (2 * OWN, 128), 1)
     own = row + OWN * member
@@ -177,14 +194,13 @@
 
 
 def router_kernel(*refs):
-    blocks, second, expo_ref, share_ref, parts = refs[0:8], refs[8:12], refs[12], refs[13], refs[14:18]
-    own_out, other_out, held0, held1 = refs[18:22]
+    blocks, expo_ref, share_ref, parts = refs[0:8], refs[8], refs[9], refs[10:14]
+    own_out, other_out, held0, held1 = refs[14:18]
     first_rows(blocks, held0)
-    for k in range(CHIPS):
-        held1[16 * k : 16 * k + 16, :] = second[k][...]
+    later_rows(blocks, held1)
     stats = []
     for k, part in enumerate(parts):
-        value = (part[...] if k == 0 else part[:, D:WIDE]).astype(F32)
+        value = part[:, D:WIDE].astype(F32)
         wide = [
             jnp.concatenate(
                 [pltpu.roll(value, 32 * k, 1)[i : i + 1], pltpu.roll(value, 16 * k, 1)[i + 7 : i + 8]],
@@ -217,6 +233,19 @@
         other_out[:, cols] = part[OWN:]
 
 
+def touch_kernel(value, out):
+    pass
+
+
+def passed(value, flops):
+    spec = pl.BlockSpec(memory_space=pl.ANY)
+    return pl.pallas_call(
+        touch_kernel, out_shape=jax.ShapeDtypeStruct(value.shape, value.dtype),
+        in_specs=[spec], out_specs=spec, input_output_aliases={0: 0},
+        cost_estimate=pl.CostEstimate(flops=flops, bytes_accessed=0, transcendentals=0),
+    )(value)
+
+
 def swapped(value):
     return lax.ppermute(value, "expert", [(e, e ^ 1) for e in range(8)])
 
@@ -241,7 +270,7 @@
 def emitted(grads, parts):
     total = grads.astype(F32)
     for part in parts:
-        total = total + part[:, :D].astype(F32)
+        total = total + part.astype(F32)
     return total.astype(BF16)
 
 
@@ -260,51 +289,47 @@
     top = lax.axis_size("pipe") - 1
     rows0, rows1 = pltpu.VMEM((128, D), BF16), pltpu.VMEM((64, D), BF16)
 
-    (packed_b,) = call(pack_kernel, [((16, WIDE), BF16)], [stash_b, arriving_b, ids_b])
-    block_b = mirrored(packed_b)
-    (block_a,) = call(pack_kernel, [((16, WIDE), BF16)], [stash_a, arriving_a, ids_a])
+    block_b = mirrored(payload(stash_b, arriving_b, ids_b))
+    block_a = payload(stash_a, arriving_a, ids_a)
     blocks_a = ring(block_a)
-    blocks_b = ring(block_b)
+    other_gate, other_up, other_down, other_router = (
+        swapped(weight) for weight in (w_gate, w_up, w_down, router)
+    )
+    blocks_b = ring(passed(after(block_b, other_gate, other_up, other_down), int(3e9)))
     first = [block for pair in zip(blocks_a, blocks_b) for block in pair]
-    other_gate, other_up, other_down, other_router = lax.optimization_barrier(
-        tuple(swapped(weight) for weight in (w_gate, w_up, w_down, router))
-    )
     gates, ups, downs = [w_gate, other_gate], [w_up, other_up], [w_down, other_down]
-    later_b = mirrored(after(stash_b[1], block_b))
-    (later,) = call(join_kernel, [((16, D), BF16)], [stash_a, later_b])
-    second = ring(later)
-
-    own_terms = ((16, D), F32)
+
+    sends = [((16, D), F32)] + [((16, D), BF16)] * 3
     *terms, ids = call(
-        first_tick_kernel, [own_terms] + [((16, D), BF16)] * 3 + [((128, IDCOLS), BF16)],
+        first_tick_kernel, sends + [((128, IDCOLS), BF16)],
         first + gates + ups + downs, [rows0], 2 * 128 * D * 128 * 10,
     )
-    terms = lax.optimization_barrier((*terms, *second))[:CHIPS]
-    grads = jnp.concatenate([arriving_a, block_b[8:, :D]], axis=0)
+    other_ids = swapped(ids)
+    grads = jnp.concatenate([arriving_a, block_b[1, :, :D]], axis=0)
     out = emitted(grads, returned(terms))
     moved = lax.ppermute(out, "pipe", [(i, i - 1) for i in range(1, top + 1)])
-    head = jnp.concatenate([head_a[0], head_b[0]], axis=0)
-    grads = jnp.where(section == top, head, moved)
-    all_grads = ring(grads)
-    other_ids = swapped(after(ids, out))
     pre, expo, share, stats = call(
         forward_kernel,
         [((64, 4 * HID), F32), ((2 * OWN, 256), F32), ((2 * OWN, 256), F32), ((16, IDCOLS), BF16)],
-        first + second + [other_ids] + gates + ups + [router, other_router],
-        [rows0, rows1, pltpu.VMEM((128, IDCOLS), F32)], 2 * 128 * D * 128 * 4,
-    )
+        first + [ids, other_ids] + gates + ups + [router, other_router],
+        [rows0, rows1], 2 * 128 * D * 128 * 4,
+    )
+    head = jnp.concatenate([head_a[0], head_b[0]], axis=0)
+    grads = jnp.where(section == top, head, moved)
+    gathered = ring(jnp.concatenate([grads, stats], axis=1))
     terms = call(
-        second_tick_kernel, [own_terms] + [((16, WIDE), BF16)] * 3,
-        all_grads + [pre, stats] + gates + ups + downs, [rows1], 2 * 64 * D * 128 * 6,
-    )
-    parts = returned(terms)
-    out = emitted(grads, parts)
+        second_tick_kernel, sends, gathered + [pre] + gates + ups + downs, [rows1],
+        2 * 64 * D * 128 * 6,
+    )
     own, other = call(
         router_kernel, [((OWN, D), F32)] * 2,
-        first + second + [after(expo, out), share, stats] + parts[1:], [rows0, rows1],
-        2 * 192 * D * 64,
-    )
-    return out[None, :8], mirrored(out[8:])[None], (own + swapped(other))[None]
+        first + [after(expo, *terms), share] + gathered, [rows0, rows1], 2 * 192 * D * 64,
+    )
+    router_grad = own + swapped(other)
+    parts = returned(terms)
+    out_a = emitted(grads[:ROWS], [part[:ROWS] for part in parts])
+    out_b = emitted(grads[ROWS:], [part[ROWS:] for part in parts])
+    return out_a[None], mirrored(out_b)[None], router_grad[None]
 
 
 def solution(mesh):

time: 180 us -> 159 us (0.88)
  local copies, waits for them, and re-layouts: 18.5 us -> 5.03 us
  waiting for transfers between devices: 47.5 us -> 38.5 us
  Pallas kernels: 7.63 us -> 16.4 us
  starting transfers between devices: 100 us -> 92.4 us
    unnamed x67 -> x37, local copies, waits for them, and re-layouts: 17 us -> 4.4 us
    ppermute x1, waiting for transfers between devices: 16.5 us -> 5.44 us  [shards(): moved = lax.ppermute(out, 'pipe', [(i, i - 1) for i in range(1, top + 1)])]
    ppermute x18 -> x15, waiting for transfers between devices: 10.2 us -> 20.1 us  [from_chip(): lax.ppermute(value, 'expert', [((e + 2 * k) % 8, e) for e in range(8)])]
    ppermute x3 -> x2, waiting for transfers between devices: 19.6 us -> 11.8 us  [mirrored(): lax.ppermute(value, 'pipe', [(i, count - 1 - i) for i in range(count)])]
    ppermute x18 -> x15, starting transfers between devices: 61.8 us -> 55.5 us  [from_chip(): lax.ppermute(value, 'expert', [((e + 2 * k) % 8, e) for e in range(8)])]
    pallas_call x7 -> x4, Pallas kernels: 7.63 us -> 13.1 us  [call(): pl.pallas_call(body, out_shape=[jax.ShapeDtypeStruct(shape, dtype) for sh...]
    pallas_call x0 -> x3, Pallas kernels: none -> 3.36 us  [the longest x2 3.36 us: payload(): pl.pallas_call(pack_kernel, out_shape=jax.ShapeDtypeStruct((3, ROWS, WIDE...]
    ppermute x3 -> x2, starting transfers between devices: 24.2 us -> 22.1 us  [mirrored(): lax.ppermute(value, 'pipe', [(i, count - 1 - i) for i in range(count)])]
  transfers between devices with their start and end apart: 28 -> 24, of which waited for: 7 -> 11; matrix products, arithmetic and copies ran while one was open for 1% -> 2% of each run, Pallas kernels for 3% -> 4%
where the time goes in v7:
time: 159 us; the launch traced here: 158 us
  starting transfers between devices  92.4 us (58%)
  waiting for transfers between devices  38.5 us (24%)
  Pallas kernels  16.4 us (10%)
  local copies, waits for them, and re-layouts  5.03 us (3%)
  other arithmetic  4.05 us (3%)
    ppermute x15, starting transfers between devices, from_chip(): lax.ppermute(value, 'expert', [((e + 2 * k) % 8, e) for e in range(8)])  55.5 us
    ppermute x2, starting transfers between devices, mirrored(): lax.ppermute(value, 'pipe', [(i, count - 1 - i) for i in range(count)])  22.1 us
    ppermute x15, waiting for transfers between devices, from_chip(): lax.ppermute(value, 'expert', [((e + 2 * k) % 8, e) for e in range(8)])  20.1 us
    pallas_call x4, Pallas kernels, call(): pl.pallas_call(body, out_shape=[jax.ShapeDtypeStruct(shape, dtype) for sh...  13.1 us
    ppermute x6, starting transfers between devices, swapped(): return lax.ppermute(value, 'expert', [(e, e ^ 1) for e in range(8)])  12 us
    ppermute x2, waiting for transfers between devices, mirrored(): lax.ppermute(value, 'pipe', [(i, count - 1 - i) for i in range(count)])  11.8 us
    ppermute x1, waiting for transfers between devices, shards(): moved = lax.ppermute(out, 'pipe', [(i, i - 1) for i in range(1, top + 1)])  5.44 us
    unnamed x37, local copies, waits for them, and re-layouts  4.4 us
  transfers between devices with their start and end apart: 24, of which 11 were waited for; matrix products, arithmetic and copies ran while one was open for 2% of the time, Pallas kernels for 4%

profile of v7, /device:TPU:6, one launch (start us, length us, event | category | flops | bytes accessed | tf_op | source)
XLA Modules:
  0.0 157.5 jit_solution(7984435837476431971)
XLA Ops:
  0.6 1.7 %shard_map.139 = bf16[3,8,3712]{2,1,0:T(8,128)(2,1)} custom-call(bf16[2,8,3584]{2,1,0:T(8,128)(2,1)} %bitcast.32, bf16[8,3584]{1,0:T(8,128)(2,1)} %bitcast.35, s32[2,8,8]{2,1,0:T(8,128)} %bitcast.38), custom_call_target="tpu_custom_call" | custom-call | tf_op jit(solution)/shard_map/pallas_call | solution.py:73
  2.3 15.1 %collective-permute-start = (bf16[3,8,3712]{2,1,0:T(8,128)(2,1)}, bf16[3,8,3712]{2,1,0:T(8,128)(2,1)S(1)}, u32[]{:S(2)}, u32[]{:S(2)}) collective-permute-start(bf16[3,8,3712]{2,1,0:T(8,128)(2,1)} %shard_map.139), channel_id=1, source_target_pairs={{0,504},{8,496},{16,488},{24,480},{32,472},{40,464},{48,456},{56,4... | collective-permute-start | bytes 534536 | tf_op jit(solution)/shard_map/ppermute | solution.py:255
  17.4 1.9 %collective-permute-start.1 = (bf16[3584,128]{1,0:T(8,128)(2,1)}, bf16[3584,128]{1,0:T(8,128)(2,1)S(1)}, u32[]{:S(2)}, u32[]{:S(2)}) collective-permute-start(bf16[3584,128]{1,0:T(8,128)(2,1)} %bitcast.19), channel_id=1, source_target_pairs={{0,1},{1,0},{2,3},{3,2},{4,5},{5,4},{6,7},{7,6},{8,9},{9,8},{10,11... | collective-permute-start | bytes 2752520 | tf_op jit(solution)/shard_map/ppermute | solution.py:250
  19.3 2.4 %collective-permute-start.2 = (bf16[3584,128]{1,0:T(8,128)(2,1)}, bf16[3584,128]{1,0:T(8,128)(2,1)}, u32[]{:S(2)}, u32[]{:S(2)}) collective-permute-start(bf16[3584,128]{1,0:T(8,128)(2,1)} %bitcast.23), channel_id=1, source_target_pairs={{0,1},{1,0},{2,3},{3,2},{4,5},{5,4},{6,7},{7,6},{8,9},{9,8},{10,11... | collective-permute-start | bytes 2752520 | tf_op jit(solution)/shard_map/ppermute | solution.py:250
  21.8 1.9 %collective-permute-start.3 = (bf16[128,3584]{1,0:T(8,128)(2,1)}, bf16[128,3584]{1,0:T(8,128)(2,1)}, u32[]{:S(2)}, u32[]{:S(2)}) collective-permute-start(bf16[128,3584]{1,0:T(8,128)(2,1)} %bitcast.27), channel_id=1, source_target_pairs={{0,1},{1,0},{2,3},{3,2},{4,5},{5,4},{6,7},{7,6},{8,9},{9,8},{10,11... | collective-permute-start | bytes 2752520 | tf_op jit(solution)/shard_map/ppermute | solution.py:250
  23.7 1.7 %shard_map.140.refs_0_ = bf16[3,8,3712]{2,1,0:T(8,128)(2,1)} custom-call(bf16[2,8,3584]{2,1,0:T(8,128)(2,1)} %bitcast.33, bf16[8,3584]{1,0:T(8,128)(2,1)} %bitcast.30, s32[2,8,8]{2,1,0:T(8,128)} %bitcast.39), custom_call_target="tpu_custom_call" | custom-call | tf_op jit(solution)/shard_map/pallas_call | solution.py:73
  25.4 2.9 %collective-permute-start.8 = (bf16[3,8,3712]{2,1,0:T(8,128)(2,1)}, bf16[3,8,3712]{2,1,0:T(8,128)(2,1)S(1)}, u32[]{:S(2)}, u32[]{:S(2)}) collective-permute-start(bf16[3,8,3712]{2,1,0:T(8,128)(2,1)} %shard_map.140.refs_0_), channel_id=1, source_target_pairs={{6,0},{7,1},{0,2},{1,3},{2,4},{3,5},{4,6},{5,7},{14,8},{15,9},{8,1... | collective-permute-start | bytes 534536 | tf_op jit(solution)/shard_map/ppermute | solution.py:259
  28.3 4.6 %collective-permute-done.value = bf16[3,8,3712]{2,1,0:T(8,128)(2,1)S(1)} collective-permute-done((bf16[3,8,3712]{2,1,0:T(8,128)(2,1)}, bf16[3,8,3712]{2,1,0:T(8,128)(2,1)S(1)}, u32[]{:S(2)}, u32[]{:S(2)}) %collective-permute-start) | collective-permute-done | bytes 178208 | tf_op jit(solution)/shard_map/ppermute | solution.py:255
  33.0 1.9 %collective-permute-start.6 = (bf16[3,8,3712]{2,1,0:T(8,128)(2,1)}, bf16[3,8,3712]{2,1,0:T(8,128)(2,1)S(1)}, u32[]{:S(2)}, u32[]{:S(2)}) collective-permute-start(bf16[3,8,3712]{2,1,0:T(8,128)(2,1)} %shard_map.140.refs_0_), channel_id=1, source_target_pairs={{4,0},{5,1},{6,2},{7,3},{0,4},{1,5},{2,6},{3,7},{12,8},{13,9},{14,... | collective-permute-start | bytes 534536 | tf_op jit(solution)/shard_map/ppermute | solution.py:259
  35.5 4.7 %collective-permute-start.4 = (bf16[3,8,3712]{2,1,0:T(8,128)(2,1)}, bf16[3,8,3712]{2,1,0:T(8,128)(2,1)}, u32[]{:S(2)}, u32[]{:S(2)}) collective-permute-start(bf16[3,8,3712]{2,1,0:T(8,128)(2,1)} %shard_map.140.refs_0_), channel_id=1, source_target_pairs={{2,0},{3,1},{4,2},{5,3},{6,4},{7,5},{0,6},{1,7},{10,8},{11,9},{12,... | collective-permute-start | bytes 534536 | tf_op jit(solution)/shard_map/ppermute | solution.py:259
  40.3 2.5 %collective-permute-start.9 = (bf16[3,8,3712]{2,1,0:T(8,128)(2,1)}, bf16[3,8,3712]{2,1,0:T(8,128)(2,1)S(1)}, u32[]{:S(2)}, u32[]{:S(2)}) collective-permute-start(bf16[3,8,3712]{2,1,0:T(8,128)(2,1)} %shard_map.141.refs_1_), channel_id=1, source_target_pairs={{6,0},{7,1},{0,2},{1,3},{2,4},{3,5},{4,6},{5,7},{14,8},{15,9},{8,1... | collective-permute-start | bytes 534536 | tf_op jit(solution)/shard_map/ppermute | solution.py:259
  42.7 3.6 %collective-permute-start.7 = (bf16[3,8,3712]{2,1,0:T(8,128)(2,1)}, bf16[3,8,3712]{2,1,0:T(8,128)(2,1)S(1)}, u32[]{:S(2)}, u32[]{:S(2)}) collective-permute-start(bf16[3,8,3712]{2,1,0:T(8,128)(2,1)} %shard_map.141.refs_1_), channel_id=1, source_target_pairs={{4,0},{5,1},{6,2},{7,3},{0,4},{1,5},{2,6},{3,7},{12,8},{13,9},{14,... | collective-permute-start | bytes 534536 | tf_op jit(solution)/shard_map/ppermute | solution.py:259
  46.4 4.6 %collective-permute-start.5 = (bf16[3,8,3712]{2,1,0:T(8,128)(2,1)}, bf16[3,8,3712]{2,1,0:T(8,128)(2,1)S(1)}, u32[]{:S(2)}, u32[]{:S(2)}) collective-permute-start(bf16[3,8,3712]{2,1,0:T(8,128)(2,1)} %shard_map.141.refs_1_), channel_id=1, source_target_pairs={{2,0},{3,1},{4,2},{5,3},{6,4},{7,5},{0,6},{1,7},{10,8},{11,9},{12,... | collective-permute-start | bytes 534536 | tf_op jit(solution)/shard_map/ppermute | solution.py:259
  51.0 2.6 %collective-permute-done.4.refs_2_ = bf16[3,8,3712]{2,1,0:T(8,128)(2,1)} collective-permute-done((bf16[3,8,3712]{2,1,0:T(8,128)(2,1)}, bf16[3,8,3712]{2,1,0:T(8,128)(2,1)}, u32[]{:S(2)}, u32[]{:S(2)}) %collective-permute-start.4) | collective-permute-done | bytes 178208 | tf_op jit(solution)/shard_map/ppermute | solution.py:259
  53.6 7.5 %collective-permute-done.7.refs_5_ = bf16[3,8,3712]{2,1,0:T(8,128)(2,1)S(1)} collective-permute-done((bf16[3,8,3712]{2,1,0:T(8,128)(2,1)}, bf16[3,8,3712]{2,1,0:T(8,128)(2,1)S(1)}, u32[]{:S(2)}, u32[]{:S(2)}) %collective-permute-start.7) | collective-permute-done | bytes 178208 | tf_op jit(solution)/shard_map/ppermute | solution.py:259
  61.1 1.0 copy-done.5
  62.1 4.7 %shard_map.142 = (f32[16,3584]{1,0:T(8,128)S(1)}, bf16[16,3584]{1,0:T(8,128)(2,1)S(1)}, bf16[16,3584]{1,0:T(8,128)(2,1)S(1)}, bf16[16,3584]{1,0:T(8,128)(2,1)S(1)}, bf16[128,128]{1,0:T(8,128)(2,1)S(1)}) custom-call(bf16[3,8,3712]{2,1,0:T(8,128)(2,1)S(1)} %copy-done.3, bf16[3,8,3712]{2,1,0:T(8,128)(2,1)S(1)} %copy-done.5, ...), custom_call_target="tpu_custom_call" | custom-call | flops 1174405120 | bytes 6930432 | tf_op jit(solution)/shard_map/pallas_call | solution.py:37
  66.9 6.9 %collective-permute-start.10 = (bf16[16,3584]{1,0:T(8,128)(2,1)S(1)}, bf16[16,3584]{1,0:T(8,128)(2,1)S(1)}, u32[]{:S(2)}, u32[]{:S(2)}) collective-permute-start(bf16[16,3584]{1,0:T(8,128)(2,1)S(1)} %get-tuple-element.22), channel_id=1, source_target_pairs={{2,0},{3,1},{4,2},{5,3},{6,4},{7,5},{0,6},{1,7},{10,8},{11,9},{12,... | collective-permute-start | bytes 344072 | tf_op jit(solution)/shard_map/ppermute | solution.py:259
  73.8 2.6 %collective-permute-start.11 = (bf16[16,3584]{1,0:T(8,128)(2,1)S(1)}, bf16[16,3584]{1,0:T(8,128)(2,1)S(1)}, u32[]{:S(2)}, u32[]{:S(2)}) collective-permute-start(bf16[16,3584]{1,0:T(8,128)(2,1)S(1)} %get-tuple-element.23), channel_id=1, source_target_pairs={{4,0},{5,1},{6,2},{7,3},{0,4},{1,5},{2,6},{3,7},{12,8},{13,9},{14,... | collective-permute-start | bytes 344072 | tf_op jit(solution)/shard_map/ppermute | solution.py:259
  76.4 1.9 %collective-permute-start.12 = (bf16[16,3584]{1,0:T(8,128)(2,1)S(1)}, bf16[16,3584]{1,0:T(8,128)(2,1)S(1)}, u32[]{:S(2)}, u32[]{:S(2)}) collective-permute-start(bf16[16,3584]{1,0:T(8,128)(2,1)S(1)} %get-tuple-element.24), channel_id=1, source_target_pairs={{6,0},{7,1},{0,2},{1,3},{2,4},{3,5},{4,6},{5,7},{14,8},{15,9},{8,1... | collective-permute-start | bytes 344072 | tf_op jit(solution)/shard_map/ppermute | solution.py:259
  78.3 1.9 %collective-permute-start.15 = (bf16[32,3584]{1,0:T(8,128)(2,1)}, bf16[32,3584]{1,0:T(8,128)(2,1)}, u32[]{:S(2)}, u32[]{:S(2)}) collective-permute-start(bf16[32,3584]{1,0:T(8,128)(2,1)} %bitcast.12.refs_14_), channel_id=1, source_target_pairs={{0,1},{1,0},{2,3},{3,2},{4,5},{5,4},{6,7},{7,6},{8,9},{9,8},{10,11... | collective-permute-start | bytes 688136 | tf_op jit(solution)/shard_map/ppermute | solution.py:250
  80.3 5.0 %collective-permute-done.11 = bf16[16,3584]{1,0:T(8,128)(2,1)S(1)} collective-permute-done((bf16[16,3584]{1,0:T(8,128)(2,1)S(1)}, bf16[16,3584]{1,0:T(8,128)(2,1)S(1)}, u32[]{:S(2)}, u32[]{:S(2)}) %collective-permute-start.11) | collective-permute-done | bytes 114720 | tf_op jit(solution)/shard_map/ppermute | solution.py:259
  85.3 1.6 %add_convert_fusion = bf16[16,3584]{1,0:T(8,128)(2,1)} fusion(bf16[16,3584]{1,0:T(8,128)(2,1)S(1)} %collective-permute-done.12, bf16[16,3584]{1,0:T(8,128)(2,1)S(1)} %collective-permute-done.11, bf16[16,3584]{1,0:T(8,128)(2,1)S(1)} %collective-permute-done.10, f32[16,3584]{1,0:T(8,128)S(1)} %get-tuple-element.21, bf16[8,3584]{1,0:T(8,128)(2,1)} %slice_bitcast_fusion, ...), kind=kLoop, calls=%fused_computation.1 | loop fusion | flops 688128 | bytes 802816 | tf_op jit(solution)/shard_map/convert_element_type | solution.py:274
  86.9 2.8 %collective-permute-start.13 = (bf16[16,3584]{1,0:T(8,128)(2,1)}, bf16[16,3584]{1,0:T(8,128)(2,1)}, u32[]{:S(2)}, u32[]{:S(2)}) collective-permute-start(bf16[16,3584]{1,0:T(8,128)(2,1)} %add_convert_fusion), channel_id=1, source_target_pairs={{8,0},{16,8},{24,16},{32,24},{40,32},{48,40},{56,48},{64,56},{72,6... | collective-permute-start | bytes 344072 | tf_op jit(solution)/shard_map/ppermute | solution.py:310
  89.6 1.9 %collective-permute-start.14 = (bf16[128,128]{1,0:T(8,128)(2,1)S(1)}, bf16[128,128]{1,0:T(8,128)(2,1)S(1)}, u32[]{:S(2)}, u32[]{:S(2)}) collective-permute-start(bf16[128,128]{1,0:T(8,128)(2,1)S(1)} %get-tuple-element.25.refs_8_), channel_id=1, source_target_pairs={{0,1},{1,0},{2,3},{3,2},{4,5},{5,4},{6,7},{7,6},{8,9},{9,8},{10,11... | collective-permute-start | bytes 98312 | tf_op jit(solution)/shard_map/ppermute | solution.py:250
  91.6 1.2 collective-permute-done.14.refs_9_
  92.7 0.9 copy-done.8
  93.7 0.9 copy-done.11
  94.6 0.9 copy-done.14
  95.5 3.3 %shard_map.143 = (f32[64,512]{1,0:T(8,128)S(1)}, f32[64,256]{1,0:T(8,128)S(1)}, f32[64,256]{1,0:T(8,128)S(1)}, bf16[16,128]{1,0:T(8,128)(2,1)S(1)}) custom-call(bf16[3,8,3712]{2,1,0:T(8,128)(2,1)S(1)} %copy-done.3, bf16[3,8,3712]{2,1,0:T(8,128)(2,1)S(1)} %copy-done.6, bf16[3,8,3712]{2,1,0:T(8,128)(2,1)} %collective-permute-done.4.refs_2_, ...), custom_call_target="tpu_custom_call" | custom-call | flops 469762048 | bytes 5619712 | tf_op jit(solution)/shard_map/pallas_call | solution.py:37
  98.8 5.4 %collective-permute-done.13 = bf16[16,3584]{1,0:T(8,128)(2,1)} collective-permute-done((bf16[16,3584]{1,0:T(8,128)(2,1)}, bf16[16,3584]{1,0:T(8,128)(2,1)}, u32[]{:S(2)}, u32[]{:S(2)}) %collective-permute-start.13) | collective-permute-done | bytes 114720 | tf_op jit(solution)/shard_map/ppermute | solution.py:310
  104.3 0.9 maximum_select_fusion
  105.2 1.9 %collective-permute-start.18 = (bf16[16,3712]{1,0:T(8,128)(2,1)S(1)}, bf16[16,3712]{1,0:T(8,128)(2,1)S(1)}, u32[]{:S(2)}, u32[]{:S(2)}) collective-permute-start(bf16[16,3712]{1,0:T(8,128)(2,1)S(1)} %pad_maximum_fusion.refs_0_.refs_10_), channel_id=1, source_target_pairs={{6,0},{7,1},{0,2},{1,3},{2,4},{3,5},{4,6},{5,7},{14,8},{15,9},{8,1... | collective-permute-start | bytes 356360 | tf_op jit(solution)/shard_map/ppermute | solution.py:259
  107.1 6.4 %collective-permute-start.17 = (bf16[16,3712]{1,0:T(8,128)(2,1)S(1)}, bf16[16,3712]{1,0:T(8,128)(2,1)S(1)}, u32[]{:S(2)}, u32[]{:S(2)}) collective-permute-start(bf16[16,3712]{1,0:T(8,128)(2,1)S(1)} %pad_maximum_fusion.refs_0_.refs_10_), channel_id=1, source_target_pairs={{4,0},{5,1},{6,2},{7,3},{0,4},{1,5},{2,6},{3,7},{12,8},{13,9},{14,... | collective-permute-start | bytes 356360 | tf_op jit(solution)/shard_map/ppermute | solution.py:259
  113.5 4.8 %collective-permute-start.16 = (bf16[16,3712]{1,0:T(8,128)(2,1)S(1)}, bf16[16,3712]{1,0:T(8,128)(2,1)S(1)}, u32[]{:S(2)}, u32[]{:S(2)}) collective-permute-start(bf16[16,3712]{1,0:T(8,128)(2,1)S(1)} %pad_maximum_fusion.refs_0_.refs_10_), channel_id=1, source_target_pairs={{2,0},{3,1},{4,2},{5,3},{6,4},{7,5},{0,6},{1,7},{10,8},{11,9},{12,... | collective-permute-start | bytes 356360 | tf_op jit(solution)/shard_map/ppermute | solution.py:259
  118.9 1.8 %collective-permute-done.16.refs_1_.refs_11_ = bf16[16,3712]{1,0:T(8,128)(2,1)S(1)} collective-permute-done((bf16[16,3712]{1,0:T(8,128)(2,1)S(1)}, bf16[16,3712]{1,0:T(8,128)(2,1)S(1)}, u32[]{:S(2)}, u32[]{:S(2)}) %collective-permute-start.16) | collective-permute-done | bytes 118816 | tf_op jit(solution)/shard_map/ppermute | solution.py:259
  120.8 3.6 %shard_map.144 = (f32[16,3584]{1,0:T(8,128)S(1)}, bf16[16,3584]{1,0:T(8,128)(2,1)S(1)}, bf16[16,3584]{1,0:T(8,128)(2,1)S(1)}, bf16[16,3584]{1,0:T(8,128)(2,1)S(1)}) custom-call(bf16[16,3712]{1,0:T(8,128)(2,1)S(1)} %pad_maximum_fusion.refs_0_.refs_10_, bf16[16,3712]{1,0:T(8,128)(2,1)S(1)} %collective-permute-done.16.refs_1_.refs_11_, ...), custom_call_target="tpu_custom_call" | custom-call | flops 352321536 | bytes 6111232 | tf_op jit(solution)/shard_map/pallas_call | solution.py:37
  124.4 6.4 %collective-permute-start.19 = (bf16[16,3584]{1,0:T(8,128)(2,1)S(1)}, bf16[16,3584]{1,0:T(8,128)(2,1)S(1)}, u32[]{:S(2)}, u32[]{:S(2)}) collective-permute-start(bf16[16,3584]{1,0:T(8,128)(2,1)S(1)} %get-tuple-element.29), channel_id=1, source_target_pairs={{2,0},{3,1},{4,2},{5,3},{6,4},{7,5},{0,6},{1,7},{10,8},{11,9},{12,... | collective-permute-start | bytes 344072 | tf_op jit(solution)/shard_map/ppermute | solution.py:259
  130.8 1.9 %collective-permute-start.20 = (bf16[16,3584]{1,0:T(8,128)(2,1)S(1)}, bf16[16,3584]{1,0:T(8,128)(2,1)S(1)}, u32[]{:S(2)}, u32[]{:S(2)}) collective-permute-start(bf16[16,3584]{1,0:T(8,128)(2,1)S(1)} %get-tuple-element.30), channel_id=1, source_target_pairs={{4,0},{5,1},{6,2},{7,3},{0,4},{1,5},{2,6},{3,7},{12,8},{13,9},{14,... | collective-permute-start | bytes 344072 | tf_op jit(solution)/shard_map/ppermute | solution.py:259
  132.7 2.5 %collective-permute-start.21 = (bf16[16,3584]{1,0:T(8,128)(2,1)S(1)}, bf16[16,3584]{1,0:T(8,128)(2,1)S(1)}, u32[]{:S(2)}, u32[]{:S(2)}) collective-permute-start(bf16[16,3584]{1,0:T(8,128)(2,1)S(1)} %get-tuple-element.31), channel_id=1, source_target_pairs={{6,0},{7,1},{0,2},{1,3},{2,4},{3,5},{4,6},{5,7},{14,8},{15,9},{8,1... | collective-permute-start | bytes 344072 | tf_op jit(solution)/shard_map/ppermute | solution.py:259
  135.2 1.4 shard_map.145
  136.6 1.9 %collective-permute-start.23 = (f32[32,3584]{1,0:T(8,128)S(1)}, f32[32,3584]{1,0:T(8,128)S(1)}, u32[]{:S(2)}, u32[]{:S(2)}) collective-permute-start(f32[32,3584]{1,0:T(8,128)S(1)} %get-tuple-element.36), channel_id=1, source_target_pairs={{0,1},{1,0},{2,3},{3,2},{4,5},{5,4},{6,7},{7,6},{8,9},{9,8},{10,11... | collective-permute-start | bytes 1376264 | tf_op jit(solution)/shard_map/ppermute | solution.py:250
  138.5 1.0 collective-permute-done.20
  139.6 1.6 %collective-permute-done.21 = bf16[16,3584]{1,0:T(8,128)(2,1)S(1)} collective-permute-done((bf16[16,3584]{1,0:T(8,128)(2,1)S(1)}, bf16[16,3584]{1,0:T(8,128)(2,1)S(1)}, u32[]{:S(2)}, u32[]{:S(2)}) %collective-permute-start.21) | collective-permute-done | bytes 114720 | tf_op jit(solution)/shard_map/ppermute | solution.py:259
  141.2 0.7 add_convert_fusion.1
  141.9 7.0 %collective-permute-start.22 = (bf16[8,3584]{1,0:T(8,128)(2,1)S(1)}, bf16[8,3584]{1,0:T(8,128)(2,1)S(1)}, u32[]{:S(2)}, u32[]{:S(2)}) collective-permute-start(bf16[8,3584]{1,0:T(8,128)(2,1)S(1)} %get-tuple-element.37), channel_id=1, source_target_pairs={{0,504},{8,496},{16,488},{24,480},{32,472},{40,464},{48,456},{56,4... | collective-permute-start | bytes 172040 | tf_op jit(solution)/shard_map/ppermute | solution.py:255
  148.9 7.1 %collective-permute-done.22 = bf16[8,3584]{1,0:T(8,128)(2,1)S(1)} collective-permute-done((bf16[8,3584]{1,0:T(8,128)(2,1)S(1)}, bf16[8,3584]{1,0:T(8,128)(2,1)S(1)}, u32[]{:S(2)}, u32[]{:S(2)}) %collective-permute-start.22) | collective-permute-done | bytes 57376 | tf_op jit(solution)/shard_map/ppermute | solution.py:255
  156.1 0.8 add_bitcast_fusion
  (50 shorter events, 1.9 us)
Async XLA Ops:
  2.3 30.7 %collective-permute-start = (bf16[3,8,3712]{2,1,0:T(8,128)(2,1)}, bf16[3,8,3712]{2,1,0:T(8,128)(2,1)S(1)}, u32[]{:S(2)}, u32[]{:S(2)}) collective-permute-start(bf16[3,8,3712]{2,1,0:T(8,128)(2,1)} %shard_map.139), channel_id=1, source_target_pairs={{0,504},{8,496},{16,488},{24,480},{32,472},{40,464},{48,456},{56,4... | collective-permute-start | bytes 534536 | tf_op jit(solution)/shard_map/ppermute | solution.py:255
  17.4 18.1 %collective-permute-start.1 = (bf16[3584,128]{1,0:T(8,128)(2,1)}, bf16[3584,128]{1,0:T(8,128)(2,1)S(1)}, u32[]{:S(2)}, u32[]{:S(2)}) collective-permute-start(bf16[3584,128]{1,0:T(8,128)(2,1)} %bitcast.19), channel_id=1, source_target_pairs={{0,1},{1,0},{2,3},{3,2},{4,5},{5,4},{6,7},{7,6},{8,9},{9,8},{10,11... | collective-permute-start | bytes 2752520 | tf_op jit(solution)/shard_map/ppermute | solution.py:250
  19.3 20.9 %collective-permute-start.2 = (bf16[3584,128]{1,0:T(8,128)(2,1)}, bf16[3584,128]{1,0:T(8,128)(2,1)}, u32[]{:S(2)}, u32[]{:S(2)}) collective-permute-start(bf16[3584,128]{1,0:T(8,128)(2,1)} %bitcast.23), channel_id=1, source_target_pairs={{0,1},{1,0},{2,3},{3,2},{4,5},{5,4},{6,7},{7,6},{8,9},{9,8},{10,11... | collective-permute-start | bytes 2752520 | tf_op jit(solution)/shard_map/ppermute | solution.py:250
  21.8 18.5 %collective-permute-start.3 = (bf16[128,3584]{1,0:T(8,128)(2,1)}, bf16[128,3584]{1,0:T(8,128)(2,1)}, u32[]{:S(2)}, u32[]{:S(2)}) collective-permute-start(bf16[128,3584]{1,0:T(8,128)(2,1)} %bitcast.27), channel_id=1, source_target_pairs={{0,1},{1,0},{2,3},{3,2},{4,5},{5,4},{6,7},{7,6},{8,9},{9,8},{10,11... | collective-permute-start | bytes 2752520 | tf_op jit(solution)/shard_map/ppermute | solution.py:250
  25.4 21.0 %collective-permute-start.8 = (bf16[3,8,3712]{2,1,0:T(8,128)(2,1)}, bf16[3,8,3712]{2,1,0:T(8,128)(2,1)S(1)}, u32[]{:S(2)}, u32[]{:S(2)}) collective-permute-start(bf16[3,8,3712]{2,1,0:T(8,128)(2,1)} %shard_map.140.refs_0_), channel_id=1, source_target_pairs={{6,0},{7,1},{0,2},{1,3},{2,4},{3,5},{4,6},{5,7},{14,8},{15,9},{8,1... | collective-permute-start | bytes 534536 | tf_op jit(solution)/shard_map/ppermute | solution.py:259
  33.0 7.3 %copy-start.4 = (bf16[3,8,3712]{2,1,0:T(8,128)(2,1)}, bf16[3,8,3712]{2,1,0:T(8,128)(2,1)S(1)}, u32[]{:S(2)}) copy-start(bf16[3,8,3712]{2,1,0:T(8,128)(2,1)S(1)} %collective-permute-done.value) | copy-start | bytes 534532
  33.0 18.0 %collective-permute-start.6 = (bf16[3,8,3712]{2,1,0:T(8,128)(2,1)}, bf16[3,8,3712]{2,1,0:T(8,128)(2,1)S(1)}, u32[]{:S(2)}, u32[]{:S(2)}) collective-permute-start(bf16[3,8,3712]{2,1,0:T(8,128)(2,1)} %shard_map.140.refs_0_), channel_id=1, source_target_pairs={{4,0},{5,1},{6,2},{7,3},{0,4},{1,5},{2,6},{3,7},{12,8},{13,9},{14,... | collective-permute-start | bytes 534536 | tf_op jit(solution)/shard_map/ppermute | solution.py:259
  35.5 25.6 %copy-start = (bf16[1,3584,128]{2,1,0:T(8,128)(2,1)S(1)}, bf16[1,3584,128]{2,1,0:T(8,128)(2,1)}, u32[]{:S(2)}) copy-start(bf16[1,3584,128]{2,1,0:T(8,128)(2,1)} %param.20) | copy-start | bytes 2752516
  35.5 25.6 %copy-start.1 = (bf16[1,3584,128]{2,1,0:T(8,128)(2,1)S(1)}, bf16[1,3584,128]{2,1,0:T(8,128)(2,1)}, u32[]{:S(2)}) copy-start(bf16[1,3584,128]{2,1,0:T(8,128)(2,1)} %param.21) | copy-start | bytes 2752516
  35.5 25.6 %copy-start.3 = (bf16[3,8,3712]{2,1,0:T(8,128)(2,1)S(1)}, bf16[3,8,3712]{2,1,0:T(8,128)(2,1)}, u32[]{:S(2)}) copy-start(bf16[3,8,3712]{2,1,0:T(8,128)(2,1)} %shard_map.140.refs_0_) | copy-start | bytes 534532
  35.5 18.1 %collective-permute-start.4 = (bf16[3,8,3712]{2,1,0:T(8,128)(2,1)}, bf16[3,8,3712]{2,1,0:T(8,128)(2,1)}, u32[]{:S(2)}, u32[]{:S(2)}) collective-permute-start(bf16[3,8,3712]{2,1,0:T(8,128)(2,1)} %shard_map.140.refs_0_), channel_id=1, source_target_pairs={{2,0},{3,1},{4,2},{5,3},{6,4},{7,5},{0,6},{1,7},{10,8},{11,9},{12,... | collective-permute-start | bytes 534536 | tf_op jit(solution)/shard_map/ppermute | solution.py:259
  40.3 13.3 %collective-permute-start.9 = (bf16[3,8,3712]{2,1,0:T(8,128)(2,1)}, bf16[3,8,3712]{2,1,0:T(8,128)(2,1)S(1)}, u32[]{:S(2)}, u32[]{:S(2)}) collective-permute-start(bf16[3,8,3712]{2,1,0:T(8,128)(2,1)} %shard_map.141.refs_1_), channel_id=1, source_target_pairs={{6,0},{7,1},{0,2},{1,3},{2,4},{3,5},{4,6},{5,7},{14,8},{15,9},{8,1... | collective-permute-start | bytes 534536 | tf_op jit(solution)/shard_map/ppermute | solution.py:259
  42.7 18.4 %collective-permute-start.7 = (bf16[3,8,3712]{2,1,0:T(8,128)(2,1)}, bf16[3,8,3712]{2,1,0:T(8,128)(2,1)S(1)}, u32[]{:S(2)}, u32[]{:S(2)}) collective-permute-start(bf16[3,8,3712]{2,1,0:T(8,128)(2,1)} %shard_map.141.refs_1_), channel_id=1, source_target_pairs={{4,0},{5,1},{6,2},{7,3},{0,4},{1,5},{2,6},{3,7},{12,8},{13,9},{14,... | collective-permute-start | bytes 534536 | tf_op jit(solution)/shard_map/ppermute | solution.py:259
  46.4 14.7 %collective-permute-start.5 = (bf16[3,8,3712]{2,1,0:T(8,128)(2,1)}, bf16[3,8,3712]{2,1,0:T(8,128)(2,1)S(1)}, u32[]{:S(2)}, u32[]{:S(2)}) collective-permute-start(bf16[3,8,3712]{2,1,0:T(8,128)(2,1)} %shard_map.141.refs_1_), channel_id=1, source_target_pairs={{2,0},{3,1},{4,2},{5,3},{6,4},{7,5},{0,6},{1,7},{10,8},{11,9},{12,... | collective-permute-start | bytes 534536 | tf_op jit(solution)/shard_map/ppermute | solution.py:259
  53.6 13.3 %copy-start.7 = (bf16[3,8,3712]{2,1,0:T(8,128)(2,1)}, bf16[3,8,3712]{2,1,0:T(8,128)(2,1)S(1)}, u32[]{:S(2)}) copy-start(bf16[3,8,3712]{2,1,0:T(8,128)(2,1)S(1)} %collective-permute-done.9.refs_7_) | copy-start | bytes 534532
  61.1 5.8 %copy-start.10 = (bf16[3,8,3712]{2,1,0:T(8,128)(2,1)}, bf16[3,8,3712]{2,1,0:T(8,128)(2,1)S(1)}, u32[]{:S(2)}) copy-start(bf16[3,8,3712]{2,1,0:T(8,128)(2,1)S(1)} %collective-permute-done.7.refs_5_) | copy-start | bytes 534532
  61.1 1.0 copy-start.5
  62.1 4.8 %copy-start.13 = (bf16[3,8,3712]{2,1,0:T(8,128)(2,1)}, bf16[3,8,3712]{2,1,0:T(8,128)(2,1)S(1)}, u32[]{:S(2)}) copy-start(bf16[3,8,3712]{2,1,0:T(8,128)(2,1)S(1)} %collective-permute-done.5.refs_3_) | copy-start | bytes 534532
  66.9 13.4 %collective-permute-start.10 = (bf16[16,3584]{1,0:T(8,128)(2,1)S(1)}, bf16[16,3584]{1,0:T(8,128)(2,1)S(1)}, u32[]{:S(2)}, u32[]{:S(2)}) collective-permute-start(bf16[16,3584]{1,0:T(8,128)(2,1)S(1)} %get-tuple-element.22), channel_id=1, source_target_pairs={{2,0},{3,1},{4,2},{5,3},{6,4},{7,5},{0,6},{1,7},{10,8},{11,9},{12,... | collective-permute-start | bytes 344072 | tf_op jit(solution)/shard_map/ppermute | solution.py:259
  73.8 11.5 %collective-permute-start.11 = (bf16[16,3584]{1,0:T(8,128)(2,1)S(1)}, bf16[16,3584]{1,0:T(8,128)(2,1)S(1)}, u32[]{:S(2)}, u32[]{:S(2)}) collective-permute-start(bf16[16,3584]{1,0:T(8,128)(2,1)S(1)} %get-tuple-element.23), channel_id=1, source_target_pairs={{4,0},{5,1},{6,2},{7,3},{0,4},{1,5},{2,6},{3,7},{12,8},{13,9},{14,... | collective-permute-start | bytes 344072 | tf_op jit(solution)/shard_map/ppermute | solution.py:259
  76.4 8.9 %collective-permute-start.12 = (bf16[16,3584]{1,0:T(8,128)(2,1)S(1)}, bf16[16,3584]{1,0:T(8,128)(2,1)S(1)}, u32[]{:S(2)}, u32[]{:S(2)}) collective-permute-start(bf16[16,3584]{1,0:T(8,128)(2,1)S(1)} %get-tuple-element.24), channel_id=1, source_target_pairs={{6,0},{7,1},{0,2},{1,3},{2,4},{3,5},{4,6},{5,7},{14,8},{15,9},{8,1... | collective-permute-start | bytes 344072 | tf_op jit(solution)/shard_map/ppermute | solution.py:259
  78.3 13.3 %collective-permute-start.15 = (bf16[32,3584]{1,0:T(8,128)(2,1)}, bf16[32,3584]{1,0:T(8,128)(2,1)}, u32[]{:S(2)}, u32[]{:S(2)}) collective-permute-start(bf16[32,3584]{1,0:T(8,128)(2,1)} %bitcast.12.refs_14_), channel_id=1, source_target_pairs={{0,1},{1,0},{2,3},{3,2},{4,5},{5,4},{6,7},{7,6},{8,9},{9,8},{10,11... | collective-permute-start | bytes 688136 | tf_op jit(solution)/shard_map/ppermute | solution.py:250
  85.3 7.5 %copy-start.6 = (bf16[3,8,3712]{2,1,0:T(8,128)(2,1)S(1)}, bf16[3,8,3712]{2,1,0:T(8,128)(2,1)}, u32[]{:S(2)}) copy-start(bf16[3,8,3712]{2,1,0:T(8,128)(2,1)} %shard_map.141.refs_1_) | copy-start | bytes 534532
  86.9 17.4 %collective-permute-start.13 = (bf16[16,3584]{1,0:T(8,128)(2,1)}, bf16[16,3584]{1,0:T(8,128)(2,1)}, u32[]{:S(2)}, u32[]{:S(2)}) collective-permute-start(bf16[16,3584]{1,0:T(8,128)(2,1)} %add_convert_fusion), channel_id=1, source_target_pairs={{8,0},{16,8},{24,16},{32,24},{40,32},{48,40},{56,48},{64,56},{72,6... | collective-permute-start | bytes 344072 | tf_op jit(solution)/shard_map/ppermute | solution.py:310
  89.6 3.1 %collective-permute-start.14 = (bf16[128,128]{1,0:T(8,128)(2,1)S(1)}, bf16[128,128]{1,0:T(8,128)(2,1)S(1)}, u32[]{:S(2)}, u32[]{:S(2)}) collective-permute-start(bf16[128,128]{1,0:T(8,128)(2,1)S(1)} %get-tuple-element.25.refs_8_), channel_id=1, source_target_pairs={{0,1},{1,0},{2,3},{3,2},{4,5},{5,4},{6,7},{7,6},{8,9},{9,8},{10,11... | collective-permute-start | bytes 98312 | tf_op jit(solution)/shard_map/ppermute | solution.py:250
  92.7 0.9 copy-start.8
  93.7 0.9 copy-start.11
  94.6 0.9 copy-start.14
  95.5 8.7 %copy-start.16 = (bf16[1,8,3584]{2,1,0:T(8,128)(2,1)S(1)}, bf16[1,8,3584]{2,1,0:T(8,128)(2,1)}, u32[]{:S(2)}) copy-start(bf16[1,8,3584]{2,1,0:T(8,128)(2,1)} %param.19) | copy-start | bytes 172036
  95.5 8.7 %copy-start.17 = (bf16[1,8,3584]{2,1,0:T(8,128)(2,1)S(1)}, bf16[1,8,3584]{2,1,0:T(8,128)(2,1)}, u32[]{:S(2)}) copy-start(bf16[1,8,3584]{2,1,0:T(8,128)(2,1)} %param.18) | copy-start | bytes 172036
  95.5 25.2 %copy-start.2 = (bf16[1,128,3584]{2,1,0:T(8,128)(2,1)S(1)}, bf16[1,128,3584]{2,1,0:T(8,128)(2,1)}, u32[]{:S(2)}) copy-start(bf16[1,128,3584]{2,1,0:T(8,128)(2,1)} %param.22) | copy-start | bytes 2752516
  105.2 13.2 %collective-permute-start.18 = (bf16[16,3712]{1,0:T(8,128)(2,1)S(1)}, bf16[16,3712]{1,0:T(8,128)(2,1)S(1)}, u32[]{:S(2)}, u32[]{:S(2)}) collective-permute-start(bf16[16,3712]{1,0:T(8,128)(2,1)S(1)} %pad_maximum_fusion.refs_0_.refs_10_), channel_id=1, source_target_pairs={{6,0},{7,1},{0,2},{1,3},{2,4},{3,5},{4,6},{5,7},{14,8},{15,9},{8,1... | collective-permute-start | bytes 356360 | tf_op jit(solution)/shard_map/ppermute | solution.py:259
  107.1 11.8 %collective-permute-start.17 = (bf16[16,3712]{1,0:T(8,128)(2,1)S(1)}, bf16[16,3712]{1,0:T(8,128)(2,1)S(1)}, u32[]{:S(2)}, u32[]{:S(2)}) collective-permute-start(bf16[16,3712]{1,0:T(8,128)(2,1)S(1)} %pad_maximum_fusion.refs_0_.refs_10_), channel_id=1, source_target_pairs={{4,0},{5,1},{6,2},{7,3},{0,4},{1,5},{2,6},{3,7},{12,8},{13,9},{14,... | collective-permute-start | bytes 356360 | tf_op jit(solution)/shard_map/ppermute | solution.py:259
  113.5 7.2 %collective-permute-start.16 = (bf16[16,3712]{1,0:T(8,128)(2,1)S(1)}, bf16[16,3712]{1,0:T(8,128)(2,1)S(1)}, u32[]{:S(2)}, u32[]{:S(2)}) collective-permute-start(bf16[16,3712]{1,0:T(8,128)(2,1)S(1)} %pad_maximum_fusion.refs_0_.refs_10_), channel_id=1, source_target_pairs={{2,0},{3,1},{4,2},{5,3},{6,4},{7,5},{0,6},{1,7},{10,8},{11,9},{12,... | collective-permute-start | bytes 356360 | tf_op jit(solution)/shard_map/ppermute | solution.py:259
  120.8 14.4 %copy-start.9 = (bf16[3,8,3712]{2,1,0:T(8,128)(2,1)S(1)}, bf16[3,8,3712]{2,1,0:T(8,128)(2,1)}, u32[]{:S(2)}) copy-start(bf16[3,8,3712]{2,1,0:T(8,128)(2,1)} %copy-done.7) | copy-start | bytes 534532
  120.8 14.4 %copy-start.12 = (bf16[3,8,3712]{2,1,0:T(8,128)(2,1)S(1)}, bf16[3,8,3712]{2,1,0:T(8,128)(2,1)}, u32[]{:S(2)}) copy-start(bf16[3,8,3712]{2,1,0:T(8,128)(2,1)} %copy-done.10) | copy-start | bytes 534532
  120.8 14.4 %copy-start.15 = (bf16[3,8,3712]{2,1,0:T(8,128)(2,1)S(1)}, bf16[3,8,3712]{2,1,0:T(8,128)(2,1)}, u32[]{:S(2)}) copy-start(bf16[3,8,3712]{2,1,0:T(8,128)(2,1)} %copy-done.13) | copy-start | bytes 534532
  124.4 14.1 %collective-permute-start.19 = (bf16[16,3584]{1,0:T(8,128)(2,1)S(1)}, bf16[16,3584]{1,0:T(8,128)(2,1)S(1)}, u32[]{:S(2)}, u32[]{:S(2)}) collective-permute-start(bf16[16,3584]{1,0:T(8,128)(2,1)S(1)} %get-tuple-element.29), channel_id=1, source_target_pairs={{2,0},{3,1},{4,2},{5,3},{6,4},{7,5},{0,6},{1,7},{10,8},{11,9},{12,... | collective-permute-start | bytes 344072 | tf_op jit(solution)/shard_map/ppermute | solution.py:259
  130.8 8.8 %collective-permute-start.20 = (bf16[16,3584]{1,0:T(8,128)(2,1)S(1)}, bf16[16,3584]{1,0:T(8,128)(2,1)S(1)}, u32[]{:S(2)}, u32[]{:S(2)}) collective-permute-start(bf16[16,3584]{1,0:T(8,128)(2,1)S(1)} %get-tuple-element.30), channel_id=1, source_target_pairs={{4,0},{5,1},{6,2},{7,3},{0,4},{1,5},{2,6},{3,7},{12,8},{13,9},{14,... | collective-permute-start | bytes 344072 | tf_op jit(solution)/shard_map/ppermute | solution.py:259
  132.7 8.5 %collective-permute-start.21 = (bf16[16,3584]{1,0:T(8,128)(2,1)S(1)}, bf16[16,3584]{1,0:T(8,128)(2,1)S(1)}, u32[]{:S(2)}, u32[]{:S(2)}) collective-permute-start(bf16[16,3584]{1,0:T(8,128)(2,1)S(1)} %get-tuple-element.31), channel_id=1, source_target_pairs={{6,0},{7,1},{0,2},{1,3},{2,4},{3,5},{4,6},{5,7},{14,8},{15,9},{8,1... | collective-permute-start | bytes 344072 | tf_op jit(solution)/shard_map/ppermute | solution.py:259
  136.6 19.5 %collective-permute-start.23 = (f32[32,3584]{1,0:T(8,128)S(1)}, f32[32,3584]{1,0:T(8,128)S(1)}, u32[]{:S(2)}, u32[]{:S(2)}) collective-permute-start(f32[32,3584]{1,0:T(8,128)S(1)} %get-tuple-element.36), channel_id=1, source_target_pairs={{0,1},{1,0},{2,3},{3,2},{4,5},{5,4},{6,7},{7,6},{8,9},{9,8},{10,11... | collective-permute-start | bytes 1376264 | tf_op jit(solution)/shard_map/ppermute | solution.py:250
  141.9 14.2 %collective-permute-start.22 = (bf16[8,3584]{1,0:T(8,128)(2,1)S(1)}, bf16[8,3584]{1,0:T(8,128)(2,1)S(1)}, u32[]{:S(2)}, u32[]{:S(2)}) collective-permute-start(bf16[8,3584]{1,0:T(8,128)(2,1)S(1)} %get-tuple-element.37), channel_id=1, source_target_pairs={{0,504},{8,496},{16,488},{24,480},{32,472},{40,464},{48,456},{56,4... | collective-permute-start | bytes 172040 | tf_op jit(solution)/shard_map/ppermute | solution.py:255

commit v8 on v7

--- a/solution.py
+++ b/solution.py
@@ -263,6 +263,17 @@
     return [value] + [from_chip(value, k) for k in range(1, CHIPS)]
 
 
+def forwarded_ring(value):
+    up, down = from_chip(value, 1), from_chip(value, CHIPS - 1)
+    chip = lax.axis_index("expert") // 2
+    passed_on = jnp.where(chip == 1, up, jnp.where(chip == 2, down, value))
+    route = [(1, 0), (2, 3), (3, 1), (0, 2)]
+    far = lax.ppermute(
+        passed_on, "expert", [(2 * a + core, 2 * b + core) for a, b in route for core in range(2)]
+    )
+    return [value, up, far, down]
+
+
 def returned(parts):
     return [parts[0]] + [from_chip(parts[CHIPS - k], k) for k in range(1, CHIPS)]
 
@@ -291,22 +302,22 @@
 
     block_b = mirrored(payload(stash_b, arriving_b, ids_b))
     block_a = payload(stash_a, arriving_a, ids_a)
-    blocks_a = ring(block_a)
-    other_gate, other_up, other_down, other_router = (
-        swapped(weight) for weight in (w_gate, w_up, w_down, router)
-    )
-    blocks_b = ring(passed(after(block_b, other_gate, other_up, other_down), int(3e9)))
+    blocks_a = forwarded_ring(block_a)
+    other_gate, other_up, other_down = (swapped(weight) for weight in (w_gate, w_up, w_down))
+    blocks_b = forwarded_ring(passed(after(block_b, other_gate, other_up, other_down), int(3e9)))
     first = [block for pair in zip(blocks_a, blocks_b) for block in pair]
+    other_router = swapped(after(router, blocks_b[1]))
     gates, ups, downs = [w_gate, other_gate], [w_up, other_up], [w_down, other_down]
 
     sends = [((16, D), F32)] + [((16, D), BF16)] * 3
     *terms, ids = call(
         first_tick_kernel, sends + [((128, IDCOLS), BF16)],
-        first + gates + ups + downs, [rows0], 2 * 128 * D * 128 * 10,
+        [after(first[0], other_router)] + first[1:] + gates + ups + downs, [rows0],
+        2 * 128 * D * 128 * 10,
     )
     other_ids = swapped(ids)
     grads = jnp.concatenate([arriving_a, block_b[1, :, :D]], axis=0)
-    out = emitted(grads, returned(terms))
+    out = after(emitted(grads, returned(terms)), other_ids)
     moved = lax.ppermute(out, "pipe", [(i, i - 1) for i in range(1, top + 1)])
     pre, expo, share, stats = call(
         forward_kernel,

time: 159 us -> 160 us (level)
  local copies, waits for them, and re-layouts: 5.03 us -> 11.8 us
  starting transfers between devices: 92.4 us -> 88.9 us
  Pallas kernels: 16.4 us -> 13.5 us
    ppermute x15 -> x13, starting transfers between devices: 55.5 us -> 43.7 us  [from_chip(): lax.ppermute(value, 'expert', [((e + 2 * k) % 8, e) for e in range(8)])]
    unnamed x37 -> x59, local copies, waits for them, and re-layouts: 4.4 us -> 11.2 us
    ppermute x0 -> x2, starting transfers between devices: none -> 5.17 us  [forwarded_ring(): lax.ppermute(passed_on, 'expert', [(2 * a + core, 2 * b + core) for a, b...]
    ppermute x0 -> x2, waiting for transfers between devices: none -> 4.84 us  [forwarded_ring(): lax.ppermute(passed_on, 'expert', [(2 * a + core, 2 * b + core) for a, b...]
    ppermute x15 -> x13, waiting for transfers between devices: 20.1 us -> 16.2 us  [from_chip(): lax.ppermute(value, 'expert', [((e + 2 * k) % 8, e) for e in range(8)])]
    ppermute x2, waiting for transfers between devices: 11.8 us -> 8.72 us  [mirrored(): lax.ppermute(value, 'pipe', [(i, count - 1 - i) for i in range(count)])]
    ppermute x2, starting transfers between devices: 22.1 us -> 25.2 us  [mirrored(): lax.ppermute(value, 'pipe', [(i, count - 1 - i) for i in range(count)])]
    pallas_call x4, Pallas kernels: 13.1 us -> 10.2 us  [call(): pl.pallas_call(body, out_shape=[jax.ShapeDtypeStruct(shape, dtype) for sh...]
  transfers between devices with their start and end apart: 24 -> 24, of which waited for: 11 -> 11; matrix products, arithmetic and copies ran while one was open for 2% -> 2% of each run, Pallas kernels for 4% -> 3%
where the time goes in v8:
time: 160 us; the launch traced here: 157 us
  starting transfers between devices  88.9 us (56%)
  waiting for transfers between devices  37.7 us (24%)
  Pallas kernels  13.5 us (8%)
  local copies, waits for them, and re-layouts  11.8 us (7%)
  other arithmetic  4.24 us (3%)
    ppermute x13, starting transfers between devices, from_chip(): lax.ppermute(value, 'expert', [((e + 2 * k) % 8, e) for e in range(8)])  43.7 us
    ppermute x2, starting transfers between devices, mirrored(): lax.ppermute(value, 'pipe', [(i, count - 1 - i) for i in range(count)])  25.2 us
    ppermute x13, waiting for transfers between devices, from_chip(): lax.ppermute(value, 'expert', [((e + 2 * k) % 8, e) for e in range(8)])  16.2 us
    ppermute x6, starting transfers between devices, swapped(): return lax.ppermute(value, 'expert', [(e, e ^ 1) for e in range(8)])  12.1 us
    unnamed x59, local copies, waits for them, and re-layouts  11.2 us
    pallas_call x4, Pallas kernels, call(): pl.pallas_call(body, out_shape=[jax.ShapeDtypeStruct(shape, dtype) for sh...  10.2 us
    ppermute x2, waiting for transfers between devices, mirrored(): lax.ppermute(value, 'pipe', [(i, count - 1 - i) for i in range(count)])  8.72 us
    ppermute x1, waiting for transfers between devices, shards(): moved = lax.ppermute(out, 'pipe', [(i, i - 1) for i in range(1, top + 1)])  7.9 us
  transfers between devices with their start and end apart: 24, of which 11 were waited for; matrix products, arithmetic and copies ran while one was open for 2% of the time, Pallas kernels for 3%

profile of v8, /device:TPU:6, one launch (start us, length us, event | category | flops | bytes accessed | tf_op | source)
XLA Modules:
  0.0 157.3 jit_solution(15416005015170851354)
XLA Ops:
  0.6 1.7 %shard_map.139 = bf16[3,8,3712]{2,1,0:T(8,128)(2,1)} custom-call(bf16[2,8,3584]{2,1,0:T(8,128)(2,1)} %bitcast.34, bf16[8,3584]{1,0:T(8,128)(2,1)} %bitcast.37, s32[2,8,8]{2,1,0:T(8,128)} %bitcast.40), custom_call_target="tpu_custom_call" | custom-call | tf_op jit(solution)/shard_map/pallas_call | solution.py:73
  2.3 15.1 %collective-permute-start = (bf16[3,8,3712]{2,1,0:T(8,128)(2,1)}, bf16[3,8,3712]{2,1,0:T(8,128)(2,1)S(1)}, u32[]{:S(2)}, u32[]{:S(2)}) collective-permute-start(bf16[3,8,3712]{2,1,0:T(8,128)(2,1)} %shard_map.139), channel_id=1, source_target_pairs={{0,504},{8,496},{16,488},{24,480},{32,472},{40,464},{48,456},{56,4... | collective-permute-start | bytes 534536 | tf_op jit(solution)/shard_map/ppermute | solution.py:255
  17.4 1.9 %collective-permute-start.1 = (bf16[3584,128]{1,0:T(8,128)(2,1)}, bf16[3584,128]{1,0:T(8,128)(2,1)S(1)}, u32[]{:S(2)}, u32[]{:S(2)}) collective-permute-start(bf16[3584,128]{1,0:T(8,128)(2,1)} %bitcast.19), channel_id=1, source_target_pairs={{0,1},{1,0},{2,3},{3,2},{4,5},{5,4},{6,7},{7,6},{8,9},{9,8},{10,11... | collective-permute-start | bytes 2752520 | tf_op jit(solution)/shard_map/ppermute | solution.py:250
  19.4 2.4 %collective-permute-start.2 = (bf16[3584,128]{1,0:T(8,128)(2,1)}, bf16[3584,128]{1,0:T(8,128)(2,1)S(1)}, u32[]{:S(2)}, u32[]{:S(2)}) collective-permute-start(bf16[3584,128]{1,0:T(8,128)(2,1)} %bitcast.23), channel_id=1, source_target_pairs={{0,1},{1,0},{2,3},{3,2},{4,5},{5,4},{6,7},{7,6},{8,9},{9,8},{10,11... | collective-permute-start | bytes 2752520 | tf_op jit(solution)/shard_map/ppermute | solution.py:250
  21.8 1.9 %collective-permute-start.3 = (bf16[128,3584]{1,0:T(8,128)(2,1)}, bf16[128,3584]{1,0:T(8,128)(2,1)S(1)}, u32[]{:S(2)}, u32[]{:S(2)}) collective-permute-start(bf16[128,3584]{1,0:T(8,128)(2,1)} %bitcast.27), channel_id=1, source_target_pairs={{0,1},{1,0},{2,3},{3,2},{4,5},{5,4},{6,7},{7,6},{8,9},{9,8},{10,11... | collective-permute-start | bytes 2752520 | tf_op jit(solution)/shard_map/ppermute | solution.py:250
  23.7 1.7 %shard_map.140.refs_0_ = bf16[3,8,3712]{2,1,0:T(8,128)(2,1)} custom-call(bf16[2,8,3584]{2,1,0:T(8,128)(2,1)} %bitcast.35, bf16[8,3584]{1,0:T(8,128)(2,1)} %bitcast.32, s32[2,8,8]{2,1,0:T(8,128)} %bitcast.41), custom_call_target="tpu_custom_call" | custom-call | tf_op jit(solution)/shard_map/pallas_call | solution.py:73
  25.4 2.9 %collective-permute-start.7 = (bf16[3,8,3712]{2,1,0:T(8,128)(2,1)}, bf16[3,8,3712]{2,1,0:T(8,128)(2,1)S(1)}, u32[]{:S(2)}, u32[]{:S(2)}) collective-permute-start(bf16[3,8,3712]{2,1,0:T(8,128)(2,1)} %shard_map.140.refs_0_), channel_id=1, source_target_pairs={{6,0},{7,1},{0,2},{1,3},{2,4},{3,5},{4,6},{5,7},{14,8},{15,9},{8,1... | collective-permute-start | bytes 534536 | tf_op jit(solution)/shard_map/ppermute | solution.py:259
  28.4 4.6 %collective-permute-done.value = bf16[3,8,3712]{2,1,0:T(8,128)(2,1)S(1)} collective-permute-done((bf16[3,8,3712]{2,1,0:T(8,128)(2,1)}, bf16[3,8,3712]{2,1,0:T(8,128)(2,1)S(1)}, u32[]{:S(2)}, u32[]{:S(2)}) %collective-permute-start) | collective-permute-done | bytes 178208 | tf_op jit(solution)/shard_map/ppermute | solution.py:255
  33.0 4.5 %collective-permute-start.6 = (bf16[3,8,3712]{2,1,0:T(8,128)(2,1)}, bf16[3,8,3712]{2,1,0:T(8,128)(2,1)S(1)}, u32[]{:S(2)}, u32[]{:S(2)}) collective-permute-start(bf16[3,8,3712]{2,1,0:T(8,128)(2,1)} %shard_map.140.refs_0_), channel_id=1, source_target_pairs={{2,0},{3,1},{4,2},{5,3},{6,4},{7,5},{0,6},{1,7},{10,8},{11,9},{12,... | collective-permute-start | bytes 534536 | tf_op jit(solution)/shard_map/ppermute | solution.py:259
  38.2 0.9 copy-done.2
  39.1 1.0 copy-done.24
  40.1 2.0 %collective-permute-start.9 = (bf16[3,8,3712]{2,1,0:T(8,128)(2,1)}, bf16[3,8,3712]{2,1,0:T(8,128)(2,1)S(1)}, u32[]{:S(2)}, u32[]{:S(2)}) collective-permute-start(bf16[3,8,3712]{2,1,0:T(8,128)(2,1)} %shard_map.141.refs_1_), channel_id=1, source_target_pairs={{6,0},{7,1},{0,2},{1,3},{2,4},{3,5},{4,6},{5,7},{14,8},{15,9},{8,1... | collective-permute-start | bytes 534536 | tf_op jit(solution)/shard_map/ppermute | solution.py:259
  42.1 5.7 %collective-permute-start.4 = (bf16[3,8,3712]{2,1,0:T(8,128)(2,1)}, bf16[3,8,3712]{2,1,0:T(8,128)(2,1)S(1)}, u32[]{:S(2)}, u32[]{:S(2)}) collective-permute-start(bf16[3,8,3712]{2,1,0:T(8,128)(2,1)} %shard_map.141.refs_1_), channel_id=1, source_target_pairs={{2,0},{3,1},{4,2},{5,3},{6,4},{7,5},{0,6},{1,7},{10,8},{11,9},{12,... | collective-permute-start | bytes 534536 | tf_op jit(solution)/shard_map/ppermute | solution.py:259
  47.9 1.9 %collective-permute-start.8 = (bf16[3,8,3712]{2,1,0:T(8,128)(2,1)S(1)}, bf16[3,8,3712]{2,1,0:T(8,128)(2,1)S(1)}, u32[]{:S(2)}, u32[]{:S(2)}) collective-permute-start(bf16[3,8,3712]{2,1,0:T(8,128)(2,1)S(1)} %select_select_fusion.1), channel_id=1, source_target_pairs={{2,0},{3,1},{4,6},{5,7},{6,2},{7,3},{0,4},{1,5},{10,8},{11,9},{12,... | collective-permute-start | bytes 534536 | tf_op jit(solution)/shard_map/ppermute | solution.py:271
  49.9 3.9 %collective-permute-done.4.refs_3_ = bf16[3,8,3712]{2,1,0:T(8,128)(2,1)S(1)} collective-permute-done((bf16[3,8,3712]{2,1,0:T(8,128)(2,1)}, bf16[3,8,3712]{2,1,0:T(8,128)(2,1)S(1)}, u32[]{:S(2)}, u32[]{:S(2)}) %collective-permute-start.4) | collective-permute-done | bytes 178208 | tf_op jit(solution)/shard_map/ppermute | solution.py:259
  53.7 2.0 %collective-permute-start.5 = (bf16[32,3584]{1,0:T(8,128)(2,1)}, bf16[32,3584]{1,0:T(8,128)(2,1)S(1)}, u32[]{:S(2)}, u32[]{:S(2)}) collective-permute-start(bf16[32,3584]{1,0:T(8,128)(2,1)} %bitcast.30), channel_id=1, source_target_pairs={{0,1},{1,0},{2,3},{3,2},{4,5},{5,4},{6,7},{7,6},{8,9},{9,8},{10,11... | collective-permute-start | bytes 688136 | tf_op jit(solution)/shard_map/ppermute | solution.py:250
  55.8 1.0 select_select_fusion
  56.9 3.2 %collective-permute-start.10 = (bf16[3,8,3712]{2,1,0:T(8,128)(2,1)S(1)}, bf16[3,8,3712]{2,1,0:T(8,128)(2,1)S(1)}, u32[]{:S(2)}, u32[]{:S(2)}) collective-permute-start(bf16[3,8,3712]{2,1,0:T(8,128)(2,1)S(1)} %select_select_fusion), channel_id=1, source_target_pairs={{2,0},{3,1},{4,6},{5,7},{6,2},{7,3},{0,4},{1,5},{10,8},{11,9},{12,... | collective-permute-start | bytes 534536 | tf_op jit(solution)/shard_map/ppermute | solution.py:271
  60.8 4.8 %collective-permute-done.10.refs_5_ = bf16[3,8,3712]{2,1,0:T(8,128)(2,1)S(1)} collective-permute-done((bf16[3,8,3712]{2,1,0:T(8,128)(2,1)S(1)}, bf16[3,8,3712]{2,1,0:T(8,128)(2,1)S(1)}, u32[]{:S(2)}, u32[]{:S(2)}) %collective-permute-start.10) | collective-permute-done | bytes 178208 | tf_op jit(solution)/shard_map/ppermute | solution.py:271
  65.7 1.2 copy-done.3
  66.9 4.4 %shard_map.142 = (f32[16,3584]{1,0:T(8,128)S(1)}, bf16[16,3584]{1,0:T(8,128)(2,1)S(1)}, bf16[16,3584]{1,0:T(8,128)(2,1)S(1)}, bf16[16,3584]{1,0:T(8,128)(2,1)S(1)}, bf16[128,128]{1,0:T(8,128)(2,1)S(1)}) custom-call(bf16[3,8,3712]{2,1,0:T(8,128)(2,1)S(1)} %copy-done.5, bf16[3,8,3712]{2,1,0:T(8,128)(2,1)S(1)} %copy-done.8, ...), custom_call_target="tpu_custom_call" | custom-call | flops 1174405120 | bytes 6930432 | tf_op jit(solution)/shard_map/pallas_call | solution.py:37
  71.4 5.3 %collective-permute-start.11 = (bf16[16,3584]{1,0:T(8,128)(2,1)S(1)}, bf16[16,3584]{1,0:T(8,128)(2,1)S(1)}, u32[]{:S(2)}, u32[]{:S(2)}) collective-permute-start(bf16[16,3584]{1,0:T(8,128)(2,1)S(1)} %get-tuple-element.27), channel_id=1, source_target_pairs={{2,0},{3,1},{4,2},{5,3},{6,4},{7,5},{0,6},{1,7},{10,8},{11,9},{12,... | collective-permute-start | bytes 344072 | tf_op jit(solution)/shard_map/ppermute | solution.py:259
  76.7 2.2 %collective-permute-start.12 = (bf16[16,3584]{1,0:T(8,128)(2,1)S(1)}, bf16[16,3584]{1,0:T(8,128)(2,1)S(1)}, u32[]{:S(2)}, u32[]{:S(2)}) collective-permute-start(bf16[16,3584]{1,0:T(8,128)(2,1)S(1)} %get-tuple-element.28), channel_id=1, source_target_pairs={{4,0},{5,1},{6,2},{7,3},{0,4},{1,5},{2,6},{3,7},{12,8},{13,9},{14,... | collective-permute-start | bytes 344072 | tf_op jit(solution)/shard_map/ppermute | solution.py:259
  78.9 2.5 %collective-permute-start.13 = (bf16[16,3584]{1,0:T(8,128)(2,1)S(1)}, bf16[16,3584]{1,0:T(8,128)(2,1)S(1)}, u32[]{:S(2)}, u32[]{:S(2)}) collective-permute-start(bf16[16,3584]{1,0:T(8,128)(2,1)S(1)} %get-tuple-element.29), channel_id=1, source_target_pairs={{6,0},{7,1},{0,2},{1,3},{2,4},{3,5},{4,6},{5,7},{14,8},{15,9},{8,1... | collective-permute-start | bytes 344072 | tf_op jit(solution)/shard_map/ppermute | solution.py:259
  81.4 1.9 %collective-permute-start.14 = (bf16[128,128]{1,0:T(8,128)(2,1)S(1)}, bf16[128,128]{1,0:T(8,128)(2,1)S(1)}, u32[]{:S(2)}, u32[]{:S(2)}) collective-permute-start(bf16[128,128]{1,0:T(8,128)(2,1)S(1)} %get-tuple-element.30.refs_8_), channel_id=1, source_target_pairs={{0,1},{1,0},{2,3},{3,2},{4,5},{5,4},{6,7},{7,6},{8,9},{9,8},{10,11... | collective-permute-start | bytes 98312 | tf_op jit(solution)/shard_map/ppermute | solution.py:250
  83.3 4.4 %collective-permute-done.12 = bf16[16,3584]{1,0:T(8,128)(2,1)S(1)} collective-permute-done((bf16[16,3584]{1,0:T(8,128)(2,1)S(1)}, bf16[16,3584]{1,0:T(8,128)(2,1)S(1)}, u32[]{:S(2)}, u32[]{:S(2)}) %collective-permute-start.12) | collective-permute-done | bytes 114720 | tf_op jit(solution)/shard_map/ppermute | solution.py:259
  88.4 2.8 %collective-permute-start.15 = (bf16[16,3584]{1,0:T(8,128)(2,1)}, bf16[16,3584]{1,0:T(8,128)(2,1)}, u32[]{:S(2)}, u32[]{:S(2)}) collective-permute-start(bf16[16,3584]{1,0:T(8,128)(2,1)} %add_convert_fusion), channel_id=1, source_target_pairs={{8,0},{16,8},{24,16},{32,24},{40,32},{48,40},{56,48},{64,56},{72,6... | collective-permute-start | bytes 344072 | tf_op jit(solution)/shard_map/ppermute | solution.py:321
  91.2 1.2 copy-done.4
  92.4 0.9 copy-done.10
  95.1 0.9 copy-done.19
  96.1 0.9 copy-done.21
  97.0 0.9 copy-done.23
  97.9 1.9 %shard_map.143 = (f32[64,512]{1,0:T(8,128)S(1)}, f32[64,256]{1,0:T(8,128)S(1)}, f32[64,256]{1,0:T(8,128)S(1)}, bf16[16,128]{1,0:T(8,128)(2,1)S(1)}) custom-call(bf16[3,8,3712]{2,1,0:T(8,128)(2,1)S(1)} %copy-done.5, bf16[3,8,3712]{2,1,0:T(8,128)(2,1)S(1)} %copy-done.8, bf16[3,8,3712]{2,1,0:T(8,128)(2,1)S(1)} %collective-permute-done.6.refs_2_, ...), custom_call_target="tpu_custom_call" | custom-call | flops 469762048 | bytes 5619712 | tf_op jit(solution)/shard_map/pallas_call | solution.py:37
  99.8 7.9 %collective-permute-done.15 = bf16[16,3584]{1,0:T(8,128)(2,1)} collective-permute-done((bf16[16,3584]{1,0:T(8,128)(2,1)}, bf16[16,3584]{1,0:T(8,128)(2,1)}, u32[]{:S(2)}, u32[]{:S(2)}) %collective-permute-start.15) | collective-permute-done | bytes 114720 | tf_op jit(solution)/shard_map/ppermute | solution.py:321
  107.7 0.9 maximum_select_fusion
  108.7 2.0 %collective-permute-start.18 = (bf16[16,3712]{1,0:T(8,128)(2,1)S(1)}, bf16[16,3712]{1,0:T(8,128)(2,1)S(1)}, u32[]{:S(2)}, u32[]{:S(2)}) collective-permute-start(bf16[16,3712]{1,0:T(8,128)(2,1)S(1)} %pad_maximum_fusion.refs_0_.refs_10_), channel_id=1, source_target_pairs={{6,0},{7,1},{0,2},{1,3},{2,4},{3,5},{4,6},{5,7},{14,8},{15,9},{8,1... | collective-permute-start | bytes 356360 | tf_op jit(solution)/shard_map/ppermute | solution.py:259
  110.7 1.9 %collective-permute-start.17 = (bf16[16,3712]{1,0:T(8,128)(2,1)S(1)}, bf16[16,3712]{1,0:T(8,128)(2,1)S(1)}, u32[]{:S(2)}, u32[]{:S(2)}) collective-permute-start(bf16[16,3712]{1,0:T(8,128)(2,1)S(1)} %pad_maximum_fusion.refs_0_.refs_10_), channel_id=1, source_target_pairs={{4,0},{5,1},{6,2},{7,3},{0,4},{1,5},{2,6},{3,7},{12,8},{13,9},{14,... | collective-permute-start | bytes 356360 | tf_op jit(solution)/shard_map/ppermute | solution.py:259
  112.6 5.6 %collective-permute-start.16 = (bf16[16,3712]{1,0:T(8,128)(2,1)S(1)}, bf16[16,3712]{1,0:T(8,128)(2,1)S(1)}, u32[]{:S(2)}, u32[]{:S(2)}) collective-permute-start(bf16[16,3712]{1,0:T(8,128)(2,1)S(1)} %pad_maximum_fusion.refs_0_.refs_10_), channel_id=1, source_target_pairs={{2,0},{3,1},{4,2},{5,3},{6,4},{7,5},{0,6},{1,7},{10,8},{11,9},{12,... | collective-permute-start | bytes 356360 | tf_op jit(solution)/shard_map/ppermute | solution.py:259
  118.4 3.6 %collective-permute-done.17.refs_2_.refs_12_ = bf16[16,3712]{1,0:T(8,128)(2,1)S(1)} collective-permute-done((bf16[16,3712]{1,0:T(8,128)(2,1)S(1)}, bf16[16,3712]{1,0:T(8,128)(2,1)S(1)}, u32[]{:S(2)}, u32[]{:S(2)}) %collective-permute-start.17) | collective-permute-done | bytes 118816 | tf_op jit(solution)/shard_map/ppermute | solution.py:259
  122.3 3.4 %shard_map.144 = (f32[16,3584]{1,0:T(8,128)S(1)}, bf16[16,3584]{1,0:T(8,128)(2,1)S(1)}, bf16[16,3584]{1,0:T(8,128)(2,1)S(1)}, bf16[16,3584]{1,0:T(8,128)(2,1)S(1)}) custom-call(bf16[16,3712]{1,0:T(8,128)(2,1)S(1)} %pad_maximum_fusion.refs_0_.refs_10_, bf16[16,3712]{1,0:T(8,128)(2,1)S(1)} %collective-permute-done.16.refs_1_.refs_11_, ...), custom_call_target="tpu_custom_call" | custom-call | flops 352321536 | bytes 6111232 | tf_op jit(solution)/shard_map/pallas_call | solution.py:37
  125.7 4.5 %collective-permute-start.19 = (bf16[16,3584]{1,0:T(8,128)(2,1)S(1)}, bf16[16,3584]{1,0:T(8,128)(2,1)S(1)}, u32[]{:S(2)}, u32[]{:S(2)}) collective-permute-start(bf16[16,3584]{1,0:T(8,128)(2,1)S(1)} %get-tuple-element.35), channel_id=1, source_target_pairs={{2,0},{3,1},{4,2},{5,3},{6,4},{7,5},{0,6},{1,7},{10,8},{11,9},{12,... | collective-permute-start | bytes 344072 | tf_op jit(solution)/shard_map/ppermute | solution.py:259
  130.2 2.3 %collective-permute-start.20 = (bf16[16,3584]{1,0:T(8,128)(2,1)S(1)}, bf16[16,3584]{1,0:T(8,128)(2,1)S(1)}, u32[]{:S(2)}, u32[]{:S(2)}) collective-permute-start(bf16[16,3584]{1,0:T(8,128)(2,1)S(1)} %get-tuple-element.36), channel_id=1, source_target_pairs={{4,0},{5,1},{6,2},{7,3},{0,4},{1,5},{2,6},{3,7},{12,8},{13,9},{14,... | collective-permute-start | bytes 344072 | tf_op jit(solution)/shard_map/ppermute | solution.py:259
  132.5 2.1 %collective-permute-start.21 = (bf16[16,3584]{1,0:T(8,128)(2,1)S(1)}, bf16[16,3584]{1,0:T(8,128)(2,1)S(1)}, u32[]{:S(2)}, u32[]{:S(2)}) collective-permute-start(bf16[16,3584]{1,0:T(8,128)(2,1)S(1)} %get-tuple-element.37), channel_id=1, source_target_pairs={{6,0},{7,1},{0,2},{1,3},{2,4},{3,5},{4,6},{5,7},{14,8},{15,9},{8,1... | collective-permute-start | bytes 344072 | tf_op jit(solution)/shard_map/ppermute | solution.py:259
  135.1 1.9 %collective-permute-start.23 = (f32[32,3584]{1,0:T(8,128)S(1)}, f32[32,3584]{1,0:T(8,128)S(1)}, u32[]{:S(2)}, u32[]{:S(2)}) collective-permute-start(f32[32,3584]{1,0:T(8,128)S(1)} %get-tuple-element.42), channel_id=1, source_target_pairs={{0,1},{1,0},{2,3},{3,2},{4,5},{5,4},{6,7},{7,6},{8,9},{9,8},{10,11... | collective-permute-start | bytes 1376264 | tf_op jit(solution)/shard_map/ppermute | solution.py:250
  137.0 2.4 %collective-permute-done.20 = bf16[16,3584]{1,0:T(8,128)(2,1)S(1)} collective-permute-done((bf16[16,3584]{1,0:T(8,128)(2,1)S(1)}, bf16[16,3584]{1,0:T(8,128)(2,1)S(1)}, u32[]{:S(2)}, u32[]{:S(2)}) %collective-permute-start.20) | collective-permute-done | bytes 114720 | tf_op jit(solution)/shard_map/ppermute | solution.py:259
  139.4 1.5 collective-permute-done.21
  141.7 10.1 %collective-permute-start.22 = (bf16[8,3584]{1,0:T(8,128)(2,1)S(1)}, bf16[8,3584]{1,0:T(8,128)(2,1)S(1)}, u32[]{:S(2)}, u32[]{:S(2)}) collective-permute-start(bf16[8,3584]{1,0:T(8,128)(2,1)S(1)} %get-tuple-element.43), channel_id=1, source_target_pairs={{0,504},{8,496},{16,488},{24,480},{32,472},{40,464},{48,456},{56,4... | collective-permute-start | bytes 172040 | tf_op jit(solution)/shard_map/ppermute | solution.py:255
  151.7 4.1 %collective-permute-done.22 = bf16[8,3584]{1,0:T(8,128)(2,1)S(1)} collective-permute-done((bf16[8,3584]{1,0:T(8,128)(2,1)S(1)}, bf16[8,3584]{1,0:T(8,128)(2,1)S(1)}, u32[]{:S(2)}, u32[]{:S(2)}) %collective-permute-start.22) | collective-permute-done | bytes 57376 | tf_op jit(solution)/shard_map/ppermute | solution.py:255
  (74 shorter events, 7.1 us)
Async XLA Ops:
  2.3 30.7 %collective-permute-start = (bf16[3,8,3712]{2,1,0:T(8,128)(2,1)}, bf16[3,8,3712]{2,1,0:T(8,128)(2,1)S(1)}, u32[]{:S(2)}, u32[]{:S(2)}) collective-permute-start(bf16[3,8,3712]{2,1,0:T(8,128)(2,1)} %shard_map.139), channel_id=1, source_target_pairs={{0,504},{8,496},{16,488},{24,480},{32,472},{40,464},{48,456},{56,4... | collective-permute-start | bytes 534536 | tf_op jit(solution)/shard_map/ppermute | solution.py:255
  17.4 20.7 %collective-permute-start.1 = (bf16[3584,128]{1,0:T(8,128)(2,1)}, bf16[3584,128]{1,0:T(8,128)(2,1)S(1)}, u32[]{:S(2)}, u32[]{:S(2)}) collective-permute-start(bf16[3584,128]{1,0:T(8,128)(2,1)} %bitcast.19), channel_id=1, source_target_pairs={{0,1},{1,0},{2,3},{3,2},{4,5},{5,4},{6,7},{7,6},{8,9},{9,8},{10,11... | collective-permute-start | bytes 2752520 | tf_op jit(solution)/shard_map/ppermute | solution.py:250
  19.4 18.8 %collective-permute-start.2 = (bf16[3584,128]{1,0:T(8,128)(2,1)}, bf16[3584,128]{1,0:T(8,128)(2,1)S(1)}, u32[]{:S(2)}, u32[]{:S(2)}) collective-permute-start(bf16[3584,128]{1,0:T(8,128)(2,1)} %bitcast.23), channel_id=1, source_target_pairs={{0,1},{1,0},{2,3},{3,2},{4,5},{5,4},{6,7},{7,6},{8,9},{9,8},{10,11... | collective-permute-start | bytes 2752520 | tf_op jit(solution)/shard_map/ppermute | solution.py:250
  21.8 17.3 %collective-permute-start.3 = (bf16[128,3584]{1,0:T(8,128)(2,1)}, bf16[128,3584]{1,0:T(8,128)(2,1)S(1)}, u32[]{:S(2)}, u32[]{:S(2)}) collective-permute-start(bf16[128,3584]{1,0:T(8,128)(2,1)} %bitcast.27), channel_id=1, source_target_pairs={{0,1},{1,0},{2,3},{3,2},{4,5},{5,4},{6,7},{7,6},{8,9},{9,8},{10,11... | collective-permute-start | bytes 2752520 | tf_op jit(solution)/shard_map/ppermute | solution.py:250
  25.4 22.5 %collective-permute-start.7 = (bf16[3,8,3712]{2,1,0:T(8,128)(2,1)}, bf16[3,8,3712]{2,1,0:T(8,128)(2,1)S(1)}, u32[]{:S(2)}, u32[]{:S(2)}) collective-permute-start(bf16[3,8,3712]{2,1,0:T(8,128)(2,1)} %shard_map.140.refs_0_), channel_id=1, source_target_pairs={{6,0},{7,1},{0,2},{1,3},{2,4},{3,5},{4,6},{5,7},{14,8},{15,9},{8,1... | collective-permute-start | bytes 534536 | tf_op jit(solution)/shard_map/ppermute | solution.py:259
  33.0 6.1 %copy-start.7 = (bf16[3,8,3712]{2,1,0:T(8,128)(2,1)}, bf16[3,8,3712]{2,1,0:T(8,128)(2,1)S(1)}, u32[]{:S(2)}) copy-start(bf16[3,8,3712]{2,1,0:T(8,128)(2,1)S(1)} %collective-permute-done.value) | copy-start | bytes 534532
  33.0 14.9 %collective-permute-start.6 = (bf16[3,8,3712]{2,1,0:T(8,128)(2,1)}, bf16[3,8,3712]{2,1,0:T(8,128)(2,1)S(1)}, u32[]{:S(2)}, u32[]{:S(2)}) collective-permute-start(bf16[3,8,3712]{2,1,0:T(8,128)(2,1)} %shard_map.140.refs_0_), channel_id=1, source_target_pairs={{2,0},{3,1},{4,2},{5,3},{6,4},{7,5},{0,6},{1,7},{10,8},{11,9},{12,... | collective-permute-start | bytes 534536 | tf_op jit(solution)/shard_map/ppermute | solution.py:259
  38.2 9.7 %copy-start.5 = (bf16[3,8,3712]{2,1,0:T(8,128)(2,1)S(1)}, bf16[3,8,3712]{2,1,0:T(8,128)(2,1)}, u32[]{:S(2)}) copy-start(bf16[3,8,3712]{2,1,0:T(8,128)(2,1)} %shard_map.140.refs_0_) | copy-start | bytes 534532
  38.2 0.9 copy-start.2
  39.1 1.0 copy-start.24
  40.1 25.6 %copy-start.1 = (bf16[1,3584,128]{2,1,0:T(8,128)(2,1)S(1)}, bf16[1,3584,128]{2,1,0:T(8,128)(2,1)}, u32[]{:S(2)}) copy-start(bf16[1,3584,128]{2,1,0:T(8,128)(2,1)} %param.21) | copy-start | bytes 2752516
  40.1 25.6 %copy-start = (bf16[1,3584,128]{2,1,0:T(8,128)(2,1)S(1)}, bf16[1,3584,128]{2,1,0:T(8,128)(2,1)}, u32[]{:S(2)}) copy-start(bf16[1,3584,128]{2,1,0:T(8,128)(2,1)} %param.20) | copy-start | bytes 2752516
  40.1 15.7 %collective-permute-start.9 = (bf16[3,8,3712]{2,1,0:T(8,128)(2,1)}, bf16[3,8,3712]{2,1,0:T(8,128)(2,1)S(1)}, u32[]{:S(2)}, u32[]{:S(2)}) collective-permute-start(bf16[3,8,3712]{2,1,0:T(8,128)(2,1)} %shard_map.141.refs_1_), channel_id=1, source_target_pairs={{6,0},{7,1},{0,2},{1,3},{2,4},{3,5},{4,6},{5,7},{14,8},{15,9},{8,1... | collective-permute-start | bytes 534536 | tf_op jit(solution)/shard_map/ppermute | solution.py:259
  42.1 11.6 %collective-permute-start.4 = (bf16[3,8,3712]{2,1,0:T(8,128)(2,1)}, bf16[3,8,3712]{2,1,0:T(8,128)(2,1)S(1)}, u32[]{:S(2)}, u32[]{:S(2)}) collective-permute-start(bf16[3,8,3712]{2,1,0:T(8,128)(2,1)} %shard_map.141.refs_1_), channel_id=1, source_target_pairs={{2,0},{3,1},{4,2},{5,3},{6,4},{7,5},{0,6},{1,7},{10,8},{11,9},{12,... | collective-permute-start | bytes 534536 | tf_op jit(solution)/shard_map/ppermute | solution.py:259
  47.9 12.9 %collective-permute-start.8 = (bf16[3,8,3712]{2,1,0:T(8,128)(2,1)S(1)}, bf16[3,8,3712]{2,1,0:T(8,128)(2,1)S(1)}, u32[]{:S(2)}, u32[]{:S(2)}) collective-permute-start(bf16[3,8,3712]{2,1,0:T(8,128)(2,1)S(1)} %select_select_fusion.1), channel_id=1, source_target_pairs={{2,0},{3,1},{4,6},{5,7},{6,2},{7,3},{0,4},{1,5},{10,8},{11,9},{12,... | collective-permute-start | bytes 534536 | tf_op jit(solution)/shard_map/ppermute | solution.py:271
  53.7 12.0 %copy-start.12 = (bf16[3,8,3712]{2,1,0:T(8,128)(2,1)}, bf16[3,8,3712]{2,1,0:T(8,128)(2,1)S(1)}, u32[]{:S(2)}) copy-start(bf16[3,8,3712]{2,1,0:T(8,128)(2,1)S(1)} %collective-permute-done.4.refs_3_) | copy-start | bytes 534532
  53.7 12.0 %copy-start.8 = (bf16[3,8,3712]{2,1,0:T(8,128)(2,1)S(1)}, bf16[3,8,3712]{2,1,0:T(8,128)(2,1)}, u32[]{:S(2)}) copy-start(bf16[3,8,3712]{2,1,0:T(8,128)(2,1)} %shard_map.141.refs_1_) | copy-start | bytes 534532
  53.7 6.4 %collective-permute-start.5 = (bf16[32,3584]{1,0:T(8,128)(2,1)}, bf16[32,3584]{1,0:T(8,128)(2,1)S(1)}, u32[]{:S(2)}, u32[]{:S(2)}) collective-permute-start(bf16[32,3584]{1,0:T(8,128)(2,1)} %bitcast.30), channel_id=1, source_target_pairs={{0,1},{1,0},{2,3},{3,2},{4,5},{5,4},{6,7},{7,6},{8,9},{9,8},{10,11... | collective-permute-start | bytes 688136 | tf_op jit(solution)/shard_map/ppermute | solution.py:250
  55.8 9.9 %copy-start.9 = (bf16[3,8,3712]{2,1,0:T(8,128)(2,1)}, bf16[3,8,3712]{2,1,0:T(8,128)(2,1)S(1)}, u32[]{:S(2)}) copy-start(bf16[3,8,3712]{2,1,0:T(8,128)(2,1)S(1)} %collective-permute-done.9.refs_7_) | copy-start | bytes 534532
  55.8 31.9 %copy-start.25 = (bf16[8,3584]{1,0:T(8,128)(2,1)S(1)}, bf16[8,3584]{1,0:T(8,128)(2,1)}, u32[]{:S(2)}) copy-start(bf16[8,3584]{1,0:T(8,128)(2,1)} %slice_bitcast_fusion) | copy-start | bytes 172036
  55.8 31.9 %copy-start.26 = (bf16[1,8,3584]{2,1,0:T(8,128)(2,1)S(1)}, bf16[1,8,3584]{2,1,0:T(8,128)(2,1)}, u32[]{:S(2)}) copy-start(bf16[1,8,3584]{2,1,0:T(8,128)(2,1)} %param.16) | copy-start | bytes 172036
  56.9 8.8 %collective-permute-start.10 = (bf16[3,8,3712]{2,1,0:T(8,128)(2,1)S(1)}, bf16[3,8,3712]{2,1,0:T(8,128)(2,1)S(1)}, u32[]{:S(2)}, u32[]{:S(2)}) collective-permute-start(bf16[3,8,3712]{2,1,0:T(8,128)(2,1)S(1)} %select_select_fusion), channel_id=1, source_target_pairs={{2,0},{3,1},{4,6},{5,7},{6,2},{7,3},{0,4},{1,5},{10,8},{11,9},{12,... | collective-permute-start | bytes 534536 | tf_op jit(solution)/shard_map/ppermute | solution.py:271
  60.8 10.5 %copy-start.15 = (bf16[3,8,3712]{2,1,0:T(8,128)(2,1)}, bf16[3,8,3712]{2,1,0:T(8,128)(2,1)S(1)}, u32[]{:S(2)}) copy-start(bf16[3,8,3712]{2,1,0:T(8,128)(2,1)S(1)} %collective-permute-done.8.refs_4_) | copy-start | bytes 534532
  65.7 1.2 copy-start.3
  66.9 4.5 %copy-start.18 = (bf16[3,8,3712]{2,1,0:T(8,128)(2,1)}, bf16[3,8,3712]{2,1,0:T(8,128)(2,1)S(1)}, u32[]{:S(2)}) copy-start(bf16[3,8,3712]{2,1,0:T(8,128)(2,1)S(1)} %collective-permute-done.10.refs_5_) | copy-start | bytes 534532
  71.4 12.0 %collective-permute-start.11 = (bf16[16,3584]{1,0:T(8,128)(2,1)S(1)}, bf16[16,3584]{1,0:T(8,128)(2,1)S(1)}, u32[]{:S(2)}, u32[]{:S(2)}) collective-permute-start(bf16[16,3584]{1,0:T(8,128)(2,1)S(1)} %get-tuple-element.27), channel_id=1, source_target_pairs={{2,0},{3,1},{4,2},{5,3},{6,4},{7,5},{0,6},{1,7},{10,8},{11,9},{12,... | collective-permute-start | bytes 344072 | tf_op jit(solution)/shard_map/ppermute | solution.py:259
  76.7 11.0 %collective-permute-start.12 = (bf16[16,3584]{1,0:T(8,128)(2,1)S(1)}, bf16[16,3584]{1,0:T(8,128)(2,1)S(1)}, u32[]{:S(2)}, u32[]{:S(2)}) collective-permute-start(bf16[16,3584]{1,0:T(8,128)(2,1)S(1)} %get-tuple-element.28), channel_id=1, source_target_pairs={{4,0},{5,1},{6,2},{7,3},{0,4},{1,5},{2,6},{3,7},{12,8},{13,9},{14,... | collective-permute-start | bytes 344072 | tf_op jit(solution)/shard_map/ppermute | solution.py:259
  78.9 8.8 %collective-permute-start.13 = (bf16[16,3584]{1,0:T(8,128)(2,1)S(1)}, bf16[16,3584]{1,0:T(8,128)(2,1)S(1)}, u32[]{:S(2)}, u32[]{:S(2)}) collective-permute-start(bf16[16,3584]{1,0:T(8,128)(2,1)S(1)} %get-tuple-element.29), channel_id=1, source_target_pairs={{6,0},{7,1},{0,2},{1,3},{2,4},{3,5},{4,6},{5,7},{14,8},{15,9},{8,1... | collective-permute-start | bytes 344072 | tf_op jit(solution)/shard_map/ppermute | solution.py:259
  81.4 7.0 %collective-permute-start.14 = (bf16[128,128]{1,0:T(8,128)(2,1)S(1)}, bf16[128,128]{1,0:T(8,128)(2,1)S(1)}, u32[]{:S(2)}, u32[]{:S(2)}) collective-permute-start(bf16[128,128]{1,0:T(8,128)(2,1)S(1)} %get-tuple-element.30.refs_8_), channel_id=1, source_target_pairs={{0,1},{1,0},{2,3},{3,2},{4,5},{5,4},{6,7},{7,6},{8,9},{9,8},{10,11... | collective-permute-start | bytes 98312 | tf_op jit(solution)/shard_map/ppermute | solution.py:250
  88.4 19.3 %collective-permute-start.15 = (bf16[16,3584]{1,0:T(8,128)(2,1)}, bf16[16,3584]{1,0:T(8,128)(2,1)}, u32[]{:S(2)}, u32[]{:S(2)}) collective-permute-start(bf16[16,3584]{1,0:T(8,128)(2,1)} %add_convert_fusion), channel_id=1, source_target_pairs={{8,0},{16,8},{24,16},{32,24},{40,32},{48,40},{56,48},{64,56},{72,6... | collective-permute-start | bytes 344072 | tf_op jit(solution)/shard_map/ppermute | solution.py:321
  91.2 1.2 copy-start.4
  96.1 0.9 copy-start.21
  97.0 0.9 copy-start.23
  97.9 9.8 %copy-start.27 = (bf16[1,8,3584]{2,1,0:T(8,128)(2,1)S(1)}, bf16[1,8,3584]{2,1,0:T(8,128)(2,1)}, u32[]{:S(2)}) copy-start(bf16[1,8,3584]{2,1,0:T(8,128)(2,1)} %param.19) | copy-start | bytes 172036
  97.9 9.8 %copy-start.28 = (bf16[1,8,3584]{2,1,0:T(8,128)(2,1)S(1)}, bf16[1,8,3584]{2,1,0:T(8,128)(2,1)}, u32[]{:S(2)}) copy-start(bf16[1,8,3584]{2,1,0:T(8,128)(2,1)} %param.18) | copy-start | bytes 172036
  97.9 24.3 %copy-start.6 = (bf16[1,128,3584]{2,1,0:T(8,128)(2,1)S(1)}, bf16[1,128,3584]{2,1,0:T(8,128)(2,1)}, u32[]{:S(2)}) copy-start(bf16[1,128,3584]{2,1,0:T(8,128)(2,1)} %param.22) | copy-start | bytes 2752516
  108.7 9.7 %collective-permute-start.18 = (bf16[16,3712]{1,0:T(8,128)(2,1)S(1)}, bf16[16,3712]{1,0:T(8,128)(2,1)S(1)}, u32[]{:S(2)}, u32[]{:S(2)}) collective-permute-start(bf16[16,3712]{1,0:T(8,128)(2,1)S(1)} %pad_maximum_fusion.refs_0_.refs_10_), channel_id=1, source_target_pairs={{6,0},{7,1},{0,2},{1,3},{2,4},{3,5},{4,6},{5,7},{14,8},{15,9},{8,1... | collective-permute-start | bytes 356360 | tf_op jit(solution)/shard_map/ppermute | solution.py:259
  110.7 11.2 %collective-permute-start.17 = (bf16[16,3712]{1,0:T(8,128)(2,1)S(1)}, bf16[16,3712]{1,0:T(8,128)(2,1)S(1)}, u32[]{:S(2)}, u32[]{:S(2)}) collective-permute-start(bf16[16,3712]{1,0:T(8,128)(2,1)S(1)} %pad_maximum_fusion.refs_0_.refs_10_), channel_id=1, source_target_pairs={{4,0},{5,1},{6,2},{7,3},{0,4},{1,5},{2,6},{3,7},{12,8},{13,9},{14,... | collective-permute-start | bytes 356360 | tf_op jit(solution)/shard_map/ppermute | solution.py:259
  112.6 9.7 %collective-permute-start.16 = (bf16[16,3712]{1,0:T(8,128)(2,1)S(1)}, bf16[16,3712]{1,0:T(8,128)(2,1)S(1)}, u32[]{:S(2)}, u32[]{:S(2)}) collective-permute-start(bf16[16,3712]{1,0:T(8,128)(2,1)S(1)} %pad_maximum_fusion.refs_0_.refs_10_), channel_id=1, source_target_pairs={{2,0},{3,1},{4,2},{5,3},{6,4},{7,5},{0,6},{1,7},{10,8},{11,9},{12,... | collective-permute-start | bytes 356360 | tf_op jit(solution)/shard_map/ppermute | solution.py:259
  122.3 12.3 %copy-start.11 = (bf16[3,8,3712]{2,1,0:T(8,128)(2,1)S(1)}, bf16[3,8,3712]{2,1,0:T(8,128)(2,1)}, u32[]{:S(2)}) copy-start(bf16[3,8,3712]{2,1,0:T(8,128)(2,1)} %copy-done.9) | copy-start | bytes 534532
  122.3 12.3 %copy-start.14 = (bf16[3,8,3712]{2,1,0:T(8,128)(2,1)S(1)}, bf16[3,8,3712]{2,1,0:T(8,128)(2,1)}, u32[]{:S(2)}) copy-start(bf16[3,8,3712]{2,1,0:T(8,128)(2,1)} %copy-done.12) | copy-start | bytes 534532
  122.3 12.3 %copy-start.17 = (bf16[3,8,3712]{2,1,0:T(8,128)(2,1)S(1)}, bf16[3,8,3712]{2,1,0:T(8,128)(2,1)}, u32[]{:S(2)}) copy-start(bf16[3,8,3712]{2,1,0:T(8,128)(2,1)} %copy-done.15) | copy-start | bytes 534532
  122.3 12.3 %copy-start.20 = (bf16[3,8,3712]{2,1,0:T(8,128)(2,1)S(1)}, bf16[3,8,3712]{2,1,0:T(8,128)(2,1)}, u32[]{:S(2)}) copy-start(bf16[3,8,3712]{2,1,0:T(8,128)(2,1)} %copy-done.18) | copy-start | bytes 534532
  125.7 11.4 %collective-permute-start.19 = (bf16[16,3584]{1,0:T(8,128)(2,1)S(1)}, bf16[16,3584]{1,0:T(8,128)(2,1)S(1)}, u32[]{:S(2)}, u32[]{:S(2)}) collective-permute-start(bf16[16,3584]{1,0:T(8,128)(2,1)S(1)} %get-tuple-element.35), channel_id=1, source_target_pairs={{2,0},{3,1},{4,2},{5,3},{6,4},{7,5},{0,6},{1,7},{10,8},{11,9},{12,... | collective-permute-start | bytes 344072 | tf_op jit(solution)/shard_map/ppermute | solution.py:259
  130.2 9.3 %collective-permute-start.20 = (bf16[16,3584]{1,0:T(8,128)(2,1)S(1)}, bf16[16,3584]{1,0:T(8,128)(2,1)S(1)}, u32[]{:S(2)}, u32[]{:S(2)}) collective-permute-start(bf16[16,3584]{1,0:T(8,128)(2,1)S(1)} %get-tuple-element.36), channel_id=1, source_target_pairs={{4,0},{5,1},{6,2},{7,3},{0,4},{1,5},{2,6},{3,7},{12,8},{13,9},{14,... | collective-permute-start | bytes 344072 | tf_op jit(solution)/shard_map/ppermute | solution.py:259
  132.5 8.5 %collective-permute-start.21 = (bf16[16,3584]{1,0:T(8,128)(2,1)S(1)}, bf16[16,3584]{1,0:T(8,128)(2,1)S(1)}, u32[]{:S(2)}, u32[]{:S(2)}) collective-permute-start(bf16[16,3584]{1,0:T(8,128)(2,1)S(1)} %get-tuple-element.37), channel_id=1, source_target_pairs={{6,0},{7,1},{0,2},{1,3},{2,4},{3,5},{4,6},{5,7},{14,8},{15,9},{8,1... | collective-permute-start | bytes 344072 | tf_op jit(solution)/shard_map/ppermute | solution.py:259
  135.1 20.7 %collective-permute-start.23 = (f32[32,3584]{1,0:T(8,128)S(1)}, f32[32,3584]{1,0:T(8,128)S(1)}, u32[]{:S(2)}, u32[]{:S(2)}) collective-permute-start(f32[32,3584]{1,0:T(8,128)S(1)} %get-tuple-element.42), channel_id=1, source_target_pairs={{0,1},{1,0},{2,3},{3,2},{4,5},{5,4},{6,7},{7,6},{8,9},{9,8},{10,11... | collective-permute-start | bytes 1376264 | tf_op jit(solution)/shard_map/ppermute | solution.py:250
  141.7 14.2 %collective-permute-start.22 = (bf16[8,3584]{1,0:T(8,128)(2,1)S(1)}, bf16[8,3584]{1,0:T(8,128)(2,1)S(1)}, u32[]{:S(2)}, u32[]{:S(2)}) collective-permute-start(bf16[8,3584]{1,0:T(8,128)(2,1)S(1)} %get-tuple-element.43), channel_id=1, source_target_pairs={{0,504},{8,496},{16,488},{24,480},{32,472},{40,464},{48,456},{56,4... | collective-permute-start | bytes 172040 | tf_op jit(solution)/shard_map/ppermute | solution.py:255
  (5 other events, 4.4 us)

commit v9 on v7

--- a/solution.py
+++ b/solution.py
@@ -80,90 +80,112 @@
     )(stash, grads, ids)
 
 
-def backward_terms(hidden, gate, up, gates, ups, outs):
+def differentials(hidden, gate, up):
     d_gate, d_up = [], []
     for h, g, u in zip(hidden, gate, up):
         q = jax.nn.sigmoid(g)
         d_gate.append((h * u * q * (1.0 + g * (1.0 - q))).astype(BF16))
         d_up.append((h * g * q).astype(BF16))
+    return d_gate, d_up
+
+
+def terms_of(d_gate, d_up, gates, ups, cols):
+    total = dot(d_gate[0], gates[0][cols, :], 1, 1)
+    total += dot(d_gate[1], gates[1][cols, :], 1, 1)
+    total += dot(d_up[0], ups[0][cols, :], 1, 1)
+    total += dot(d_up[1], ups[1][cols, :], 1, 1)
+    return total
+
+
+def stream_rows(blocks, held):
+    for k, block in enumerate(blocks):
+        held[16 * k : 16 * k + 16, :] = packed([block[0, :, 0:D], block[1, :, 0:D]])
+    for k in range(0, CHIPS, 2):
+        pair = [blocks[k][2, :, 0:D], blocks[k + 1][2, :, 0:D]]
+        held[64 + 8 * k : 80 + 8 * k, :] = packed(pair)
+
+
+def first_tick(blocks, weights, pre, ids, held):
+    gates, ups, downs = weights[0:2], weights[2:4], weights[4:6]
+    stream_rows(blocks, held)
+    for k, block in enumerate(blocks):
+        ids[16 * k : 16 * k + 16, :] = packed([block[0, :, D:WIDE], block[1, :, D:WIDE]])
+    rows = held[...]
+
+    def pick(value, offset):
+        return jnp.concatenate(
+            [value[16 * k + offset : 16 * k + offset + 8] for k in range(CHIPS)], axis=0
+        )
+
+    values = [dot(rows, w[...], 1, 0) for w in (*gates, *ups)]
+    for i, value in enumerate(values):
+        pre[:, HID * i : HID * i + HID] = value[64:96]
+    hidden = [pick(dot(rows[0:64], w[...], 1, 1), 8) for w in downs]
+    picked = [pick(value, 0) for value in values]
+    return (*differentials(hidden, picked[0:2], picked[2:4]), gates, ups)
+
+
+def first_a_kernel(*refs):
+    blocks, weights, (terms, pre, ids, held) = refs[:4], refs[4:10], refs[10:14]
+    operands = first_tick(blocks, weights, pre, ids, held)
     for low in range(0, D, WIDTH):
         cols = pl.ds(low, WIDTH)
-        total = dot(d_gate[0], gates[0][cols, :], 1, 1)
-        total += dot(d_gate[1], gates[1][cols, :], 1, 1)
-        total += dot(d_up[0], ups[0][cols, :], 1, 1)
-        total += dot(d_up[1], ups[1][cols, :], 1, 1)
+        terms[:, cols] = terms_of(*operands, cols)
+
+
+def first_b_kernel(*refs):
+    blocks, weights, terms_a, outs, (pre, ids, held) = (
+        refs[:4], refs[4:10], refs[10], refs[11:15], refs[15:18]
+    )
+    operands = first_tick(blocks, weights, pre, ids, held)
+    for low in range(0, D, WIDTH):
+        cols = pl.ds(low, WIDTH)
+        terms_b = terms_of(*operands, cols)
         for k in range(CHIPS):
-            outs[k][:, cols] = total[16 * k : 16 * k + 16].astype(outs[k].dtype)
-
-
-def first_rows(blocks, held):
-    for b, block in enumerate(blocks):
-        held[16 * b : 16 * b + 16, :] = packed([block[0, :, 0:D], block[1, :, 0:D]])
-
-
-def later_rows(blocks, held):
-    for k in range(CHIPS):
-        pair = [blocks[2 * k][2, :, 0:D], blocks[2 * k + 1][2, :, 0:D]]
-        held[16 * k : 16 * k + 16, :] = packed(pair)
-
-
-def first_tick_kernel(*refs):
-    blocks, weights, outs, ids, held = refs[:8], refs[8:14], refs[14:18], refs[18], refs[19]
-    gates, ups, downs = weights[0:2], weights[2:4], weights[4:6]
-    first_rows(blocks, held)
-    for b, block in enumerate(blocks):
-        ids[16 * b : 16 * b + 16, :] = packed([block[0, :, D:WIDE], block[1, :, D:WIDE]])
-    rows = held[...]
-
-    def pick(value, offset):
-        return jnp.concatenate(
-            [value[16 * b + offset : 16 * b + offset + 8] for b in range(2 * CHIPS)], axis=0
-        )
-
-    gate = [pick(dot(rows, w[...], 1, 0), 0) for w in gates]
-    up = [pick(dot(rows, w[...], 1, 0), 0) for w in ups]
-    hidden = [pick(dot(rows, w[...], 1, 1), 8) for w in downs]
-    backward_terms(hidden, gate, up, gates, ups, outs)
+            both = [terms_a[8 * k : 8 * k + 8, cols], terms_b[8 * k : 8 * k + 8]]
+            outs[k][:, cols] = jnp.concatenate(both, axis=0).astype(outs[k].dtype)
 
 
 def second_tick_kernel(*refs):
-    blocks, pre, weights = refs[:4], refs[4], refs[5:11]
-    outs, held = refs[11:15], refs[15]
+    blocks, pre_a, pre_b, weights = refs[:4], refs[4], refs[5], refs[6:12]
+    outs, held = refs[12:16], refs[16]
     gates, ups, downs = weights[0:2], weights[2:4], weights[4:6]
     for k in range(CHIPS):
         held[16 * k : 16 * k + 16, :] = blocks[k][:, 0:D]
     rows = held[...]
     hidden = [dot(rows, w[...], 1, 1) for w in downs]
-    gate = [pre[:, 0:HID], pre[:, HID : 2 * HID]]
-    up = [pre[:, 2 * HID : 3 * HID], pre[:, 3 * HID : 4 * HID]]
-    backward_terms(hidden, gate, up, gates, ups, outs)
+    pre = jnp.concatenate(
+        [p[8 * k : 8 * k + 8, :] for k in range(CHIPS) for p in (pre_a, pre_b)], axis=0
+    )
+    parts = [pre[:, HID * i : HID * i + HID] for i in range(4)]
+    operands = (*differentials(hidden, parts[0:2], parts[2:4]), gates, ups)
+    for low in range(0, D, WIDTH):
+        cols = pl.ds(low, WIDTH)
+        total = terms_of(*operands, cols)
+        for k in range(CHIPS):
+            outs[k][:, cols] = total[16 * k : 16 * k + 16].astype(outs[k].dtype)
 
 
 def forward_kernel(*refs):
-    blocks, own_ids, other_ids = refs[0:8], refs[8], refs[9]
-    weights, routers = refs[10:14], refs[14:16]
-    pre, expo_ref, share_ref, stats_ref = refs[16:20]
-    held0, held1 = refs[20:22]
+    streams, own_ids, other_ids, routers = (refs[0:4], refs[4:8]), refs[8:10], refs[10], refs[11:13]
+    expo_ref, share_ref, stats_ref, held = refs[13:17]
     member = lax.axis_index("expert")
-    first_rows(blocks, held0)
-    later_rows(blocks, held1)
-    rows0, rows1 = held0[...], held1[...]
-    for i, w in enumerate(weights):
-        pre[:, HID * i : HID * i + HID] = dot(rows1, w[...], 1, 0)
-    logits = jnp.concatenate(
-        [
-            jnp.concatenate([dot(r[...], rows, 1, 1) for r in routers], axis=0)
-            for rows in (rows0, jnp.concatenate([rows1, rows1], axis=0))
-        ],
-        axis=1,
-    )
-    ids = [own_ids[...].astype(F32).T, other_ids[...].astype(F32).T]
+    logits = []
+    for blocks in streams:
+        stream_rows(blocks, held)
+        held[96:128, :] = held[64:96, :]
+        rows = held[...]
+        logits.append(jnp.concatenate([dot(r[...], rows, 1, 1) for r in routers], axis=0))
+    logits = jnp.concatenate(logits, axis=1)
+    ids = [
+        jnp.concatenate([own_ids[0][...], own_ids[1][...]], axis=0).astype(F32).T,
+        other_ids[...].astype(F32).T,
+    ]
     row = lax.broadcasted_iota(jnp.int32, (2 * OWN, 128), 0)
     column = lax.broadcasted_iota(jnp.int32, (2 * OWN, 128), 1)
     own = row + OWN * member
     other = row - OWN + OWN * (member + 1 - 2 * lax.rem(member, 2))
     experts = jnp.where(row < OWN, own, other).astype(F32)
-    stream_b = (column % 32) >= 16
     scale = EXPERTS / (TOKENS * TOPK)
     shares = []
     for tick in range(2):
@@ -172,12 +194,12 @@
             for j in range(TOPK):
                 slot = TOPK * tick + j
                 hits += (experts == ids[core][slot : slot + 1, :]).astype(F32)
-        count_a = jnp.sum(jnp.where(stream_b, 0.0, hits), axis=1, keepdims=True)
-        count_b = jnp.sum(jnp.where(stream_b, hits, 0.0), axis=1, keepdims=True)
+        count_a = jnp.sum(jnp.where(column < 64, hits, 0.0), axis=1, keepdims=True)
+        count_b = jnp.sum(jnp.where(column < 64, 0.0, hits), axis=1, keepdims=True)
         shares.append((count_a * scale, count_b * scale))
-    share0 = jnp.where(stream_b, shares[0][1], shares[0][0])
-    share1 = jnp.where((column % 16) >= 8, shares[1][1], shares[1][0])
-    share = jnp.concatenate([share0, share1], axis=1)
+    share = jnp.concatenate(
+        [jnp.where(column < 64, shares[0][i], shares[1][i]) for i in range(2)], axis=1
+    )
     peak = jnp.max(logits, axis=0, keepdims=True)
     expo = jnp.exp(logits - peak)
     total = jnp.sum(expo, axis=0, keepdims=True)
@@ -193,23 +215,22 @@
     stats_ref[...] = jnp.concatenate(rows + [jnp.zeros((2, 128), F32)], axis=0).astype(BF16)
 
 
+def turned(value, k):
+    if k == 0:
+        return value
+    early, late = value[:, 0:64], value[:, 64:96]
+    early = pltpu.roll(jnp.concatenate([early, early], axis=1), 16 * k, 1)
+    late = pltpu.roll(jnp.concatenate([late] * 4, axis=1), 8 * k, 1)
+    return jnp.concatenate([early[:, 0:64], late[:, 0:64]], axis=1)
+
+
 def router_kernel(*refs):
-    blocks, expo_ref, share_ref, parts = refs[0:8], refs[8], refs[9], refs[10:14]
-    own_out, other_out, held0, held1 = refs[14:18]
-    first_rows(blocks, held0)
-    later_rows(blocks, held1)
+    streams, expo_ref, share_ref, parts = (refs[0:4], refs[4:8]), refs[8], refs[9], refs[10:14]
+    own_out, other_out, held = refs[14:17]
     stats = []
     for k, part in enumerate(parts):
-        value = part[:, D:WIDE].astype(F32)
-        wide = [
-            jnp.concatenate(
-                [pltpu.roll(value, 32 * k, 1)[i : i + 1], pltpu.roll(value, 16 * k, 1)[i + 7 : i + 8]],
-                axis=1,
-            )
-            if k
-            else jnp.concatenate([value[i : i + 1], value[i + 7 : i + 8]], axis=1)
-            for i in range(7)
-        ]
+        value = turned(part[:, D:WIDE].astype(F32), k)
+        wide = [jnp.concatenate([value[i : i + 1], value[i + 7 : i + 8]], axis=1) for i in range(7)]
         stats.append((wide[0] + wide[1] + wide[2], wide[3] + wide[4], wide[5] + wide[6]))
     mine = stats[0]
     peaks = [s[0] for s in stats]
@@ -224,11 +245,15 @@
         2.0 * z_weight * log_total - balance_weight * mean_share + balance_weight * share_ref[...]
     ) * probs
     column = lax.broadcasted_iota(jnp.int32, (2 * OWN, 128), 1)
-    slopes0 = jnp.where((column % 16) < 8, slopes[:, 0:128], 0.0).astype(BF16)
-    slopes1 = slopes[:, 128:192].astype(BF16)
+    kept = ((column % 16) < 8) & (column < 64) | (column >= 64) & (column < 96)
+    for i, blocks in enumerate(streams):
+        stream_rows(blocks, held.at[pl.ds(96 * i, 96), :])
+    chosen = [
+        jnp.where(kept, slopes[:, 128 * i : 128 * i + 128], 0.0).astype(BF16)[:, 0:96] for i in range(2)
+    ]
     for low in range(0, D, WIDTH):
         cols = pl.ds(low, WIDTH)
-        part = dot(slopes0, held0[:, cols], 1, 0) + dot(slopes1, held1[:, cols], 1, 0)
+        part = dot(chosen[0], held[0:96, cols], 1, 0) + dot(chosen[1], held[96:192, cols], 1, 0)
         own_out[:, cols] = part[0:OWN]
         other_out[:, cols] = part[OWN:]
 
@@ -287,49 +312,50 @@
     w_gate, w_up, w_down, router = w_gate[0], w_up[0], w_down[0], router[0]
     section = lax.axis_index("pipe")
     top = lax.axis_size("pipe") - 1
-    rows0, rows1 = pltpu.VMEM((128, D), BF16), pltpu.VMEM((64, D), BF16)
-
     block_b = mirrored(payload(stash_b, arriving_b, ids_b))
     block_a = payload(stash_a, arriving_a, ids_a)
     blocks_a = ring(block_a)
-    other_gate, other_up, other_down, other_router = (
-        swapped(weight) for weight in (w_gate, w_up, w_down, router)
-    )
+    other_gate, other_up, other_down = (swapped(weight) for weight in (w_gate, w_up, w_down))
     blocks_b = ring(passed(after(block_b, other_gate, other_up, other_down), int(3e9)))
-    first = [block for pair in zip(blocks_a, blocks_b) for block in pair]
-    gates, ups, downs = [w_gate, other_gate], [w_up, other_up], [w_down, other_down]
-
+    weights = [w_gate, other_gate, w_up, other_up, w_down, other_down]
+    rows = [pltpu.VMEM((96, D), BF16)]
+
+    terms_a, pre_a, ids_a = call(
+        first_a_kernel, [((32, D), F32), ((32, 4 * HID), F32), ((64, IDCOLS), BF16)],
+        blocks_a + weights, rows, 2 * 96 * D * 128 * 8,
+    )
     sends = [((16, D), F32)] + [((16, D), BF16)] * 3
-    *terms, ids = call(
-        first_tick_kernel, sends + [((128, IDCOLS), BF16)],
-        first + gates + ups + downs, [rows0], 2 * 128 * D * 128 * 10,
-    )
-    other_ids = swapped(ids)
+    *terms, pre_b, ids_b = call(
+        first_b_kernel, sends + [((32, 4 * HID), F32), ((64, IDCOLS), BF16)],
+        blocks_b + weights + [terms_a], rows, 2 * 96 * D * 128 * 8,
+    )
+    other_router = swapped(after(router, terms[0]))
+    other_ids = swapped(jnp.concatenate([ids_a, ids_b], axis=0))
     grads = jnp.concatenate([arriving_a, block_b[1, :, :D]], axis=0)
-    out = emitted(grads, returned(terms))
+    out = after(emitted(grads, returned(terms)), other_ids)
     moved = lax.ppermute(out, "pipe", [(i, i - 1) for i in range(1, top + 1)])
-    pre, expo, share, stats = call(
-        forward_kernel,
-        [((64, 4 * HID), F32), ((2 * OWN, 256), F32), ((2 * OWN, 256), F32), ((16, IDCOLS), BF16)],
-        first + [ids, other_ids] + gates + ups + [router, other_router],
-        [rows0, rows1], 2 * 128 * D * 128 * 4,
+    expo, share, stats = call(
+        forward_kernel, [((2 * OWN, 256), F32), ((2 * OWN, 256), F32), ((16, IDCOLS), BF16)],
+        blocks_a + blocks_b + [ids_a, ids_b, other_ids, router, other_router],
+        [pltpu.VMEM((128, D), BF16)], 2 * 256 * D * 64,
     )
     head = jnp.concatenate([head_a[0], head_b[0]], axis=0)
     grads = jnp.where(section == top, head, moved)
     gathered = ring(jnp.concatenate([grads, stats], axis=1))
     terms = call(
-        second_tick_kernel, sends, gathered + [pre] + gates + ups + downs, [rows1],
+        second_tick_kernel, sends, gathered + [pre_a, pre_b] + weights, [pltpu.VMEM((64, D), BF16)],
         2 * 64 * D * 128 * 6,
     )
     own, other = call(
         router_kernel, [((OWN, D), F32)] * 2,
-        first + [after(expo, *terms), share] + gathered, [rows0, rows1], 2 * 192 * D * 64,
+        blocks_a + blocks_b + [after(expo, *terms), share] + gathered,
+        [pltpu.VMEM((192, D), BF16)], 2 * 192 * D * 64,
     )
     router_grad = own + swapped(other)
     parts = returned(terms)
     out_a = emitted(grads[:ROWS], [part[:ROWS] for part in parts])
     out_b = emitted(grads[ROWS:], [part[ROWS:] for part in parts])
-    return out_a[None], mirrored(out_b)[None], router_grad[None]
+    return out_a[None], after(mirrored(out_b), router_grad)[None], router_grad[None]
 
 
 def solution(mesh):

time: 159 us -> 155 us (0.975)
  Pallas kernels: 16.4 us -> 20.7 us
  local copies, waits for them, and re-layouts: 5.03 us -> 1.37 us
  starting transfers between devices: 92.4 us -> 90.3 us
  other arithmetic: 4.05 us -> 2.27 us
    ppermute x1, waiting for transfers between devices: 5.44 us -> 12.3 us  [shards(): moved = lax.ppermute(out, 'pipe', [(i, i - 1) for i in range(1, top + 1)])]
    ppermute x15, waiting for transfers between devices: 20.1 us -> 13.7 us  [from_chip(): lax.ppermute(value, 'expert', [((e + 2 * k) % 8, e) for e in range(8)])]
    pallas_call x4 -> x5, Pallas kernels: 13.1 us -> 17.3 us  [call(): pl.pallas_call(body, out_shape=[jax.ShapeDtypeStruct(shape, dtype) for sh...]
    unnamed x37 -> x39, local copies, waits for them, and re-layouts: 4.4 us -> 0.74 us
    ppermute x15, starting transfers between devices: 55.5 us -> 53.5 us  [from_chip(): lax.ppermute(value, 'expert', [((e + 2 * k) % 8, e) for e in range(8)])]
  transfers between devices with their start and end apart: 24 -> 24, of which waited for: 11 -> 9; matrix products, arithmetic and copies ran while one was open for 2% -> 2% of each run, Pallas kernels for 4% -> 7%
where the time goes in v9:
time: 155 us; the launch traced here: 153 us
  starting transfers between devices  90.3 us (58%)
  waiting for transfers between devices  37.6 us (24%)
  Pallas kernels  20.7 us (13%)
  other arithmetic  2.27 us (1%)
    ppermute x15, starting transfers between devices, from_chip(): lax.ppermute(value, 'expert', [((e + 2 * k) % 8, e) for e in range(8)])  53.5 us
    ppermute x2, starting transfers between devices, mirrored(): lax.ppermute(value, 'pipe', [(i, count - 1 - i) for i in range(count)])  21.4 us
    pallas_call x5, Pallas kernels, call(): pl.pallas_call(body, out_shape=[jax.ShapeDtypeStruct(shape, dtype) for sh...  17.3 us
    ppermute x15, waiting for transfers between devices, from_chip(): lax.ppermute(value, 'expert', [((e + 2 * k) % 8, e) for e in range(8)])  13.7 us
    ppermute x6, starting transfers between devices, swapped(): return lax.ppermute(value, 'expert', [(e, e ^ 1) for e in range(8)])  12.6 us
    ppermute x1, waiting for transfers between devices, shards(): moved = lax.ppermute(out, 'pipe', [(i, i - 1) for i in range(1, top + 1)])  12.3 us
    ppermute x2, waiting for transfers between devices, mirrored(): lax.ppermute(value, 'pipe', [(i, count - 1 - i) for i in range(count)])  11.7 us
    pallas_call x2, Pallas kernels, payload(): pl.pallas_call(pack_kernel, out_shape=jax.ShapeDtypeStruct((3, ROWS, WIDE...  3.37 us
  transfers between devices with their start and end apart: 24, of which 9 were waited for; matrix products, arithmetic and copies ran while one was open for 2% of the time, Pallas kernels for 7%

profile of v9, /device:TPU:6, one launch (start us, length us, event | category | flops | bytes accessed | tf_op | source)
XLA Modules:
  0.0 153.5 jit_solution(10012756685095075846)
XLA Ops:
  0.6 1.7 %shard_map.139 = bf16[3,8,3712]{2,1,0:T(8,128)(2,1)} custom-call(bf16[2,8,3584]{2,1,0:T(8,128)(2,1)} %bitcast.33, bf16[8,3584]{1,0:T(8,128)(2,1)} %bitcast.36, s32[2,8,8]{2,1,0:T(8,128)} %bitcast.39), custom_call_target="tpu_custom_call" | custom-call | tf_op jit(solution)/shard_map/pallas_call | solution.py:73
  2.3 15.1 %collective-permute-start = (bf16[3,8,3712]{2,1,0:T(8,128)(2,1)}, bf16[3,8,3712]{2,1,0:T(8,128)(2,1)S(1)}, u32[]{:S(2)}, u32[]{:S(2)}) collective-permute-start(bf16[3,8,3712]{2,1,0:T(8,128)(2,1)} %shard_map.139), channel_id=1, source_target_pairs={{0,504},{8,496},{16,488},{24,480},{32,472},{40,464},{48,456},{56,4... | collective-permute-start | bytes 534536 | tf_op jit(solution)/shard_map/ppermute | solution.py:280
  17.4 1.9 %collective-permute-start.1 = (bf16[3584,128]{1,0:T(8,128)(2,1)}, bf16[3584,128]{1,0:T(8,128)(2,1)}, u32[]{:S(2)}, u32[]{:S(2)}) collective-permute-start(bf16[3584,128]{1,0:T(8,128)(2,1)} %bitcast.18), channel_id=1, source_target_pairs={{0,1},{1,0},{2,3},{3,2},{4,5},{5,4},{6,7},{7,6},{8,9},{9,8},{10,11... | collective-permute-start | bytes 2752520 | tf_op jit(solution)/shard_map/ppermute | solution.py:275
  19.4 2.4 %collective-permute-start.2 = (bf16[3584,128]{1,0:T(8,128)(2,1)}, bf16[3584,128]{1,0:T(8,128)(2,1)}, u32[]{:S(2)}, u32[]{:S(2)}) collective-permute-start(bf16[3584,128]{1,0:T(8,128)(2,1)} %bitcast.22), channel_id=1, source_target_pairs={{0,1},{1,0},{2,3},{3,2},{4,5},{5,4},{6,7},{7,6},{8,9},{9,8},{10,11... | collective-permute-start | bytes 2752520 | tf_op jit(solution)/shard_map/ppermute | solution.py:275
  21.8 1.9 %collective-permute-start.3 = (bf16[128,3584]{1,0:T(8,128)(2,1)}, bf16[128,3584]{1,0:T(8,128)(2,1)}, u32[]{:S(2)}, u32[]{:S(2)}) collective-permute-start(bf16[128,3584]{1,0:T(8,128)(2,1)} %bitcast.26), channel_id=1, source_target_pairs={{0,1},{1,0},{2,3},{3,2},{4,5},{5,4},{6,7},{7,6},{8,9},{9,8},{10,11... | collective-permute-start | bytes 2752520 | tf_op jit(solution)/shard_map/ppermute | solution.py:275
  23.7 1.7 %shard_map.141.refs_0_ = bf16[3,8,3712]{2,1,0:T(8,128)(2,1)} custom-call(bf16[2,8,3584]{2,1,0:T(8,128)(2,1)} %bitcast.34, bf16[8,3584]{1,0:T(8,128)(2,1)} %bitcast.31, s32[2,8,8]{2,1,0:T(8,128)} %bitcast.40), custom_call_target="tpu_custom_call" | custom-call | tf_op jit(solution)/shard_map/pallas_call | solution.py:73
  25.4 2.9 %collective-permute-start.9 = (bf16[3,8,3712]{2,1,0:T(8,128)(2,1)}, bf16[3,8,3712]{2,1,0:T(8,128)(2,1)S(1)}, u32[]{:S(2)}, u32[]{:S(2)}) collective-permute-start(bf16[3,8,3712]{2,1,0:T(8,128)(2,1)} %shard_map.141.refs_0_), channel_id=1, source_target_pairs={{6,0},{7,1},{0,2},{1,3},{2,4},{3,5},{4,6},{5,7},{14,8},{15,9},{8,1... | collective-permute-start | bytes 534536 | tf_op jit(solution)/shard_map/ppermute | solution.py:284
  28.3 4.6 %collective-permute-done.value = bf16[3,8,3712]{2,1,0:T(8,128)(2,1)S(1)} collective-permute-done((bf16[3,8,3712]{2,1,0:T(8,128)(2,1)}, bf16[3,8,3712]{2,1,0:T(8,128)(2,1)S(1)}, u32[]{:S(2)}, u32[]{:S(2)}) %collective-permute-start) | collective-permute-done | bytes 178208 | tf_op jit(solution)/shard_map/ppermute | solution.py:280
  33.0 1.9 %collective-permute-start.8 = (bf16[3,8,3712]{2,1,0:T(8,128)(2,1)}, bf16[3,8,3712]{2,1,0:T(8,128)(2,1)S(1)}, u32[]{:S(2)}, u32[]{:S(2)}) collective-permute-start(bf16[3,8,3712]{2,1,0:T(8,128)(2,1)} %shard_map.141.refs_0_), channel_id=1, source_target_pairs={{4,0},{5,1},{6,2},{7,3},{0,4},{1,5},{2,6},{3,7},{12,8},{13,9},{14,... | collective-permute-start | bytes 534536 | tf_op jit(solution)/shard_map/ppermute | solution.py:284
  34.9 0.6 slice_bitcast_fusion
  35.6 4.8 %collective-permute-start.7 = (bf16[3,8,3712]{2,1,0:T(8,128)(2,1)}, bf16[3,8,3712]{2,1,0:T(8,128)(2,1)}, u32[]{:S(2)}, u32[]{:S(2)}) collective-permute-start(bf16[3,8,3712]{2,1,0:T(8,128)(2,1)} %shard_map.141.refs_0_), channel_id=1, source_target_pairs={{2,0},{3,1},{4,2},{5,3},{6,4},{7,5},{0,6},{1,7},{10,8},{11,9},{12,... | collective-permute-start | bytes 534536 | tf_op jit(solution)/shard_map/ppermute | solution.py:284
  40.4 2.6 %collective-permute-start.6 = (bf16[3,8,3712]{2,1,0:T(8,128)(2,1)}, bf16[3,8,3712]{2,1,0:T(8,128)(2,1)S(1)}, u32[]{:S(2)}, u32[]{:S(2)}) collective-permute-start(bf16[3,8,3712]{2,1,0:T(8,128)(2,1)} %shard_map.140.refs_0_.refs_4_), channel_id=1, source_target_pairs={{6,0},{7,1},{0,2},{1,3},{2,4},{3,5},{4,6},{5,7},{14,8},{15,9},{8,1... | collective-permute-start | bytes 534536 | tf_op jit(solution)/shard_map/ppermute | solution.py:284
  43.0 3.6 %collective-permute-start.5 = (bf16[3,8,3712]{2,1,0:T(8,128)(2,1)}, bf16[3,8,3712]{2,1,0:T(8,128)(2,1)S(1)}, u32[]{:S(2)}, u32[]{:S(2)}) collective-permute-start(bf16[3,8,3712]{2,1,0:T(8,128)(2,1)} %shard_map.140.refs_0_.refs_4_), channel_id=1, source_target_pairs={{4,0},{5,1},{6,2},{7,3},{0,4},{1,5},{2,6},{3,7},{12,8},{13,9},{14,... | collective-permute-start | bytes 534536 | tf_op jit(solution)/shard_map/ppermute | solution.py:284
  46.7 4.6 %collective-permute-start.4 = (bf16[3,8,3712]{2,1,0:T(8,128)(2,1)}, bf16[3,8,3712]{2,1,0:T(8,128)(2,1)S(1)}, u32[]{:S(2)}, u32[]{:S(2)}) collective-permute-start(bf16[3,8,3712]{2,1,0:T(8,128)(2,1)} %shard_map.140.refs_0_.refs_4_), channel_id=1, source_target_pairs={{2,0},{3,1},{4,2},{5,3},{6,4},{7,5},{0,6},{1,7},{10,8},{11,9},{12,... | collective-permute-start | bytes 534536 | tf_op jit(solution)/shard_map/ppermute | solution.py:284
  51.3 2.3 %collective-permute-done.7.refs_1_ = bf16[3,8,3712]{2,1,0:T(8,128)(2,1)} collective-permute-done((bf16[3,8,3712]{2,1,0:T(8,128)(2,1)}, bf16[3,8,3712]{2,1,0:T(8,128)(2,1)}, u32[]{:S(2)}, u32[]{:S(2)}) %collective-permute-start.7) | collective-permute-done | bytes 178208 | tf_op jit(solution)/shard_map/ppermute | solution.py:284
  53.6 4.5 %shard_map.142 = (f32[32,3584]{1,0:T(8,128)S(1)}, f32[32,512]{1,0:T(8,128)S(1)}, bf16[64,128]{1,0:T(8,128)(2,1)S(1)}) custom-call(bf16[3,8,3712]{2,1,0:T(8,128)(2,1)S(1)} %copy-done.4, bf16[3,8,3712]{2,1,0:T(8,128)(2,1)} %collective-permute-done.7.refs_1_, bf16[3,8,3712]{2,1,0:T(8,128)(2,1)S(1)} %collective-permute-done.8.refs_2_, ...), custom_call_target="tpu_custom_call" | custom-call | flops 704643072 | bytes 6217728 | tf_op jit(solution)/shard_map/pallas_call | solution.py:37
  58.1 0.0 collective-permute-done.6.refs_3_.refs_7_
  58.2 3.0 %collective-permute-done.5.refs_2_.refs_6_ = bf16[3,8,3712]{2,1,0:T(8,128)(2,1)S(1)} collective-permute-done((bf16[3,8,3712]{2,1,0:T(8,128)(2,1)}, bf16[3,8,3712]{2,1,0:T(8,128)(2,1)S(1)}, u32[]{:S(2)}, u32[]{:S(2)}) %collective-permute-start.5) | collective-permute-done | bytes 178208 | tf_op jit(solution)/shard_map/ppermute | solution.py:284
  61.1 0.0 copy-start.16
  61.1 4.9 %shard_map.143 = (f32[16,3584]{1,0:T(8,128)S(1)}, bf16[16,3584]{1,0:T(8,128)(2,1)S(1)}, bf16[16,3584]{1,0:T(8,128)(2,1)S(1)}, bf16[16,3584]{1,0:T(8,128)(2,1)S(1...) custom-call(bf16[3,8,3712]{2,1,0:T(8,128)(2,1)S(1)} %copy-done.6, ...), custom_call_target="tpu_custom_call" | custom-call | flops 704643072 | bytes 6676480 | tf_op jit(solution)/shard_map/pallas_call | solution.py:37
  66.0 0.0 copy-done.7
  66.1 7.0 %collective-permute-start.10 = (bf16[16,3584]{1,0:T(8,128)(2,1)S(1)}, bf16[16,3584]{1,0:T(8,128)(2,1)S(1)}, u32[]{:S(2)}, u32[]{:S(2)}) collective-permute-start(bf16[16,3584]{1,0:T(8,128)(2,1)S(1)} %get-tuple-element.29), channel_id=1, source_target_pairs={{2,0},{3,1},{4,2},{5,3},{6,4},{7,5},{0,6},{1,7},{10,8},{11,9},{12,... | collective-permute-start | bytes 344072 | tf_op jit(solution)/shard_map/ppermute | solution.py:284
  73.1 2.6 %collective-permute-start.11 = (bf16[16,3584]{1,0:T(8,128)(2,1)S(1)}, bf16[16,3584]{1,0:T(8,128)(2,1)S(1)}, u32[]{:S(2)}, u32[]{:S(2)}) collective-permute-start(bf16[16,3584]{1,0:T(8,128)(2,1)S(1)} %get-tuple-element.30), channel_id=1, source_target_pairs={{4,0},{5,1},{6,2},{7,3},{0,4},{1,5},{2,6},{3,7},{12,8},{13,9},{14,... | collective-permute-start | bytes 344072 | tf_op jit(solution)/shard_map/ppermute | solution.py:284
  75.7 1.9 %collective-permute-start.12 = (bf16[16,3584]{1,0:T(8,128)(2,1)S(1)}, bf16[16,3584]{1,0:T(8,128)(2,1)S(1)}, u32[]{:S(2)}, u32[]{:S(2)}) collective-permute-start(bf16[16,3584]{1,0:T(8,128)(2,1)S(1)} %get-tuple-element.31), channel_id=1, source_target_pairs={{6,0},{7,1},{0,2},{1,3},{2,4},{3,5},{4,6},{5,7},{14,8},{15,9},{8,1... | collective-permute-start | bytes 344072 | tf_op jit(solution)/shard_map/ppermute | solution.py:284
  77.7 2.1 %collective-permute-start.13 = (bf16[128,128]{1,0:T(8,128)(2,1)S(1)}, bf16[128,128]{1,0:T(8,128)(2,1)S(1)}, u32[]{:S(2)}, u32[]{:S(2)}) collective-permute-start(bf16[128,128]{1,0:T(8,128)(2,1)S(1)} %pad_maximum_fusion.1), channel_id=1, source_target_pairs={{0,1},{1,0},{2,3},{3,2},{4,5},{5,4},{6,7},{7,6},{8,9},{9,8},{10,11... | collective-permute-start | bytes 98312 | tf_op jit(solution)/shard_map/ppermute | solution.py:275
  79.7 2.4 %collective-permute-start.15 = (bf16[32,3584]{1,0:T(8,128)(2,1)}, bf16[32,3584]{1,0:T(8,128)(2,1)}, u32[]{:S(2)}, u32[]{:S(2)}) collective-permute-start(bf16[32,3584]{1,0:T(8,128)(2,1)} %bitcast.12.refs_11_), channel_id=1, source_target_pairs={{0,1},{1,0},{2,3},{3,2},{4,5},{5,4},{6,7},{7,6},{8,9},{9,8},{10,11... | collective-permute-start | bytes 688136 | tf_op jit(solution)/shard_map/ppermute | solution.py:275
  82.2 2.4 %collective-permute-done.11 = bf16[16,3584]{1,0:T(8,128)(2,1)S(1)} collective-permute-done((bf16[16,3584]{1,0:T(8,128)(2,1)S(1)}, bf16[16,3584]{1,0:T(8,128)(2,1)S(1)}, u32[]{:S(2)}, u32[]{:S(2)}) %collective-permute-start.11) | collective-permute-done | bytes 114720 | tf_op jit(solution)/shard_map/ppermute | solution.py:284
  84.6 0.7 add_convert_fusion
  85.3 2.8 %collective-permute-start.14 = (bf16[16,3584]{1,0:T(8,128)(2,1)}, bf16[16,3584]{1,0:T(8,128)(2,1)S(1)}, u32[]{:S(2)}, u32[]{:S(2)}) collective-permute-start(bf16[16,3584]{1,0:T(8,128)(2,1)} %add_convert_fusion), channel_id=1, source_target_pairs={{8,0},{16,8},{24,16},{32,24},{40,32},{48,40},{56,48},{64,56},{72,6... | collective-permute-start | bytes 344072 | tf_op jit(solution)/shard_map/ppermute | solution.py:336
  88.2 2.5 %shard_map.144 = (f32[64,256]{1,0:T(8,128)S(1)}, f32[64,256]{1,0:T(8,128)S(1)}, bf16[16,128]{1,0:T(8,128)(2,1)S(1)}) custom-call(bf16[3,8,3712]{2,1,0:T(8,128)(2,1)S(1)} %copy-done.4, bf16[3,8,3712]{2,1,0:T(8,128)(2,1)} %collective-permute-done.7.refs_1_, bf16[3,8,3712]{2,1,0:T(8,128)(2,1)S(1)} %collective-permute-done.8.refs_2_, ...), custom_call_target="tpu_custom_call" | custom-call | flops 117440512 | bytes 1949696 | tf_op jit(solution)/shard_map/pallas_call | solution.py:37
  90.7 12.3 %collective-permute-done.14 = bf16[16,3584]{1,0:T(8,128)(2,1)S(1)} collective-permute-done((bf16[16,3584]{1,0:T(8,128)(2,1)}, bf16[16,3584]{1,0:T(8,128)(2,1)S(1)}, u32[]{:S(2)}, u32[]{:S(2)}) %collective-permute-start.14) | collective-permute-done | bytes 114720 | tf_op jit(solution)/shard_map/ppermute | solution.py:336
  103.1 5.3 %collective-permute-start.18 = (bf16[16,3712]{1,0:T(8,128)(2,1)S(1)}, bf16[16,3712]{1,0:T(8,128)(2,1)S(1)}, u32[]{:S(2)}, u32[]{:S(2)}) collective-permute-start(bf16[16,3712]{1,0:T(8,128)(2,1)S(1)} %pad_maximum_fusion.refs_0_.refs_10_), channel_id=1, source_target_pairs={{6,0},{7,1},{0,2},{1,3},{2,4},{3,5},{4,6},{5,7},{14,8},{15,9},{8,1... | collective-permute-start | bytes 356360 | tf_op jit(solution)/shard_map/ppermute | solution.py:284
  108.3 1.9 %collective-permute-start.17 = (bf16[16,3712]{1,0:T(8,128)(2,1)S(1)}, bf16[16,3712]{1,0:T(8,128)(2,1)S(1)}, u32[]{:S(2)}, u32[]{:S(2)}) collective-permute-start(bf16[16,3712]{1,0:T(8,128)(2,1)S(1)} %pad_maximum_fusion.refs_0_.refs_10_), channel_id=1, source_target_pairs={{4,0},{5,1},{6,2},{7,3},{0,4},{1,5},{2,6},{3,7},{12,8},{13,9},{14,... | collective-permute-start | bytes 356360 | tf_op jit(solution)/shard_map/ppermute | solution.py:284
  110.3 4.6 %collective-permute-start.16 = (bf16[16,3712]{1,0:T(8,128)(2,1)S(1)}, bf16[16,3712]{1,0:T(8,128)(2,1)S(1)}, u32[]{:S(2)}, u32[]{:S(2)}) collective-permute-start(bf16[16,3712]{1,0:T(8,128)(2,1)S(1)} %pad_maximum_fusion.refs_0_.refs_10_), channel_id=1, source_target_pairs={{2,0},{3,1},{4,2},{5,3},{6,4},{7,5},{0,6},{1,7},{10,8},{11,9},{12,... | collective-permute-start | bytes 356360 | tf_op jit(solution)/shard_map/ppermute | solution.py:284
  114.9 3.5 %collective-permute-done.17.refs_2_.refs_12_ = bf16[16,3712]{1,0:T(8,128)(2,1)S(1)} collective-permute-done((bf16[16,3712]{1,0:T(8,128)(2,1)S(1)}, bf16[16,3712]{1,0:T(8,128)(2,1)S(1)}, u32[]{:S(2)}, u32[]{:S(2)}) %collective-permute-start.17) | collective-permute-done | bytes 118816 | tf_op jit(solution)/shard_map/ppermute | solution.py:284
  118.3 3.9 %shard_map.145 = (f32[16,3584]{1,0:T(8,128)S(1)}, bf16[16,3584]{1,0:T(8,128)(2,1)S(1)}, bf16[16,3584]{1,0:T(8,128)(2,1)S(1)}, bf16[16,3584]{1,0:T(8,128)(2,1)S(1)}) custom-call(bf16[16,3712]{1,0:T(8,128)(2,1)S(1)} %pad_maximum_fusion.refs_0_.refs_10_, bf16[16,3712]{1,0:T(8,128)(2,1)S(1)} %collective-permute-done.16.refs_1_.refs_11_, ...), custom_call_target="tpu_custom_call" | custom-call | flops 352321536 | bytes 6111232 | tf_op jit(solution)/shard_map/pallas_call | solution.py:37
  122.2 5.3 %collective-permute-start.19 = (bf16[16,3584]{1,0:T(8,128)(2,1)S(1)}, bf16[16,3584]{1,0:T(8,128)(2,1)S(1)}, u32[]{:S(2)}, u32[]{:S(2)}) collective-permute-start(bf16[16,3584]{1,0:T(8,128)(2,1)S(1)} %get-tuple-element.40), channel_id=1, source_target_pairs={{2,0},{3,1},{4,2},{5,3},{6,4},{7,5},{0,6},{1,7},{10,8},{11,9},{12,... | collective-permute-start | bytes 344072 | tf_op jit(solution)/shard_map/ppermute | solution.py:284
  127.5 1.9 %collective-permute-start.20 = (bf16[16,3584]{1,0:T(8,128)(2,1)S(1)}, bf16[16,3584]{1,0:T(8,128)(2,1)S(1)}, u32[]{:S(2)}, u32[]{:S(2)}) collective-permute-start(bf16[16,3584]{1,0:T(8,128)(2,1)S(1)} %get-tuple-element.41), channel_id=1, source_target_pairs={{4,0},{5,1},{6,2},{7,3},{0,4},{1,5},{2,6},{3,7},{12,8},{13,9},{14,... | collective-permute-start | bytes 344072 | tf_op jit(solution)/shard_map/ppermute | solution.py:284
  129.5 2.5 %collective-permute-start.21 = (bf16[16,3584]{1,0:T(8,128)(2,1)S(1)}, bf16[16,3584]{1,0:T(8,128)(2,1)S(1)}, u32[]{:S(2)}, u32[]{:S(2)}) collective-permute-start(bf16[16,3584]{1,0:T(8,128)(2,1)S(1)} %get-tuple-element.42), channel_id=1, source_target_pairs={{6,0},{7,1},{0,2},{1,3},{2,4},{3,5},{4,6},{5,7},{14,8},{15,9},{8,1... | collective-permute-start | bytes 344072 | tf_op jit(solution)/shard_map/ppermute | solution.py:284
  131.9 1.6 %shard_map.146 = (f32[32,3584]{1,0:T(8,128)S(1)}, f32[32,3584]{1,0:T(8,128)S(1)}) custom-call(bf16[3,8,3712]{2,1,0:T(8,128)(2,1)S(1)} %copy-done.4, bf16[3,8,3712]{2,1,0:T(8,128)(2,1)} %collective-permute-done.7.refs_1_, bf16[3,8,3712]{2,1,0:T(8,128)(2,1)S(1)} %collective-permute-done.8.refs_2_, bf16[3,8,3712]{2,1,0:T(8,128)(2,1)S(1)} %collective-permute-done.9.refs_3_, ...), custom_call_target="tpu_custom_call" | custom-call | flops 88080384 | bytes 2031616 | tf_op jit(solution)/shard_map/pallas_call | solution.py:37
  133.5 1.9 %collective-permute-start.23 = (f32[32,3584]{1,0:T(8,128)S(1)}, f32[32,3584]{1,0:T(8,128)S(1)}, u32[]{:S(2)}, u32[]{:S(2)}) collective-permute-start(f32[32,3584]{1,0:T(8,128)S(1)} %get-tuple-element.47), channel_id=1, source_target_pairs={{0,1},{1,0},{2,3},{3,2},{4,5},{5,4},{6,7},{7,6},{8,9},{9,8},{10,11... | collective-permute-start | bytes 1376264 | tf_op jit(solution)/shard_map/ppermute | solution.py:275
  135.4 0.8 collective-permute-done.20
  136.3 1.7 %collective-permute-done.21 = bf16[16,3584]{1,0:T(8,128)(2,1)S(1)} collective-permute-done((bf16[16,3584]{1,0:T(8,128)(2,1)S(1)}, bf16[16,3584]{1,0:T(8,128)(2,1)S(1)}, u32[]{:S(2)}, u32[]{:S(2)}) %collective-permute-start.21) | collective-permute-done | bytes 114720 | tf_op jit(solution)/shard_map/ppermute | solution.py:284
  137.9 0.7 add_convert_fusion.1
  138.6 6.3 %collective-permute-start.22 = (bf16[8,3584]{1,0:T(8,128)(2,1)S(1)}, bf16[8,3584]{1,0:T(8,128)(2,1)S(1)}, u32[]{:S(2)}, u32[]{:S(2)}) collective-permute-start(bf16[8,3584]{1,0:T(8,128)(2,1)S(1)} %get-tuple-element.49), channel_id=1, source_target_pairs={{0,504},{8,496},{16,488},{24,480},{32,472},{40,464},{48,456},{56,4... | collective-permute-start | bytes 172040 | tf_op jit(solution)/shard_map/ppermute | solution.py:280
  145.0 0.8 add.51
  145.8 7.0 %collective-permute-done.22 = bf16[8,3584]{1,0:T(8,128)(2,1)S(1)} collective-permute-done((bf16[8,3584]{1,0:T(8,128)(2,1)S(1)}, bf16[8,3584]{1,0:T(8,128)(2,1)S(1)}, u32[]{:S(2)}, u32[]{:S(2)}) %collective-permute-start.22) | collective-permute-done | bytes 57376 | tf_op jit(solution)/shard_map/ppermute | solution.py:280
  152.8 0.6 copy.18
  (54 shorter events, 0.2 us)
Async XLA Ops:
  2.3 30.7 %collective-permute-start = (bf16[3,8,3712]{2,1,0:T(8,128)(2,1)}, bf16[3,8,3712]{2,1,0:T(8,128)(2,1)S(1)}, u32[]{:S(2)}, u32[]{:S(2)}) collective-permute-start(bf16[3,8,3712]{2,1,0:T(8,128)(2,1)} %shard_map.139), channel_id=1, source_target_pairs={{0,504},{8,496},{16,488},{24,480},{32,472},{40,464},{48,456},{56,4... | collective-permute-start | bytes 534536 | tf_op jit(solution)/shard_map/ppermute | solution.py:280
  17.4 18.1 %collective-permute-start.1 = (bf16[3584,128]{1,0:T(8,128)(2,1)}, bf16[3584,128]{1,0:T(8,128)(2,1)}, u32[]{:S(2)}, u32[]{:S(2)}) collective-permute-start(bf16[3584,128]{1,0:T(8,128)(2,1)} %bitcast.18), channel_id=1, source_target_pairs={{0,1},{1,0},{2,3},{3,2},{4,5},{5,4},{6,7},{7,6},{8,9},{9,8},{10,11... | collective-permute-start | bytes 2752520 | tf_op jit(solution)/shard_map/ppermute | solution.py:275
  19.4 21.0 %collective-permute-start.2 = (bf16[3584,128]{1,0:T(8,128)(2,1)}, bf16[3584,128]{1,0:T(8,128)(2,1)}, u32[]{:S(2)}, u32[]{:S(2)}) collective-permute-start(bf16[3584,128]{1,0:T(8,128)(2,1)} %bitcast.22), channel_id=1, source_target_pairs={{0,1},{1,0},{2,3},{3,2},{4,5},{5,4},{6,7},{7,6},{8,9},{9,8},{10,11... | collective-permute-start | bytes 2752520 | tf_op jit(solution)/shard_map/ppermute | solution.py:275
  21.8 18.6 %collective-permute-start.3 = (bf16[128,3584]{1,0:T(8,128)(2,1)}, bf16[128,3584]{1,0:T(8,128)(2,1)}, u32[]{:S(2)}, u32[]{:S(2)}) collective-permute-start(bf16[128,3584]{1,0:T(8,128)(2,1)} %bitcast.26), channel_id=1, source_target_pairs={{0,1},{1,0},{2,3},{3,2},{4,5},{5,4},{6,7},{7,6},{8,9},{9,8},{10,11... | collective-permute-start | bytes 2752520 | tf_op jit(solution)/shard_map/ppermute | solution.py:275
  25.4 21.3 %collective-permute-start.9 = (bf16[3,8,3712]{2,1,0:T(8,128)(2,1)}, bf16[3,8,3712]{2,1,0:T(8,128)(2,1)S(1)}, u32[]{:S(2)}, u32[]{:S(2)}) collective-permute-start(bf16[3,8,3712]{2,1,0:T(8,128)(2,1)} %shard_map.141.refs_0_), channel_id=1, source_target_pairs={{6,0},{7,1},{0,2},{1,3},{2,4},{3,5},{4,6},{5,7},{14,8},{15,9},{8,1... | collective-permute-start | bytes 534536 | tf_op jit(solution)/shard_map/ppermute | solution.py:284
  33.0 7.4 %copy-start.5 = (bf16[3,8,3712]{2,1,0:T(8,128)(2,1)}, bf16[3,8,3712]{2,1,0:T(8,128)(2,1)S(1)}, u32[]{:S(2)}) copy-start(bf16[3,8,3712]{2,1,0:T(8,128)(2,1)S(1)} %collective-permute-done.value) | copy-start | bytes 534532
  33.0 18.3 %collective-permute-start.8 = (bf16[3,8,3712]{2,1,0:T(8,128)(2,1)}, bf16[3,8,3712]{2,1,0:T(8,128)(2,1)S(1)}, u32[]{:S(2)}, u32[]{:S(2)}) collective-permute-start(bf16[3,8,3712]{2,1,0:T(8,128)(2,1)} %shard_map.141.refs_0_), channel_id=1, source_target_pairs={{4,0},{5,1},{6,2},{7,3},{0,4},{1,5},{2,6},{3,7},{12,8},{13,9},{14,... | collective-permute-start | bytes 534536 | tf_op jit(solution)/shard_map/ppermute | solution.py:284
  35.5 18.1 %copy-start = (bf16[1,3584,128]{2,1,0:T(8,128)(2,1)S(1)}, bf16[1,3584,128]{2,1,0:T(8,128)(2,1)}, u32[]{:S(2)}) copy-start(bf16[1,3584,128]{2,1,0:T(8,128)(2,1)} %param.20) | copy-start | bytes 2752516
  35.5 18.1 %copy-start.1 = (bf16[1,3584,128]{2,1,0:T(8,128)(2,1)S(1)}, bf16[1,3584,128]{2,1,0:T(8,128)(2,1)}, u32[]{:S(2)}) copy-start(bf16[1,3584,128]{2,1,0:T(8,128)(2,1)} %param.21) | copy-start | bytes 2752516
  35.5 18.1 %copy-start.2 = (bf16[1,128,3584]{2,1,0:T(8,128)(2,1)S(1)}, bf16[1,128,3584]{2,1,0:T(8,128)(2,1)}, u32[]{:S(2)}) copy-start(bf16[1,128,3584]{2,1,0:T(8,128)(2,1)} %param.22) | copy-start | bytes 2752516
  35.5 18.1 %copy-start.4 = (bf16[3,8,3712]{2,1,0:T(8,128)(2,1)S(1)}, bf16[3,8,3712]{2,1,0:T(8,128)(2,1)}, u32[]{:S(2)}) copy-start(bf16[3,8,3712]{2,1,0:T(8,128)(2,1)} %shard_map.141.refs_0_) | copy-start | bytes 534532
  35.6 18.1 %collective-permute-start.7 = (bf16[3,8,3712]{2,1,0:T(8,128)(2,1)}, bf16[3,8,3712]{2,1,0:T(8,128)(2,1)}, u32[]{:S(2)}, u32[]{:S(2)}) collective-permute-start(bf16[3,8,3712]{2,1,0:T(8,128)(2,1)} %shard_map.141.refs_0_), channel_id=1, source_target_pairs={{2,0},{3,1},{4,2},{5,3},{6,4},{7,5},{0,6},{1,7},{10,8},{11,9},{12,... | collective-permute-start | bytes 534536 | tf_op jit(solution)/shard_map/ppermute | solution.py:284
  40.4 20.7 %copy-start.6 = (bf16[3,8,3712]{2,1,0:T(8,128)(2,1)S(1)}, bf16[3,8,3712]{2,1,0:T(8,128)(2,1)}, u32[]{:S(2)}) copy-start(bf16[3,8,3712]{2,1,0:T(8,128)(2,1)} %shard_map.140.refs_0_.refs_4_) | copy-start | bytes 534532
  40.4 17.7 %collective-permute-start.6 = (bf16[3,8,3712]{2,1,0:T(8,128)(2,1)}, bf16[3,8,3712]{2,1,0:T(8,128)(2,1)S(1)}, u32[]{:S(2)}, u32[]{:S(2)}) collective-permute-start(bf16[3,8,3712]{2,1,0:T(8,128)(2,1)} %shard_map.140.refs_0_.refs_4_), channel_id=1, source_target_pairs={{6,0},{7,1},{0,2},{1,3},{2,4},{3,5},{4,6},{5,7},{14,8},{15,9},{8,1... | collective-permute-start | bytes 534536 | tf_op jit(solution)/shard_map/ppermute | solution.py:284
  43.0 18.1 %collective-permute-start.5 = (bf16[3,8,3712]{2,1,0:T(8,128)(2,1)}, bf16[3,8,3712]{2,1,0:T(8,128)(2,1)S(1)}, u32[]{:S(2)}, u32[]{:S(2)}) collective-permute-start(bf16[3,8,3712]{2,1,0:T(8,128)(2,1)} %shard_map.140.refs_0_.refs_4_), channel_id=1, source_target_pairs={{4,0},{5,1},{6,2},{7,3},{0,4},{1,5},{2,6},{3,7},{12,8},{13,9},{14,... | collective-permute-start | bytes 534536 | tf_op jit(solution)/shard_map/ppermute | solution.py:284
  46.7 14.4 %collective-permute-start.4 = (bf16[3,8,3712]{2,1,0:T(8,128)(2,1)}, bf16[3,8,3712]{2,1,0:T(8,128)(2,1)S(1)}, u32[]{:S(2)}, u32[]{:S(2)}) collective-permute-start(bf16[3,8,3712]{2,1,0:T(8,128)(2,1)} %shard_map.140.refs_0_.refs_4_), channel_id=1, source_target_pairs={{2,0},{3,1},{4,2},{5,3},{6,4},{7,5},{0,6},{1,7},{10,8},{11,9},{12,... | collective-permute-start | bytes 534536 | tf_op jit(solution)/shard_map/ppermute | solution.py:284
  58.1 7.9 %copy-start.7 = (bf16[3,8,3712]{2,1,0:T(8,128)(2,1)}, bf16[3,8,3712]{2,1,0:T(8,128)(2,1)S(1)}, u32[]{:S(2)}) copy-start(bf16[3,8,3712]{2,1,0:T(8,128)(2,1)S(1)} %collective-permute-done.6.refs_3_.refs_7_) | copy-start | bytes 534532
  61.1 4.9 %copy-start.9 = (bf16[3,8,3712]{2,1,0:T(8,128)(2,1)}, bf16[3,8,3712]{2,1,0:T(8,128)(2,1)S(1)}, u32[]{:S(2)}) copy-start(bf16[3,8,3712]{2,1,0:T(8,128)(2,1)S(1)} %collective-permute-done.5.refs_2_.refs_6_) | copy-start | bytes 534532
  61.1 4.9 %copy-start.11 = (bf16[3,8,3712]{2,1,0:T(8,128)(2,1)}, bf16[3,8,3712]{2,1,0:T(8,128)(2,1)S(1)}, u32[]{:S(2)}) copy-start(bf16[3,8,3712]{2,1,0:T(8,128)(2,1)S(1)} %collective-permute-done.4.refs_1_.refs_5_) | copy-start | bytes 534532
  61.1 23.4 %copy-start.16 = (bf16[1,8,3584]{2,1,0:T(8,128)(2,1)S(1)}, bf16[1,8,3584]{2,1,0:T(8,128)(2,1)}, u32[]{:S(2)}) copy-start(bf16[1,8,3584]{2,1,0:T(8,128)(2,1)} %param.16) | copy-start | bytes 172036
  66.1 19.2 %copy-start.13 = (f32[32,512]{1,0:T(8,128)}, f32[32,512]{1,0:T(8,128)S(1)}, u32[]{:S(2)}) copy-start(f32[32,512]{1,0:T(8,128)S(1)} %get-tuple-element.38.refs_5_) | copy-start | bytes 196612
  66.1 18.5 %copy-start.15 = (bf16[8,3584]{1,0:T(8,128)(2,1)S(1)}, bf16[8,3584]{1,0:T(8,128)(2,1)}, u32[]{:S(2)}) copy-start(bf16[8,3584]{1,0:T(8,128)(2,1)} %slice_bitcast_fusion) | copy-start | bytes 172036
  66.1 16.1 %collective-permute-start.10 = (bf16[16,3584]{1,0:T(8,128)(2,1)S(1)}, bf16[16,3584]{1,0:T(8,128)(2,1)S(1)}, u32[]{:S(2)}, u32[]{:S(2)}) collective-permute-start(bf16[16,3584]{1,0:T(8,128)(2,1)S(1)} %get-tuple-element.29), channel_id=1, source_target_pairs={{2,0},{3,1},{4,2},{5,3},{6,4},{7,5},{0,6},{1,7},{10,8},{11,9},{12,... | collective-permute-start | bytes 344072 | tf_op jit(solution)/shard_map/ppermute | solution.py:284
  73.1 11.5 %collective-permute-start.11 = (bf16[16,3584]{1,0:T(8,128)(2,1)S(1)}, bf16[16,3584]{1,0:T(8,128)(2,1)S(1)}, u32[]{:S(2)}, u32[]{:S(2)}) collective-permute-start(bf16[16,3584]{1,0:T(8,128)(2,1)S(1)} %get-tuple-element.30), channel_id=1, source_target_pairs={{4,0},{5,1},{6,2},{7,3},{0,4},{1,5},{2,6},{3,7},{12,8},{13,9},{14,... | collective-permute-start | bytes 344072 | tf_op jit(solution)/shard_map/ppermute | solution.py:284
  75.7 8.9 %collective-permute-start.12 = (bf16[16,3584]{1,0:T(8,128)(2,1)S(1)}, bf16[16,3584]{1,0:T(8,128)(2,1)S(1)}, u32[]{:S(2)}, u32[]{:S(2)}) collective-permute-start(bf16[16,3584]{1,0:T(8,128)(2,1)S(1)} %get-tuple-element.31), channel_id=1, source_target_pairs={{6,0},{7,1},{0,2},{1,3},{2,4},{3,5},{4,6},{5,7},{14,8},{15,9},{8,1... | collective-permute-start | bytes 344072 | tf_op jit(solution)/shard_map/ppermute | solution.py:284
  77.6 10.5 %copy-start.8 = (bf16[3,8,3712]{2,1,0:T(8,128)(2,1)S(1)}, bf16[3,8,3712]{2,1,0:T(8,128)(2,1)}, u32[]{:S(2)}) copy-start(bf16[3,8,3712]{2,1,0:T(8,128)(2,1)} %copy-done.7) | copy-start | bytes 534532
  77.7 10.5 %copy-start.10 = (bf16[3,8,3712]{2,1,0:T(8,128)(2,1)S(1)}, bf16[3,8,3712]{2,1,0:T(8,128)(2,1)}, u32[]{:S(2)}) copy-start(bf16[3,8,3712]{2,1,0:T(8,128)(2,1)} %copy-done.9) | copy-start | bytes 534532
  77.7 10.5 %copy-start.12 = (bf16[3,8,3712]{2,1,0:T(8,128)(2,1)S(1)}, bf16[3,8,3712]{2,1,0:T(8,128)(2,1)}, u32[]{:S(2)}) copy-start(bf16[3,8,3712]{2,1,0:T(8,128)(2,1)} %copy-done.11) | copy-start | bytes 534532
  77.7 7.6 %collective-permute-start.13 = (bf16[128,128]{1,0:T(8,128)(2,1)S(1)}, bf16[128,128]{1,0:T(8,128)(2,1)S(1)}, u32[]{:S(2)}, u32[]{:S(2)}) collective-permute-start(bf16[128,128]{1,0:T(8,128)(2,1)S(1)} %pad_maximum_fusion.1), channel_id=1, source_target_pairs={{0,1},{1,0},{2,3},{3,2},{4,5},{5,4},{6,7},{7,6},{8,9},{9,8},{10,11... | collective-permute-start | bytes 98312 | tf_op jit(solution)/shard_map/ppermute | solution.py:275
  79.7 8.4 %collective-permute-start.15 = (bf16[32,3584]{1,0:T(8,128)(2,1)}, bf16[32,3584]{1,0:T(8,128)(2,1)}, u32[]{:S(2)}, u32[]{:S(2)}) collective-permute-start(bf16[32,3584]{1,0:T(8,128)(2,1)} %bitcast.12.refs_11_), channel_id=1, source_target_pairs={{0,1},{1,0},{2,3},{3,2},{4,5},{5,4},{6,7},{7,6},{8,9},{9,8},{10,11... | collective-permute-start | bytes 688136 | tf_op jit(solution)/shard_map/ppermute | solution.py:275
  85.3 17.7 %collective-permute-start.14 = (bf16[16,3584]{1,0:T(8,128)(2,1)}, bf16[16,3584]{1,0:T(8,128)(2,1)S(1)}, u32[]{:S(2)}, u32[]{:S(2)}) collective-permute-start(bf16[16,3584]{1,0:T(8,128)(2,1)} %add_convert_fusion), channel_id=1, source_target_pairs={{8,0},{16,8},{24,16},{32,24},{40,32},{48,40},{56,48},{64,56},{72,6... | collective-permute-start | bytes 344072 | tf_op jit(solution)/shard_map/ppermute | solution.py:336
  88.1 14.9 %copy-start.17 = (bf16[1,8,3584]{2,1,0:T(8,128)(2,1)S(1)}, bf16[1,8,3584]{2,1,0:T(8,128)(2,1)}, u32[]{:S(2)}) copy-start(bf16[1,8,3584]{2,1,0:T(8,128)(2,1)} %param.19) | copy-start | bytes 172036
  88.1 14.9 %copy-start.18 = (bf16[1,8,3584]{2,1,0:T(8,128)(2,1)S(1)}, bf16[1,8,3584]{2,1,0:T(8,128)(2,1)}, u32[]{:S(2)}) copy-start(bf16[1,8,3584]{2,1,0:T(8,128)(2,1)} %param.18) | copy-start | bytes 172036
  88.1 30.2 %copy-start.3 = (bf16[1,128,3584]{2,1,0:T(8,128)(2,1)S(1)}, bf16[1,128,3584]{2,1,0:T(8,128)(2,1)}, u32[]{:S(2)}) copy-start(bf16[1,128,3584]{2,1,0:T(8,128)(2,1)} %param.22) | copy-start | bytes 2752516
  103.0 15.3 %copy-start.14 = (f32[32,512]{1,0:T(8,128)S(1)}, f32[32,512]{1,0:T(8,128)}, u32[]{:S(2)}) copy-start(f32[32,512]{1,0:T(8,128)} %copy-done.13) | copy-start | bytes 196612
  103.1 11.8 %collective-permute-start.18 = (bf16[16,3712]{1,0:T(8,128)(2,1)S(1)}, bf16[16,3712]{1,0:T(8,128)(2,1)S(1)}, u32[]{:S(2)}, u32[]{:S(2)}) collective-permute-start(bf16[16,3712]{1,0:T(8,128)(2,1)S(1)} %pad_maximum_fusion.refs_0_.refs_10_), channel_id=1, source_target_pairs={{6,0},{7,1},{0,2},{1,3},{2,4},{3,5},{4,6},{5,7},{14,8},{15,9},{8,1... | collective-permute-start | bytes 356360 | tf_op jit(solution)/shard_map/ppermute | solution.py:284
  108.3 10.0 %collective-permute-start.17 = (bf16[16,3712]{1,0:T(8,128)(2,1)S(1)}, bf16[16,3712]{1,0:T(8,128)(2,1)S(1)}, u32[]{:S(2)}, u32[]{:S(2)}) collective-permute-start(bf16[16,3712]{1,0:T(8,128)(2,1)S(1)} %pad_maximum_fusion.refs_0_.refs_10_), channel_id=1, source_target_pairs={{4,0},{5,1},{6,2},{7,3},{0,4},{1,5},{2,6},{3,7},{12,8},{13,9},{14,... | collective-permute-start | bytes 356360 | tf_op jit(solution)/shard_map/ppermute | solution.py:284
  110.3 8.0 %collective-permute-start.16 = (bf16[16,3712]{1,0:T(8,128)(2,1)S(1)}, bf16[16,3712]{1,0:T(8,128)(2,1)S(1)}, u32[]{:S(2)}, u32[]{:S(2)}) collective-permute-start(bf16[16,3712]{1,0:T(8,128)(2,1)S(1)} %pad_maximum_fusion.refs_0_.refs_10_), channel_id=1, source_target_pairs={{2,0},{3,1},{4,2},{5,3},{6,4},{7,5},{0,6},{1,7},{10,8},{11,9},{12,... | collective-permute-start | bytes 356360 | tf_op jit(solution)/shard_map/ppermute | solution.py:284
  122.2 13.3 %collective-permute-start.19 = (bf16[16,3584]{1,0:T(8,128)(2,1)S(1)}, bf16[16,3584]{1,0:T(8,128)(2,1)S(1)}, u32[]{:S(2)}, u32[]{:S(2)}) collective-permute-start(bf16[16,3584]{1,0:T(8,128)(2,1)S(1)} %get-tuple-element.40), channel_id=1, source_target_pairs={{2,0},{3,1},{4,2},{5,3},{6,4},{7,5},{0,6},{1,7},{10,8},{11,9},{12,... | collective-permute-start | bytes 344072 | tf_op jit(solution)/shard_map/ppermute | solution.py:284
  127.5 8.7 %collective-permute-start.20 = (bf16[16,3584]{1,0:T(8,128)(2,1)S(1)}, bf16[16,3584]{1,0:T(8,128)(2,1)S(1)}, u32[]{:S(2)}, u32[]{:S(2)}) collective-permute-start(bf16[16,3584]{1,0:T(8,128)(2,1)S(1)} %get-tuple-element.41), channel_id=1, source_target_pairs={{4,0},{5,1},{6,2},{7,3},{0,4},{1,5},{2,6},{3,7},{12,8},{13,9},{14,... | collective-permute-start | bytes 344072 | tf_op jit(solution)/shard_map/ppermute | solution.py:284
  129.5 8.5 %collective-permute-start.21 = (bf16[16,3584]{1,0:T(8,128)(2,1)S(1)}, bf16[16,3584]{1,0:T(8,128)(2,1)S(1)}, u32[]{:S(2)}, u32[]{:S(2)}) collective-permute-start(bf16[16,3584]{1,0:T(8,128)(2,1)S(1)} %get-tuple-element.42), channel_id=1, source_target_pairs={{6,0},{7,1},{0,2},{1,3},{2,4},{3,5},{4,6},{5,7},{14,8},{15,9},{8,1... | collective-permute-start | bytes 344072 | tf_op jit(solution)/shard_map/ppermute | solution.py:284
  133.5 11.5 %collective-permute-start.23 = (f32[32,3584]{1,0:T(8,128)S(1)}, f32[32,3584]{1,0:T(8,128)S(1)}, u32[]{:S(2)}, u32[]{:S(2)}) collective-permute-start(f32[32,3584]{1,0:T(8,128)S(1)} %get-tuple-element.47), channel_id=1, source_target_pairs={{0,1},{1,0},{2,3},{3,2},{4,5},{5,4},{6,7},{7,6},{8,9},{9,8},{10,11... | collective-permute-start | bytes 1376264 | tf_op jit(solution)/shard_map/ppermute | solution.py:275
  138.6 14.2 %collective-permute-start.22 = (bf16[8,3584]{1,0:T(8,128)(2,1)S(1)}, bf16[8,3584]{1,0:T(8,128)(2,1)S(1)}, u32[]{:S(2)}, u32[]{:S(2)}) collective-permute-start(bf16[8,3584]{1,0:T(8,128)(2,1)S(1)} %get-tuple-element.49), channel_id=1, source_target_pairs={{0,504},{8,496},{16,488},{24,480},{32,472},{40,464},{48,456},{56,4... | collective-permute-start | bytes 172040 | tf_op jit(solution)/shard_map/ppermute | solution.py:280

commit v10 on v9

--- a/solution.py
+++ b/solution.py
@@ -324,12 +324,12 @@
         first_a_kernel, [((32, D), F32), ((32, 4 * HID), F32), ((64, IDCOLS), BF16)],
         blocks_a + weights, rows, 2 * 96 * D * 128 * 8,
     )
+    other_router = swapped(after(router, block_b))
     sends = [((16, D), F32)] + [((16, D), BF16)] * 3
     *terms, pre_b, ids_b = call(
         first_b_kernel, sends + [((32, 4 * HID), F32), ((64, IDCOLS), BF16)],
-        blocks_b + weights + [terms_a], rows, 2 * 96 * D * 128 * 8,
-    )
-    other_router = swapped(after(router, terms[0]))
+        blocks_b + weights + [after(terms_a, other_router)], rows, 2 * 96 * D * 128 * 8,
+    )
     other_ids = swapped(jnp.concatenate([ids_a, ids_b], axis=0))
     grads = jnp.concatenate([arriving_a, block_b[1, :, :D]], axis=0)
     out = after(emitted(grads, returned(terms)), other_ids)
@@ -346,16 +346,16 @@
         second_tick_kernel, sends, gathered + [pre_a, pre_b] + weights, [pltpu.VMEM((64, D), BF16)],
         2 * 64 * D * 128 * 6,
     )
-    own, other = call(
-        router_kernel, [((OWN, D), F32)] * 2,
-        blocks_a + blocks_b + [after(expo, *terms), share] + gathered,
-        [pltpu.VMEM((192, D), BF16)], 2 * 192 * D * 64,
-    )
-    router_grad = own + swapped(other)
     parts = returned(terms)
     out_a = emitted(grads[:ROWS], [part[:ROWS] for part in parts])
     out_b = emitted(grads[ROWS:], [part[ROWS:] for part in parts])
-    return out_a[None], after(mirrored(out_b), router_grad)[None], router_grad[None]
+    own, other = call(
+        router_kernel, [((OWN, D), F32)] * 2,
+        blocks_a + blocks_b + [after(expo, out_b), share] + gathered,
+        [pltpu.VMEM((192, D), BF16)], 2 * 192 * D * 64,
+    )
+    router_grad = own + swapped(other)
+    return out_a[None], passed(mirrored(out_b), int(3e11))[None], router_grad[None]
 
 
 def solution(mesh):

time: 155 us -> 161 us (1.039)
  the two profiles are of different devices: /device:TPU:6 before, /device:TPU:25 now
where the time goes in v10:
time: 161 us; the launch traced here: 160 us
  starting transfers between devices  102 us (63%)
  waiting for transfers between devices  28.4 us (18%)
  Pallas kernels  21.3 us (13%)
  other arithmetic  4.19 us (3%)
  local copies, waits for them, and re-layouts  3.35 us (2%)
    ppermute x15, starting transfers between devices, from_chip(): lax.ppermute(value, 'expert', [((e + 2 * k) % 8, e) for e in range(8)])  48.4 us
    ppermute x2, starting transfers between devices, mirrored(): lax.ppermute(value, 'pipe', [(i, count - 1 - i) for i in range(count)])  25 us
    ppermute x15, waiting for transfers between devices, from_chip(): lax.ppermute(value, 'expert', [((e + 2 * k) % 8, e) for e in range(8)])  24.1 us
    ppermute x6, starting transfers between devices, swapped(): return lax.ppermute(value, 'expert', [(e, e ^ 1) for e in range(8)])  19.2 us
    pallas_call x5, Pallas kernels, call(): pl.pallas_call(body, out_shape=[jax.ShapeDtypeStruct(shape, dtype) for sh...  17.9 us
    ppermute x1, starting transfers between devices, shards(): moved = lax.ppermute(out, 'pipe', [(i, i - 1) for i in range(1, top + 1)])  9.16 us
    pallas_call x2, Pallas kernels, payload(): pl.pallas_call(pack_kernel, out_shape=jax.ShapeDtypeStruct((3, ROWS, WIDE...  3.35 us
  transfers between devices with their start and end apart: 24, of which 8 were waited for; matrix products, arithmetic and copies ran while one was open for 1% of the time, Pallas kernels for 7%

profile of v10, /device:TPU:25, one launch (start us, length us, event | category | flops | bytes accessed | tf_op | source)
XLA Modules:
  0.0 160.2 jit_solution(12939039129191650894)
XLA Ops:
  0.6 1.7 %shard_map.139 = bf16[3,8,3712]{2,1,0:T(8,128)(2,1)} custom-call(bf16[2,8,3584]{2,1,0:T(8,128)(2,1)} %bitcast.35, bf16[8,3584]{1,0:T(8,128)(2,1)} %bitcast.38, s32[2,8,8]{2,1,0:T(8,128)} %bitcast.41), custom_call_target="tpu_custom_call" | custom-call | tf_op jit(solution)/shard_map/pallas_call | solution.py:73
  2.3 14.3 %collective-permute-start = (bf16[3,8,3712]{2,1,0:T(8,128)(2,1)}, bf16[3,8,3712]{2,1,0:T(8,128)(2,1)S(1)}, u32[]{:S(2)}, u32[]{:S(2)}) collective-permute-start(bf16[3,8,3712]{2,1,0:T(8,128)(2,1)} %shard_map.139), channel_id=1, source_target_pairs={{0,504},{8,496},{16,488},{24,480},{32,472},{40,464},{48,456},{56,4... | collective-permute-start | bytes 534536 | tf_op jit(solution)/shard_map/ppermute | solution.py:280
  16.6 2.9 %collective-permute-start.1 = (bf16[3584,128]{1,0:T(8,128)(2,1)}, bf16[3584,128]{1,0:T(8,128)(2,1)}, u32[]{:S(2)}, u32[]{:S(2)}) collective-permute-start(bf16[3584,128]{1,0:T(8,128)(2,1)} %bitcast.19), channel_id=1, source_target_pairs={{0,1},{1,0},{2,3},{3,2},{4,5},{5,4},{6,7},{7,6},{8,9},{9,8},{10,11... | collective-permute-start | bytes 2752520 | tf_op jit(solution)/shard_map/ppermute | solution.py:275
  19.5 1.9 %collective-permute-start.2 = (bf16[3584,128]{1,0:T(8,128)(2,1)}, bf16[3584,128]{1,0:T(8,128)(2,1)}, u32[]{:S(2)}, u32[]{:S(2)}) collective-permute-start(bf16[3584,128]{1,0:T(8,128)(2,1)} %bitcast.23), channel_id=1, source_target_pairs={{0,1},{1,0},{2,3},{3,2},{4,5},{5,4},{6,7},{7,6},{8,9},{9,8},{10,11... | collective-permute-start | bytes 2752520 | tf_op jit(solution)/shard_map/ppermute | solution.py:275
  21.4 2.4 %collective-permute-start.3 = (bf16[128,3584]{1,0:T(8,128)(2,1)}, bf16[128,3584]{1,0:T(8,128)(2,1)}, u32[]{:S(2)}, u32[]{:S(2)}) collective-permute-start(bf16[128,3584]{1,0:T(8,128)(2,1)} %bitcast.27), channel_id=1, source_target_pairs={{0,1},{1,0},{2,3},{3,2},{4,5},{5,4},{6,7},{7,6},{8,9},{9,8},{10,11... | collective-permute-start | bytes 2752520 | tf_op jit(solution)/shard_map/ppermute | solution.py:275
  23.8 1.7 %shard_map.141.refs_0_ = bf16[3,8,3712]{2,1,0:T(8,128)(2,1)} custom-call(bf16[2,8,3584]{2,1,0:T(8,128)(2,1)} %bitcast.36, bf16[8,3584]{1,0:T(8,128)(2,1)} %bitcast.33, s32[2,8,8]{2,1,0:T(8,128)} %bitcast.42), custom_call_target="tpu_custom_call" | custom-call | tf_op jit(solution)/shard_map/pallas_call | solution.py:73
  25.5 3.6 %collective-permute-start.7 = (bf16[3,8,3712]{2,1,0:T(8,128)(2,1)}, bf16[3,8,3712]{2,1,0:T(8,128)(2,1)S(1)}, u32[]{:S(2)}, u32[]{:S(2)}) collective-permute-start(bf16[3,8,3712]{2,1,0:T(8,128)(2,1)} %shard_map.141.refs_0_), channel_id=1, source_target_pairs={{2,0},{3,1},{4,2},{5,3},{6,4},{7,5},{0,6},{1,7},{10,8},{11,9},{12,... | collective-permute-start | bytes 534536 | tf_op jit(solution)/shard_map/ppermute | solution.py:284
  29.1 3.1 %collective-permute-done.value = bf16[3,8,3712]{2,1,0:T(8,128)(2,1)S(1)} collective-permute-done((bf16[3,8,3712]{2,1,0:T(8,128)(2,1)}, bf16[3,8,3712]{2,1,0:T(8,128)(2,1)S(1)}, u32[]{:S(2)}, u32[]{:S(2)}) %collective-permute-start) | collective-permute-done | bytes 178208 | tf_op jit(solution)/shard_map/ppermute | solution.py:280
  32.2 1.9 %collective-permute-start.8 = (bf16[3,8,3712]{2,1,0:T(8,128)(2,1)}, bf16[3,8,3712]{2,1,0:T(8,128)(2,1)S(1)}, u32[]{:S(2)}, u32[]{:S(2)}) collective-permute-start(bf16[3,8,3712]{2,1,0:T(8,128)(2,1)} %shard_map.141.refs_0_), channel_id=1, source_target_pairs={{4,0},{5,1},{6,2},{7,3},{0,4},{1,5},{2,6},{3,7},{12,8},{13,9},{14,... | collective-permute-start | bytes 534536 | tf_op jit(solution)/shard_map/ppermute | solution.py:284
  34.1 0.6 slice_bitcast_fusion
  34.8 4.7 %collective-permute-start.9 = (bf16[3,8,3712]{2,1,0:T(8,128)(2,1)}, bf16[3,8,3712]{2,1,0:T(8,128)(2,1)}, u32[]{:S(2)}, u32[]{:S(2)}) collective-permute-start(bf16[3,8,3712]{2,1,0:T(8,128)(2,1)} %shard_map.141.refs_0_), channel_id=1, source_target_pairs={{6,0},{7,1},{0,2},{1,3},{2,4},{3,5},{4,6},{5,7},{14,8},{15,9},{8,1... | collective-permute-start | bytes 534536 | tf_op jit(solution)/shard_map/ppermute | solution.py:284
  39.5 3.4 %collective-permute-start.10 = (bf16[32,3584]{1,0:T(8,128)(2,1)}, bf16[32,3584]{1,0:T(8,128)(2,1)}, u32[]{:S(2)}, u32[]{:S(2)}) collective-permute-start(bf16[32,3584]{1,0:T(8,128)(2,1)} %bitcast.31), channel_id=1, source_target_pairs={{0,1},{1,0},{2,3},{3,2},{4,5},{5,4},{6,7},{7,6},{8,9},{9,8},{10,11... | collective-permute-start | bytes 688136 | tf_op jit(solution)/shard_map/ppermute | solution.py:275
  42.9 2.6 %collective-permute-start.4 = (bf16[3,8,3712]{2,1,0:T(8,128)(2,1)}, bf16[3,8,3712]{2,1,0:T(8,128)(2,1)S(1)}, u32[]{:S(2)}, u32[]{:S(2)}) collective-permute-start(bf16[3,8,3712]{2,1,0:T(8,128)(2,1)} %shard_map.140.refs_0_.refs_4_), channel_id=1, source_target_pairs={{2,0},{3,1},{4,2},{5,3},{6,4},{7,5},{0,6},{1,7},{10,8},{11,9},{12,... | collective-permute-start | bytes 534536 | tf_op jit(solution)/shard_map/ppermute | solution.py:284
  45.5 2.7 %collective-permute-start.5 = (bf16[3,8,3712]{2,1,0:T(8,128)(2,1)}, bf16[3,8,3712]{2,1,0:T(8,128)(2,1)S(1)}, u32[]{:S(2)}, u32[]{:S(2)}) collective-permute-start(bf16[3,8,3712]{2,1,0:T(8,128)(2,1)} %shard_map.140.refs_0_.refs_4_), channel_id=1, source_target_pairs={{4,0},{5,1},{6,2},{7,3},{0,4},{1,5},{2,6},{3,7},{12,8},{13,9},{14,... | collective-permute-start | bytes 534536 | tf_op jit(solution)/shard_map/ppermute | solution.py:284
  48.3 0.9 collective-permute-done.8.refs_2_
  49.1 1.9 %collective-permute-start.6 = (bf16[3,8,3712]{2,1,0:T(8,128)(2,1)}, bf16[3,8,3712]{2,1,0:T(8,128)(2,1)S(1)}, u32[]{:S(2)}, u32[]{:S(2)}) collective-permute-start(bf16[3,8,3712]{2,1,0:T(8,128)(2,1)} %shard_map.140.refs_0_.refs_4_), channel_id=1, source_target_pairs={{6,0},{7,1},{0,2},{1,3},{2,4},{3,5},{4,6},{5,7},{14,8},{15,9},{8,1... | collective-permute-start | bytes 534536 | tf_op jit(solution)/shard_map/ppermute | solution.py:284
  51.1 4.5 %shard_map.142 = (f32[32,3584]{1,0:T(8,128)S(1)}, f32[32,512]{1,0:T(8,128)S(1)}, bf16[64,128]{1,0:T(8,128)(2,1)S(1)}) custom-call(bf16[3,8,3712]{2,1,0:T(8,128)(2,1)S(1)} %copy-done.4, bf16[3,8,3712]{2,1,0:T(8,128)(2,1)S(1)} %collective-permute-done.7.refs_1_, bf16[3,8,3712]{2,1,0:T(8,128)(2,1)S(1)} %collective-permute-done.8.refs_2_, ...), custom_call_target="tpu_custom_call" | custom-call | flops 704643072 | bytes 6217728 | tf_op jit(solution)/shard_map/pallas_call | solution.py:37
  55.7 8.8 %collective-permute-done.5.refs_2_.refs_6_ = bf16[3,8,3712]{2,1,0:T(8,128)(2,1)S(1)} collective-permute-done((bf16[3,8,3712]{2,1,0:T(8,128)(2,1)}, bf16[3,8,3712]{2,1,0:T(8,128)(2,1)S(1)}, u32[]{:S(2)}, u32[]{:S(2)}) %collective-permute-start.5) | collective-permute-done | bytes 178208 | tf_op jit(solution)/shard_map/ppermute | solution.py:284
  64.5 4.9 %shard_map.143 = (f32[16,3584]{1,0:T(8,128)S(1)}, bf16[16,3584]{1,0:T(8,128)(2,1)S(1)}, bf16[16,3584]{1,0:T(8,128)(2,1)S(1)}, bf16[16,3584]{1,0:T(8,128)(2,1)S(1...) custom-call(bf16[3,8,3712]{2,1,0:T(8,128)(2,1)S(1)} %copy-done.6, ...), custom_call_target="tpu_custom_call" | custom-call | flops 704643072 | bytes 6676480 | tf_op jit(solution)/shard_map/pallas_call | solution.py:37
  69.4 2.1 %collective-permute-start.11 = (bf16[16,3584]{1,0:T(8,128)(2,1)S(1)}, bf16[16,3584]{1,0:T(8,128)(2,1)S(1)}, u32[]{:S(2)}, u32[]{:S(2)}) collective-permute-start(bf16[16,3584]{1,0:T(8,128)(2,1)S(1)} %get-tuple-element.31), channel_id=1, source_target_pairs={{2,0},{3,1},{4,2},{5,3},{6,4},{7,5},{0,6},{1,7},{10,8},{11,9},{12,... | collective-permute-start | bytes 344072 | tf_op jit(solution)/shard_map/ppermute | solution.py:284
  71.4 2.1 %collective-permute-start.12 = (bf16[16,3584]{1,0:T(8,128)(2,1)S(1)}, bf16[16,3584]{1,0:T(8,128)(2,1)S(1)}, u32[]{:S(2)}, u32[]{:S(2)}) collective-permute-start(bf16[16,3584]{1,0:T(8,128)(2,1)S(1)} %get-tuple-element.32), channel_id=1, source_target_pairs={{4,0},{5,1},{6,2},{7,3},{0,4},{1,5},{2,6},{3,7},{12,8},{13,9},{14,... | collective-permute-start | bytes 344072 | tf_op jit(solution)/shard_map/ppermute | solution.py:284
  73.6 3.4 %collective-permute-start.13 = (bf16[16,3584]{1,0:T(8,128)(2,1)S(1)}, bf16[16,3584]{1,0:T(8,128)(2,1)S(1)}, u32[]{:S(2)}, u32[]{:S(2)}) collective-permute-start(bf16[16,3584]{1,0:T(8,128)(2,1)S(1)} %get-tuple-element.33), channel_id=1, source_target_pairs={{6,0},{7,1},{0,2},{1,3},{2,4},{3,5},{4,6},{5,7},{14,8},{15,9},{8,1... | collective-permute-start | bytes 344072 | tf_op jit(solution)/shard_map/ppermute | solution.py:284
  77.0 3.1 %collective-permute-start.14 = (bf16[128,128]{1,0:T(8,128)(2,1)S(1)}, bf16[128,128]{1,0:T(8,128)(2,1)S(1)}, u32[]{:S(2)}, u32[]{:S(2)}) collective-permute-start(bf16[128,128]{1,0:T(8,128)(2,1)S(1)} %pad_maximum_fusion.1), channel_id=1, source_target_pairs={{0,1},{1,0},{2,3},{3,2},{4,5},{5,4},{6,7},{7,6},{8,9},{9,8},{10,11... | collective-permute-start | bytes 98312 | tf_op jit(solution)/shard_map/ppermute | solution.py:275
  80.1 3.2 %collective-permute-done.12 = bf16[16,3584]{1,0:T(8,128)(2,1)S(1)} collective-permute-done((bf16[16,3584]{1,0:T(8,128)(2,1)S(1)}, bf16[16,3584]{1,0:T(8,128)(2,1)S(1)}, u32[]{:S(2)}, u32[]{:S(2)}) %collective-permute-start.12) | collective-permute-done | bytes 114720 | tf_op jit(solution)/shard_map/ppermute | solution.py:284
  83.4 0.7 add_convert_fusion
  84.1 0.6 copy-done.14
  84.7 9.2 %collective-permute-start.15 = (bf16[16,3584]{1,0:T(8,128)(2,1)}, bf16[16,3584]{1,0:T(8,128)(2,1)}, u32[]{:S(2)}, u32[]{:S(2)}) collective-permute-start(bf16[16,3584]{1,0:T(8,128)(2,1)} %add_convert_fusion), channel_id=1, source_target_pairs={{8,0},{16,8},{24,16},{32,24},{40,32},{48,40},{56,48},{64,56},{72,6... | collective-permute-start | bytes 344072 | tf_op jit(solution)/shard_map/ppermute | solution.py:336
  94.0 0.7 copy-done.15
  94.7 2.4 %shard_map.144 = (f32[64,256]{1,0:T(8,128)S(1)}, f32[64,256]{1,0:T(8,128)S(1)}, bf16[16,128]{1,0:T(8,128)(2,1)S(1)}) custom-call(bf16[3,8,3712]{2,1,0:T(8,128)(2,1)S(1)} %copy-done.4, bf16[3,8,3712]{2,1,0:T(8,128)(2,1)S(1)} %collective-permute-done.7.refs_1_, bf16[3,8,3712]{2,1,0:T(8,128)(2,1)S(1)} %collective-permute-done.8.refs_2_, ...), custom_call_target="tpu_custom_call" | custom-call | flops 117440512 | bytes 1949696 | tf_op jit(solution)/shard_map/pallas_call | solution.py:37
  97.2 0.9 maximum_select_fusion
  98.2 8.5 %collective-permute-start.16 = (bf16[16,3712]{1,0:T(8,128)(2,1)S(1)}, bf16[16,3712]{1,0:T(8,128)(2,1)S(1)}, u32[]{:S(2)}, u32[]{:S(2)}) collective-permute-start(bf16[16,3712]{1,0:T(8,128)(2,1)S(1)} %pad_maximum_fusion.refs_0_.refs_10_), channel_id=1, source_target_pairs={{2,0},{3,1},{4,2},{5,3},{6,4},{7,5},{0,6},{1,7},{10,8},{11,9},{12,... | collective-permute-start | bytes 356360 | tf_op jit(solution)/shard_map/ppermute | solution.py:284
  106.7 2.3 %collective-permute-start.17 = (bf16[16,3712]{1,0:T(8,128)(2,1)S(1)}, bf16[16,3712]{1,0:T(8,128)(2,1)S(1)}, u32[]{:S(2)}, u32[]{:S(2)}) collective-permute-start(bf16[16,3712]{1,0:T(8,128)(2,1)S(1)} %pad_maximum_fusion.refs_0_.refs_10_), channel_id=1, source_target_pairs={{4,0},{5,1},{6,2},{7,3},{0,4},{1,5},{2,6},{3,7},{12,8},{13,9},{14,... | collective-permute-start | bytes 356360 | tf_op jit(solution)/shard_map/ppermute | solution.py:284
  109.0 3.4 %collective-permute-start.18 = (bf16[16,3712]{1,0:T(8,128)(2,1)S(1)}, bf16[16,3712]{1,0:T(8,128)(2,1)S(1)}, u32[]{:S(2)}, u32[]{:S(2)}) collective-permute-start(bf16[16,3712]{1,0:T(8,128)(2,1)S(1)} %pad_maximum_fusion.refs_0_.refs_10_), channel_id=1, source_target_pairs={{6,0},{7,1},{0,2},{1,3},{2,4},{3,5},{4,6},{5,7},{14,8},{15,9},{8,1... | collective-permute-start | bytes 356360 | tf_op jit(solution)/shard_map/ppermute | solution.py:284
  112.4 5.8 %collective-permute-done.17.refs_2_.refs_12_ = bf16[16,3712]{1,0:T(8,128)(2,1)S(1)} collective-permute-done((bf16[16,3712]{1,0:T(8,128)(2,1)S(1)}, bf16[16,3712]{1,0:T(8,128)(2,1)S(1)}, u32[]{:S(2)}, u32[]{:S(2)}) %collective-permute-start.17) | collective-permute-done | bytes 118816 | tf_op jit(solution)/shard_map/ppermute | solution.py:284
  118.1 3.8 %shard_map.145 = (f32[16,3584]{1,0:T(8,128)S(1)}, bf16[16,3584]{1,0:T(8,128)(2,1)S(1)}, bf16[16,3584]{1,0:T(8,128)(2,1)S(1)}, bf16[16,3584]{1,0:T(8,128)(2,1)S(1)}) custom-call(bf16[16,3712]{1,0:T(8,128)(2,1)S(1)} %pad_maximum_fusion.refs_0_.refs_10_, bf16[16,3712]{1,0:T(8,128)(2,1)S(1)} %collective-permute-done.16.refs_1_.refs_11_, ...), custom_call_target="tpu_custom_call" | custom-call | flops 352321536 | bytes 6111232 | tf_op jit(solution)/shard_map/pallas_call | solution.py:37
  122.0 3.0 %collective-permute-start.19 = (bf16[16,3584]{1,0:T(8,128)(2,1)S(1)}, bf16[16,3584]{1,0:T(8,128)(2,1)S(1)}, u32[]{:S(2)}, u32[]{:S(2)}) collective-permute-start(bf16[16,3584]{1,0:T(8,128)(2,1)S(1)} %get-tuple-element.41), channel_id=1, source_target_pairs={{2,0},{3,1},{4,2},{5,3},{6,4},{7,5},{0,6},{1,7},{10,8},{11,9},{12,... | collective-permute-start | bytes 344072 | tf_op jit(solution)/shard_map/ppermute | solution.py:284
  125.0 3.0 %collective-permute-start.20 = (bf16[16,3584]{1,0:T(8,128)(2,1)S(1)}, bf16[16,3584]{1,0:T(8,128)(2,1)S(1)}, u32[]{:S(2)}, u32[]{:S(2)}) collective-permute-start(bf16[16,3584]{1,0:T(8,128)(2,1)S(1)} %get-tuple-element.42), channel_id=1, source_target_pairs={{4,0},{5,1},{6,2},{7,3},{0,4},{1,5},{2,6},{3,7},{12,8},{13,9},{14,... | collective-permute-start | bytes 344072 | tf_op jit(solution)/shard_map/ppermute | solution.py:284
  128.0 3.4 %collective-permute-start.21 = (bf16[16,3584]{1,0:T(8,128)(2,1)S(1)}, bf16[16,3584]{1,0:T(8,128)(2,1)S(1)}, u32[]{:S(2)}, u32[]{:S(2)}) collective-permute-start(bf16[16,3584]{1,0:T(8,128)(2,1)S(1)} %get-tuple-element.43), channel_id=1, source_target_pairs={{6,0},{7,1},{0,2},{1,3},{2,4},{3,5},{4,6},{5,7},{14,8},{15,9},{8,1... | collective-permute-start | bytes 344072 | tf_op jit(solution)/shard_map/ppermute | solution.py:284
  131.3 1.6 %collective-permute-done.20 = bf16[16,3584]{1,0:T(8,128)(2,1)S(1)} collective-permute-done((bf16[16,3584]{1,0:T(8,128)(2,1)S(1)}, bf16[16,3584]{1,0:T(8,128)(2,1)S(1)}, u32[]{:S(2)}, u32[]{:S(2)}) %collective-permute-start.20) | collective-permute-done | bytes 114720 | tf_op jit(solution)/shard_map/ppermute | solution.py:284
  133.0 3.8 %collective-permute-done.21 = bf16[16,3584]{1,0:T(8,128)(2,1)S(1)} collective-permute-done((bf16[16,3584]{1,0:T(8,128)(2,1)S(1)}, bf16[16,3584]{1,0:T(8,128)(2,1)S(1)}, u32[]{:S(2)}, u32[]{:S(2)}) %collective-permute-start.21) | collective-permute-done | bytes 114720 | tf_op jit(solution)/shard_map/ppermute | solution.py:284
  136.8 0.7 add_convert_fusion.1
  137.5 10.7 %collective-permute-start.22 = (bf16[8,3584]{1,0:T(8,128)(2,1)S(1)}, bf16[8,3584]{1,0:T(8,128)(2,1)S(1)}, u32[]{:S(2)}, u32[]{:S(2)}) collective-permute-start(bf16[8,3584]{1,0:T(8,128)(2,1)S(1)} %get-tuple-element.49), channel_id=1, source_target_pairs={{0,504},{8,496},{16,488},{24,480},{32,472},{40,464},{48,456},{56,4... | collective-permute-start | bytes 172040 | tf_op jit(solution)/shard_map/ppermute | solution.py:280
  148.2 2.3 %shard_map.147 = (f32[32,3584]{1,0:T(8,128)S(1)}, f32[32,3584]{1,0:T(8,128)}) custom-call(bf16[3,8,3712]{2,1,0:T(8,128)(2,1)S(1)} %copy-done.4, bf16[3,8,3712]{2,1,0:T(8,128)(2,1)S(1)} %collective-permute-done.7.refs_1_, bf16[3,8,3712]{2,1,0:T(8,128)(2,1)S(1)} %collective-permute-done.8.refs_2_, bf16[3,8,3712]{2,1,0:T(8,128)(2,1)} %collective-permute-done.9.refs_3_, ...), custom_call_target="tpu_custom_call" | custom-call | flops 88080384 | bytes 2031616 | tf_op jit(solution)/shard_map/pallas_call | solution.py:37
  150.6 5.4 %collective-permute-start.23 = (f32[32,3584]{1,0:T(8,128)}, f32[32,3584]{1,0:T(8,128)}, u32[]{:S(2)}, u32[]{:S(2)}) collective-permute-start(f32[32,3584]{1,0:T(8,128)} %get-tuple-element.48), channel_id=1, source_target_pairs={{0,1},{1,0},{2,3},{3,2},{4,5},{5,4},{6,7},{7,6},{8,9},{9,8},{10,11... | collective-permute-start | bytes 1376264 | tf_op jit(solution)/shard_map/ppermute | solution.py:275
  156.0 0.6 copy-done.18
  156.6 1.1 collective-permute-done.23
  157.8 1.8 %add_bitcast_fusion = f32[1,32,3584]{2,1,0:T(8,128)} fusion(f32[32,3584]{1,0:T(8,128)S(1)} %get-tuple-element.47, f32[32,3584]{1,0:T(8,128)} %collective-permute-done.23), kind=kLoop, calls=%fused_computation | loop fusion | flops 114688 | bytes 1376256 | tf_op jit(solution)/shard_map/broadcast_in_dim | solution.py:358
  159.6 0.6 copy.20
  (61 shorter events, 0.2 us)
Async XLA Ops:
  2.3 29.9 %collective-permute-start = (bf16[3,8,3712]{2,1,0:T(8,128)(2,1)}, bf16[3,8,3712]{2,1,0:T(8,128)(2,1)S(1)}, u32[]{:S(2)}, u32[]{:S(2)}) collective-permute-start(bf16[3,8,3712]{2,1,0:T(8,128)(2,1)} %shard_map.139), channel_id=1, source_target_pairs={{0,504},{8,496},{16,488},{24,480},{32,472},{40,464},{48,456},{56,4... | collective-permute-start | bytes 534536 | tf_op jit(solution)/shard_map/ppermute | solution.py:280
  16.6 18.2 %collective-permute-start.1 = (bf16[3584,128]{1,0:T(8,128)(2,1)}, bf16[3584,128]{1,0:T(8,128)(2,1)}, u32[]{:S(2)}, u32[]{:S(2)}) collective-permute-start(bf16[3584,128]{1,0:T(8,128)(2,1)} %bitcast.19), channel_id=1, source_target_pairs={{0,1},{1,0},{2,3},{3,2},{4,5},{5,4},{6,7},{7,6},{8,9},{9,8},{10,11... | collective-permute-start | bytes 2752520 | tf_op jit(solution)/shard_map/ppermute | solution.py:275
  19.5 20.0 %collective-permute-start.2 = (bf16[3584,128]{1,0:T(8,128)(2,1)}, bf16[3584,128]{1,0:T(8,128)(2,1)}, u32[]{:S(2)}, u32[]{:S(2)}) collective-permute-start(bf16[3584,128]{1,0:T(8,128)(2,1)} %bitcast.23), channel_id=1, source_target_pairs={{0,1},{1,0},{2,3},{3,2},{4,5},{5,4},{6,7},{7,6},{8,9},{9,8},{10,11... | collective-permute-start | bytes 2752520 | tf_op jit(solution)/shard_map/ppermute | solution.py:275
  21.4 21.5 %collective-permute-start.3 = (bf16[128,3584]{1,0:T(8,128)(2,1)}, bf16[128,3584]{1,0:T(8,128)(2,1)}, u32[]{:S(2)}, u32[]{:S(2)}) collective-permute-start(bf16[128,3584]{1,0:T(8,128)(2,1)} %bitcast.27), channel_id=1, source_target_pairs={{0,1},{1,0},{2,3},{3,2},{4,5},{5,4},{6,7},{7,6},{8,9},{9,8},{10,11... | collective-permute-start | bytes 2752520 | tf_op jit(solution)/shard_map/ppermute | solution.py:275
  25.5 20.0 %collective-permute-start.7 = (bf16[3,8,3712]{2,1,0:T(8,128)(2,1)}, bf16[3,8,3712]{2,1,0:T(8,128)(2,1)S(1)}, u32[]{:S(2)}, u32[]{:S(2)}) collective-permute-start(bf16[3,8,3712]{2,1,0:T(8,128)(2,1)} %shard_map.141.refs_0_), channel_id=1, source_target_pairs={{2,0},{3,1},{4,2},{5,3},{6,4},{7,5},{0,6},{1,7},{10,8},{11,9},{12,... | collective-permute-start | bytes 534536 | tf_op jit(solution)/shard_map/ppermute | solution.py:284
  32.2 10.7 %copy-start.5 = (bf16[3,8,3712]{2,1,0:T(8,128)(2,1)}, bf16[3,8,3712]{2,1,0:T(8,128)(2,1)S(1)}, u32[]{:S(2)}) copy-start(bf16[3,8,3712]{2,1,0:T(8,128)(2,1)S(1)} %collective-permute-done.value) | copy-start | bytes 534532
  32.2 16.9 %collective-permute-start.8 = (bf16[3,8,3712]{2,1,0:T(8,128)(2,1)}, bf16[3,8,3712]{2,1,0:T(8,128)(2,1)S(1)}, u32[]{:S(2)}, u32[]{:S(2)}) collective-permute-start(bf16[3,8,3712]{2,1,0:T(8,128)(2,1)} %shard_map.141.refs_0_), channel_id=1, source_target_pairs={{4,0},{5,1},{6,2},{7,3},{0,4},{1,5},{2,6},{3,7},{12,8},{13,9},{14,... | collective-permute-start | bytes 534536 | tf_op jit(solution)/shard_map/ppermute | solution.py:284
  34.8 16.3 %copy-start = (bf16[1,3584,128]{2,1,0:T(8,128)(2,1)S(1)}, bf16[1,3584,128]{2,1,0:T(8,128)(2,1)}, u32[]{:S(2)}) copy-start(bf16[1,3584,128]{2,1,0:T(8,128)(2,1)} %param.20) | copy-start | bytes 2752516
  34.8 16.3 %copy-start.1 = (bf16[1,3584,128]{2,1,0:T(8,128)(2,1)S(1)}, bf16[1,3584,128]{2,1,0:T(8,128)(2,1)}, u32[]{:S(2)}) copy-start(bf16[1,3584,128]{2,1,0:T(8,128)(2,1)} %param.21) | copy-start | bytes 2752516
  34.8 16.3 %copy-start.2 = (bf16[1,128,3584]{2,1,0:T(8,128)(2,1)S(1)}, bf16[1,128,3584]{2,1,0:T(8,128)(2,1)}, u32[]{:S(2)}) copy-start(bf16[1,128,3584]{2,1,0:T(8,128)(2,1)} %param.22) | copy-start | bytes 2752516
  34.8 16.3 %copy-start.4 = (bf16[3,8,3712]{2,1,0:T(8,128)(2,1)S(1)}, bf16[3,8,3712]{2,1,0:T(8,128)(2,1)}, u32[]{:S(2)}) copy-start(bf16[3,8,3712]{2,1,0:T(8,128)(2,1)} %shard_map.141.refs_0_) | copy-start | bytes 534532
  34.8 16.3 %collective-permute-start.9 = (bf16[3,8,3712]{2,1,0:T(8,128)(2,1)}, bf16[3,8,3712]{2,1,0:T(8,128)(2,1)}, u32[]{:S(2)}, u32[]{:S(2)}) collective-permute-start(bf16[3,8,3712]{2,1,0:T(8,128)(2,1)} %shard_map.141.refs_0_), channel_id=1, source_target_pairs={{6,0},{7,1},{0,2},{1,3},{2,4},{3,5},{4,6},{5,7},{14,8},{15,9},{8,1... | collective-permute-start | bytes 534536 | tf_op jit(solution)/shard_map/ppermute | solution.py:284
  39.5 16.1 %collective-permute-start.10 = (bf16[32,3584]{1,0:T(8,128)(2,1)}, bf16[32,3584]{1,0:T(8,128)(2,1)}, u32[]{:S(2)}, u32[]{:S(2)}) collective-permute-start(bf16[32,3584]{1,0:T(8,128)(2,1)} %bitcast.31), channel_id=1, source_target_pairs={{0,1},{1,0},{2,3},{3,2},{4,5},{5,4},{6,7},{7,6},{8,9},{9,8},{10,11... | collective-permute-start | bytes 688136 | tf_op jit(solution)/shard_map/ppermute | solution.py:275
  42.9 21.5 %copy-start.6 = (bf16[3,8,3712]{2,1,0:T(8,128)(2,1)S(1)}, bf16[3,8,3712]{2,1,0:T(8,128)(2,1)}, u32[]{:S(2)}) copy-start(bf16[3,8,3712]{2,1,0:T(8,128)(2,1)} %shard_map.140.refs_0_.refs_4_) | copy-start | bytes 534532
  42.9 12.7 %collective-permute-start.4 = (bf16[3,8,3712]{2,1,0:T(8,128)(2,1)}, bf16[3,8,3712]{2,1,0:T(8,128)(2,1)S(1)}, u32[]{:S(2)}, u32[]{:S(2)}) collective-permute-start(bf16[3,8,3712]{2,1,0:T(8,128)(2,1)} %shard_map.140.refs_0_.refs_4_), channel_id=1, source_target_pairs={{2,0},{3,1},{4,2},{5,3},{6,4},{7,5},{0,6},{1,7},{10,8},{11,9},{12,... | collective-permute-start | bytes 534536 | tf_op jit(solution)/shard_map/ppermute | solution.py:284
  45.5 18.9 %collective-permute-start.5 = (bf16[3,8,3712]{2,1,0:T(8,128)(2,1)}, bf16[3,8,3712]{2,1,0:T(8,128)(2,1)S(1)}, u32[]{:S(2)}, u32[]{:S(2)}) collective-permute-start(bf16[3,8,3712]{2,1,0:T(8,128)(2,1)} %shard_map.140.refs_0_.refs_4_), channel_id=1, source_target_pairs={{4,0},{5,1},{6,2},{7,3},{0,4},{1,5},{2,6},{3,7},{12,8},{13,9},{14,... | collective-permute-start | bytes 534536 | tf_op jit(solution)/shard_map/ppermute | solution.py:284
  49.1 15.3 %collective-permute-start.6 = (bf16[3,8,3712]{2,1,0:T(8,128)(2,1)}, bf16[3,8,3712]{2,1,0:T(8,128)(2,1)S(1)}, u32[]{:S(2)}, u32[]{:S(2)}) collective-permute-start(bf16[3,8,3712]{2,1,0:T(8,128)(2,1)} %shard_map.140.refs_0_.refs_4_), channel_id=1, source_target_pairs={{6,0},{7,1},{0,2},{1,3},{2,4},{3,5},{4,6},{5,7},{14,8},{15,9},{8,1... | collective-permute-start | bytes 534536 | tf_op jit(solution)/shard_map/ppermute | solution.py:284
  55.6 13.7 %copy-start.7 = (bf16[3,8,3712]{2,1,0:T(8,128)(2,1)}, bf16[3,8,3712]{2,1,0:T(8,128)(2,1)S(1)}, u32[]{:S(2)}) copy-start(bf16[3,8,3712]{2,1,0:T(8,128)(2,1)S(1)} %collective-permute-done.4.refs_1_.refs_5_) | copy-start | bytes 534532
  64.4 4.9 %copy-start.9 = (bf16[3,8,3712]{2,1,0:T(8,128)(2,1)}, bf16[3,8,3712]{2,1,0:T(8,128)(2,1)S(1)}, u32[]{:S(2)}) copy-start(bf16[3,8,3712]{2,1,0:T(8,128)(2,1)S(1)} %collective-permute-done.5.refs_2_.refs_6_) | copy-start | bytes 534532
  64.4 4.9 %copy-start.11 = (bf16[3,8,3712]{2,1,0:T(8,128)(2,1)}, bf16[3,8,3712]{2,1,0:T(8,128)(2,1)S(1)}, u32[]{:S(2)}) copy-start(bf16[3,8,3712]{2,1,0:T(8,128)(2,1)S(1)} %collective-permute-done.6.refs_3_.refs_7_) | copy-start | bytes 534532
  64.4 18.9 %copy-start.17 = (bf16[1,8,3584]{2,1,0:T(8,128)(2,1)S(1)}, bf16[1,8,3584]{2,1,0:T(8,128)(2,1)}, u32[]{:S(2)}) copy-start(bf16[1,8,3584]{2,1,0:T(8,128)(2,1)} %param.16) | copy-start | bytes 172036
  69.4 14.0 %copy-start.16 = (bf16[8,3584]{1,0:T(8,128)(2,1)S(1)}, bf16[8,3584]{1,0:T(8,128)(2,1)}, u32[]{:S(2)}) copy-start(bf16[8,3584]{1,0:T(8,128)(2,1)} %slice_bitcast_fusion) | copy-start | bytes 172036
  69.4 10.7 %collective-permute-start.11 = (bf16[16,3584]{1,0:T(8,128)(2,1)S(1)}, bf16[16,3584]{1,0:T(8,128)(2,1)S(1)}, u32[]{:S(2)}, u32[]{:S(2)}) collective-permute-start(bf16[16,3584]{1,0:T(8,128)(2,1)S(1)} %get-tuple-element.31), channel_id=1, source_target_pairs={{2,0},{3,1},{4,2},{5,3},{6,4},{7,5},{0,6},{1,7},{10,8},{11,9},{12,... | collective-permute-start | bytes 344072 | tf_op jit(solution)/shard_map/ppermute | solution.py:284
  71.4 11.9 %collective-permute-start.12 = (bf16[16,3584]{1,0:T(8,128)(2,1)S(1)}, bf16[16,3584]{1,0:T(8,128)(2,1)S(1)}, u32[]{:S(2)}, u32[]{:S(2)}) collective-permute-start(bf16[16,3584]{1,0:T(8,128)(2,1)S(1)} %get-tuple-element.32), channel_id=1, source_target_pairs={{4,0},{5,1},{6,2},{7,3},{0,4},{1,5},{2,6},{3,7},{12,8},{13,9},{14,... | collective-permute-start | bytes 344072 | tf_op jit(solution)/shard_map/ppermute | solution.py:284
  73.6 9.8 %collective-permute-start.13 = (bf16[16,3584]{1,0:T(8,128)(2,1)S(1)}, bf16[16,3584]{1,0:T(8,128)(2,1)S(1)}, u32[]{:S(2)}, u32[]{:S(2)}) collective-permute-start(bf16[16,3584]{1,0:T(8,128)(2,1)S(1)} %get-tuple-element.33), channel_id=1, source_target_pairs={{6,0},{7,1},{0,2},{1,3},{2,4},{3,5},{4,6},{5,7},{14,8},{15,9},{8,1... | collective-permute-start | bytes 344072 | tf_op jit(solution)/shard_map/ppermute | solution.py:284
  77.0 7.2 %collective-permute-start.14 = (bf16[128,128]{1,0:T(8,128)(2,1)S(1)}, bf16[128,128]{1,0:T(8,128)(2,1)S(1)}, u32[]{:S(2)}, u32[]{:S(2)}) collective-permute-start(bf16[128,128]{1,0:T(8,128)(2,1)S(1)} %pad_maximum_fusion.1), channel_id=1, source_target_pairs={{0,1},{1,0},{2,3},{3,2},{4,5},{5,4},{6,7},{7,6},{8,9},{9,8},{10,11... | collective-permute-start | bytes 98312 | tf_op jit(solution)/shard_map/ppermute | solution.py:275
  83.4 10.6 %copy-start.8 = (bf16[3,8,3712]{2,1,0:T(8,128)(2,1)S(1)}, bf16[3,8,3712]{2,1,0:T(8,128)(2,1)}, u32[]{:S(2)}) copy-start(bf16[3,8,3712]{2,1,0:T(8,128)(2,1)} %copy-done.7) | copy-start | bytes 534532
  83.4 10.5 %copy-start.10 = (bf16[3,8,3712]{2,1,0:T(8,128)(2,1)S(1)}, bf16[3,8,3712]{2,1,0:T(8,128)(2,1)}, u32[]{:S(2)}) copy-start(bf16[3,8,3712]{2,1,0:T(8,128)(2,1)} %copy-done.9) | copy-start | bytes 534532
  83.4 10.5 %copy-start.12 = (bf16[3,8,3712]{2,1,0:T(8,128)(2,1)S(1)}, bf16[3,8,3712]{2,1,0:T(8,128)(2,1)}, u32[]{:S(2)}) copy-start(bf16[3,8,3712]{2,1,0:T(8,128)(2,1)} %copy-done.11) | copy-start | bytes 534532
  83.4 10.5 %copy-start.13 = (bf16[1,32,3584]{2,1,0:T(8,128)(2,1)S(1)}, bf16[1,32,3584]{2,1,0:T(8,128)(2,1)}, u32[]{:S(2)}) copy-start(bf16[1,32,3584]{2,1,0:T(8,128)(2,1)} %param.23) | copy-start | bytes 688132
  84.1 0.6 copy-start.14
  84.7 12.4 %collective-permute-start.15 = (bf16[16,3584]{1,0:T(8,128)(2,1)}, bf16[16,3584]{1,0:T(8,128)(2,1)}, u32[]{:S(2)}, u32[]{:S(2)}) collective-permute-start(bf16[16,3584]{1,0:T(8,128)(2,1)} %add_convert_fusion), channel_id=1, source_target_pairs={{8,0},{16,8},{24,16},{32,24},{40,32},{48,40},{56,48},{64,56},{72,6... | collective-permute-start | bytes 344072 | tf_op jit(solution)/shard_map/ppermute | solution.py:336
  94.0 0.8 copy-start.15
  94.7 2.5 %copy-start.20 = (bf16[1,8,3584]{2,1,0:T(8,128)(2,1)S(1)}, bf16[1,8,3584]{2,1,0:T(8,128)(2,1)}, u32[]{:S(2)}) copy-start(bf16[1,8,3584]{2,1,0:T(8,128)(2,1)} %param.19) | copy-start | bytes 172036
  94.7 2.5 %copy-start.21 = (bf16[1,8,3584]{2,1,0:T(8,128)(2,1)S(1)}, bf16[1,8,3584]{2,1,0:T(8,128)(2,1)}, u32[]{:S(2)}) copy-start(bf16[1,8,3584]{2,1,0:T(8,128)(2,1)} %param.18) | copy-start | bytes 172036
  94.7 23.4 %copy-start.3 = (bf16[1,128,3584]{2,1,0:T(8,128)(2,1)S(1)}, bf16[1,128,3584]{2,1,0:T(8,128)(2,1)}, u32[]{:S(2)}) copy-start(bf16[1,128,3584]{2,1,0:T(8,128)(2,1)} %param.22) | copy-start | bytes 2752516
  98.2 14.2 %collective-permute-start.16 = (bf16[16,3712]{1,0:T(8,128)(2,1)S(1)}, bf16[16,3712]{1,0:T(8,128)(2,1)S(1)}, u32[]{:S(2)}, u32[]{:S(2)}) collective-permute-start(bf16[16,3712]{1,0:T(8,128)(2,1)S(1)} %pad_maximum_fusion.refs_0_.refs_10_), channel_id=1, source_target_pairs={{2,0},{3,1},{4,2},{5,3},{6,4},{7,5},{0,6},{1,7},{10,8},{11,9},{12,... | collective-permute-start | bytes 356360 | tf_op jit(solution)/shard_map/ppermute | solution.py:284
  106.7 11.5 %collective-permute-start.17 = (bf16[16,3712]{1,0:T(8,128)(2,1)S(1)}, bf16[16,3712]{1,0:T(8,128)(2,1)S(1)}, u32[]{:S(2)}, u32[]{:S(2)}) collective-permute-start(bf16[16,3712]{1,0:T(8,128)(2,1)S(1)} %pad_maximum_fusion.refs_0_.refs_10_), channel_id=1, source_target_pairs={{4,0},{5,1},{6,2},{7,3},{0,4},{1,5},{2,6},{3,7},{12,8},{13,9},{14,... | collective-permute-start | bytes 356360 | tf_op jit(solution)/shard_map/ppermute | solution.py:284
  109.0 9.1 %collective-permute-start.18 = (bf16[16,3712]{1,0:T(8,128)(2,1)S(1)}, bf16[16,3712]{1,0:T(8,128)(2,1)S(1)}, u32[]{:S(2)}, u32[]{:S(2)}) collective-permute-start(bf16[16,3712]{1,0:T(8,128)(2,1)S(1)} %pad_maximum_fusion.refs_0_.refs_10_), channel_id=1, source_target_pairs={{6,0},{7,1},{0,2},{1,3},{2,4},{3,5},{4,6},{5,7},{14,8},{15,9},{8,1... | collective-permute-start | bytes 356360 | tf_op jit(solution)/shard_map/ppermute | solution.py:284
  122.0 9.4 %collective-permute-start.19 = (bf16[16,3584]{1,0:T(8,128)(2,1)S(1)}, bf16[16,3584]{1,0:T(8,128)(2,1)S(1)}, u32[]{:S(2)}, u32[]{:S(2)}) collective-permute-start(bf16[16,3584]{1,0:T(8,128)(2,1)S(1)} %get-tuple-element.41), channel_id=1, source_target_pairs={{2,0},{3,1},{4,2},{5,3},{6,4},{7,5},{0,6},{1,7},{10,8},{11,9},{12,... | collective-permute-start | bytes 344072 | tf_op jit(solution)/shard_map/ppermute | solution.py:284
  125.0 8.0 %collective-permute-start.20 = (bf16[16,3584]{1,0:T(8,128)(2,1)S(1)}, bf16[16,3584]{1,0:T(8,128)(2,1)S(1)}, u32[]{:S(2)}, u32[]{:S(2)}) collective-permute-start(bf16[16,3584]{1,0:T(8,128)(2,1)S(1)} %get-tuple-element.42), channel_id=1, source_target_pairs={{4,0},{5,1},{6,2},{7,3},{0,4},{1,5},{2,6},{3,7},{12,8},{13,9},{14,... | collective-permute-start | bytes 344072 | tf_op jit(solution)/shard_map/ppermute | solution.py:284
  128.0 8.9 %collective-permute-start.21 = (bf16[16,3584]{1,0:T(8,128)(2,1)S(1)}, bf16[16,3584]{1,0:T(8,128)(2,1)S(1)}, u32[]{:S(2)}, u32[]{:S(2)}) collective-permute-start(bf16[16,3584]{1,0:T(8,128)(2,1)S(1)} %get-tuple-element.43), channel_id=1, source_target_pairs={{6,0},{7,1},{0,2},{1,3},{2,4},{3,5},{4,6},{5,7},{14,8},{15,9},{8,1... | collective-permute-start | bytes 344072 | tf_op jit(solution)/shard_map/ppermute | solution.py:284
  137.5 18.5 %collective-permute-start.22 = (bf16[8,3584]{1,0:T(8,128)(2,1)S(1)}, bf16[8,3584]{1,0:T(8,128)(2,1)S(1)}, u32[]{:S(2)}, u32[]{:S(2)}) collective-permute-start(bf16[8,3584]{1,0:T(8,128)(2,1)S(1)} %get-tuple-element.49), channel_id=1, source_target_pairs={{0,504},{8,496},{16,488},{24,480},{32,472},{40,464},{48,456},{56,4... | collective-permute-start | bytes 172040 | tf_op jit(solution)/shard_map/ppermute | solution.py:280
  150.6 7.2 %collective-permute-start.23 = (f32[32,3584]{1,0:T(8,128)}, f32[32,3584]{1,0:T(8,128)}, u32[]{:S(2)}, u32[]{:S(2)}) collective-permute-start(f32[32,3584]{1,0:T(8,128)} %get-tuple-element.48), channel_id=1, source_target_pairs={{0,1},{1,0},{2,3},{3,2},{4,5},{5,4},{6,7},{7,6},{8,9},{9,8},{10,11... | collective-permute-start | bytes 1376264 | tf_op jit(solution)/shard_map/ppermute | solution.py:275
  156.0 0.6 copy-start.18
  157.8 1.8 %copy-start.19 = (bf16[8,3584]{1,0:T(8,128)(2,1)S(1)}, bf16[8,3584]{1,0:T(8,128)(2,1)}, u32[]{:S(2)}) copy-start(bf16[8,3584]{1,0:T(8,128)(2,1)} %shard_map.146) | copy-start | bytes 172036

commit v11 on v9

--- a/solution.py
+++ b/solution.py
@@ -18,7 +18,7 @@
 IDCOLS = 128
 WIDE = D + IDCOLS
 WIDTH = 512
-VMEM_LIMIT = 48 * 1024 * 1024
+VMEM_LIMIT = 40 * 1024 * 1024
 z_weight = 0.01
 balance_weight = 1.0
 F32 = jnp.float32
@@ -81,20 +81,10 @@
 
 
 def differentials(hidden, gate, up):
-    d_gate, d_up = [], []
-    for h, g, u in zip(hidden, gate, up):
-        q = jax.nn.sigmoid(g)
-        d_gate.append((h * u * q * (1.0 + g * (1.0 - q))).astype(BF16))
-        d_up.append((h * g * q).astype(BF16))
-    return d_gate, d_up
-
-
-def terms_of(d_gate, d_up, gates, ups, cols):
-    total = dot(d_gate[0], gates[0][cols, :], 1, 1)
-    total += dot(d_gate[1], gates[1][cols, :], 1, 1)
-    total += dot(d_up[0], ups[0][cols, :], 1, 1)
-    total += dot(d_up[1], ups[1][cols, :], 1, 1)
-    return total
+    q = jax.nn.sigmoid(gate)
+    d_gate = (hidden * up * q * (1.0 + gate * (1.0 - q))).astype(BF16)
+    d_up = (hidden * gate * q).astype(BF16)
+    return jnp.concatenate([d_gate, d_up], axis=1)
 
 
 def stream_rows(blocks, held):
@@ -105,8 +95,7 @@
         held[64 + 8 * k : 80 + 8 * k, :] = packed(pair)
 
 
-def first_tick(blocks, weights, pre, ids, held):
-    gates, ups, downs = weights[0:2], weights[2:4], weights[4:6]
+def first_tick(blocks, wide, downs, pre, ids, held):
     stream_rows(blocks, held)
     for k, block in enumerate(blocks):
         ids[16 * k : 16 * k + 16, :] = packed([block[0, :, D:WIDE], block[1, :, D:WIDE]])
@@ -117,51 +106,50 @@
             [value[16 * k + offset : 16 * k + offset + 8] for k in range(CHIPS)], axis=0
         )
 
-    values = [dot(rows, w[...], 1, 0) for w in (*gates, *ups)]
-    for i, value in enumerate(values):
-        pre[:, HID * i : HID * i + HID] = value[64:96]
-    hidden = [pick(dot(rows[0:64], w[...], 1, 1), 8) for w in downs]
-    picked = [pick(value, 0) for value in values]
-    return (*differentials(hidden, picked[0:2], picked[2:4]), gates, ups)
+    values = dot(rows, wide[...], 1, 0)
+    pre[...] = values[64:96]
+    hidden = pick(dot(rows[0:64], downs[...], 1, 1), 8)
+    values = pick(values, 0)
+    return differentials(hidden, values[:, 0 : 2 * HID], values[:, 2 * HID :])
 
 
 def first_a_kernel(*refs):
-    blocks, weights, (terms, pre, ids, held) = refs[:4], refs[4:10], refs[10:14]
-    operands = first_tick(blocks, weights, pre, ids, held)
+    blocks, weights, (terms, pre, ids, wide, downs, held) = refs[:4], refs[4:10], refs[10:16]
+    for i, w in enumerate(weights[0:4]):
+        wide[:, HID * i : HID * i + HID] = w[...]
+    for i, w in enumerate(weights[4:6]):
+        downs[HID * i : HID * i + HID, :] = w[...]
+    operand = first_tick(blocks, wide, downs, pre, ids, held)
     for low in range(0, D, WIDTH):
         cols = pl.ds(low, WIDTH)
-        terms[:, cols] = terms_of(*operands, cols)
+        terms[:, cols] = dot(operand, wide[cols, :], 1, 1)
 
 
 def first_b_kernel(*refs):
-    blocks, weights, terms_a, outs, (pre, ids, held) = (
-        refs[:4], refs[4:10], refs[10], refs[11:15], refs[15:18]
-    )
-    operands = first_tick(blocks, weights, pre, ids, held)
+    blocks, wide, downs, terms_a, outs = refs[:4], refs[4], refs[5], refs[6], refs[7:11]
+    pre, ids, held = refs[11:14]
+    operand = first_tick(blocks, wide, downs, pre, ids, held)
     for low in range(0, D, WIDTH):
         cols = pl.ds(low, WIDTH)
-        terms_b = terms_of(*operands, cols)
+        terms_b = dot(operand, wide[cols, :], 1, 1)
         for k in range(CHIPS):
             both = [terms_a[8 * k : 8 * k + 8, cols], terms_b[8 * k : 8 * k + 8]]
             outs[k][:, cols] = jnp.concatenate(both, axis=0).astype(outs[k].dtype)
 
 
 def second_tick_kernel(*refs):
-    blocks, pre_a, pre_b, weights = refs[:4], refs[4], refs[5], refs[6:12]
-    outs, held = refs[12:16], refs[16]
-    gates, ups, downs = weights[0:2], weights[2:4], weights[4:6]
+    blocks, pre_a, pre_b, wide, downs = refs[:4], *refs[4:8]
+    outs, held = refs[8:12], refs[12]
     for k in range(CHIPS):
         held[16 * k : 16 * k + 16, :] = blocks[k][:, 0:D]
-    rows = held[...]
-    hidden = [dot(rows, w[...], 1, 1) for w in downs]
+    hidden = dot(held[...], downs[...], 1, 1)
     pre = jnp.concatenate(
         [p[8 * k : 8 * k + 8, :] for k in range(CHIPS) for p in (pre_a, pre_b)], axis=0
     )
-    parts = [pre[:, HID * i : HID * i + HID] for i in range(4)]
-    operands = (*differentials(hidden, parts[0:2], parts[2:4]), gates, ups)
+    operand = differentials(hidden, pre[:, 0 : 2 * HID], pre[:, 2 * HID :])
     for low in range(0, D, WIDTH):
         cols = pl.ds(low, WIDTH)
-        total = terms_of(*operands, cols)
+        total = dot(operand, wide[cols, :], 1, 1)
         for k in range(CHIPS):
             outs[k][:, cols] = total[16 * k : 16 * k + 16].astype(outs[k].dtype)
 
@@ -320,14 +308,16 @@
     weights = [w_gate, other_gate, w_up, other_up, w_down, other_down]
     rows = [pltpu.VMEM((96, D), BF16)]
 
-    terms_a, pre_a, ids_a = call(
-        first_a_kernel, [((32, D), F32), ((32, 4 * HID), F32), ((64, IDCOLS), BF16)],
+    terms_a, pre_a, ids_a, wide, downs = call(
+        first_a_kernel,
+        [((32, D), F32), ((32, 4 * HID), F32), ((64, IDCOLS), BF16)]
+        + [((D, 4 * HID), BF16), ((2 * HID, D), BF16)],
         blocks_a + weights, rows, 2 * 96 * D * 128 * 8,
     )
     sends = [((16, D), F32)] + [((16, D), BF16)] * 3
     *terms, pre_b, ids_b = call(
         first_b_kernel, sends + [((32, 4 * HID), F32), ((64, IDCOLS), BF16)],
-        blocks_b + weights + [terms_a], rows, 2 * 96 * D * 128 * 8,
+        blocks_b + [wide, downs, terms_a], rows, 2 * 96 * D * 128 * 8,
     )
     other_router = swapped(after(router, terms[0]))
     other_ids = swapped(jnp.concatenate([ids_a, ids_b], axis=0))
@@ -343,7 +333,7 @@
     grads = jnp.where(section == top, head, moved)
     gathered = ring(jnp.concatenate([grads, stats], axis=1))
     terms = call(
-        second_tick_kernel, sends, gathered + [pre_a, pre_b] + weights, [pltpu.VMEM((64, D), BF16)],
+        second_tick_kernel, sends, gathered + [pre_a, pre_b, wide, downs], [pltpu.VMEM((64, D), BF16)],
         2 * 64 * D * 128 * 6,
     )
     own, other = call(

time: 155 us -> 159 us (1.026)
  local copies, waits for them, and re-layouts: 1.37 us -> 13.2 us
  starting transfers between devices: 90.3 us -> 82.8 us
  Pallas kernels: 20.7 us -> 16.1 us
  waiting for transfers between devices: 37.6 us -> 41.6 us
    unnamed x39 -> x43, local copies, waits for them, and re-layouts: 0.74 us -> 12.6 us
    ppermute x15, starting transfers between devices: 53.5 us -> 46.1 us  [from_chip(): lax.ppermute(value, 'expert', [((e + 2 * k) % 8, e) for e in range(8)])]
    pallas_call x5, Pallas kernels: 17.3 us -> 12.7 us  [call(): pl.pallas_call(body, out_shape=[jax.ShapeDtypeStruct(shape, dtype) for sh...]
    ppermute x15, waiting for transfers between devices: 13.7 us -> 16.1 us  [from_chip(): lax.ppermute(value, 'expert', [((e + 2 * k) % 8, e) for e in range(8)])]
    ppermute x1, waiting for transfers between devices: 12.3 us -> 14.7 us  [shards(): moved = lax.ppermute(out, 'pipe', [(i, i - 1) for i in range(1, top + 1)])]
  transfers between devices with their start and end apart: 24 -> 24, of which waited for: 9 -> 8; matrix products, arithmetic and copies ran while one was open for 2% -> 2% of each run, Pallas kernels for 7% -> 6%
where the time goes in v11:
time: 159 us; the launch traced here: 158 us
  starting transfers between devices  82.8 us (52%)
  waiting for transfers between devices  41.6 us (26%)
  Pallas kernels  16.1 us (10%)
  local copies, waits for them, and re-layouts  13.2 us (8%)
  other arithmetic  3.21 us (2%)
    ppermute x15, starting transfers between devices, from_chip(): lax.ppermute(value, 'expert', [((e + 2 * k) % 8, e) for e in range(8)])  46.1 us
    ppermute x2, starting transfers between devices, mirrored(): lax.ppermute(value, 'pipe', [(i, count - 1 - i) for i in range(count)])  21.5 us
    ppermute x15, waiting for transfers between devices, from_chip(): lax.ppermute(value, 'expert', [((e + 2 * k) % 8, e) for e in range(8)])  16.1 us
    ppermute x1, waiting for transfers between devices, shards(): moved = lax.ppermute(out, 'pipe', [(i, i - 1) for i in range(1, top + 1)])  14.7 us
    pallas_call x5, Pallas kernels, call(): pl.pallas_call(body, out_shape=[jax.ShapeDtypeStruct(shape, dtype) for sh...  12.7 us
    unnamed x43, local copies, waits for them, and re-layouts  12.6 us
    ppermute x6, starting transfers between devices, swapped(): return lax.ppermute(value, 'expert', [(e, e ^ 1) for e in range(8)])  12.5 us
    ppermute x2, waiting for transfers between devices, mirrored(): lax.ppermute(value, 'pipe', [(i, count - 1 - i) for i in range(count)])  10.8 us
  transfers between devices with their start and end apart: 24, of which 8 were waited for; matrix products, arithmetic and copies ran while one was open for 2% of the time, Pallas kernels for 6%

profile of v11, /device:TPU:6, one launch (start us, length us, event | category | flops | bytes accessed | tf_op | source)
XLA Modules:
  0.0 158.0 jit_solution(12923303217994315676)
XLA Ops:
  0.6 1.7 %shard_map.139 = bf16[3,8,3712]{2,1,0:T(8,128)(2,1)} custom-call(bf16[2,8,3584]{2,1,0:T(8,128)(2,1)} %bitcast.29, bf16[8,3584]{1,0:T(8,128)(2,1)} %bitcast.32, s32[2,8,8]{2,1,0:T(8,128)} %bitcast.35), custom_call_target="tpu_custom_call" | custom-call | tf_op jit(solution)/shard_map/pallas_call | solution.py:73
  2.3 15.1 %collective-permute-start = (bf16[3,8,3712]{2,1,0:T(8,128)(2,1)}, bf16[3,8,3712]{2,1,0:T(8,128)(2,1)S(1)}, u32[]{:S(2)}, u32[]{:S(2)}) collective-permute-start(bf16[3,8,3712]{2,1,0:T(8,128)(2,1)} %shard_map.139), channel_id=1, source_target_pairs={{0,504},{8,496},{16,488},{24,480},{32,472},{40,464},{48,456},{56,4... | collective-permute-start | bytes 534536 | tf_op jit(solution)/shard_map/ppermute | solution.py:268
  17.4 1.9 %collective-permute-start.1 = (bf16[3584,128]{1,0:T(8,128)(2,1)}, bf16[3584,128]{1,0:T(8,128)(2,1)S(1)}, u32[]{:S(2)}, u32[]{:S(2)}) collective-permute-start(bf16[3584,128]{1,0:T(8,128)(2,1)} %bitcast.18), channel_id=1, source_target_pairs={{0,1},{1,0},{2,3},{3,2},{4,5},{5,4},{6,7},{7,6},{8,9},{9,8},{10,11... | collective-permute-start | bytes 2752520 | tf_op jit(solution)/shard_map/ppermute | solution.py:263
  19.4 2.4 %collective-permute-start.2 = (bf16[3584,128]{1,0:T(8,128)(2,1)}, bf16[3584,128]{1,0:T(8,128)(2,1)S(1)}, u32[]{:S(2)}, u32[]{:S(2)}) collective-permute-start(bf16[3584,128]{1,0:T(8,128)(2,1)} %bitcast.20), channel_id=1, source_target_pairs={{0,1},{1,0},{2,3},{3,2},{4,5},{5,4},{6,7},{7,6},{8,9},{9,8},{10,11... | collective-permute-start | bytes 2752520 | tf_op jit(solution)/shard_map/ppermute | solution.py:263
  21.8 1.9 %collective-permute-start.3 = (bf16[128,3584]{1,0:T(8,128)(2,1)}, bf16[128,3584]{1,0:T(8,128)(2,1)}, u32[]{:S(2)}, u32[]{:S(2)}) collective-permute-start(bf16[128,3584]{1,0:T(8,128)(2,1)} %bitcast.22), channel_id=1, source_target_pairs={{0,1},{1,0},{2,3},{3,2},{4,5},{5,4},{6,7},{7,6},{8,9},{9,8},{10,11... | collective-permute-start | bytes 2752520 | tf_op jit(solution)/shard_map/ppermute | solution.py:263
  23.7 1.7 %shard_map.141.refs_0_ = bf16[3,8,3712]{2,1,0:T(8,128)(2,1)} custom-call(bf16[2,8,3584]{2,1,0:T(8,128)(2,1)} %bitcast.30, bf16[8,3584]{1,0:T(8,128)(2,1)} %bitcast.27, s32[2,8,8]{2,1,0:T(8,128)} %bitcast.36), custom_call_target="tpu_custom_call" | custom-call | tf_op jit(solution)/shard_map/pallas_call | solution.py:73
  25.4 3.8 %collective-permute-start.7 = (bf16[3,8,3712]{2,1,0:T(8,128)(2,1)}, bf16[3,8,3712]{2,1,0:T(8,128)(2,1)S(1)}, u32[]{:S(2)}, u32[]{:S(2)}) collective-permute-start(bf16[3,8,3712]{2,1,0:T(8,128)(2,1)} %shard_map.141.refs_0_), channel_id=1, source_target_pairs={{2,0},{3,1},{4,2},{5,3},{6,4},{7,5},{0,6},{1,7},{10,8},{11,9},{12,... | collective-permute-start | bytes 534536 | tf_op jit(solution)/shard_map/ppermute | solution.py:272
  29.2 3.7 %collective-permute-done.value = bf16[3,8,3712]{2,1,0:T(8,128)(2,1)S(1)} collective-permute-done((bf16[3,8,3712]{2,1,0:T(8,128)(2,1)}, bf16[3,8,3712]{2,1,0:T(8,128)(2,1)S(1)}, u32[]{:S(2)}, u32[]{:S(2)}) %collective-permute-start) | collective-permute-done | bytes 178208 | tf_op jit(solution)/shard_map/ppermute | solution.py:268
  33.0 1.9 %collective-permute-start.8 = (bf16[3,8,3712]{2,1,0:T(8,128)(2,1)}, bf16[3,8,3712]{2,1,0:T(8,128)(2,1)S(1)}, u32[]{:S(2)}, u32[]{:S(2)}) collective-permute-start(bf16[3,8,3712]{2,1,0:T(8,128)(2,1)} %shard_map.141.refs_0_), channel_id=1, source_target_pairs={{4,0},{5,1},{6,2},{7,3},{0,4},{1,5},{2,6},{3,7},{12,8},{13,9},{14,... | collective-permute-start | bytes 534536 | tf_op jit(solution)/shard_map/ppermute | solution.py:272
  35.5 5.1 %collective-permute-start.9 = (bf16[3,8,3712]{2,1,0:T(8,128)(2,1)}, bf16[3,8,3712]{2,1,0:T(8,128)(2,1)S(1)}, u32[]{:S(2)}, u32[]{:S(2)}) collective-permute-start(bf16[3,8,3712]{2,1,0:T(8,128)(2,1)} %shard_map.141.refs_0_), channel_id=1, source_target_pairs={{6,0},{7,1},{0,2},{1,3},{2,4},{3,5},{4,6},{5,7},{14,8},{15,9},{8,1... | collective-permute-start | bytes 534536 | tf_op jit(solution)/shard_map/ppermute | solution.py:272
  40.7 0.9 copy-done.10
  41.6 2.8 %collective-permute-start.4 = (bf16[3,8,3712]{2,1,0:T(8,128)(2,1)}, bf16[3,8,3712]{2,1,0:T(8,128)(2,1)S(1)}, u32[]{:S(2)}, u32[]{:S(2)}) collective-permute-start(bf16[3,8,3712]{2,1,0:T(8,128)(2,1)} %shard_map.140.refs_0_.refs_4_), channel_id=1, source_target_pairs={{2,0},{3,1},{4,2},{5,3},{6,4},{7,5},{0,6},{1,7},{10,8},{11,9},{12,... | collective-permute-start | bytes 534536 | tf_op jit(solution)/shard_map/ppermute | solution.py:272
  44.4 3.0 %collective-permute-start.5 = (bf16[3,8,3712]{2,1,0:T(8,128)(2,1)}, bf16[3,8,3712]{2,1,0:T(8,128)(2,1)S(1)}, u32[]{:S(2)}, u32[]{:S(2)}) collective-permute-start(bf16[3,8,3712]{2,1,0:T(8,128)(2,1)} %shard_map.140.refs_0_.refs_4_), channel_id=1, source_target_pairs={{4,0},{5,1},{6,2},{7,3},{0,4},{1,5},{2,6},{3,7},{12,8},{13,9},{14,... | collective-permute-start | bytes 534536 | tf_op jit(solution)/shard_map/ppermute | solution.py:272
  47.4 2.1 %collective-permute-start.6 = (bf16[3,8,3712]{2,1,0:T(8,128)(2,1)}, bf16[3,8,3712]{2,1,0:T(8,128)(2,1)S(1)}, u32[]{:S(2)}, u32[]{:S(2)}) collective-permute-start(bf16[3,8,3712]{2,1,0:T(8,128)(2,1)} %shard_map.140.refs_0_.refs_4_), channel_id=1, source_target_pairs={{6,0},{7,1},{0,2},{1,3},{2,4},{3,5},{4,6},{5,7},{14,8},{15,9},{8,1... | collective-permute-start | bytes 534536 | tf_op jit(solution)/shard_map/ppermute | solution.py:272
  49.7 1.2 copy-done.5
  50.9 1.2 copy-done.6
  52.1 1.2 copy-done.7
  53.2 1.2 copy-done.9
  54.4 1.2 copy-done.11
  55.6 4.3 %shard_map.142 = (f32[32,3584]{1,0:T(8,128)S(1)}, f32[32,512]{1,0:T(8,128)S(1)}, bf16[64,128]{1,0:T(8,128)(2,1)S(1)}, bf16[3584,512]{1,0:T(8,128)(2,1)S(1)}, bf16[256,3584]{1,0:T(8,128)(2,1)S(1)}) custom-call(bf16[3,8,3712]{2,1,0:T(8,128)(2,1)S(1)} %copy-done.2, bf16[3,8,3712]{2,1,0:T(8,128)(2,1)S(1)} %collective-permute-done.7.refs_1_, ...), custom_call_target="tpu_custom_call" | custom-call | flops 704643072 | bytes 6217728 | tf_op jit(solution)/shard_map/pallas_call | solution.py:37
  60.0 4.9 %collective-permute-done.5.refs_2_.refs_6_ = bf16[3,8,3712]{2,1,0:T(8,128)(2,1)S(1)} collective-permute-done((bf16[3,8,3712]{2,1,0:T(8,128)(2,1)}, bf16[3,8,3712]{2,1,0:T(8,128)(2,1)S(1)}, u32[]{:S(2)}, u32[]{:S(2)}) %collective-permute-start.5) | collective-permute-done | bytes 178208 | tf_op jit(solution)/shard_map/ppermute | solution.py:272
  64.8 3.0 %shard_map.143 = (f32[16,3584]{1,0:T(8,128)S(1)}, bf16[16,3584]{1,0:T(8,128)(2,1)S(1)}, bf16[16,3584]{1,0:T(8,128)(2,1)S(1)}, bf16[16,3584]{1,0:T(8,128)(2,1)S(1...) custom-call(bf16[3,8,3712]{2,1,0:T(8,128)(2,1)S(1)} %copy-done.4, ...), custom_call_target="tpu_custom_call" | custom-call | flops 704643072 | bytes 6676480 | tf_op jit(solution)/shard_map/pallas_call | solution.py:37
  67.9 1.9 %collective-permute-start.10 = (bf16[16,3584]{1,0:T(8,128)(2,1)S(1)}, bf16[16,3584]{1,0:T(8,128)(2,1)S(1)}, u32[]{:S(2)}, u32[]{:S(2)}) collective-permute-start(bf16[16,3584]{1,0:T(8,128)(2,1)S(1)} %get-tuple-element.33), channel_id=1, source_target_pairs={{2,0},{3,1},{4,2},{5,3},{6,4},{7,5},{0,6},{1,7},{10,8},{11,9},{12,... | collective-permute-start | bytes 344072 | tf_op jit(solution)/shard_map/ppermute | solution.py:272
  69.8 5.0 %collective-permute-start.11 = (bf16[16,3584]{1,0:T(8,128)(2,1)S(1)}, bf16[16,3584]{1,0:T(8,128)(2,1)S(1)}, u32[]{:S(2)}, u32[]{:S(2)}) collective-permute-start(bf16[16,3584]{1,0:T(8,128)(2,1)S(1)} %get-tuple-element.34), channel_id=1, source_target_pairs={{4,0},{5,1},{6,2},{7,3},{0,4},{1,5},{2,6},{3,7},{12,8},{13,9},{14,... | collective-permute-start | bytes 344072 | tf_op jit(solution)/shard_map/ppermute | solution.py:272
  74.8 3.9 %collective-permute-start.12 = (bf16[16,3584]{1,0:T(8,128)(2,1)S(1)}, bf16[16,3584]{1,0:T(8,128)(2,1)S(1)}, u32[]{:S(2)}, u32[]{:S(2)}) collective-permute-start(bf16[16,3584]{1,0:T(8,128)(2,1)S(1)} %get-tuple-element.35), channel_id=1, source_target_pairs={{6,0},{7,1},{0,2},{1,3},{2,4},{3,5},{4,6},{5,7},{14,8},{15,9},{8,1... | collective-permute-start | bytes 344072 | tf_op jit(solution)/shard_map/ppermute | solution.py:272
  78.8 1.9 %collective-permute-start.13 = (bf16[128,128]{1,0:T(8,128)(2,1)S(1)}, bf16[128,128]{1,0:T(8,128)(2,1)S(1)}, u32[]{:S(2)}, u32[]{:S(2)}) collective-permute-start(bf16[128,128]{1,0:T(8,128)(2,1)S(1)} %pad_maximum_fusion.1), channel_id=1, source_target_pairs={{0,1},{1,0},{2,3},{3,2},{4,5},{5,4},{6,7},{7,6},{8,9},{9,8},{10,11... | collective-permute-start | bytes 98312 | tf_op jit(solution)/shard_map/ppermute | solution.py:263
  80.7 2.4 %collective-permute-start.15 = (bf16[32,3584]{1,0:T(8,128)(2,1)S(1)}, bf16[32,3584]{1,0:T(8,128)(2,1)}, u32[]{:S(2)}, u32[]{:S(2)}) collective-permute-start(bf16[32,3584]{1,0:T(8,128)(2,1)S(1)} %bitcast.24), channel_id=1, source_target_pairs={{0,1},{1,0},{2,3},{3,2},{4,5},{5,4},{6,7},{7,6},{8,9},{9,8},{10,11... | collective-permute-start | bytes 688136 | tf_op jit(solution)/shard_map/ppermute | solution.py:263
  84.8 2.8 %collective-permute-start.14 = (bf16[16,3584]{1,0:T(8,128)(2,1)}, bf16[16,3584]{1,0:T(8,128)(2,1)}, u32[]{:S(2)}, u32[]{:S(2)}) collective-permute-start(bf16[16,3584]{1,0:T(8,128)(2,1)} %add_convert_fusion), channel_id=1, source_target_pairs={{8,0},{16,8},{24,16},{32,24},{40,32},{48,40},{56,48},{64,56},{72,6... | collective-permute-start | bytes 344072 | tf_op jit(solution)/shard_map/ppermute | solution.py:326
  87.7 0.7 copy-done.18
  88.4 2.3 %shard_map.144 = (f32[64,256]{1,0:T(8,128)S(1)}, f32[64,256]{1,0:T(8,128)S(1)}, bf16[16,128]{1,0:T(8,128)(2,1)S(1)}) custom-call(bf16[3,8,3712]{2,1,0:T(8,128)(2,1)S(1)} %copy-done.2, bf16[3,8,3712]{2,1,0:T(8,128)(2,1)S(1)} %collective-permute-done.7.refs_1_, bf16[3,8,3712]{2,1,0:T(8,128)(2,1)S(1)} %collective-permute-done.8.refs_2_, ...), custom_call_target="tpu_custom_call" | custom-call | flops 117440512 | bytes 1949696 | tf_op jit(solution)/shard_map/pallas_call | solution.py:37
  90.7 14.7 %collective-permute-done.14 = bf16[16,3584]{1,0:T(8,128)(2,1)} collective-permute-done((bf16[16,3584]{1,0:T(8,128)(2,1)}, bf16[16,3584]{1,0:T(8,128)(2,1)}, u32[]{:S(2)}, u32[]{:S(2)}) %collective-permute-start.14) | collective-permute-done | bytes 114720 | tf_op jit(solution)/shard_map/ppermute | solution.py:326
  105.4 1.0 maximum_select_fusion
  106.4 1.9 %collective-permute-start.16 = (bf16[16,3712]{1,0:T(8,128)(2,1)S(1)}, bf16[16,3712]{1,0:T(8,128)(2,1)S(1)}, u32[]{:S(2)}, u32[]{:S(2)}) collective-permute-start(bf16[16,3712]{1,0:T(8,128)(2,1)S(1)} %pad_maximum_fusion.refs_0_.refs_10_), channel_id=1, source_target_pairs={{2,0},{3,1},{4,2},{5,3},{6,4},{7,5},{0,6},{1,7},{10,8},{11,9},{12,... | collective-permute-start | bytes 356360 | tf_op jit(solution)/shard_map/ppermute | solution.py:272
  108.3 1.9 %collective-permute-start.17 = (bf16[16,3712]{1,0:T(8,128)(2,1)S(1)}, bf16[16,3712]{1,0:T(8,128)(2,1)S(1)}, u32[]{:S(2)}, u32[]{:S(2)}) collective-permute-start(bf16[16,3712]{1,0:T(8,128)(2,1)S(1)} %pad_maximum_fusion.refs_0_.refs_10_), channel_id=1, source_target_pairs={{4,0},{5,1},{6,2},{7,3},{0,4},{1,5},{2,6},{3,7},{12,8},{13,9},{14,... | collective-permute-start | bytes 356360 | tf_op jit(solution)/shard_map/ppermute | solution.py:272
  110.2 3.9 %collective-permute-start.18 = (bf16[16,3712]{1,0:T(8,128)(2,1)S(1)}, bf16[16,3712]{1,0:T(8,128)(2,1)S(1)}, u32[]{:S(2)}, u32[]{:S(2)}) collective-permute-start(bf16[16,3712]{1,0:T(8,128)(2,1)S(1)} %pad_maximum_fusion.refs_0_.refs_10_), channel_id=1, source_target_pairs={{6,0},{7,1},{0,2},{1,3},{2,4},{3,5},{4,6},{5,7},{14,8},{15,9},{8,1... | collective-permute-start | bytes 356360 | tf_op jit(solution)/shard_map/ppermute | solution.py:272
  114.2 7.0 %collective-permute-done.17.refs_2_.refs_12_ = bf16[16,3712]{1,0:T(8,128)(2,1)S(1)} collective-permute-done((bf16[16,3712]{1,0:T(8,128)(2,1)S(1)}, bf16[16,3712]{1,0:T(8,128)(2,1)S(1)}, u32[]{:S(2)}, u32[]{:S(2)}) %collective-permute-start.17) | collective-permute-done | bytes 118816 | tf_op jit(solution)/shard_map/ppermute | solution.py:272
  121.2 2.0 %copy-done.1 = bf16[3584,512]{1,0:T(8,128)(2,1)S(1)} copy-done((bf16[3584,512]{1,0:T(8,128)(2,1)S(1)}, bf16[3584,512]{1,0:T(8,128)(2,1)}, u32[]{:S(2)}) %copy-start.1) | copy-done | bytes 3670040
  123.2 0.8 copy-done.14
  124.0 0.8 copy-done.16
  124.9 2.5 %shard_map.145 = (f32[16,3584]{1,0:T(8,128)S(1)}, bf16[16,3584]{1,0:T(8,128)(2,1)S(1)}, bf16[16,3584]{1,0:T(8,128)(2,1)S(1)}, bf16[16,3584]{1,0:T(8,128)(2,1)S(1)}) custom-call(bf16[16,3712]{1,0:T(8,128)(2,1)S(1)} %pad_maximum_fusion.refs_0_.refs_10_, bf16[16,3712]{1,0:T(8,128)(2,1)S(1)} %collective-permute-done.16.refs_1_.refs_11_, ...), custom_call_target="tpu_custom_call" | custom-call | flops 352321536 | bytes 6111232 | tf_op jit(solution)/shard_map/pallas_call | solution.py:37
  127.4 3.7 %collective-permute-start.19 = (bf16[16,3584]{1,0:T(8,128)(2,1)S(1)}, bf16[16,3584]{1,0:T(8,128)(2,1)S(1)}, u32[]{:S(2)}, u32[]{:S(2)}) collective-permute-start(bf16[16,3584]{1,0:T(8,128)(2,1)S(1)} %get-tuple-element.44), channel_id=1, source_target_pairs={{2,0},{3,1},{4,2},{5,3},{6,4},{7,5},{0,6},{1,7},{10,8},{11,9},{12,... | collective-permute-start | bytes 344072 | tf_op jit(solution)/shard_map/ppermute | solution.py:272
  131.1 1.9 %collective-permute-start.20 = (bf16[16,3584]{1,0:T(8,128)(2,1)S(1)}, bf16[16,3584]{1,0:T(8,128)(2,1)S(1)}, u32[]{:S(2)}, u32[]{:S(2)}) collective-permute-start(bf16[16,3584]{1,0:T(8,128)(2,1)S(1)} %get-tuple-element.45), channel_id=1, source_target_pairs={{4,0},{5,1},{6,2},{7,3},{0,4},{1,5},{2,6},{3,7},{12,8},{13,9},{14,... | collective-permute-start | bytes 344072 | tf_op jit(solution)/shard_map/ppermute | solution.py:272
  133.1 3.1 %collective-permute-start.21 = (bf16[16,3584]{1,0:T(8,128)(2,1)S(1)}, bf16[16,3584]{1,0:T(8,128)(2,1)S(1)}, u32[]{:S(2)}, u32[]{:S(2)}) collective-permute-start(bf16[16,3584]{1,0:T(8,128)(2,1)S(1)} %get-tuple-element.46), channel_id=1, source_target_pairs={{6,0},{7,1},{0,2},{1,3},{2,4},{3,5},{4,6},{5,7},{14,8},{15,9},{8,1... | collective-permute-start | bytes 344072 | tf_op jit(solution)/shard_map/ppermute | solution.py:272
  136.8 1.9 %collective-permute-start.23 = (f32[32,3584]{1,0:T(8,128)S(1)}, f32[32,3584]{1,0:T(8,128)S(1)}, u32[]{:S(2)}, u32[]{:S(2)}) collective-permute-start(f32[32,3584]{1,0:T(8,128)S(1)} %get-tuple-element.51), channel_id=1, source_target_pairs={{0,1},{1,0},{2,3},{3,2},{4,5},{5,4},{6,7},{7,6},{8,9},{9,8},{10,11... | collective-permute-start | bytes 1376264 | tf_op jit(solution)/shard_map/ppermute | solution.py:263
  138.7 3.7 %collective-permute-done.20 = bf16[16,3584]{1,0:T(8,128)(2,1)S(1)} collective-permute-done((bf16[16,3584]{1,0:T(8,128)(2,1)S(1)}, bf16[16,3584]{1,0:T(8,128)(2,1)S(1)}, u32[]{:S(2)}, u32[]{:S(2)}) %collective-permute-start.20) | collective-permute-done | bytes 114720 | tf_op jit(solution)/shard_map/ppermute | solution.py:272
  143.1 6.4 %collective-permute-start.22 = (bf16[8,3584]{1,0:T(8,128)(2,1)S(1)}, bf16[8,3584]{1,0:T(8,128)(2,1)S(1)}, u32[]{:S(2)}, u32[]{:S(2)}) collective-permute-start(bf16[8,3584]{1,0:T(8,128)(2,1)S(1)} %get-tuple-element.53), channel_id=1, source_target_pairs={{0,504},{8,496},{16,488},{24,480},{32,472},{40,464},{48,456},{56,4... | collective-permute-start | bytes 172040 | tf_op jit(solution)/shard_map/ppermute | solution.py:268
  149.5 0.8 add.51
  150.3 7.1 %collective-permute-done.22 = bf16[8,3584]{1,0:T(8,128)(2,1)S(1)} collective-permute-done((bf16[8,3584]{1,0:T(8,128)(2,1)S(1)}, bf16[8,3584]{1,0:T(8,128)(2,1)S(1)}, u32[]{:S(2)}, u32[]{:S(2)}) %collective-permute-start.22) | collective-permute-done | bytes 57376 | tf_op jit(solution)/shard_map/ppermute | solution.py:268
  (58 shorter events, 4.6 us)
Async XLA Ops:
  2.3 30.7 %collective-permute-start = (bf16[3,8,3712]{2,1,0:T(8,128)(2,1)}, bf16[3,8,3712]{2,1,0:T(8,128)(2,1)S(1)}, u32[]{:S(2)}, u32[]{:S(2)}) collective-permute-start(bf16[3,8,3712]{2,1,0:T(8,128)(2,1)} %shard_map.139), channel_id=1, source_target_pairs={{0,504},{8,496},{16,488},{24,480},{32,472},{40,464},{48,456},{56,4... | collective-permute-start | bytes 534536 | tf_op jit(solution)/shard_map/ppermute | solution.py:268
  17.4 18.1 %collective-permute-start.1 = (bf16[3584,128]{1,0:T(8,128)(2,1)}, bf16[3584,128]{1,0:T(8,128)(2,1)S(1)}, u32[]{:S(2)}, u32[]{:S(2)}) collective-permute-start(bf16[3584,128]{1,0:T(8,128)(2,1)} %bitcast.18), channel_id=1, source_target_pairs={{0,1},{1,0},{2,3},{3,2},{4,5},{5,4},{6,7},{7,6},{8,9},{9,8},{10,11... | collective-permute-start | bytes 2752520 | tf_op jit(solution)/shard_map/ppermute | solution.py:263
  19.4 21.3 %collective-permute-start.2 = (bf16[3584,128]{1,0:T(8,128)(2,1)}, bf16[3584,128]{1,0:T(8,128)(2,1)S(1)}, u32[]{:S(2)}, u32[]{:S(2)}) collective-permute-start(bf16[3584,128]{1,0:T(8,128)(2,1)} %bitcast.20), channel_id=1, source_target_pairs={{0,1},{1,0},{2,3},{3,2},{4,5},{5,4},{6,7},{7,6},{8,9},{9,8},{10,11... | collective-permute-start | bytes 2752520 | tf_op jit(solution)/shard_map/ppermute | solution.py:263
  21.8 18.9 %collective-permute-start.3 = (bf16[128,3584]{1,0:T(8,128)(2,1)}, bf16[128,3584]{1,0:T(8,128)(2,1)}, u32[]{:S(2)}, u32[]{:S(2)}) collective-permute-start(bf16[128,3584]{1,0:T(8,128)(2,1)} %bitcast.22), channel_id=1, source_target_pairs={{0,1},{1,0},{2,3},{3,2},{4,5},{5,4},{6,7},{7,6},{8,9},{9,8},{10,11... | collective-permute-start | bytes 2752520 | tf_op jit(solution)/shard_map/ppermute | solution.py:263
  25.4 22.0 %collective-permute-start.7 = (bf16[3,8,3712]{2,1,0:T(8,128)(2,1)}, bf16[3,8,3712]{2,1,0:T(8,128)(2,1)S(1)}, u32[]{:S(2)}, u32[]{:S(2)}) collective-permute-start(bf16[3,8,3712]{2,1,0:T(8,128)(2,1)} %shard_map.141.refs_0_), channel_id=1, source_target_pairs={{2,0},{3,1},{4,2},{5,3},{6,4},{7,5},{0,6},{1,7},{10,8},{11,9},{12,... | collective-permute-start | bytes 534536 | tf_op jit(solution)/shard_map/ppermute | solution.py:272
  33.0 7.7 %copy-start.3 = (bf16[3,8,3712]{2,1,0:T(8,128)(2,1)}, bf16[3,8,3712]{2,1,0:T(8,128)(2,1)S(1)}, u32[]{:S(2)}) copy-start(bf16[3,8,3712]{2,1,0:T(8,128)(2,1)S(1)} %collective-permute-done.value) | copy-start | bytes 534532
  33.0 16.7 %collective-permute-start.8 = (bf16[3,8,3712]{2,1,0:T(8,128)(2,1)}, bf16[3,8,3712]{2,1,0:T(8,128)(2,1)S(1)}, u32[]{:S(2)}, u32[]{:S(2)}) collective-permute-start(bf16[3,8,3712]{2,1,0:T(8,128)(2,1)} %shard_map.141.refs_0_), channel_id=1, source_target_pairs={{4,0},{5,1},{6,2},{7,3},{0,4},{1,5},{2,6},{3,7},{12,8},{13,9},{14,... | collective-permute-start | bytes 534536 | tf_op jit(solution)/shard_map/ppermute | solution.py:272
  35.5 14.2 %copy-start.2 = (bf16[3,8,3712]{2,1,0:T(8,128)(2,1)S(1)}, bf16[3,8,3712]{2,1,0:T(8,128)(2,1)}, u32[]{:S(2)}) copy-start(bf16[3,8,3712]{2,1,0:T(8,128)(2,1)} %shard_map.141.refs_0_) | copy-start | bytes 534532
  35.5 5.2 %copy-start.8 = (bf16[3584,128]{1,0:T(8,128)(2,1)}, bf16[3584,128]{1,0:T(8,128)(2,1)S(1)}, u32[]{:S(2)}) copy-start(bf16[3584,128]{1,0:T(8,128)(2,1)S(1)} %collective-permute-done.1.refs_5_) | copy-start | bytes 2752516
  35.5 14.2 %collective-permute-start.9 = (bf16[3,8,3712]{2,1,0:T(8,128)(2,1)}, bf16[3,8,3712]{2,1,0:T(8,128)(2,1)S(1)}, u32[]{:S(2)}, u32[]{:S(2)}) collective-permute-start(bf16[3,8,3712]{2,1,0:T(8,128)(2,1)} %shard_map.141.refs_0_), channel_id=1, source_target_pairs={{6,0},{7,1},{0,2},{1,3},{2,4},{3,5},{4,6},{5,7},{14,8},{15,9},{8,1... | collective-permute-start | bytes 534536 | tf_op jit(solution)/shard_map/ppermute | solution.py:272
  40.7 0.9 copy-start.10
  41.6 23.2 %copy-start.4 = (bf16[3,8,3712]{2,1,0:T(8,128)(2,1)S(1)}, bf16[3,8,3712]{2,1,0:T(8,128)(2,1)}, u32[]{:S(2)}) copy-start(bf16[3,8,3712]{2,1,0:T(8,128)(2,1)} %shard_map.140.refs_0_.refs_4_) | copy-start | bytes 534532
  41.6 18.3 %collective-permute-start.4 = (bf16[3,8,3712]{2,1,0:T(8,128)(2,1)}, bf16[3,8,3712]{2,1,0:T(8,128)(2,1)S(1)}, u32[]{:S(2)}, u32[]{:S(2)}) collective-permute-start(bf16[3,8,3712]{2,1,0:T(8,128)(2,1)} %shard_map.140.refs_0_.refs_4_), channel_id=1, source_target_pairs={{2,0},{3,1},{4,2},{5,3},{6,4},{7,5},{0,6},{1,7},{10,8},{11,9},{12,... | collective-permute-start | bytes 534536 | tf_op jit(solution)/shard_map/ppermute | solution.py:272
  44.4 20.4 %collective-permute-start.5 = (bf16[3,8,3712]{2,1,0:T(8,128)(2,1)}, bf16[3,8,3712]{2,1,0:T(8,128)(2,1)S(1)}, u32[]{:S(2)}, u32[]{:S(2)}) collective-permute-start(bf16[3,8,3712]{2,1,0:T(8,128)(2,1)} %shard_map.140.refs_0_.refs_4_), channel_id=1, source_target_pairs={{4,0},{5,1},{6,2},{7,3},{0,4},{1,5},{2,6},{3,7},{12,8},{13,9},{14,... | collective-permute-start | bytes 534536 | tf_op jit(solution)/shard_map/ppermute | solution.py:272
  47.4 17.4 %collective-permute-start.6 = (bf16[3,8,3712]{2,1,0:T(8,128)(2,1)}, bf16[3,8,3712]{2,1,0:T(8,128)(2,1)S(1)}, u32[]{:S(2)}, u32[]{:S(2)}) collective-permute-start(bf16[3,8,3712]{2,1,0:T(8,128)(2,1)} %shard_map.140.refs_0_.refs_4_), channel_id=1, source_target_pairs={{6,0},{7,1},{0,2},{1,3},{2,4},{3,5},{4,6},{5,7},{14,8},{15,9},{8,1... | collective-permute-start | bytes 534536 | tf_op jit(solution)/shard_map/ppermute | solution.py:272
  49.7 1.2 copy-start.5
  50.9 1.2 copy-start.6
  52.1 1.2 copy-start.7
  53.2 1.2 copy-start.9
  54.4 1.2 copy-start.11
  59.9 24.3 %copy-start = (bf16[3584,512]{1,0:T(8,128)(2,1)}, bf16[3584,512]{1,0:T(8,128)(2,1)S(1)}, u32[]{:S(2)}) copy-start(bf16[3584,512]{1,0:T(8,128)(2,1)S(1)} %get-tuple-element.29.refs_4_.refs_6_) | copy-start | bytes 11010052
  59.9 24.3 %copy-start.13 = (f32[32,512]{1,0:T(8,128)}, f32[32,512]{1,0:T(8,128)S(1)}, u32[]{:S(2)}) copy-start(f32[32,512]{1,0:T(8,128)S(1)} %get-tuple-element.41.refs_4_) | copy-start | bytes 196612
  59.9 20.8 %copy-start.12 = (bf16[1,32,3584]{2,1,0:T(8,128)(2,1)S(1)}, bf16[1,32,3584]{2,1,0:T(8,128)(2,1)}, u32[]{:S(2)}) copy-start(bf16[1,32,3584]{2,1,0:T(8,128)(2,1)} %param.23) | copy-start | bytes 688132
  59.9 23.6 %copy-start.19 = (bf16[8,3584]{1,0:T(8,128)(2,1)S(1)}, bf16[8,3584]{1,0:T(8,128)(2,1)}, u32[]{:S(2)}) copy-start(bf16[8,3584]{1,0:T(8,128)(2,1)} %slice_bitcast_fusion) | copy-start | bytes 172036
  59.9 23.6 %copy-start.20 = (bf16[1,8,3584]{2,1,0:T(8,128)(2,1)S(1)}, bf16[1,8,3584]{2,1,0:T(8,128)(2,1)}, u32[]{:S(2)}) copy-start(bf16[1,8,3584]{2,1,0:T(8,128)(2,1)} %param.16) | copy-start | bytes 172036
  67.9 16.4 %copy-start.15 = (f32[32,512]{1,0:T(8,128)}, f32[32,512]{1,0:T(8,128)S(1)}, u32[]{:S(2)}) copy-start(f32[32,512]{1,0:T(8,128)S(1)} %get-tuple-element.42.refs_5_) | copy-start | bytes 196612
  67.9 15.3 %collective-permute-start.10 = (bf16[16,3584]{1,0:T(8,128)(2,1)S(1)}, bf16[16,3584]{1,0:T(8,128)(2,1)S(1)}, u32[]{:S(2)}, u32[]{:S(2)}) collective-permute-start(bf16[16,3584]{1,0:T(8,128)(2,1)S(1)} %get-tuple-element.33), channel_id=1, source_target_pairs={{2,0},{3,1},{4,2},{5,3},{6,4},{7,5},{0,6},{1,7},{10,8},{11,9},{12,... | collective-permute-start | bytes 344072 | tf_op jit(solution)/shard_map/ppermute | solution.py:272
  69.8 13.7 %collective-permute-start.11 = (bf16[16,3584]{1,0:T(8,128)(2,1)S(1)}, bf16[16,3584]{1,0:T(8,128)(2,1)S(1)}, u32[]{:S(2)}, u32[]{:S(2)}) collective-permute-start(bf16[16,3584]{1,0:T(8,128)(2,1)S(1)} %get-tuple-element.34), channel_id=1, source_target_pairs={{4,0},{5,1},{6,2},{7,3},{0,4},{1,5},{2,6},{3,7},{12,8},{13,9},{14,... | collective-permute-start | bytes 344072 | tf_op jit(solution)/shard_map/ppermute | solution.py:272
  74.8 8.7 %collective-permute-start.12 = (bf16[16,3584]{1,0:T(8,128)(2,1)S(1)}, bf16[16,3584]{1,0:T(8,128)(2,1)S(1)}, u32[]{:S(2)}, u32[]{:S(2)}) collective-permute-start(bf16[16,3584]{1,0:T(8,128)(2,1)S(1)} %get-tuple-element.35), channel_id=1, source_target_pairs={{6,0},{7,1},{0,2},{1,3},{2,4},{3,5},{4,6},{5,7},{14,8},{15,9},{8,1... | collective-permute-start | bytes 344072 | tf_op jit(solution)/shard_map/ppermute | solution.py:272
  78.8 5.5 %collective-permute-start.13 = (bf16[128,128]{1,0:T(8,128)(2,1)S(1)}, bf16[128,128]{1,0:T(8,128)(2,1)S(1)}, u32[]{:S(2)}, u32[]{:S(2)}) collective-permute-start(bf16[128,128]{1,0:T(8,128)(2,1)S(1)} %pad_maximum_fusion.1), channel_id=1, source_target_pairs={{0,1},{1,0},{2,3},{3,2},{4,5},{5,4},{6,7},{7,6},{8,9},{9,8},{10,11... | collective-permute-start | bytes 98312 | tf_op jit(solution)/shard_map/ppermute | solution.py:263
  80.7 7.0 %collective-permute-start.15 = (bf16[32,3584]{1,0:T(8,128)(2,1)S(1)}, bf16[32,3584]{1,0:T(8,128)(2,1)}, u32[]{:S(2)}, u32[]{:S(2)}) collective-permute-start(bf16[32,3584]{1,0:T(8,128)(2,1)S(1)} %bitcast.24), channel_id=1, source_target_pairs={{0,1},{1,0},{2,3},{3,2},{4,5},{5,4},{6,7},{7,6},{8,9},{9,8},{10,11... | collective-permute-start | bytes 688136 | tf_op jit(solution)/shard_map/ppermute | solution.py:263
  84.2 0.6 copy-start.17
  84.8 20.5 %collective-permute-start.14 = (bf16[16,3584]{1,0:T(8,128)(2,1)}, bf16[16,3584]{1,0:T(8,128)(2,1)}, u32[]{:S(2)}, u32[]{:S(2)}) collective-permute-start(bf16[16,3584]{1,0:T(8,128)(2,1)} %add_convert_fusion), channel_id=1, source_target_pairs={{8,0},{16,8},{24,16},{32,24},{40,32},{48,40},{56,48},{64,56},{72,6... | collective-permute-start | bytes 344072 | tf_op jit(solution)/shard_map/ppermute | solution.py:326
  87.7 0.8 copy-start.18
  106.4 7.8 %collective-permute-start.16 = (bf16[16,3712]{1,0:T(8,128)(2,1)S(1)}, bf16[16,3712]{1,0:T(8,128)(2,1)S(1)}, u32[]{:S(2)}, u32[]{:S(2)}) collective-permute-start(bf16[16,3712]{1,0:T(8,128)(2,1)S(1)} %pad_maximum_fusion.refs_0_.refs_10_), channel_id=1, source_target_pairs={{2,0},{3,1},{4,2},{5,3},{6,4},{7,5},{0,6},{1,7},{10,8},{11,9},{12,... | collective-permute-start | bytes 356360 | tf_op jit(solution)/shard_map/ppermute | solution.py:272
  108.3 12.9 %collective-permute-start.17 = (bf16[16,3712]{1,0:T(8,128)(2,1)S(1)}, bf16[16,3712]{1,0:T(8,128)(2,1)S(1)}, u32[]{:S(2)}, u32[]{:S(2)}) collective-permute-start(bf16[16,3712]{1,0:T(8,128)(2,1)S(1)} %pad_maximum_fusion.refs_0_.refs_10_), channel_id=1, source_target_pairs={{4,0},{5,1},{6,2},{7,3},{0,4},{1,5},{2,6},{3,7},{12,8},{13,9},{14,... | collective-permute-start | bytes 356360 | tf_op jit(solution)/shard_map/ppermute | solution.py:272
  110.2 11.0 %collective-permute-start.18 = (bf16[16,3712]{1,0:T(8,128)(2,1)S(1)}, bf16[16,3712]{1,0:T(8,128)(2,1)S(1)}, u32[]{:S(2)}, u32[]{:S(2)}) collective-permute-start(bf16[16,3712]{1,0:T(8,128)(2,1)S(1)} %pad_maximum_fusion.refs_0_.refs_10_), channel_id=1, source_target_pairs={{6,0},{7,1},{0,2},{1,3},{2,4},{3,5},{4,6},{5,7},{14,8},{15,9},{8,1... | collective-permute-start | bytes 356360 | tf_op jit(solution)/shard_map/ppermute | solution.py:272
  121.2 2.0 %copy-start.1 = (bf16[3584,512]{1,0:T(8,128)(2,1)S(1)}, bf16[3584,512]{1,0:T(8,128)(2,1)}, u32[]{:S(2)}) copy-start(bf16[3584,512]{1,0:T(8,128)(2,1)} %copy-done) | copy-start | bytes 11010052
  123.2 0.8 copy-start.14
  124.0 0.8 copy-start.16
  127.4 11.3 %collective-permute-start.19 = (bf16[16,3584]{1,0:T(8,128)(2,1)S(1)}, bf16[16,3584]{1,0:T(8,128)(2,1)S(1)}, u32[]{:S(2)}, u32[]{:S(2)}) collective-permute-start(bf16[16,3584]{1,0:T(8,128)(2,1)S(1)} %get-tuple-element.44), channel_id=1, source_target_pairs={{2,0},{3,1},{4,2},{5,3},{6,4},{7,5},{0,6},{1,7},{10,8},{11,9},{12,... | collective-permute-start | bytes 344072 | tf_op jit(solution)/shard_map/ppermute | solution.py:272
  131.1 11.3 %collective-permute-start.20 = (bf16[16,3584]{1,0:T(8,128)(2,1)S(1)}, bf16[16,3584]{1,0:T(8,128)(2,1)S(1)}, u32[]{:S(2)}, u32[]{:S(2)}) collective-permute-start(bf16[16,3584]{1,0:T(8,128)(2,1)S(1)} %get-tuple-element.45), channel_id=1, source_target_pairs={{4,0},{5,1},{6,2},{7,3},{0,4},{1,5},{2,6},{3,7},{12,8},{13,9},{14,... | collective-permute-start | bytes 344072 | tf_op jit(solution)/shard_map/ppermute | solution.py:272
  133.1 9.3 %collective-permute-start.21 = (bf16[16,3584]{1,0:T(8,128)(2,1)S(1)}, bf16[16,3584]{1,0:T(8,128)(2,1)S(1)}, u32[]{:S(2)}, u32[]{:S(2)}) collective-permute-start(bf16[16,3584]{1,0:T(8,128)(2,1)S(1)} %get-tuple-element.46), channel_id=1, source_target_pairs={{6,0},{7,1},{0,2},{1,3},{2,4},{3,5},{4,6},{5,7},{14,8},{15,9},{8,1... | collective-permute-start | bytes 344072 | tf_op jit(solution)/shard_map/ppermute | solution.py:272
  136.8 12.7 %collective-permute-start.23 = (f32[32,3584]{1,0:T(8,128)S(1)}, f32[32,3584]{1,0:T(8,128)S(1)}, u32[]{:S(2)}, u32[]{:S(2)}) collective-permute-start(f32[32,3584]{1,0:T(8,128)S(1)} %get-tuple-element.51), channel_id=1, source_target_pairs={{0,1},{1,0},{2,3},{3,2},{4,5},{5,4},{6,7},{7,6},{8,9},{9,8},{10,11... | collective-permute-start | bytes 1376264 | tf_op jit(solution)/shard_map/ppermute | solution.py:263
  143.1 14.3 %collective-permute-start.22 = (bf16[8,3584]{1,0:T(8,128)(2,1)S(1)}, bf16[8,3584]{1,0:T(8,128)(2,1)S(1)}, u32[]{:S(2)}, u32[]{:S(2)}) collective-permute-start(bf16[8,3584]{1,0:T(8,128)(2,1)S(1)} %get-tuple-element.53), channel_id=1, source_target_pairs={{0,504},{8,496},{16,488},{24,480},{32,472},{40,464},{48,456},{56,4... | collective-permute-start | bytes 172040 | tf_op jit(solution)/shard_map/ppermute | solution.py:268

commit v12 on v11

--- a/solution.py
+++ b/solution.py
@@ -18,7 +18,7 @@
 IDCOLS = 128
 WIDE = D + IDCOLS
 WIDTH = 512
-VMEM_LIMIT = 40 * 1024 * 1024
+VMEM_LIMIT = 48 * 1024 * 1024
 z_weight = 0.01
 balance_weight = 1.0
 F32 = jnp.float32

time: 159 us -> 160 us (level)
  Pallas kernels: 16.1 us -> 21.4 us
  waiting for transfers between devices: 41.6 us -> 36.8 us
  local copies, waits for them, and re-layouts: 13.2 us -> 9.73 us
  starting transfers between devices: 82.8 us -> 85.9 us
    pallas_call x5, Pallas kernels: 12.7 us -> 18 us  [call(): pl.pallas_call(body, out_shape=[jax.ShapeDtypeStruct(shape, dtype) for sh...]
    unnamed x43 -> x39, local copies, waits for them, and re-layouts: 12.6 us -> 9.11 us
    ppermute x1, waiting for transfers between devices: 14.7 us -> 12.1 us  [shards(): moved = lax.ppermute(out, 'pipe', [(i, i - 1) for i in range(1, top + 1)])]
    ppermute x2, starting transfers between devices: 21.5 us -> 23.4 us  [mirrored(): lax.ppermute(value, 'pipe', [(i, count - 1 - i) for i in range(count)])]
    ppermute x2, waiting for transfers between devices: 10.8 us -> 8.99 us  [mirrored(): lax.ppermute(value, 'pipe', [(i, count - 1 - i) for i in range(count)])]
where the time goes in v12:
time: 160 us; the launch traced here: 158 us
  starting transfers between devices  85.9 us (54%)
  waiting for transfers between devices  36.8 us (23%)
  Pallas kernels  21.4 us (13%)
  local copies, waits for them, and re-layouts  9.73 us (6%)
  other arithmetic  3.21 us (2%)
    ppermute x15, starting transfers between devices, from_chip(): lax.ppermute(value, 'expert', [((e + 2 * k) % 8, e) for e in range(8)])  47.3 us
    ppermute x2, starting transfers between devices, mirrored(): lax.ppermute(value, 'pipe', [(i, count - 1 - i) for i in range(count)])  23.4 us
    pallas_call x5, Pallas kernels, call(): pl.pallas_call(body, out_shape=[jax.ShapeDtypeStruct(shape, dtype) for sh...  18 us
    ppermute x15, waiting for transfers between devices, from_chip(): lax.ppermute(value, 'expert', [((e + 2 * k) % 8, e) for e in range(8)])  15.7 us
    ppermute x6, starting transfers between devices, swapped(): return lax.ppermute(value, 'expert', [(e, e ^ 1) for e in range(8)])  12.5 us
    ppermute x1, waiting for transfers between devices, shards(): moved = lax.ppermute(out, 'pipe', [(i, i - 1) for i in range(1, top + 1)])  12.1 us
    unnamed x39, local copies, waits for them, and re-layouts  9.11 us
    ppermute x2, waiting for transfers between devices, mirrored(): lax.ppermute(value, 'pipe', [(i, count - 1 - i) for i in range(count)])  8.99 us
  transfers between devices with their start and end apart: 24, of which 8 were waited for; matrix products, arithmetic and copies ran while one was open for 2% of the time, Pallas kernels for 6%

profile of v12, /device:TPU:6, one launch (start us, length us, event | category | flops | bytes accessed | tf_op | source)
XLA Modules:
  0.0 158.0 jit_solution(18245103149036577892)
XLA Ops:
  0.6 1.7 %shard_map.139 = bf16[3,8,3712]{2,1,0:T(8,128)(2,1)} custom-call(bf16[2,8,3584]{2,1,0:T(8,128)(2,1)} %bitcast.29, bf16[8,3584]{1,0:T(8,128)(2,1)} %bitcast.32, s32[2,8,8]{2,1,0:T(8,128)} %bitcast.35), custom_call_target="tpu_custom_call" | custom-call | tf_op jit(solution)/shard_map/pallas_call | solution.py:73
  2.3 15.1 %collective-permute-start = (bf16[3,8,3712]{2,1,0:T(8,128)(2,1)}, bf16[3,8,3712]{2,1,0:T(8,128)(2,1)S(1)}, u32[]{:S(2)}, u32[]{:S(2)}) collective-permute-start(bf16[3,8,3712]{2,1,0:T(8,128)(2,1)} %shard_map.139), channel_id=1, source_target_pairs={{0,504},{8,496},{16,488},{24,480},{32,472},{40,464},{48,456},{56,4... | collective-permute-start | bytes 534536 | tf_op jit(solution)/shard_map/ppermute | solution.py:268
  17.4 1.9 %collective-permute-start.1 = (bf16[3584,128]{1,0:T(8,128)(2,1)}, bf16[3584,128]{1,0:T(8,128)(2,1)S(1)}, u32[]{:S(2)}, u32[]{:S(2)}) collective-permute-start(bf16[3584,128]{1,0:T(8,128)(2,1)} %bitcast.18), channel_id=1, source_target_pairs={{0,1},{1,0},{2,3},{3,2},{4,5},{5,4},{6,7},{7,6},{8,9},{9,8},{10,11... | collective-permute-start | bytes 2752520 | tf_op jit(solution)/shard_map/ppermute | solution.py:263
  19.4 2.4 %collective-permute-start.2 = (bf16[3584,128]{1,0:T(8,128)(2,1)}, bf16[3584,128]{1,0:T(8,128)(2,1)}, u32[]{:S(2)}, u32[]{:S(2)}) collective-permute-start(bf16[3584,128]{1,0:T(8,128)(2,1)} %bitcast.20), channel_id=1, source_target_pairs={{0,1},{1,0},{2,3},{3,2},{4,5},{5,4},{6,7},{7,6},{8,9},{9,8},{10,11... | collective-permute-start | bytes 2752520 | tf_op jit(solution)/shard_map/ppermute | solution.py:263
  21.8 1.9 %collective-permute-start.3 = (bf16[128,3584]{1,0:T(8,128)(2,1)}, bf16[128,3584]{1,0:T(8,128)(2,1)}, u32[]{:S(2)}, u32[]{:S(2)}) collective-permute-start(bf16[128,3584]{1,0:T(8,128)(2,1)} %bitcast.22), channel_id=1, source_target_pairs={{0,1},{1,0},{2,3},{3,2},{4,5},{5,4},{6,7},{7,6},{8,9},{9,8},{10,11... | collective-permute-start | bytes 2752520 | tf_op jit(solution)/shard_map/ppermute | solution.py:263
  23.7 1.7 %shard_map.141.refs_0_ = bf16[3,8,3712]{2,1,0:T(8,128)(2,1)} custom-call(bf16[2,8,3584]{2,1,0:T(8,128)(2,1)} %bitcast.30, bf16[8,3584]{1,0:T(8,128)(2,1)} %bitcast.27, s32[2,8,8]{2,1,0:T(8,128)} %bitcast.36), custom_call_target="tpu_custom_call" | custom-call | tf_op jit(solution)/shard_map/pallas_call | solution.py:73
  25.4 3.8 %collective-permute-start.7 = (bf16[3,8,3712]{2,1,0:T(8,128)(2,1)}, bf16[3,8,3712]{2,1,0:T(8,128)(2,1)S(1)}, u32[]{:S(2)}, u32[]{:S(2)}) collective-permute-start(bf16[3,8,3712]{2,1,0:T(8,128)(2,1)} %shard_map.141.refs_0_), channel_id=1, source_target_pairs={{2,0},{3,1},{4,2},{5,3},{6,4},{7,5},{0,6},{1,7},{10,8},{11,9},{12,... | collective-permute-start | bytes 534536 | tf_op jit(solution)/shard_map/ppermute | solution.py:272
  29.2 3.7 %collective-permute-done.value = bf16[3,8,3712]{2,1,0:T(8,128)(2,1)S(1)} collective-permute-done((bf16[3,8,3712]{2,1,0:T(8,128)(2,1)}, bf16[3,8,3712]{2,1,0:T(8,128)(2,1)S(1)}, u32[]{:S(2)}, u32[]{:S(2)}) %collective-permute-start) | collective-permute-done | bytes 178208 | tf_op jit(solution)/shard_map/ppermute | solution.py:268
  33.0 1.9 %collective-permute-start.8 = (bf16[3,8,3712]{2,1,0:T(8,128)(2,1)}, bf16[3,8,3712]{2,1,0:T(8,128)(2,1)S(1)}, u32[]{:S(2)}, u32[]{:S(2)}) collective-permute-start(bf16[3,8,3712]{2,1,0:T(8,128)(2,1)} %shard_map.141.refs_0_), channel_id=1, source_target_pairs={{4,0},{5,1},{6,2},{7,3},{0,4},{1,5},{2,6},{3,7},{12,8},{13,9},{14,... | collective-permute-start | bytes 534536 | tf_op jit(solution)/shard_map/ppermute | solution.py:272
  35.6 0.9 copy-done.8
  36.5 5.1 %collective-permute-start.9 = (bf16[3,8,3712]{2,1,0:T(8,128)(2,1)}, bf16[3,8,3712]{2,1,0:T(8,128)(2,1)S(1)}, u32[]{:S(2)}, u32[]{:S(2)}) collective-permute-start(bf16[3,8,3712]{2,1,0:T(8,128)(2,1)} %shard_map.141.refs_0_), channel_id=1, source_target_pairs={{6,0},{7,1},{0,2},{1,3},{2,4},{3,5},{4,6},{5,7},{14,8},{15,9},{8,1... | collective-permute-start | bytes 534536 | tf_op jit(solution)/shard_map/ppermute | solution.py:272
  41.6 2.8 %collective-permute-start.4 = (bf16[3,8,3712]{2,1,0:T(8,128)(2,1)}, bf16[3,8,3712]{2,1,0:T(8,128)(2,1)S(1)}, u32[]{:S(2)}, u32[]{:S(2)}) collective-permute-start(bf16[3,8,3712]{2,1,0:T(8,128)(2,1)} %shard_map.140.refs_0_.refs_4_), channel_id=1, source_target_pairs={{2,0},{3,1},{4,2},{5,3},{6,4},{7,5},{0,6},{1,7},{10,8},{11,9},{12,... | collective-permute-start | bytes 534536 | tf_op jit(solution)/shard_map/ppermute | solution.py:272
  44.4 3.0 %collective-permute-start.5 = (bf16[3,8,3712]{2,1,0:T(8,128)(2,1)}, bf16[3,8,3712]{2,1,0:T(8,128)(2,1)S(1)}, u32[]{:S(2)}, u32[]{:S(2)}) collective-permute-start(bf16[3,8,3712]{2,1,0:T(8,128)(2,1)} %shard_map.140.refs_0_.refs_4_), channel_id=1, source_target_pairs={{4,0},{5,1},{6,2},{7,3},{0,4},{1,5},{2,6},{3,7},{12,8},{13,9},{14,... | collective-permute-start | bytes 534536 | tf_op jit(solution)/shard_map/ppermute | solution.py:272
  47.5 2.1 %collective-permute-start.6 = (bf16[3,8,3712]{2,1,0:T(8,128)(2,1)}, bf16[3,8,3712]{2,1,0:T(8,128)(2,1)S(1)}, u32[]{:S(2)}, u32[]{:S(2)}) collective-permute-start(bf16[3,8,3712]{2,1,0:T(8,128)(2,1)} %shard_map.140.refs_0_.refs_4_), channel_id=1, source_target_pairs={{6,0},{7,1},{0,2},{1,3},{2,4},{3,5},{4,6},{5,7},{14,8},{15,9},{8,1... | collective-permute-start | bytes 534536 | tf_op jit(solution)/shard_map/ppermute | solution.py:272
  49.8 1.2 copy-done.7
  50.9 1.2 copy-done.9
  52.1 5.3 %shard_map.142 = (f32[32,3584]{1,0:T(8,128)S(1)}, f32[32,512]{1,0:T(8,128)S(1)}, bf16[64,128]{1,0:T(8,128)(2,1)S(1)}, bf16[3584,512]{1,0:T(8,128)(2,1)}, bf16[256,3584]{1,0:T(8,128)(2,1)}) custom-call(bf16[3,8,3712]{2,1,0:T(8,128)(2,1)S(1)} %copy-done.2, bf16[3,8,3712]{2,1,0:T(8,128)(2,1)S(1)} %collective-permute-done.7.refs_1_, ...), custom_call_target="tpu_custom_call" | custom-call | flops 704643072 | bytes 6217728 | tf_op jit(solution)/shard_map/pallas_call | solution.py:37
  58.1 6.8 %collective-permute-done.5.refs_2_.refs_6_ = bf16[3,8,3712]{2,1,0:T(8,128)(2,1)S(1)} collective-permute-done((bf16[3,8,3712]{2,1,0:T(8,128)(2,1)}, bf16[3,8,3712]{2,1,0:T(8,128)(2,1)S(1)}, u32[]{:S(2)}, u32[]{:S(2)}) %collective-permute-start.5) | collective-permute-done | bytes 178208 | tf_op jit(solution)/shard_map/ppermute | solution.py:272
  64.8 1.5 copy-done
  66.3 5.2 %shard_map.143 = (f32[16,3584]{1,0:T(8,128)S(1)}, bf16[16,3584]{1,0:T(8,128)(2,1)S(1)}, bf16[16,3584]{1,0:T(8,128)(2,1)S(1)}, bf16[16,3584]{1,0:T(8,128)(2,1)S(1...) custom-call(bf16[3,8,3712]{2,1,0:T(8,128)(2,1)S(1)} %copy-done.4, ...), custom_call_target="tpu_custom_call" | custom-call | flops 704643072 | bytes 6676480 | tf_op jit(solution)/shard_map/pallas_call | solution.py:37
  71.6 1.9 %collective-permute-start.10 = (bf16[16,3584]{1,0:T(8,128)(2,1)S(1)}, bf16[16,3584]{1,0:T(8,128)(2,1)S(1)}, u32[]{:S(2)}, u32[]{:S(2)}) collective-permute-start(bf16[16,3584]{1,0:T(8,128)(2,1)S(1)} %get-tuple-element.33), channel_id=1, source_target_pairs={{2,0},{3,1},{4,2},{5,3},{6,4},{7,5},{0,6},{1,7},{10,8},{11,9},{12,... | collective-permute-start | bytes 344072 | tf_op jit(solution)/shard_map/ppermute | solution.py:272
  73.5 3.0 %collective-permute-start.11 = (bf16[16,3584]{1,0:T(8,128)(2,1)S(1)}, bf16[16,3584]{1,0:T(8,128)(2,1)S(1)}, u32[]{:S(2)}, u32[]{:S(2)}) collective-permute-start(bf16[16,3584]{1,0:T(8,128)(2,1)S(1)} %get-tuple-element.34), channel_id=1, source_target_pairs={{4,0},{5,1},{6,2},{7,3},{0,4},{1,5},{2,6},{3,7},{12,8},{13,9},{14,... | collective-permute-start | bytes 344072 | tf_op jit(solution)/shard_map/ppermute | solution.py:272
  76.5 3.9 %collective-permute-start.12 = (bf16[16,3584]{1,0:T(8,128)(2,1)S(1)}, bf16[16,3584]{1,0:T(8,128)(2,1)S(1)}, u32[]{:S(2)}, u32[]{:S(2)}) collective-permute-start(bf16[16,3584]{1,0:T(8,128)(2,1)S(1)} %get-tuple-element.35), channel_id=1, source_target_pairs={{6,0},{7,1},{0,2},{1,3},{2,4},{3,5},{4,6},{5,7},{14,8},{15,9},{8,1... | collective-permute-start | bytes 344072 | tf_op jit(solution)/shard_map/ppermute | solution.py:272
  80.5 1.9 %collective-permute-start.13 = (bf16[128,128]{1,0:T(8,128)(2,1)S(1)}, bf16[128,128]{1,0:T(8,128)(2,1)S(1)}, u32[]{:S(2)}, u32[]{:S(2)}) collective-permute-start(bf16[128,128]{1,0:T(8,128)(2,1)S(1)} %pad_maximum_fusion.1), channel_id=1, source_target_pairs={{0,1},{1,0},{2,3},{3,2},{4,5},{5,4},{6,7},{7,6},{8,9},{9,8},{10,11... | collective-permute-start | bytes 98312 | tf_op jit(solution)/shard_map/ppermute | solution.py:263
  82.4 2.4 %collective-permute-start.15 = (bf16[32,3584]{1,0:T(8,128)(2,1)S(1)}, bf16[32,3584]{1,0:T(8,128)(2,1)}, u32[]{:S(2)}, u32[]{:S(2)}) collective-permute-start(bf16[32,3584]{1,0:T(8,128)(2,1)S(1)} %bitcast.24), channel_id=1, source_target_pairs={{0,1},{1,0},{2,3},{3,2},{4,5},{5,4},{6,7},{7,6},{8,9},{9,8},{10,11... | collective-permute-start | bytes 688136 | tf_op jit(solution)/shard_map/ppermute | solution.py:263
  84.9 1.4 collective-permute-done.11
  86.3 0.7 add_convert_fusion
  87.6 2.8 %collective-permute-start.14 = (bf16[16,3584]{1,0:T(8,128)(2,1)}, bf16[16,3584]{1,0:T(8,128)(2,1)}, u32[]{:S(2)}, u32[]{:S(2)}) collective-permute-start(bf16[16,3584]{1,0:T(8,128)(2,1)} %add_convert_fusion), channel_id=1, source_target_pairs={{8,0},{16,8},{24,16},{32,24},{40,32},{48,40},{56,48},{64,56},{72,6... | collective-permute-start | bytes 344072 | tf_op jit(solution)/shard_map/ppermute | solution.py:326
  90.4 0.7 copy-done.16
  91.2 2.3 %shard_map.144 = (f32[64,256]{1,0:T(8,128)S(1)}, f32[64,256]{1,0:T(8,128)S(1)}, bf16[16,128]{1,0:T(8,128)(2,1)S(1)}) custom-call(bf16[3,8,3712]{2,1,0:T(8,128)(2,1)S(1)} %copy-done.2, bf16[3,8,3712]{2,1,0:T(8,128)(2,1)S(1)} %collective-permute-done.7.refs_1_, bf16[3,8,3712]{2,1,0:T(8,128)(2,1)S(1)} %collective-permute-done.8.refs_2_, ...), custom_call_target="tpu_custom_call" | custom-call | flops 117440512 | bytes 1949696 | tf_op jit(solution)/shard_map/pallas_call | solution.py:37
  93.5 12.1 %collective-permute-done.14 = bf16[16,3584]{1,0:T(8,128)(2,1)} collective-permute-done((bf16[16,3584]{1,0:T(8,128)(2,1)}, bf16[16,3584]{1,0:T(8,128)(2,1)}, u32[]{:S(2)}, u32[]{:S(2)}) %collective-permute-start.14) | collective-permute-done | bytes 114720 | tf_op jit(solution)/shard_map/ppermute | solution.py:326
  105.5 1.0 maximum_select_fusion
  106.5 3.1 %collective-permute-start.16 = (bf16[16,3712]{1,0:T(8,128)(2,1)S(1)}, bf16[16,3712]{1,0:T(8,128)(2,1)S(1)}, u32[]{:S(2)}, u32[]{:S(2)}) collective-permute-start(bf16[16,3712]{1,0:T(8,128)(2,1)S(1)} %pad_maximum_fusion.refs_0_.refs_10_), channel_id=1, source_target_pairs={{2,0},{3,1},{4,2},{5,3},{6,4},{7,5},{0,6},{1,7},{10,8},{11,9},{12,... | collective-permute-start | bytes 356360 | tf_op jit(solution)/shard_map/ppermute | solution.py:272
  109.6 3.3 %collective-permute-start.17 = (bf16[16,3712]{1,0:T(8,128)(2,1)S(1)}, bf16[16,3712]{1,0:T(8,128)(2,1)S(1)}, u32[]{:S(2)}, u32[]{:S(2)}) collective-permute-start(bf16[16,3712]{1,0:T(8,128)(2,1)S(1)} %pad_maximum_fusion.refs_0_.refs_10_), channel_id=1, source_target_pairs={{4,0},{5,1},{6,2},{7,3},{0,4},{1,5},{2,6},{3,7},{12,8},{13,9},{14,... | collective-permute-start | bytes 356360 | tf_op jit(solution)/shard_map/ppermute | solution.py:272
  112.9 3.9 %collective-permute-start.18 = (bf16[16,3712]{1,0:T(8,128)(2,1)S(1)}, bf16[16,3712]{1,0:T(8,128)(2,1)S(1)}, u32[]{:S(2)}, u32[]{:S(2)}) collective-permute-start(bf16[16,3712]{1,0:T(8,128)(2,1)S(1)} %pad_maximum_fusion.refs_0_.refs_10_), channel_id=1, source_target_pairs={{6,0},{7,1},{0,2},{1,3},{2,4},{3,5},{4,6},{5,7},{14,8},{15,9},{8,1... | collective-permute-start | bytes 356360 | tf_op jit(solution)/shard_map/ppermute | solution.py:272
  116.9 4.7 %collective-permute-done.17.refs_2_.refs_12_ = bf16[16,3712]{1,0:T(8,128)(2,1)S(1)} collective-permute-done((bf16[16,3712]{1,0:T(8,128)(2,1)S(1)}, bf16[16,3712]{1,0:T(8,128)(2,1)S(1)}, u32[]{:S(2)}, u32[]{:S(2)}) %collective-permute-start.17) | collective-permute-done | bytes 118816 | tf_op jit(solution)/shard_map/ppermute | solution.py:272
  121.6 0.8 copy-done.12
  122.5 0.8 copy-done.14
  123.3 4.6 %shard_map.145 = (f32[16,3584]{1,0:T(8,128)S(1)}, bf16[16,3584]{1,0:T(8,128)(2,1)S(1)}, bf16[16,3584]{1,0:T(8,128)(2,1)S(1)}, bf16[16,3584]{1,0:T(8,128)(2,1)S(1)}) custom-call(bf16[16,3712]{1,0:T(8,128)(2,1)S(1)} %pad_maximum_fusion.refs_0_.refs_10_, bf16[16,3712]{1,0:T(8,128)(2,1)S(1)} %collective-permute-done.16.refs_1_.refs_11_, ...), custom_call_target="tpu_custom_call" | custom-call | flops 352321536 | bytes 6111232 | tf_op jit(solution)/shard_map/pallas_call | solution.py:37
  127.9 3.2 %collective-permute-start.19 = (bf16[16,3584]{1,0:T(8,128)(2,1)S(1)}, bf16[16,3584]{1,0:T(8,128)(2,1)S(1)}, u32[]{:S(2)}, u32[]{:S(2)}) collective-permute-start(bf16[16,3584]{1,0:T(8,128)(2,1)S(1)} %get-tuple-element.44), channel_id=1, source_target_pairs={{2,0},{3,1},{4,2},{5,3},{6,4},{7,5},{0,6},{1,7},{10,8},{11,9},{12,... | collective-permute-start | bytes 344072 | tf_op jit(solution)/shard_map/ppermute | solution.py:272
  131.1 2.2 %collective-permute-start.20 = (bf16[16,3584]{1,0:T(8,128)(2,1)S(1)}, bf16[16,3584]{1,0:T(8,128)(2,1)S(1)}, u32[]{:S(2)}, u32[]{:S(2)}) collective-permute-start(bf16[16,3584]{1,0:T(8,128)(2,1)S(1)} %get-tuple-element.45), channel_id=1, source_target_pairs={{4,0},{5,1},{6,2},{7,3},{0,4},{1,5},{2,6},{3,7},{12,8},{13,9},{14,... | collective-permute-start | bytes 344072 | tf_op jit(solution)/shard_map/ppermute | solution.py:272
  133.3 3.9 %collective-permute-start.21 = (bf16[16,3584]{1,0:T(8,128)(2,1)S(1)}, bf16[16,3584]{1,0:T(8,128)(2,1)S(1)}, u32[]{:S(2)}, u32[]{:S(2)}) collective-permute-start(bf16[16,3584]{1,0:T(8,128)(2,1)S(1)} %get-tuple-element.46), channel_id=1, source_target_pairs={{6,0},{7,1},{0,2},{1,3},{2,4},{3,5},{4,6},{5,7},{14,8},{15,9},{8,1... | collective-permute-start | bytes 344072 | tf_op jit(solution)/shard_map/ppermute | solution.py:272
  137.8 1.9 %collective-permute-start.23 = (f32[32,3584]{1,0:T(8,128)S(1)}, f32[32,3584]{1,0:T(8,128)S(1)}, u32[]{:S(2)}, u32[]{:S(2)}) collective-permute-start(f32[32,3584]{1,0:T(8,128)S(1)} %get-tuple-element.51), channel_id=1, source_target_pairs={{0,1},{1,0},{2,3},{3,2},{4,5},{5,4},{6,7},{7,6},{8,9},{9,8},{10,11... | collective-permute-start | bytes 1376264 | tf_op jit(solution)/shard_map/ppermute | solution.py:263
  139.8 2.6 %collective-permute-done.20 = bf16[16,3584]{1,0:T(8,128)(2,1)S(1)} collective-permute-done((bf16[16,3584]{1,0:T(8,128)(2,1)S(1)}, bf16[16,3584]{1,0:T(8,128)(2,1)S(1)}, u32[]{:S(2)}, u32[]{:S(2)}) %collective-permute-start.20) | collective-permute-done | bytes 114720 | tf_op jit(solution)/shard_map/ppermute | solution.py:272
  142.4 0.7 add_convert_fusion.1
  143.1 8.3 %collective-permute-start.22 = (bf16[8,3584]{1,0:T(8,128)(2,1)S(1)}, bf16[8,3584]{1,0:T(8,128)(2,1)S(1)}, u32[]{:S(2)}, u32[]{:S(2)}) collective-permute-start(bf16[8,3584]{1,0:T(8,128)(2,1)S(1)} %get-tuple-element.53), channel_id=1, source_target_pairs={{0,504},{8,496},{16,488},{24,480},{32,472},{40,464},{48,456},{56,4... | collective-permute-start | bytes 172040 | tf_op jit(solution)/shard_map/ppermute | solution.py:268
  151.3 0.8 add.51
  152.1 5.3 %collective-permute-done.22 = bf16[8,3584]{1,0:T(8,128)(2,1)S(1)} collective-permute-done((bf16[8,3584]{1,0:T(8,128)(2,1)S(1)}, bf16[8,3584]{1,0:T(8,128)(2,1)S(1)}, u32[]{:S(2)}, u32[]{:S(2)}) %collective-permute-start.22) | collective-permute-done | bytes 57376 | tf_op jit(solution)/shard_map/ppermute | solution.py:268
  (54 shorter events, 3.4 us)
Async XLA Ops:
  2.3 30.7 %collective-permute-start = (bf16[3,8,3712]{2,1,0:T(8,128)(2,1)}, bf16[3,8,3712]{2,1,0:T(8,128)(2,1)S(1)}, u32[]{:S(2)}, u32[]{:S(2)}) collective-permute-start(bf16[3,8,3712]{2,1,0:T(8,128)(2,1)} %shard_map.139), channel_id=1, source_target_pairs={{0,504},{8,496},{16,488},{24,480},{32,472},{40,464},{48,456},{56,4... | collective-permute-start | bytes 534536 | tf_op jit(solution)/shard_map/ppermute | solution.py:268
  17.4 18.1 %collective-permute-start.1 = (bf16[3584,128]{1,0:T(8,128)(2,1)}, bf16[3584,128]{1,0:T(8,128)(2,1)S(1)}, u32[]{:S(2)}, u32[]{:S(2)}) collective-permute-start(bf16[3584,128]{1,0:T(8,128)(2,1)} %bitcast.18), channel_id=1, source_target_pairs={{0,1},{1,0},{2,3},{3,2},{4,5},{5,4},{6,7},{7,6},{8,9},{9,8},{10,11... | collective-permute-start | bytes 2752520 | tf_op jit(solution)/shard_map/ppermute | solution.py:263
  19.4 22.2 %collective-permute-start.2 = (bf16[3584,128]{1,0:T(8,128)(2,1)}, bf16[3584,128]{1,0:T(8,128)(2,1)}, u32[]{:S(2)}, u32[]{:S(2)}) collective-permute-start(bf16[3584,128]{1,0:T(8,128)(2,1)} %bitcast.20), channel_id=1, source_target_pairs={{0,1},{1,0},{2,3},{3,2},{4,5},{5,4},{6,7},{7,6},{8,9},{9,8},{10,11... | collective-permute-start | bytes 2752520 | tf_op jit(solution)/shard_map/ppermute | solution.py:263
  21.8 19.8 %collective-permute-start.3 = (bf16[128,3584]{1,0:T(8,128)(2,1)}, bf16[128,3584]{1,0:T(8,128)(2,1)}, u32[]{:S(2)}, u32[]{:S(2)}) collective-permute-start(bf16[128,3584]{1,0:T(8,128)(2,1)} %bitcast.22), channel_id=1, source_target_pairs={{0,1},{1,0},{2,3},{3,2},{4,5},{5,4},{6,7},{7,6},{8,9},{9,8},{10,11... | collective-permute-start | bytes 2752520 | tf_op jit(solution)/shard_map/ppermute | solution.py:263
  25.4 22.1 %collective-permute-start.7 = (bf16[3,8,3712]{2,1,0:T(8,128)(2,1)}, bf16[3,8,3712]{2,1,0:T(8,128)(2,1)S(1)}, u32[]{:S(2)}, u32[]{:S(2)}) collective-permute-start(bf16[3,8,3712]{2,1,0:T(8,128)(2,1)} %shard_map.141.refs_0_), channel_id=1, source_target_pairs={{2,0},{3,1},{4,2},{5,3},{6,4},{7,5},{0,6},{1,7},{10,8},{11,9},{12,... | collective-permute-start | bytes 534536 | tf_op jit(solution)/shard_map/ppermute | solution.py:272
  33.0 8.6 %copy-start.3 = (bf16[3,8,3712]{2,1,0:T(8,128)(2,1)}, bf16[3,8,3712]{2,1,0:T(8,128)(2,1)S(1)}, u32[]{:S(2)}) copy-start(bf16[3,8,3712]{2,1,0:T(8,128)(2,1)S(1)} %collective-permute-done.value) | copy-start | bytes 534532
  33.0 16.7 %collective-permute-start.8 = (bf16[3,8,3712]{2,1,0:T(8,128)(2,1)}, bf16[3,8,3712]{2,1,0:T(8,128)(2,1)S(1)}, u32[]{:S(2)}, u32[]{:S(2)}) collective-permute-start(bf16[3,8,3712]{2,1,0:T(8,128)(2,1)} %shard_map.141.refs_0_), channel_id=1, source_target_pairs={{4,0},{5,1},{6,2},{7,3},{0,4},{1,5},{2,6},{3,7},{12,8},{13,9},{14,... | collective-permute-start | bytes 534536 | tf_op jit(solution)/shard_map/ppermute | solution.py:272
  35.5 14.2 %copy-start.2 = (bf16[3,8,3712]{2,1,0:T(8,128)(2,1)S(1)}, bf16[3,8,3712]{2,1,0:T(8,128)(2,1)}, u32[]{:S(2)}) copy-start(bf16[3,8,3712]{2,1,0:T(8,128)(2,1)} %shard_map.141.refs_0_) | copy-start | bytes 534532
  35.5 14.2 %copy-start.5 = (bf16[1,3584,128]{2,1,0:T(8,128)(2,1)S(1)}, bf16[1,3584,128]{2,1,0:T(8,128)(2,1)}, u32[]{:S(2)}) copy-start(bf16[1,3584,128]{2,1,0:T(8,128)(2,1)} %param.20) | copy-start | bytes 2752516
  35.5 14.2 %copy-start.6 = (bf16[1,3584,128]{2,1,0:T(8,128)(2,1)S(1)}, bf16[1,3584,128]{2,1,0:T(8,128)(2,1)}, u32[]{:S(2)}) copy-start(bf16[1,3584,128]{2,1,0:T(8,128)(2,1)} %param.21) | copy-start | bytes 2752516
  35.5 0.9 copy-start.8
  36.5 13.3 %collective-permute-start.9 = (bf16[3,8,3712]{2,1,0:T(8,128)(2,1)}, bf16[3,8,3712]{2,1,0:T(8,128)(2,1)S(1)}, u32[]{:S(2)}, u32[]{:S(2)}) collective-permute-start(bf16[3,8,3712]{2,1,0:T(8,128)(2,1)} %shard_map.141.refs_0_), channel_id=1, source_target_pairs={{6,0},{7,1},{0,2},{1,3},{2,4},{3,5},{4,6},{5,7},{14,8},{15,9},{8,1... | collective-permute-start | bytes 534536 | tf_op jit(solution)/shard_map/ppermute | solution.py:272
  41.6 23.2 %copy-start.4 = (bf16[3,8,3712]{2,1,0:T(8,128)(2,1)S(1)}, bf16[3,8,3712]{2,1,0:T(8,128)(2,1)}, u32[]{:S(2)}) copy-start(bf16[3,8,3712]{2,1,0:T(8,128)(2,1)} %shard_map.140.refs_0_.refs_4_) | copy-start | bytes 534532
  41.6 16.4 %collective-permute-start.4 = (bf16[3,8,3712]{2,1,0:T(8,128)(2,1)}, bf16[3,8,3712]{2,1,0:T(8,128)(2,1)S(1)}, u32[]{:S(2)}, u32[]{:S(2)}) collective-permute-start(bf16[3,8,3712]{2,1,0:T(8,128)(2,1)} %shard_map.140.refs_0_.refs_4_), channel_id=1, source_target_pairs={{2,0},{3,1},{4,2},{5,3},{6,4},{7,5},{0,6},{1,7},{10,8},{11,9},{12,... | collective-permute-start | bytes 534536 | tf_op jit(solution)/shard_map/ppermute | solution.py:272
  44.4 20.4 %collective-permute-start.5 = (bf16[3,8,3712]{2,1,0:T(8,128)(2,1)}, bf16[3,8,3712]{2,1,0:T(8,128)(2,1)S(1)}, u32[]{:S(2)}, u32[]{:S(2)}) collective-permute-start(bf16[3,8,3712]{2,1,0:T(8,128)(2,1)} %shard_map.140.refs_0_.refs_4_), channel_id=1, source_target_pairs={{4,0},{5,1},{6,2},{7,3},{0,4},{1,5},{2,6},{3,7},{12,8},{13,9},{14,... | collective-permute-start | bytes 534536 | tf_op jit(solution)/shard_map/ppermute | solution.py:272
  47.5 17.4 %collective-permute-start.6 = (bf16[3,8,3712]{2,1,0:T(8,128)(2,1)}, bf16[3,8,3712]{2,1,0:T(8,128)(2,1)S(1)}, u32[]{:S(2)}, u32[]{:S(2)}) collective-permute-start(bf16[3,8,3712]{2,1,0:T(8,128)(2,1)} %shard_map.140.refs_0_.refs_4_), channel_id=1, source_target_pairs={{6,0},{7,1},{0,2},{1,3},{2,4},{3,5},{4,6},{5,7},{14,8},{15,9},{8,1... | collective-permute-start | bytes 534536 | tf_op jit(solution)/shard_map/ppermute | solution.py:272
  49.8 1.2 copy-start.7
  50.9 1.2 copy-start.9
  52.1 30.3 %copy-start.10 = (bf16[1,32,3584]{2,1,0:T(8,128)(2,1)S(1)}, bf16[1,32,3584]{2,1,0:T(8,128)(2,1)}, u32[]{:S(2)}) copy-start(bf16[1,32,3584]{2,1,0:T(8,128)(2,1)} %param.23) | copy-start | bytes 688132
  52.1 34.2 %copy-start.17 = (bf16[8,3584]{1,0:T(8,128)(2,1)S(1)}, bf16[8,3584]{1,0:T(8,128)(2,1)}, u32[]{:S(2)}) copy-start(bf16[8,3584]{1,0:T(8,128)(2,1)} %slice_bitcast_fusion) | copy-start | bytes 172036
  52.1 34.2 %copy-start.18 = (bf16[1,8,3584]{2,1,0:T(8,128)(2,1)S(1)}, bf16[1,8,3584]{2,1,0:T(8,128)(2,1)}, u32[]{:S(2)}) copy-start(bf16[1,8,3584]{2,1,0:T(8,128)(2,1)} %param.16) | copy-start | bytes 172036
  57.4 0.6 copy-start.11
  64.8 1.5 copy-start
  66.3 55.3 %copy-start.1 = (bf16[256,3584]{1,0:T(8,128)(2,1)S(1)}, bf16[256,3584]{1,0:T(8,128)(2,1)}, u32[]{:S(2)}) copy-start(bf16[256,3584]{1,0:T(8,128)(2,1)} %get-tuple-element.30.refs_5_.refs_7_) | copy-start | bytes 5505028
  71.6 15.5 %copy-start.13 = (f32[32,512]{1,0:T(8,128)}, f32[32,512]{1,0:T(8,128)S(1)}, u32[]{:S(2)}) copy-start(f32[32,512]{1,0:T(8,128)S(1)} %get-tuple-element.42.refs_5_) | copy-start | bytes 196612
  71.6 13.3 %collective-permute-start.10 = (bf16[16,3584]{1,0:T(8,128)(2,1)S(1)}, bf16[16,3584]{1,0:T(8,128)(2,1)S(1)}, u32[]{:S(2)}, u32[]{:S(2)}) collective-permute-start(bf16[16,3584]{1,0:T(8,128)(2,1)S(1)} %get-tuple-element.33), channel_id=1, source_target_pairs={{2,0},{3,1},{4,2},{5,3},{6,4},{7,5},{0,6},{1,7},{10,8},{11,9},{12,... | collective-permute-start | bytes 344072 | tf_op jit(solution)/shard_map/ppermute | solution.py:272
  73.5 12.8 %collective-permute-start.11 = (bf16[16,3584]{1,0:T(8,128)(2,1)S(1)}, bf16[16,3584]{1,0:T(8,128)(2,1)S(1)}, u32[]{:S(2)}, u32[]{:S(2)}) collective-permute-start(bf16[16,3584]{1,0:T(8,128)(2,1)S(1)} %get-tuple-element.34), channel_id=1, source_target_pairs={{4,0},{5,1},{6,2},{7,3},{0,4},{1,5},{2,6},{3,7},{12,8},{13,9},{14,... | collective-permute-start | bytes 344072 | tf_op jit(solution)/shard_map/ppermute | solution.py:272
  76.5 9.7 %collective-permute-start.12 = (bf16[16,3584]{1,0:T(8,128)(2,1)S(1)}, bf16[16,3584]{1,0:T(8,128)(2,1)S(1)}, u32[]{:S(2)}, u32[]{:S(2)}) collective-permute-start(bf16[16,3584]{1,0:T(8,128)(2,1)S(1)} %get-tuple-element.35), channel_id=1, source_target_pairs={{6,0},{7,1},{0,2},{1,3},{2,4},{3,5},{4,6},{5,7},{14,8},{15,9},{8,1... | collective-permute-start | bytes 344072 | tf_op jit(solution)/shard_map/ppermute | solution.py:272
  80.5 6.5 %collective-permute-start.13 = (bf16[128,128]{1,0:T(8,128)(2,1)S(1)}, bf16[128,128]{1,0:T(8,128)(2,1)S(1)}, u32[]{:S(2)}, u32[]{:S(2)}) collective-permute-start(bf16[128,128]{1,0:T(8,128)(2,1)S(1)} %pad_maximum_fusion.1), channel_id=1, source_target_pairs={{0,1},{1,0},{2,3},{3,2},{4,5},{5,4},{6,7},{7,6},{8,9},{9,8},{10,11... | collective-permute-start | bytes 98312 | tf_op jit(solution)/shard_map/ppermute | solution.py:263
  82.4 8.0 %collective-permute-start.15 = (bf16[32,3584]{1,0:T(8,128)(2,1)S(1)}, bf16[32,3584]{1,0:T(8,128)(2,1)}, u32[]{:S(2)}, u32[]{:S(2)}) collective-permute-start(bf16[32,3584]{1,0:T(8,128)(2,1)S(1)} %bitcast.24), channel_id=1, source_target_pairs={{0,1},{1,0},{2,3},{3,2},{4,5},{5,4},{6,7},{7,6},{8,9},{9,8},{10,11... | collective-permute-start | bytes 688136 | tf_op jit(solution)/shard_map/ppermute | solution.py:263
  87.0 0.6 copy-start.15
  87.6 17.9 %collective-permute-start.14 = (bf16[16,3584]{1,0:T(8,128)(2,1)}, bf16[16,3584]{1,0:T(8,128)(2,1)}, u32[]{:S(2)}, u32[]{:S(2)}) collective-permute-start(bf16[16,3584]{1,0:T(8,128)(2,1)} %add_convert_fusion), channel_id=1, source_target_pairs={{8,0},{16,8},{24,16},{32,24},{40,32},{48,40},{56,48},{64,56},{72,6... | collective-permute-start | bytes 344072 | tf_op jit(solution)/shard_map/ppermute | solution.py:326
  90.4 0.8 copy-start.16
  106.5 10.4 %collective-permute-start.16 = (bf16[16,3712]{1,0:T(8,128)(2,1)S(1)}, bf16[16,3712]{1,0:T(8,128)(2,1)S(1)}, u32[]{:S(2)}, u32[]{:S(2)}) collective-permute-start(bf16[16,3712]{1,0:T(8,128)(2,1)S(1)} %pad_maximum_fusion.refs_0_.refs_10_), channel_id=1, source_target_pairs={{2,0},{3,1},{4,2},{5,3},{6,4},{7,5},{0,6},{1,7},{10,8},{11,9},{12,... | collective-permute-start | bytes 356360 | tf_op jit(solution)/shard_map/ppermute | solution.py:272
  109.6 12.0 %collective-permute-start.17 = (bf16[16,3712]{1,0:T(8,128)(2,1)S(1)}, bf16[16,3712]{1,0:T(8,128)(2,1)S(1)}, u32[]{:S(2)}, u32[]{:S(2)}) collective-permute-start(bf16[16,3712]{1,0:T(8,128)(2,1)S(1)} %pad_maximum_fusion.refs_0_.refs_10_), channel_id=1, source_target_pairs={{4,0},{5,1},{6,2},{7,3},{0,4},{1,5},{2,6},{3,7},{12,8},{13,9},{14,... | collective-permute-start | bytes 356360 | tf_op jit(solution)/shard_map/ppermute | solution.py:272
  112.9 8.7 %collective-permute-start.18 = (bf16[16,3712]{1,0:T(8,128)(2,1)S(1)}, bf16[16,3712]{1,0:T(8,128)(2,1)S(1)}, u32[]{:S(2)}, u32[]{:S(2)}) collective-permute-start(bf16[16,3712]{1,0:T(8,128)(2,1)S(1)} %pad_maximum_fusion.refs_0_.refs_10_), channel_id=1, source_target_pairs={{6,0},{7,1},{0,2},{1,3},{2,4},{3,5},{4,6},{5,7},{14,8},{15,9},{8,1... | collective-permute-start | bytes 356360 | tf_op jit(solution)/shard_map/ppermute | solution.py:272
  121.6 0.8 copy-start.12
  122.5 0.8 copy-start.14
  127.9 11.9 %collective-permute-start.19 = (bf16[16,3584]{1,0:T(8,128)(2,1)S(1)}, bf16[16,3584]{1,0:T(8,128)(2,1)S(1)}, u32[]{:S(2)}, u32[]{:S(2)}) collective-permute-start(bf16[16,3584]{1,0:T(8,128)(2,1)S(1)} %get-tuple-element.44), channel_id=1, source_target_pairs={{2,0},{3,1},{4,2},{5,3},{6,4},{7,5},{0,6},{1,7},{10,8},{11,9},{12,... | collective-permute-start | bytes 344072 | tf_op jit(solution)/shard_map/ppermute | solution.py:272
  131.1 11.3 %collective-permute-start.20 = (bf16[16,3584]{1,0:T(8,128)(2,1)S(1)}, bf16[16,3584]{1,0:T(8,128)(2,1)S(1)}, u32[]{:S(2)}, u32[]{:S(2)}) collective-permute-start(bf16[16,3584]{1,0:T(8,128)(2,1)S(1)} %get-tuple-element.45), channel_id=1, source_target_pairs={{4,0},{5,1},{6,2},{7,3},{0,4},{1,5},{2,6},{3,7},{12,8},{13,9},{14,... | collective-permute-start | bytes 344072 | tf_op jit(solution)/shard_map/ppermute | solution.py:272
  133.3 9.1 %collective-permute-start.21 = (bf16[16,3584]{1,0:T(8,128)(2,1)S(1)}, bf16[16,3584]{1,0:T(8,128)(2,1)S(1)}, u32[]{:S(2)}, u32[]{:S(2)}) collective-permute-start(bf16[16,3584]{1,0:T(8,128)(2,1)S(1)} %get-tuple-element.46), channel_id=1, source_target_pairs={{6,0},{7,1},{0,2},{1,3},{2,4},{3,5},{4,6},{5,7},{14,8},{15,9},{8,1... | collective-permute-start | bytes 344072 | tf_op jit(solution)/shard_map/ppermute | solution.py:272
  137.8 13.5 %collective-permute-start.23 = (f32[32,3584]{1,0:T(8,128)S(1)}, f32[32,3584]{1,0:T(8,128)S(1)}, u32[]{:S(2)}, u32[]{:S(2)}) collective-permute-start(f32[32,3584]{1,0:T(8,128)S(1)} %get-tuple-element.51), channel_id=1, source_target_pairs={{0,1},{1,0},{2,3},{3,2},{4,5},{5,4},{6,7},{7,6},{8,9},{9,8},{10,11... | collective-permute-start | bytes 1376264 | tf_op jit(solution)/shard_map/ppermute | solution.py:263
  143.1 14.3 %collective-permute-start.22 = (bf16[8,3584]{1,0:T(8,128)(2,1)S(1)}, bf16[8,3584]{1,0:T(8,128)(2,1)S(1)}, u32[]{:S(2)}, u32[]{:S(2)}) collective-permute-start(bf16[8,3584]{1,0:T(8,128)(2,1)S(1)} %get-tuple-element.53), channel_id=1, source_target_pairs={{0,504},{8,496},{16,488},{24,480},{32,472},{40,464},{48,456},{56,4... | collective-permute-start | bytes 172040 | tf_op jit(solution)/shard_map/ppermute | solution.py:268

commit v13 on v9

--- a/solution.py
+++ b/solution.py
@@ -289,7 +289,7 @@
 
 
 def returned(parts):
-    return [parts[0]] + [from_chip(parts[CHIPS - k], k) for k in range(1, CHIPS)]
+    return [parts[0]] + [from_chip(parts[CHIPS - k], k) for k in range(CHIPS - 1, 0, -1)]
 
 
 def emitted(grads, parts):

time: 155 us -> 156 us (level)
  waiting for transfers between devices: 37.6 us -> 40.4 us
    ppermute x1, waiting for transfers between devices: 12.3 us -> 14.7 us  [shards(): moved = lax.ppermute(out, 'pipe', [(i, i - 1) for i in range(1, top + 1)])]
  transfers between devices with their start and end apart: 24 -> 24, of which waited for: 9 -> 10; matrix products, arithmetic and copies ran while one was open for 2% -> 2% of each run, Pallas kernels for 7% -> 7%
where the time goes in v13:
time: 156 us; the launch traced here: 155 us
  starting transfers between devices  88.8 us (57%)
  waiting for transfers between devices  40.4 us (26%)
  Pallas kernels  20.7 us (13%)
  other arithmetic  2.27 us (1%)
    ppermute x15, starting transfers between devices, from_chip(): lax.ppermute(value, 'expert', [((e + 2 * k) % 8, e) for e in range(8)])  52.2 us
    ppermute x2, starting transfers between devices, mirrored(): lax.ppermute(value, 'pipe', [(i, count - 1 - i) for i in range(count)])  21.2 us
    pallas_call x5, Pallas kernels, call(): pl.pallas_call(body, out_shape=[jax.ShapeDtypeStruct(shape, dtype) for sh...  17.3 us
    ppermute x1, waiting for transfers between devices, shards(): moved = lax.ppermute(out, 'pipe', [(i, i - 1) for i in range(1, top + 1)])  14.7 us
    ppermute x15, waiting for transfers between devices, from_chip(): lax.ppermute(value, 'expert', [((e + 2 * k) % 8, e) for e in range(8)])  13.5 us
    ppermute x6, starting transfers between devices, swapped(): return lax.ppermute(value, 'expert', [(e, e ^ 1) for e in range(8)])  12.6 us
    ppermute x2, waiting for transfers between devices, mirrored(): lax.ppermute(value, 'pipe', [(i, count - 1 - i) for i in range(count)])  12.2 us
    pallas_call x2, Pallas kernels, payload(): pl.pallas_call(pack_kernel, out_shape=jax.ShapeDtypeStruct((3, ROWS, WIDE...  3.37 us
  transfers between devices with their start and end apart: 24, of which 10 were waited for; matrix products, arithmetic and copies ran while one was open for 2% of the time, Pallas kernels for 7%

profile of v13, /device:TPU:6, one launch (start us, length us, event | category | flops | bytes accessed | tf_op | source)
XLA Modules:
  0.0 154.6 jit_solution(1807759321869046000)
XLA Ops:
  0.6 1.7 %shard_map.139 = bf16[3,8,3712]{2,1,0:T(8,128)(2,1)} custom-call(bf16[2,8,3584]{2,1,0:T(8,128)(2,1)} %bitcast.33, bf16[8,3584]{1,0:T(8,128)(2,1)} %bitcast.36, s32[2,8,8]{2,1,0:T(8,128)} %bitcast.39), custom_call_target="tpu_custom_call" | custom-call | tf_op jit(solution)/shard_map/pallas_call | solution.py:73
  2.3 15.1 %collective-permute-start = (bf16[3,8,3712]{2,1,0:T(8,128)(2,1)}, bf16[3,8,3712]{2,1,0:T(8,128)(2,1)S(1)}, u32[]{:S(2)}, u32[]{:S(2)}) collective-permute-start(bf16[3,8,3712]{2,1,0:T(8,128)(2,1)} %shard_map.139), channel_id=1, source_target_pairs={{0,504},{8,496},{16,488},{24,480},{32,472},{40,464},{48,456},{56,4... | collective-permute-start | bytes 534536 | tf_op jit(solution)/shard_map/ppermute | solution.py:280
  17.4 1.9 %collective-permute-start.1 = (bf16[3584,128]{1,0:T(8,128)(2,1)}, bf16[3584,128]{1,0:T(8,128)(2,1)}, u32[]{:S(2)}, u32[]{:S(2)}) collective-permute-start(bf16[3584,128]{1,0:T(8,128)(2,1)} %bitcast.18), channel_id=1, source_target_pairs={{0,1},{1,0},{2,3},{3,2},{4,5},{5,4},{6,7},{7,6},{8,9},{9,8},{10,11... | collective-permute-start | bytes 2752520 | tf_op jit(solution)/shard_map/ppermute | solution.py:275
  19.4 2.4 %collective-permute-start.2 = (bf16[3584,128]{1,0:T(8,128)(2,1)}, bf16[3584,128]{1,0:T(8,128)(2,1)}, u32[]{:S(2)}, u32[]{:S(2)}) collective-permute-start(bf16[3584,128]{1,0:T(8,128)(2,1)} %bitcast.22), channel_id=1, source_target_pairs={{0,1},{1,0},{2,3},{3,2},{4,5},{5,4},{6,7},{7,6},{8,9},{9,8},{10,11... | collective-permute-start | bytes 2752520 | tf_op jit(solution)/shard_map/ppermute | solution.py:275
  21.8 1.9 %collective-permute-start.3 = (bf16[128,3584]{1,0:T(8,128)(2,1)}, bf16[128,3584]{1,0:T(8,128)(2,1)}, u32[]{:S(2)}, u32[]{:S(2)}) collective-permute-start(bf16[128,3584]{1,0:T(8,128)(2,1)} %bitcast.26), channel_id=1, source_target_pairs={{0,1},{1,0},{2,3},{3,2},{4,5},{5,4},{6,7},{7,6},{8,9},{9,8},{10,11... | collective-permute-start | bytes 2752520 | tf_op jit(solution)/shard_map/ppermute | solution.py:275
  23.7 1.7 %shard_map.141.refs_0_ = bf16[3,8,3712]{2,1,0:T(8,128)(2,1)} custom-call(bf16[2,8,3584]{2,1,0:T(8,128)(2,1)} %bitcast.34, bf16[8,3584]{1,0:T(8,128)(2,1)} %bitcast.31, s32[2,8,8]{2,1,0:T(8,128)} %bitcast.40), custom_call_target="tpu_custom_call" | custom-call | tf_op jit(solution)/shard_map/pallas_call | solution.py:73
  25.4 2.9 %collective-permute-start.9 = (bf16[3,8,3712]{2,1,0:T(8,128)(2,1)}, bf16[3,8,3712]{2,1,0:T(8,128)(2,1)S(1)}, u32[]{:S(2)}, u32[]{:S(2)}) collective-permute-start(bf16[3,8,3712]{2,1,0:T(8,128)(2,1)} %shard_map.141.refs_0_), channel_id=1, source_target_pairs={{6,0},{7,1},{0,2},{1,3},{2,4},{3,5},{4,6},{5,7},{14,8},{15,9},{8,1... | collective-permute-start | bytes 534536 | tf_op jit(solution)/shard_map/ppermute | solution.py:284
  28.3 4.6 %collective-permute-done.value = bf16[3,8,3712]{2,1,0:T(8,128)(2,1)S(1)} collective-permute-done((bf16[3,8,3712]{2,1,0:T(8,128)(2,1)}, bf16[3,8,3712]{2,1,0:T(8,128)(2,1)S(1)}, u32[]{:S(2)}, u32[]{:S(2)}) %collective-permute-start) | collective-permute-done | bytes 178208 | tf_op jit(solution)/shard_map/ppermute | solution.py:280
  33.0 1.9 %collective-permute-start.8 = (bf16[3,8,3712]{2,1,0:T(8,128)(2,1)}, bf16[3,8,3712]{2,1,0:T(8,128)(2,1)S(1)}, u32[]{:S(2)}, u32[]{:S(2)}) collective-permute-start(bf16[3,8,3712]{2,1,0:T(8,128)(2,1)} %shard_map.141.refs_0_), channel_id=1, source_target_pairs={{4,0},{5,1},{6,2},{7,3},{0,4},{1,5},{2,6},{3,7},{12,8},{13,9},{14,... | collective-permute-start | bytes 534536 | tf_op jit(solution)/shard_map/ppermute | solution.py:284
  34.9 0.6 slice_bitcast_fusion
  35.6 4.8 %collective-permute-start.7 = (bf16[3,8,3712]{2,1,0:T(8,128)(2,1)}, bf16[3,8,3712]{2,1,0:T(8,128)(2,1)}, u32[]{:S(2)}, u32[]{:S(2)}) collective-permute-start(bf16[3,8,3712]{2,1,0:T(8,128)(2,1)} %shard_map.141.refs_0_), channel_id=1, source_target_pairs={{2,0},{3,1},{4,2},{5,3},{6,4},{7,5},{0,6},{1,7},{10,8},{11,9},{12,... | collective-permute-start | bytes 534536 | tf_op jit(solution)/shard_map/ppermute | solution.py:284
  40.4 2.6 %collective-permute-start.6 = (bf16[3,8,3712]{2,1,0:T(8,128)(2,1)}, bf16[3,8,3712]{2,1,0:T(8,128)(2,1)S(1)}, u32[]{:S(2)}, u32[]{:S(2)}) collective-permute-start(bf16[3,8,3712]{2,1,0:T(8,128)(2,1)} %shard_map.140.refs_0_.refs_4_), channel_id=1, source_target_pairs={{6,0},{7,1},{0,2},{1,3},{2,4},{3,5},{4,6},{5,7},{14,8},{15,9},{8,1... | collective-permute-start | bytes 534536 | tf_op jit(solution)/shard_map/ppermute | solution.py:284
  43.0 3.6 %collective-permute-start.5 = (bf16[3,8,3712]{2,1,0:T(8,128)(2,1)}, bf16[3,8,3712]{2,1,0:T(8,128)(2,1)S(1)}, u32[]{:S(2)}, u32[]{:S(2)}) collective-permute-start(bf16[3,8,3712]{2,1,0:T(8,128)(2,1)} %shard_map.140.refs_0_.refs_4_), channel_id=1, source_target_pairs={{4,0},{5,1},{6,2},{7,3},{0,4},{1,5},{2,6},{3,7},{12,8},{13,9},{14,... | collective-permute-start | bytes 534536 | tf_op jit(solution)/shard_map/ppermute | solution.py:284
  46.7 4.6 %collective-permute-start.4 = (bf16[3,8,3712]{2,1,0:T(8,128)(2,1)}, bf16[3,8,3712]{2,1,0:T(8,128)(2,1)S(1)}, u32[]{:S(2)}, u32[]{:S(2)}) collective-permute-start(bf16[3,8,3712]{2,1,0:T(8,128)(2,1)} %shard_map.140.refs_0_.refs_4_), channel_id=1, source_target_pairs={{2,0},{3,1},{4,2},{5,3},{6,4},{7,5},{0,6},{1,7},{10,8},{11,9},{12,... | collective-permute-start | bytes 534536 | tf_op jit(solution)/shard_map/ppermute | solution.py:284
  51.3 2.3 %collective-permute-done.7.refs_1_ = bf16[3,8,3712]{2,1,0:T(8,128)(2,1)} collective-permute-done((bf16[3,8,3712]{2,1,0:T(8,128)(2,1)}, bf16[3,8,3712]{2,1,0:T(8,128)(2,1)}, u32[]{:S(2)}, u32[]{:S(2)}) %collective-permute-start.7) | collective-permute-done | bytes 178208 | tf_op jit(solution)/shard_map/ppermute | solution.py:284
  53.6 4.5 %shard_map.142 = (f32[32,3584]{1,0:T(8,128)S(1)}, f32[32,512]{1,0:T(8,128)S(1)}, bf16[64,128]{1,0:T(8,128)(2,1)S(1)}) custom-call(bf16[3,8,3712]{2,1,0:T(8,128)(2,1)S(1)} %copy-done.4, bf16[3,8,3712]{2,1,0:T(8,128)(2,1)} %collective-permute-done.7.refs_1_, bf16[3,8,3712]{2,1,0:T(8,128)(2,1)S(1)} %collective-permute-done.8.refs_2_, ...), custom_call_target="tpu_custom_call" | custom-call | flops 704643072 | bytes 6217728 | tf_op jit(solution)/shard_map/pallas_call | solution.py:37
  58.1 0.0 collective-permute-done.6.refs_3_.refs_7_
  58.2 3.0 %collective-permute-done.5.refs_2_.refs_6_ = bf16[3,8,3712]{2,1,0:T(8,128)(2,1)S(1)} collective-permute-done((bf16[3,8,3712]{2,1,0:T(8,128)(2,1)}, bf16[3,8,3712]{2,1,0:T(8,128)(2,1)S(1)}, u32[]{:S(2)}, u32[]{:S(2)}) %collective-permute-start.5) | collective-permute-done | bytes 178208 | tf_op jit(solution)/shard_map/ppermute | solution.py:284
  61.1 4.9 %shard_map.143 = (f32[16,3584]{1,0:T(8,128)S(1)}, bf16[16,3584]{1,0:T(8,128)(2,1)S(1)}, bf16[16,3584]{1,0:T(8,128)(2,1)S(1)}, bf16[16,3584]{1,0:T(8,128)(2,1)S(1...) custom-call(bf16[3,8,3712]{2,1,0:T(8,128)(2,1)S(1)} %copy-done.6, ...), custom_call_target="tpu_custom_call" | custom-call | flops 704643072 | bytes 6676480 | tf_op jit(solution)/shard_map/pallas_call | solution.py:37
  66.0 0.0 copy-done.7
  66.1 6.2 %collective-permute-start.10 = (bf16[16,3584]{1,0:T(8,128)(2,1)S(1)}, bf16[16,3584]{1,0:T(8,128)(2,1)S(1)}, u32[]{:S(2)}, u32[]{:S(2)}) collective-permute-start(bf16[16,3584]{1,0:T(8,128)(2,1)S(1)} %get-tuple-element.29), channel_id=1, source_target_pairs={{6,0},{7,1},{0,2},{1,3},{2,4},{3,5},{4,6},{5,7},{14,8},{15,9},{8,1... | collective-permute-start | bytes 344072 | tf_op jit(solution)/shard_map/ppermute | solution.py:284
  72.3 3.2 %collective-permute-start.11 = (bf16[16,3584]{1,0:T(8,128)(2,1)S(1)}, bf16[16,3584]{1,0:T(8,128)(2,1)S(1)}, u32[]{:S(2)}, u32[]{:S(2)}) collective-permute-start(bf16[16,3584]{1,0:T(8,128)(2,1)S(1)} %get-tuple-element.30), channel_id=1, source_target_pairs={{4,0},{5,1},{6,2},{7,3},{0,4},{1,5},{2,6},{3,7},{12,8},{13,9},{14,... | collective-permute-start | bytes 344072 | tf_op jit(solution)/shard_map/ppermute | solution.py:284
  75.6 2.9 %collective-permute-start.12 = (bf16[16,3584]{1,0:T(8,128)(2,1)S(1)}, bf16[16,3584]{1,0:T(8,128)(2,1)S(1)}, u32[]{:S(2)}, u32[]{:S(2)}) collective-permute-start(bf16[16,3584]{1,0:T(8,128)(2,1)S(1)} %get-tuple-element.31), channel_id=1, source_target_pairs={{2,0},{3,1},{4,2},{5,3},{6,4},{7,5},{0,6},{1,7},{10,8},{11,9},{12,... | collective-permute-start | bytes 344072 | tf_op jit(solution)/shard_map/ppermute | solution.py:284
  78.6 2.1 %collective-permute-start.13 = (bf16[128,128]{1,0:T(8,128)(2,1)S(1)}, bf16[128,128]{1,0:T(8,128)(2,1)S(1)}, u32[]{:S(2)}, u32[]{:S(2)}) collective-permute-start(bf16[128,128]{1,0:T(8,128)(2,1)S(1)} %pad_maximum_fusion.1), channel_id=1, source_target_pairs={{0,1},{1,0},{2,3},{3,2},{4,5},{5,4},{6,7},{7,6},{8,9},{9,8},{10,11... | collective-permute-start | bytes 98312 | tf_op jit(solution)/shard_map/ppermute | solution.py:275
  80.6 2.4 %collective-permute-start.15 = (bf16[32,3584]{1,0:T(8,128)(2,1)}, bf16[32,3584]{1,0:T(8,128)(2,1)}, u32[]{:S(2)}, u32[]{:S(2)}) collective-permute-start(bf16[32,3584]{1,0:T(8,128)(2,1)} %bitcast.12.refs_11_), channel_id=1, source_target_pairs={{0,1},{1,0},{2,3},{3,2},{4,5},{5,4},{6,7},{7,6},{8,9},{9,8},{10,11... | collective-permute-start | bytes 688136 | tf_op jit(solution)/shard_map/ppermute | solution.py:275
  83.1 1.3 collective-permute-done.12
  84.3 0.7 add_convert_fusion
  85.1 2.8 %collective-permute-start.14 = (bf16[16,3584]{1,0:T(8,128)(2,1)}, bf16[16,3584]{1,0:T(8,128)(2,1)S(1)}, u32[]{:S(2)}, u32[]{:S(2)}) collective-permute-start(bf16[16,3584]{1,0:T(8,128)(2,1)} %add_convert_fusion), channel_id=1, source_target_pairs={{8,0},{16,8},{24,16},{32,24},{40,32},{48,40},{56,48},{64,56},{72,6... | collective-permute-start | bytes 344072 | tf_op jit(solution)/shard_map/ppermute | solution.py:336
  87.9 2.5 %shard_map.144 = (f32[64,256]{1,0:T(8,128)S(1)}, f32[64,256]{1,0:T(8,128)S(1)}, bf16[16,128]{1,0:T(8,128)(2,1)S(1)}) custom-call(bf16[3,8,3712]{2,1,0:T(8,128)(2,1)S(1)} %copy-done.4, bf16[3,8,3712]{2,1,0:T(8,128)(2,1)} %collective-permute-done.7.refs_1_, bf16[3,8,3712]{2,1,0:T(8,128)(2,1)S(1)} %collective-permute-done.8.refs_2_, ...), custom_call_target="tpu_custom_call" | custom-call | flops 117440512 | bytes 1949696 | tf_op jit(solution)/shard_map/pallas_call | solution.py:37
  90.5 14.7 %collective-permute-done.14 = bf16[16,3584]{1,0:T(8,128)(2,1)S(1)} collective-permute-done((bf16[16,3584]{1,0:T(8,128)(2,1)}, bf16[16,3584]{1,0:T(8,128)(2,1)S(1)}, u32[]{:S(2)}, u32[]{:S(2)}) %collective-permute-start.14) | collective-permute-done | bytes 114720 | tf_op jit(solution)/shard_map/ppermute | solution.py:336
  105.2 1.9 %collective-permute-start.18 = (bf16[16,3712]{1,0:T(8,128)(2,1)S(1)}, bf16[16,3712]{1,0:T(8,128)(2,1)S(1)}, u32[]{:S(2)}, u32[]{:S(2)}) collective-permute-start(bf16[16,3712]{1,0:T(8,128)(2,1)S(1)} %pad_maximum_fusion.refs_0_.refs_10_), channel_id=1, source_target_pairs={{6,0},{7,1},{0,2},{1,3},{2,4},{3,5},{4,6},{5,7},{14,8},{15,9},{8,1... | collective-permute-start | bytes 356360 | tf_op jit(solution)/shard_map/ppermute | solution.py:284
  107.1 1.9 %collective-permute-start.17 = (bf16[16,3712]{1,0:T(8,128)(2,1)S(1)}, bf16[16,3712]{1,0:T(8,128)(2,1)S(1)}, u32[]{:S(2)}, u32[]{:S(2)}) collective-permute-start(bf16[16,3712]{1,0:T(8,128)(2,1)S(1)} %pad_maximum_fusion.refs_0_.refs_10_), channel_id=1, source_target_pairs={{4,0},{5,1},{6,2},{7,3},{0,4},{1,5},{2,6},{3,7},{12,8},{13,9},{14,... | collective-permute-start | bytes 356360 | tf_op jit(solution)/shard_map/ppermute | solution.py:284
  109.1 5.7 %collective-permute-start.16 = (bf16[16,3712]{1,0:T(8,128)(2,1)S(1)}, bf16[16,3712]{1,0:T(8,128)(2,1)S(1)}, u32[]{:S(2)}, u32[]{:S(2)}) collective-permute-start(bf16[16,3712]{1,0:T(8,128)(2,1)S(1)} %pad_maximum_fusion.refs_0_.refs_10_), channel_id=1, source_target_pairs={{2,0},{3,1},{4,2},{5,3},{6,4},{7,5},{0,6},{1,7},{10,8},{11,9},{12,... | collective-permute-start | bytes 356360 | tf_op jit(solution)/shard_map/ppermute | solution.py:284
  114.8 4.2 %collective-permute-done.17.refs_2_.refs_12_ = bf16[16,3712]{1,0:T(8,128)(2,1)S(1)} collective-permute-done((bf16[16,3712]{1,0:T(8,128)(2,1)S(1)}, bf16[16,3712]{1,0:T(8,128)(2,1)S(1)}, u32[]{:S(2)}, u32[]{:S(2)}) %collective-permute-start.17) | collective-permute-done | bytes 118816 | tf_op jit(solution)/shard_map/ppermute | solution.py:284
  119.0 1.3 collective-permute-done.16.refs_1_.refs_11_
  120.4 3.8 %shard_map.145 = (f32[16,3584]{1,0:T(8,128)S(1)}, bf16[16,3584]{1,0:T(8,128)(2,1)S(1)}, bf16[16,3584]{1,0:T(8,128)(2,1)S(1)}, bf16[16,3584]{1,0:T(8,128)(2,1)S(1)}) custom-call(bf16[16,3712]{1,0:T(8,128)(2,1)S(1)} %pad_maximum_fusion.refs_0_.refs_10_, bf16[16,3712]{1,0:T(8,128)(2,1)S(1)} %collective-permute-done.16.refs_1_.refs_11_, ...), custom_call_target="tpu_custom_call" | custom-call | flops 352321536 | bytes 6111232 | tf_op jit(solution)/shard_map/pallas_call | solution.py:37
  124.2 3.6 %collective-permute-start.19 = (bf16[16,3584]{1,0:T(8,128)(2,1)S(1)}, bf16[16,3584]{1,0:T(8,128)(2,1)S(1)}, u32[]{:S(2)}, u32[]{:S(2)}) collective-permute-start(bf16[16,3584]{1,0:T(8,128)(2,1)S(1)} %get-tuple-element.40), channel_id=1, source_target_pairs={{6,0},{7,1},{0,2},{1,3},{2,4},{3,5},{4,6},{5,7},{14,8},{15,9},{8,1... | collective-permute-start | bytes 344072 | tf_op jit(solution)/shard_map/ppermute | solution.py:284
  127.8 2.2 %collective-permute-start.20 = (bf16[16,3584]{1,0:T(8,128)(2,1)S(1)}, bf16[16,3584]{1,0:T(8,128)(2,1)S(1)}, u32[]{:S(2)}, u32[]{:S(2)}) collective-permute-start(bf16[16,3584]{1,0:T(8,128)(2,1)S(1)} %get-tuple-element.41), channel_id=1, source_target_pairs={{4,0},{5,1},{6,2},{7,3},{0,4},{1,5},{2,6},{3,7},{12,8},{13,9},{14,... | collective-permute-start | bytes 344072 | tf_op jit(solution)/shard_map/ppermute | solution.py:284
  130.0 4.0 %collective-permute-start.21 = (bf16[16,3584]{1,0:T(8,128)(2,1)S(1)}, bf16[16,3584]{1,0:T(8,128)(2,1)S(1)}, u32[]{:S(2)}, u32[]{:S(2)}) collective-permute-start(bf16[16,3584]{1,0:T(8,128)(2,1)S(1)} %get-tuple-element.42), channel_id=1, source_target_pairs={{2,0},{3,1},{4,2},{5,3},{6,4},{7,5},{0,6},{1,7},{10,8},{11,9},{12,... | collective-permute-start | bytes 344072 | tf_op jit(solution)/shard_map/ppermute | solution.py:284
  134.0 1.6 %shard_map.146 = (f32[32,3584]{1,0:T(8,128)S(1)}, f32[32,3584]{1,0:T(8,128)S(1)}) custom-call(bf16[3,8,3712]{2,1,0:T(8,128)(2,1)S(1)} %copy-done.4, bf16[3,8,3712]{2,1,0:T(8,128)(2,1)} %collective-permute-done.7.refs_1_, bf16[3,8,3712]{2,1,0:T(8,128)(2,1)S(1)} %collective-permute-done.8.refs_2_, bf16[3,8,3712]{2,1,0:T(8,128)(2,1)S(1)} %collective-permute-done.9.refs_3_, ...), custom_call_target="tpu_custom_call" | custom-call | flops 88080384 | bytes 2031616 | tf_op jit(solution)/shard_map/pallas_call | solution.py:37
  135.6 1.9 %collective-permute-start.23 = (f32[32,3584]{1,0:T(8,128)S(1)}, f32[32,3584]{1,0:T(8,128)S(1)}, u32[]{:S(2)}, u32[]{:S(2)}) collective-permute-start(f32[32,3584]{1,0:T(8,128)S(1)} %get-tuple-element.47), channel_id=1, source_target_pairs={{0,1},{1,0},{2,3},{3,2},{4,5},{5,4},{6,7},{7,6},{8,9},{9,8},{10,11... | collective-permute-start | bytes 1376264 | tf_op jit(solution)/shard_map/ppermute | solution.py:275
  137.5 0.2 collective-permute-done.20
  137.7 1.1 collective-permute-done.21
  138.9 0.7 add_convert_fusion.1
  139.6 6.1 %collective-permute-start.22 = (bf16[8,3584]{1,0:T(8,128)(2,1)S(1)}, bf16[8,3584]{1,0:T(8,128)(2,1)S(1)}, u32[]{:S(2)}, u32[]{:S(2)}) collective-permute-start(bf16[8,3584]{1,0:T(8,128)(2,1)S(1)} %get-tuple-element.49), channel_id=1, source_target_pairs={{0,504},{8,496},{16,488},{24,480},{32,472},{40,464},{48,456},{56,4... | collective-permute-start | bytes 172040 | tf_op jit(solution)/shard_map/ppermute | solution.py:280
  145.6 0.8 add.51
  146.4 7.5 %collective-permute-done.22 = bf16[8,3584]{1,0:T(8,128)(2,1)S(1)} collective-permute-done((bf16[8,3584]{1,0:T(8,128)(2,1)S(1)}, bf16[8,3584]{1,0:T(8,128)(2,1)S(1)}, u32[]{:S(2)}, u32[]{:S(2)}) %collective-permute-start.22) | collective-permute-done | bytes 57376 | tf_op jit(solution)/shard_map/ppermute | solution.py:280
  154.0 0.6 copy.18
  (54 shorter events, 0.2 us)
Async XLA Ops:
  2.3 30.7 %collective-permute-start = (bf16[3,8,3712]{2,1,0:T(8,128)(2,1)}, bf16[3,8,3712]{2,1,0:T(8,128)(2,1)S(1)}, u32[]{:S(2)}, u32[]{:S(2)}) collective-permute-start(bf16[3,8,3712]{2,1,0:T(8,128)(2,1)} %shard_map.139), channel_id=1, source_target_pairs={{0,504},{8,496},{16,488},{24,480},{32,472},{40,464},{48,456},{56,4... | collective-permute-start | bytes 534536 | tf_op jit(solution)/shard_map/ppermute | solution.py:280
  17.4 18.1 %collective-permute-start.1 = (bf16[3584,128]{1,0:T(8,128)(2,1)}, bf16[3584,128]{1,0:T(8,128)(2,1)}, u32[]{:S(2)}, u32[]{:S(2)}) collective-permute-start(bf16[3584,128]{1,0:T(8,128)(2,1)} %bitcast.18), channel_id=1, source_target_pairs={{0,1},{1,0},{2,3},{3,2},{4,5},{5,4},{6,7},{7,6},{8,9},{9,8},{10,11... | collective-permute-start | bytes 2752520 | tf_op jit(solution)/shard_map/ppermute | solution.py:275
  19.4 21.0 %collective-permute-start.2 = (bf16[3584,128]{1,0:T(8,128)(2,1)}, bf16[3584,128]{1,0:T(8,128)(2,1)}, u32[]{:S(2)}, u32[]{:S(2)}) collective-permute-start(bf16[3584,128]{1,0:T(8,128)(2,1)} %bitcast.22), channel_id=1, source_target_pairs={{0,1},{1,0},{2,3},{3,2},{4,5},{5,4},{6,7},{7,6},{8,9},{9,8},{10,11... | collective-permute-start | bytes 2752520 | tf_op jit(solution)/shard_map/ppermute | solution.py:275
  21.8 18.6 %collective-permute-start.3 = (bf16[128,3584]{1,0:T(8,128)(2,1)}, bf16[128,3584]{1,0:T(8,128)(2,1)}, u32[]{:S(2)}, u32[]{:S(2)}) collective-permute-start(bf16[128,3584]{1,0:T(8,128)(2,1)} %bitcast.26), channel_id=1, source_target_pairs={{0,1},{1,0},{2,3},{3,2},{4,5},{5,4},{6,7},{7,6},{8,9},{9,8},{10,11... | collective-permute-start | bytes 2752520 | tf_op jit(solution)/shard_map/ppermute | solution.py:275
  25.4 21.3 %collective-permute-start.9 = (bf16[3,8,3712]{2,1,0:T(8,128)(2,1)}, bf16[3,8,3712]{2,1,0:T(8,128)(2,1)S(1)}, u32[]{:S(2)}, u32[]{:S(2)}) collective-permute-start(bf16[3,8,3712]{2,1,0:T(8,128)(2,1)} %shard_map.141.refs_0_), channel_id=1, source_target_pairs={{6,0},{7,1},{0,2},{1,3},{2,4},{3,5},{4,6},{5,7},{14,8},{15,9},{8,1... | collective-permute-start | bytes 534536 | tf_op jit(solution)/shard_map/ppermute | solution.py:284
  33.0 7.4 %copy-start.5 = (bf16[3,8,3712]{2,1,0:T(8,128)(2,1)}, bf16[3,8,3712]{2,1,0:T(8,128)(2,1)S(1)}, u32[]{:S(2)}) copy-start(bf16[3,8,3712]{2,1,0:T(8,128)(2,1)S(1)} %collective-permute-done.value) | copy-start | bytes 534532
  33.0 18.3 %collective-permute-start.8 = (bf16[3,8,3712]{2,1,0:T(8,128)(2,1)}, bf16[3,8,3712]{2,1,0:T(8,128)(2,1)S(1)}, u32[]{:S(2)}, u32[]{:S(2)}) collective-permute-start(bf16[3,8,3712]{2,1,0:T(8,128)(2,1)} %shard_map.141.refs_0_), channel_id=1, source_target_pairs={{4,0},{5,1},{6,2},{7,3},{0,4},{1,5},{2,6},{3,7},{12,8},{13,9},{14,... | collective-permute-start | bytes 534536 | tf_op jit(solution)/shard_map/ppermute | solution.py:284
  35.5 18.1 %copy-start = (bf16[1,3584,128]{2,1,0:T(8,128)(2,1)S(1)}, bf16[1,3584,128]{2,1,0:T(8,128)(2,1)}, u32[]{:S(2)}) copy-start(bf16[1,3584,128]{2,1,0:T(8,128)(2,1)} %param.20) | copy-start | bytes 2752516
  35.5 18.1 %copy-start.1 = (bf16[1,3584,128]{2,1,0:T(8,128)(2,1)S(1)}, bf16[1,3584,128]{2,1,0:T(8,128)(2,1)}, u32[]{:S(2)}) copy-start(bf16[1,3584,128]{2,1,0:T(8,128)(2,1)} %param.21) | copy-start | bytes 2752516
  35.5 18.1 %copy-start.2 = (bf16[1,128,3584]{2,1,0:T(8,128)(2,1)S(1)}, bf16[1,128,3584]{2,1,0:T(8,128)(2,1)}, u32[]{:S(2)}) copy-start(bf16[1,128,3584]{2,1,0:T(8,128)(2,1)} %param.22) | copy-start | bytes 2752516
  35.5 18.1 %copy-start.4 = (bf16[3,8,3712]{2,1,0:T(8,128)(2,1)S(1)}, bf16[3,8,3712]{2,1,0:T(8,128)(2,1)}, u32[]{:S(2)}) copy-start(bf16[3,8,3712]{2,1,0:T(8,128)(2,1)} %shard_map.141.refs_0_) | copy-start | bytes 534532
  35.6 18.1 %collective-permute-start.7 = (bf16[3,8,3712]{2,1,0:T(8,128)(2,1)}, bf16[3,8,3712]{2,1,0:T(8,128)(2,1)}, u32[]{:S(2)}, u32[]{:S(2)}) collective-permute-start(bf16[3,8,3712]{2,1,0:T(8,128)(2,1)} %shard_map.141.refs_0_), channel_id=1, source_target_pairs={{2,0},{3,1},{4,2},{5,3},{6,4},{7,5},{0,6},{1,7},{10,8},{11,9},{12,... | collective-permute-start | bytes 534536 | tf_op jit(solution)/shard_map/ppermute | solution.py:284
  40.4 20.7 %copy-start.6 = (bf16[3,8,3712]{2,1,0:T(8,128)(2,1)S(1)}, bf16[3,8,3712]{2,1,0:T(8,128)(2,1)}, u32[]{:S(2)}) copy-start(bf16[3,8,3712]{2,1,0:T(8,128)(2,1)} %shard_map.140.refs_0_.refs_4_) | copy-start | bytes 534532
  40.4 17.7 %collective-permute-start.6 = (bf16[3,8,3712]{2,1,0:T(8,128)(2,1)}, bf16[3,8,3712]{2,1,0:T(8,128)(2,1)S(1)}, u32[]{:S(2)}, u32[]{:S(2)}) collective-permute-start(bf16[3,8,3712]{2,1,0:T(8,128)(2,1)} %shard_map.140.refs_0_.refs_4_), channel_id=1, source_target_pairs={{6,0},{7,1},{0,2},{1,3},{2,4},{3,5},{4,6},{5,7},{14,8},{15,9},{8,1... | collective-permute-start | bytes 534536 | tf_op jit(solution)/shard_map/ppermute | solution.py:284
  43.0 18.1 %collective-permute-start.5 = (bf16[3,8,3712]{2,1,0:T(8,128)(2,1)}, bf16[3,8,3712]{2,1,0:T(8,128)(2,1)S(1)}, u32[]{:S(2)}, u32[]{:S(2)}) collective-permute-start(bf16[3,8,3712]{2,1,0:T(8,128)(2,1)} %shard_map.140.refs_0_.refs_4_), channel_id=1, source_target_pairs={{4,0},{5,1},{6,2},{7,3},{0,4},{1,5},{2,6},{3,7},{12,8},{13,9},{14,... | collective-permute-start | bytes 534536 | tf_op jit(solution)/shard_map/ppermute | solution.py:284
  46.7 14.4 %collective-permute-start.4 = (bf16[3,8,3712]{2,1,0:T(8,128)(2,1)}, bf16[3,8,3712]{2,1,0:T(8,128)(2,1)S(1)}, u32[]{:S(2)}, u32[]{:S(2)}) collective-permute-start(bf16[3,8,3712]{2,1,0:T(8,128)(2,1)} %shard_map.140.refs_0_.refs_4_), channel_id=1, source_target_pairs={{2,0},{3,1},{4,2},{5,3},{6,4},{7,5},{0,6},{1,7},{10,8},{11,9},{12,... | collective-permute-start | bytes 534536 | tf_op jit(solution)/shard_map/ppermute | solution.py:284
  58.1 7.9 %copy-start.7 = (bf16[3,8,3712]{2,1,0:T(8,128)(2,1)}, bf16[3,8,3712]{2,1,0:T(8,128)(2,1)S(1)}, u32[]{:S(2)}) copy-start(bf16[3,8,3712]{2,1,0:T(8,128)(2,1)S(1)} %collective-permute-done.6.refs_3_.refs_7_) | copy-start | bytes 534532
  61.1 4.9 %copy-start.9 = (bf16[3,8,3712]{2,1,0:T(8,128)(2,1)}, bf16[3,8,3712]{2,1,0:T(8,128)(2,1)S(1)}, u32[]{:S(2)}) copy-start(bf16[3,8,3712]{2,1,0:T(8,128)(2,1)S(1)} %collective-permute-done.5.refs_2_.refs_6_) | copy-start | bytes 534532
  61.1 4.9 %copy-start.11 = (bf16[3,8,3712]{2,1,0:T(8,128)(2,1)}, bf16[3,8,3712]{2,1,0:T(8,128)(2,1)S(1)}, u32[]{:S(2)}) copy-start(bf16[3,8,3712]{2,1,0:T(8,128)(2,1)S(1)} %collective-permute-done.4.refs_1_.refs_5_) | copy-start | bytes 534532
  61.1 23.2 %copy-start.16 = (bf16[1,8,3584]{2,1,0:T(8,128)(2,1)S(1)}, bf16[1,8,3584]{2,1,0:T(8,128)(2,1)}, u32[]{:S(2)}) copy-start(bf16[1,8,3584]{2,1,0:T(8,128)(2,1)} %param.16) | copy-start | bytes 172036
  66.1 19.0 %copy-start.13 = (f32[32,512]{1,0:T(8,128)}, f32[32,512]{1,0:T(8,128)S(1)}, u32[]{:S(2)}) copy-start(f32[32,512]{1,0:T(8,128)S(1)} %get-tuple-element.38.refs_5_) | copy-start | bytes 196612
  66.1 18.3 %copy-start.15 = (bf16[8,3584]{1,0:T(8,128)(2,1)S(1)}, bf16[8,3584]{1,0:T(8,128)(2,1)}, u32[]{:S(2)}) copy-start(bf16[8,3584]{1,0:T(8,128)(2,1)} %slice_bitcast_fusion) | copy-start | bytes 172036
  66.1 17.0 %collective-permute-start.10 = (bf16[16,3584]{1,0:T(8,128)(2,1)S(1)}, bf16[16,3584]{1,0:T(8,128)(2,1)S(1)}, u32[]{:S(2)}, u32[]{:S(2)}) collective-permute-start(bf16[16,3584]{1,0:T(8,128)(2,1)S(1)} %get-tuple-element.29), channel_id=1, source_target_pairs={{6,0},{7,1},{0,2},{1,3},{2,4},{3,5},{4,6},{5,7},{14,8},{15,9},{8,1... | collective-permute-start | bytes 344072 | tf_op jit(solution)/shard_map/ppermute | solution.py:284
  72.3 10.7 %collective-permute-start.11 = (bf16[16,3584]{1,0:T(8,128)(2,1)S(1)}, bf16[16,3584]{1,0:T(8,128)(2,1)S(1)}, u32[]{:S(2)}, u32[]{:S(2)}) collective-permute-start(bf16[16,3584]{1,0:T(8,128)(2,1)S(1)} %get-tuple-element.30), channel_id=1, source_target_pairs={{4,0},{5,1},{6,2},{7,3},{0,4},{1,5},{2,6},{3,7},{12,8},{13,9},{14,... | collective-permute-start | bytes 344072 | tf_op jit(solution)/shard_map/ppermute | solution.py:284
  75.6 8.8 %collective-permute-start.12 = (bf16[16,3584]{1,0:T(8,128)(2,1)S(1)}, bf16[16,3584]{1,0:T(8,128)(2,1)S(1)}, u32[]{:S(2)}, u32[]{:S(2)}) collective-permute-start(bf16[16,3584]{1,0:T(8,128)(2,1)S(1)} %get-tuple-element.31), channel_id=1, source_target_pairs={{2,0},{3,1},{4,2},{5,3},{6,4},{7,5},{0,6},{1,7},{10,8},{11,9},{12,... | collective-permute-start | bytes 344072 | tf_op jit(solution)/shard_map/ppermute | solution.py:284
  78.5 9.4 %copy-start.8 = (bf16[3,8,3712]{2,1,0:T(8,128)(2,1)S(1)}, bf16[3,8,3712]{2,1,0:T(8,128)(2,1)}, u32[]{:S(2)}) copy-start(bf16[3,8,3712]{2,1,0:T(8,128)(2,1)} %copy-done.7) | copy-start | bytes 534532
  78.5 9.4 %copy-start.10 = (bf16[3,8,3712]{2,1,0:T(8,128)(2,1)S(1)}, bf16[3,8,3712]{2,1,0:T(8,128)(2,1)}, u32[]{:S(2)}) copy-start(bf16[3,8,3712]{2,1,0:T(8,128)(2,1)} %copy-done.9) | copy-start | bytes 534532
  78.6 9.4 %copy-start.12 = (bf16[3,8,3712]{2,1,0:T(8,128)(2,1)S(1)}, bf16[3,8,3712]{2,1,0:T(8,128)(2,1)}, u32[]{:S(2)}) copy-start(bf16[3,8,3712]{2,1,0:T(8,128)(2,1)} %copy-done.11) | copy-start | bytes 534532
  78.6 6.5 %collective-permute-start.13 = (bf16[128,128]{1,0:T(8,128)(2,1)S(1)}, bf16[128,128]{1,0:T(8,128)(2,1)S(1)}, u32[]{:S(2)}, u32[]{:S(2)}) collective-permute-start(bf16[128,128]{1,0:T(8,128)(2,1)S(1)} %pad_maximum_fusion.1), channel_id=1, source_target_pairs={{0,1},{1,0},{2,3},{3,2},{4,5},{5,4},{6,7},{7,6},{8,9},{9,8},{10,11... | collective-permute-start | bytes 98312 | tf_op jit(solution)/shard_map/ppermute | solution.py:275
  80.6 7.3 %collective-permute-start.15 = (bf16[32,3584]{1,0:T(8,128)(2,1)}, bf16[32,3584]{1,0:T(8,128)(2,1)}, u32[]{:S(2)}, u32[]{:S(2)}) collective-permute-start(bf16[32,3584]{1,0:T(8,128)(2,1)} %bitcast.12.refs_11_), channel_id=1, source_target_pairs={{0,1},{1,0},{2,3},{3,2},{4,5},{5,4},{6,7},{7,6},{8,9},{9,8},{10,11... | collective-permute-start | bytes 688136 | tf_op jit(solution)/shard_map/ppermute | solution.py:275
  85.1 20.1 %collective-permute-start.14 = (bf16[16,3584]{1,0:T(8,128)(2,1)}, bf16[16,3584]{1,0:T(8,128)(2,1)S(1)}, u32[]{:S(2)}, u32[]{:S(2)}) collective-permute-start(bf16[16,3584]{1,0:T(8,128)(2,1)} %add_convert_fusion), channel_id=1, source_target_pairs={{8,0},{16,8},{24,16},{32,24},{40,32},{48,40},{56,48},{64,56},{72,6... | collective-permute-start | bytes 344072 | tf_op jit(solution)/shard_map/ppermute | solution.py:336
  87.9 17.3 %copy-start.17 = (bf16[1,8,3584]{2,1,0:T(8,128)(2,1)S(1)}, bf16[1,8,3584]{2,1,0:T(8,128)(2,1)}, u32[]{:S(2)}) copy-start(bf16[1,8,3584]{2,1,0:T(8,128)(2,1)} %param.19) | copy-start | bytes 172036
  87.9 17.3 %copy-start.18 = (bf16[1,8,3584]{2,1,0:T(8,128)(2,1)S(1)}, bf16[1,8,3584]{2,1,0:T(8,128)(2,1)}, u32[]{:S(2)}) copy-start(bf16[1,8,3584]{2,1,0:T(8,128)(2,1)} %param.18) | copy-start | bytes 172036
  87.9 32.5 %copy-start.3 = (bf16[1,128,3584]{2,1,0:T(8,128)(2,1)S(1)}, bf16[1,128,3584]{2,1,0:T(8,128)(2,1)}, u32[]{:S(2)}) copy-start(bf16[1,128,3584]{2,1,0:T(8,128)(2,1)} %param.22) | copy-start | bytes 2752516
  105.2 15.2 %copy-start.14 = (f32[32,512]{1,0:T(8,128)S(1)}, f32[32,512]{1,0:T(8,128)}, u32[]{:S(2)}) copy-start(f32[32,512]{1,0:T(8,128)} %copy-done.13) | copy-start | bytes 196612
  105.2 9.6 %collective-permute-start.18 = (bf16[16,3712]{1,0:T(8,128)(2,1)S(1)}, bf16[16,3712]{1,0:T(8,128)(2,1)S(1)}, u32[]{:S(2)}, u32[]{:S(2)}) collective-permute-start(bf16[16,3712]{1,0:T(8,128)(2,1)S(1)} %pad_maximum_fusion.refs_0_.refs_10_), channel_id=1, source_target_pairs={{6,0},{7,1},{0,2},{1,3},{2,4},{3,5},{4,6},{5,7},{14,8},{15,9},{8,1... | collective-permute-start | bytes 356360 | tf_op jit(solution)/shard_map/ppermute | solution.py:284
  107.1 11.9 %collective-permute-start.17 = (bf16[16,3712]{1,0:T(8,128)(2,1)S(1)}, bf16[16,3712]{1,0:T(8,128)(2,1)S(1)}, u32[]{:S(2)}, u32[]{:S(2)}) collective-permute-start(bf16[16,3712]{1,0:T(8,128)(2,1)S(1)} %pad_maximum_fusion.refs_0_.refs_10_), channel_id=1, source_target_pairs={{4,0},{5,1},{6,2},{7,3},{0,4},{1,5},{2,6},{3,7},{12,8},{13,9},{14,... | collective-permute-start | bytes 356360 | tf_op jit(solution)/shard_map/ppermute | solution.py:284
  109.1 11.3 %collective-permute-start.16 = (bf16[16,3712]{1,0:T(8,128)(2,1)S(1)}, bf16[16,3712]{1,0:T(8,128)(2,1)S(1)}, u32[]{:S(2)}, u32[]{:S(2)}) collective-permute-start(bf16[16,3712]{1,0:T(8,128)(2,1)S(1)} %pad_maximum_fusion.refs_0_.refs_10_), channel_id=1, source_target_pairs={{2,0},{3,1},{4,2},{5,3},{6,4},{7,5},{0,6},{1,7},{10,8},{11,9},{12,... | collective-permute-start | bytes 356360 | tf_op jit(solution)/shard_map/ppermute | solution.py:284
  124.2 13.3 %collective-permute-start.19 = (bf16[16,3584]{1,0:T(8,128)(2,1)S(1)}, bf16[16,3584]{1,0:T(8,128)(2,1)S(1)}, u32[]{:S(2)}, u32[]{:S(2)}) collective-permute-start(bf16[16,3584]{1,0:T(8,128)(2,1)S(1)} %get-tuple-element.40), channel_id=1, source_target_pairs={{6,0},{7,1},{0,2},{1,3},{2,4},{3,5},{4,6},{5,7},{14,8},{15,9},{8,1... | collective-permute-start | bytes 344072 | tf_op jit(solution)/shard_map/ppermute | solution.py:284
  127.8 9.9 %collective-permute-start.20 = (bf16[16,3584]{1,0:T(8,128)(2,1)S(1)}, bf16[16,3584]{1,0:T(8,128)(2,1)S(1)}, u32[]{:S(2)}, u32[]{:S(2)}) collective-permute-start(bf16[16,3584]{1,0:T(8,128)(2,1)S(1)} %get-tuple-element.41), channel_id=1, source_target_pairs={{4,0},{5,1},{6,2},{7,3},{0,4},{1,5},{2,6},{3,7},{12,8},{13,9},{14,... | collective-permute-start | bytes 344072 | tf_op jit(solution)/shard_map/ppermute | solution.py:284
  130.0 8.9 %collective-permute-start.21 = (bf16[16,3584]{1,0:T(8,128)(2,1)S(1)}, bf16[16,3584]{1,0:T(8,128)(2,1)S(1)}, u32[]{:S(2)}, u32[]{:S(2)}) collective-permute-start(bf16[16,3584]{1,0:T(8,128)(2,1)S(1)} %get-tuple-element.42), channel_id=1, source_target_pairs={{2,0},{3,1},{4,2},{5,3},{6,4},{7,5},{0,6},{1,7},{10,8},{11,9},{12,... | collective-permute-start | bytes 344072 | tf_op jit(solution)/shard_map/ppermute | solution.py:284
  135.6 10.0 %collective-permute-start.23 = (f32[32,3584]{1,0:T(8,128)S(1)}, f32[32,3584]{1,0:T(8,128)S(1)}, u32[]{:S(2)}, u32[]{:S(2)}) collective-permute-start(f32[32,3584]{1,0:T(8,128)S(1)} %get-tuple-element.47), channel_id=1, source_target_pairs={{0,1},{1,0},{2,3},{3,2},{4,5},{5,4},{6,7},{7,6},{8,9},{9,8},{10,11... | collective-permute-start | bytes 1376264 | tf_op jit(solution)/shard_map/ppermute | solution.py:275
  139.6 14.4 %collective-permute-start.22 = (bf16[8,3584]{1,0:T(8,128)(2,1)S(1)}, bf16[8,3584]{1,0:T(8,128)(2,1)S(1)}, u32[]{:S(2)}, u32[]{:S(2)}) collective-permute-start(bf16[8,3584]{1,0:T(8,128)(2,1)S(1)} %get-tuple-element.49), channel_id=1, source_target_pairs={{0,504},{8,496},{16,488},{24,480},{32,472},{40,464},{48,456},{56,4... | collective-permute-start | bytes 172040 | tf_op jit(solution)/shard_map/ppermute | solution.py:280

commit v14 on v9

--- a/solution.py
+++ b/solution.py
@@ -332,7 +332,7 @@
     other_router = swapped(after(router, terms[0]))
     other_ids = swapped(jnp.concatenate([ids_a, ids_b], axis=0))
     grads = jnp.concatenate([arriving_a, block_b[1, :, :D]], axis=0)
-    out = after(emitted(grads, returned(terms)), other_ids)
+    out = emitted(grads, returned(terms))
     moved = lax.ppermute(out, "pipe", [(i, i - 1) for i in range(1, top + 1)])
     expo, share, stats = call(
         forward_kernel, [((2 * OWN, 256), F32), ((2 * OWN, 256), F32), ((16, IDCOLS), BF16)],

time: 155 us -> 155 us (level)
  waiting for transfers between devices: 37.6 us -> 39.4 us
    ppermute x1, waiting for transfers between devices: 12.3 us -> 8.95 us  [shards(): moved = lax.ppermute(out, 'pipe', [(i, i - 1) for i in range(1, top + 1)])]
    ppermute x2, starting transfers between devices: 21.4 us -> 19 us  [mirrored(): lax.ppermute(value, 'pipe', [(i, count - 1 - i) for i in range(count)])]
    ppermute x2, waiting for transfers between devices: 11.7 us -> 14.1 us  [mirrored(): lax.ppermute(value, 'pipe', [(i, count - 1 - i) for i in range(count)])]
    ppermute x15, starting transfers between devices: 53.5 us -> 55.7 us  [from_chip(): lax.ppermute(value, 'expert', [((e + 2 * k) % 8, e) for e in range(8)])]
  transfers between devices with their start and end apart: 24 -> 24, of which waited for: 9 -> 11; matrix products, arithmetic and copies ran while one was open for 2% -> 2% of each run, Pallas kernels for 7% -> 7%
where the time goes in v14:
time: 155 us; the launch traced here: 154 us
  starting transfers between devices  89.5 us (58%)
  waiting for transfers between devices  39.4 us (25%)
  Pallas kernels  20.6 us (13%)
  other arithmetic  2.26 us (1%)
    ppermute x15, starting transfers between devices, from_chip(): lax.ppermute(value, 'expert', [((e + 2 * k) % 8, e) for e in range(8)])  55.7 us
    ppermute x2, starting transfers between devices, mirrored(): lax.ppermute(value, 'pipe', [(i, count - 1 - i) for i in range(count)])  19 us
    pallas_call x5, Pallas kernels, call(): pl.pallas_call(body, out_shape=[jax.ShapeDtypeStruct(shape, dtype) for sh...  17.2 us
    ppermute x15, waiting for transfers between devices, from_chip(): lax.ppermute(value, 'expert', [((e + 2 * k) % 8, e) for e in range(8)])  15.2 us
    ppermute x2, waiting for transfers between devices, mirrored(): lax.ppermute(value, 'pipe', [(i, count - 1 - i) for i in range(count)])  14.1 us
    ppermute x6, starting transfers between devices, swapped(): return lax.ppermute(value, 'expert', [(e, e ^ 1) for e in range(8)])  12 us
    ppermute x1, waiting for transfers between devices, shards(): moved = lax.ppermute(out, 'pipe', [(i, i - 1) for i in range(1, top + 1)])  8.95 us
    pallas_call x2, Pallas kernels, payload(): pl.pallas_call(pack_kernel, out_shape=jax.ShapeDtypeStruct((3, ROWS, WIDE...  3.37 us
  transfers between devices with their start and end apart: 24, of which 11 were waited for; matrix products, arithmetic and copies ran while one was open for 2% of the time, Pallas kernels for 7%

profile of v14, /device:TPU:6, one launch (start us, length us, event | category | flops | bytes accessed | tf_op | source)
XLA Modules:
  0.0 154.3 jit_solution(6528573591152902744)
XLA Ops:
  0.6 1.7 %shard_map.139 = bf16[3,8,3712]{2,1,0:T(8,128)(2,1)} custom-call(bf16[2,8,3584]{2,1,0:T(8,128)(2,1)} %bitcast.33, bf16[8,3584]{1,0:T(8,128)(2,1)} %bitcast.36, s32[2,8,8]{2,1,0:T(8,128)} %bitcast.39), custom_call_target="tpu_custom_call" | custom-call | tf_op jit(solution)/shard_map/pallas_call | solution.py:73
  2.3 15.1 %collective-permute-start = (bf16[3,8,3712]{2,1,0:T(8,128)(2,1)}, bf16[3,8,3712]{2,1,0:T(8,128)(2,1)S(1)}, u32[]{:S(2)}, u32[]{:S(2)}) collective-permute-start(bf16[3,8,3712]{2,1,0:T(8,128)(2,1)} %shard_map.139), channel_id=1, source_target_pairs={{0,504},{8,496},{16,488},{24,480},{32,472},{40,464},{48,456},{56,4... | collective-permute-start | bytes 534536 | tf_op jit(solution)/shard_map/ppermute | solution.py:280
  17.4 1.9 %collective-permute-start.1 = (bf16[3584,128]{1,0:T(8,128)(2,1)}, bf16[3584,128]{1,0:T(8,128)(2,1)}, u32[]{:S(2)}, u32[]{:S(2)}) collective-permute-start(bf16[3584,128]{1,0:T(8,128)(2,1)} %bitcast.18), channel_id=1, source_target_pairs={{0,1},{1,0},{2,3},{3,2},{4,5},{5,4},{6,7},{7,6},{8,9},{9,8},{10,11... | collective-permute-start | bytes 2752520 | tf_op jit(solution)/shard_map/ppermute | solution.py:275
  19.4 2.4 %collective-permute-start.2 = (bf16[3584,128]{1,0:T(8,128)(2,1)}, bf16[3584,128]{1,0:T(8,128)(2,1)}, u32[]{:S(2)}, u32[]{:S(2)}) collective-permute-start(bf16[3584,128]{1,0:T(8,128)(2,1)} %bitcast.22), channel_id=1, source_target_pairs={{0,1},{1,0},{2,3},{3,2},{4,5},{5,4},{6,7},{7,6},{8,9},{9,8},{10,11... | collective-permute-start | bytes 2752520 | tf_op jit(solution)/shard_map/ppermute | solution.py:275
  21.8 1.9 %collective-permute-start.3 = (bf16[128,3584]{1,0:T(8,128)(2,1)}, bf16[128,3584]{1,0:T(8,128)(2,1)}, u32[]{:S(2)}, u32[]{:S(2)}) collective-permute-start(bf16[128,3584]{1,0:T(8,128)(2,1)} %bitcast.26), channel_id=1, source_target_pairs={{0,1},{1,0},{2,3},{3,2},{4,5},{5,4},{6,7},{7,6},{8,9},{9,8},{10,11... | collective-permute-start | bytes 2752520 | tf_op jit(solution)/shard_map/ppermute | solution.py:275
  23.7 1.7 %shard_map.141.refs_0_ = bf16[3,8,3712]{2,1,0:T(8,128)(2,1)} custom-call(bf16[2,8,3584]{2,1,0:T(8,128)(2,1)} %bitcast.34, bf16[8,3584]{1,0:T(8,128)(2,1)} %bitcast.31, s32[2,8,8]{2,1,0:T(8,128)} %bitcast.40), custom_call_target="tpu_custom_call" | custom-call | tf_op jit(solution)/shard_map/pallas_call | solution.py:73
  25.4 2.9 %collective-permute-start.9 = (bf16[3,8,3712]{2,1,0:T(8,128)(2,1)}, bf16[3,8,3712]{2,1,0:T(8,128)(2,1)S(1)}, u32[]{:S(2)}, u32[]{:S(2)}) collective-permute-start(bf16[3,8,3712]{2,1,0:T(8,128)(2,1)} %shard_map.141.refs_0_), channel_id=1, source_target_pairs={{6,0},{7,1},{0,2},{1,3},{2,4},{3,5},{4,6},{5,7},{14,8},{15,9},{8,1... | collective-permute-start | bytes 534536 | tf_op jit(solution)/shard_map/ppermute | solution.py:284
  28.3 4.6 %collective-permute-done.value = bf16[3,8,3712]{2,1,0:T(8,128)(2,1)S(1)} collective-permute-done((bf16[3,8,3712]{2,1,0:T(8,128)(2,1)}, bf16[3,8,3712]{2,1,0:T(8,128)(2,1)S(1)}, u32[]{:S(2)}, u32[]{:S(2)}) %collective-permute-start) | collective-permute-done | bytes 178208 | tf_op jit(solution)/shard_map/ppermute | solution.py:280
  33.0 1.9 %collective-permute-start.8 = (bf16[3,8,3712]{2,1,0:T(8,128)(2,1)}, bf16[3,8,3712]{2,1,0:T(8,128)(2,1)S(1)}, u32[]{:S(2)}, u32[]{:S(2)}) collective-permute-start(bf16[3,8,3712]{2,1,0:T(8,128)(2,1)} %shard_map.141.refs_0_), channel_id=1, source_target_pairs={{4,0},{5,1},{6,2},{7,3},{0,4},{1,5},{2,6},{3,7},{12,8},{13,9},{14,... | collective-permute-start | bytes 534536 | tf_op jit(solution)/shard_map/ppermute | solution.py:284
  34.9 0.6 slice_bitcast_fusion
  35.6 4.8 %collective-permute-start.7 = (bf16[3,8,3712]{2,1,0:T(8,128)(2,1)}, bf16[3,8,3712]{2,1,0:T(8,128)(2,1)}, u32[]{:S(2)}, u32[]{:S(2)}) collective-permute-start(bf16[3,8,3712]{2,1,0:T(8,128)(2,1)} %shard_map.141.refs_0_), channel_id=1, source_target_pairs={{2,0},{3,1},{4,2},{5,3},{6,4},{7,5},{0,6},{1,7},{10,8},{11,9},{12,... | collective-permute-start | bytes 534536 | tf_op jit(solution)/shard_map/ppermute | solution.py:284
  40.4 2.6 %collective-permute-start.6 = (bf16[3,8,3712]{2,1,0:T(8,128)(2,1)}, bf16[3,8,3712]{2,1,0:T(8,128)(2,1)S(1)}, u32[]{:S(2)}, u32[]{:S(2)}) collective-permute-start(bf16[3,8,3712]{2,1,0:T(8,128)(2,1)} %shard_map.140.refs_0_.refs_4_), channel_id=1, source_target_pairs={{6,0},{7,1},{0,2},{1,3},{2,4},{3,5},{4,6},{5,7},{14,8},{15,9},{8,1... | collective-permute-start | bytes 534536 | tf_op jit(solution)/shard_map/ppermute | solution.py:284
  43.0 3.6 %collective-permute-start.5 = (bf16[3,8,3712]{2,1,0:T(8,128)(2,1)}, bf16[3,8,3712]{2,1,0:T(8,128)(2,1)S(1)}, u32[]{:S(2)}, u32[]{:S(2)}) collective-permute-start(bf16[3,8,3712]{2,1,0:T(8,128)(2,1)} %shard_map.140.refs_0_.refs_4_), channel_id=1, source_target_pairs={{4,0},{5,1},{6,2},{7,3},{0,4},{1,5},{2,6},{3,7},{12,8},{13,9},{14,... | collective-permute-start | bytes 534536 | tf_op jit(solution)/shard_map/ppermute | solution.py:284
  46.7 4.6 %collective-permute-start.4 = (bf16[3,8,3712]{2,1,0:T(8,128)(2,1)}, bf16[3,8,3712]{2,1,0:T(8,128)(2,1)S(1)}, u32[]{:S(2)}, u32[]{:S(2)}) collective-permute-start(bf16[3,8,3712]{2,1,0:T(8,128)(2,1)} %shard_map.140.refs_0_.refs_4_), channel_id=1, source_target_pairs={{2,0},{3,1},{4,2},{5,3},{6,4},{7,5},{0,6},{1,7},{10,8},{11,9},{12,... | collective-permute-start | bytes 534536 | tf_op jit(solution)/shard_map/ppermute | solution.py:284
  51.3 2.3 %collective-permute-done.7.refs_1_ = bf16[3,8,3712]{2,1,0:T(8,128)(2,1)} collective-permute-done((bf16[3,8,3712]{2,1,0:T(8,128)(2,1)}, bf16[3,8,3712]{2,1,0:T(8,128)(2,1)}, u32[]{:S(2)}, u32[]{:S(2)}) %collective-permute-start.7) | collective-permute-done | bytes 178208 | tf_op jit(solution)/shard_map/ppermute | solution.py:284
  53.6 4.5 %shard_map.142 = (f32[32,3584]{1,0:T(8,128)S(1)}, f32[32,512]{1,0:T(8,128)S(1)}, bf16[64,128]{1,0:T(8,128)(2,1)S(1)}) custom-call(bf16[3,8,3712]{2,1,0:T(8,128)(2,1)S(1)} %copy-done.4, bf16[3,8,3712]{2,1,0:T(8,128)(2,1)} %collective-permute-done.7.refs_1_, bf16[3,8,3712]{2,1,0:T(8,128)(2,1)S(1)} %collective-permute-done.8.refs_2_, ...), custom_call_target="tpu_custom_call" | custom-call | flops 704643072 | bytes 6217728 | tf_op jit(solution)/shard_map/pallas_call | solution.py:37
  58.1 0.0 collective-permute-done.6.refs_3_.refs_7_
  58.2 3.0 %collective-permute-done.5.refs_2_.refs_6_ = bf16[3,8,3712]{2,1,0:T(8,128)(2,1)S(1)} collective-permute-done((bf16[3,8,3712]{2,1,0:T(8,128)(2,1)}, bf16[3,8,3712]{2,1,0:T(8,128)(2,1)S(1)}, u32[]{:S(2)}, u32[]{:S(2)}) %collective-permute-start.5) | collective-permute-done | bytes 178208 | tf_op jit(solution)/shard_map/ppermute | solution.py:284
  61.2 4.9 %shard_map.143 = (f32[16,3584]{1,0:T(8,128)S(1)}, bf16[16,3584]{1,0:T(8,128)(2,1)S(1)}, bf16[16,3584]{1,0:T(8,128)(2,1)S(1)}, bf16[16,3584]{1,0:T(8,128)(2,1)S(1...) custom-call(bf16[3,8,3712]{2,1,0:T(8,128)(2,1)S(1)} %copy-done.6, ...), custom_call_target="tpu_custom_call" | custom-call | flops 704643072 | bytes 6676480 | tf_op jit(solution)/shard_map/pallas_call | solution.py:37
  66.1 6.9 %collective-permute-start.10 = (bf16[16,3584]{1,0:T(8,128)(2,1)S(1)}, bf16[16,3584]{1,0:T(8,128)(2,1)S(1)}, u32[]{:S(2)}, u32[]{:S(2)}) collective-permute-start(bf16[16,3584]{1,0:T(8,128)(2,1)S(1)} %get-tuple-element.28), channel_id=1, source_target_pairs={{2,0},{3,1},{4,2},{5,3},{6,4},{7,5},{0,6},{1,7},{10,8},{11,9},{12,... | collective-permute-start | bytes 344072 | tf_op jit(solution)/shard_map/ppermute | solution.py:284
  73.0 2.6 %collective-permute-start.11 = (bf16[16,3584]{1,0:T(8,128)(2,1)S(1)}, bf16[16,3584]{1,0:T(8,128)(2,1)S(1)}, u32[]{:S(2)}, u32[]{:S(2)}) collective-permute-start(bf16[16,3584]{1,0:T(8,128)(2,1)S(1)} %get-tuple-element.29), channel_id=1, source_target_pairs={{4,0},{5,1},{6,2},{7,3},{0,4},{1,5},{2,6},{3,7},{12,8},{13,9},{14,... | collective-permute-start | bytes 344072 | tf_op jit(solution)/shard_map/ppermute | solution.py:284
  75.6 1.9 %collective-permute-start.12 = (bf16[16,3584]{1,0:T(8,128)(2,1)S(1)}, bf16[16,3584]{1,0:T(8,128)(2,1)S(1)}, u32[]{:S(2)}, u32[]{:S(2)}) collective-permute-start(bf16[16,3584]{1,0:T(8,128)(2,1)S(1)} %get-tuple-element.30), channel_id=1, source_target_pairs={{6,0},{7,1},{0,2},{1,3},{2,4},{3,5},{4,6},{5,7},{14,8},{15,9},{8,1... | collective-permute-start | bytes 344072 | tf_op jit(solution)/shard_map/ppermute | solution.py:284
  77.5 1.9 %collective-permute-start.15 = (bf16[32,3584]{1,0:T(8,128)(2,1)}, bf16[32,3584]{1,0:T(8,128)(2,1)}, u32[]{:S(2)}, u32[]{:S(2)}) collective-permute-start(bf16[32,3584]{1,0:T(8,128)(2,1)} %bitcast.12.refs_11_), channel_id=1, source_target_pairs={{0,1},{1,0},{2,3},{3,2},{4,5},{5,4},{6,7},{7,6},{8,9},{9,8},{10,11... | collective-permute-start | bytes 688136 | tf_op jit(solution)/shard_map/ppermute | solution.py:275
  79.5 5.0 %collective-permute-done.11 = bf16[16,3584]{1,0:T(8,128)(2,1)S(1)} collective-permute-done((bf16[16,3584]{1,0:T(8,128)(2,1)S(1)}, bf16[16,3584]{1,0:T(8,128)(2,1)S(1)}, u32[]{:S(2)}, u32[]{:S(2)}) %collective-permute-start.11) | collective-permute-done | bytes 114720 | tf_op jit(solution)/shard_map/ppermute | solution.py:284
  84.5 0.7 add_convert_fusion
  85.2 2.8 %collective-permute-start.13 = (bf16[16,3584]{1,0:T(8,128)(2,1)}, bf16[16,3584]{1,0:T(8,128)(2,1)S(1)}, u32[]{:S(2)}, u32[]{:S(2)}) collective-permute-start(bf16[16,3584]{1,0:T(8,128)(2,1)} %add_convert_fusion), channel_id=1, source_target_pairs={{8,0},{16,8},{24,16},{32,24},{40,32},{48,40},{56,48},{64,56},{72,6... | collective-permute-start | bytes 344072 | tf_op jit(solution)/shard_map/ppermute | solution.py:336
  88.0 1.9 %collective-permute-start.14 = (bf16[128,128]{1,0:T(8,128)(2,1)S(1)}, bf16[128,128]{1,0:T(8,128)(2,1)S(1)}, u32[]{:S(2)}, u32[]{:S(2)}) collective-permute-start(bf16[128,128]{1,0:T(8,128)(2,1)S(1)} %pad_maximum_fusion.1), channel_id=1, source_target_pairs={{0,1},{1,0},{2,3},{3,2},{4,5},{5,4},{6,7},{7,6},{8,9},{9,8},{10,11... | collective-permute-start | bytes 98312 | tf_op jit(solution)/shard_map/ppermute | solution.py:275
  90.0 1.1 collective-permute-done.14.refs_10_
  91.1 2.5 %shard_map.144 = (f32[64,256]{1,0:T(8,128)S(1)}, f32[64,256]{1,0:T(8,128)S(1)}, bf16[16,128]{1,0:T(8,128)(2,1)S(1)}) custom-call(bf16[3,8,3712]{2,1,0:T(8,128)(2,1)S(1)} %copy-done.4, bf16[3,8,3712]{2,1,0:T(8,128)(2,1)} %collective-permute-done.7.refs_1_, bf16[3,8,3712]{2,1,0:T(8,128)(2,1)S(1)} %collective-permute-done.8.refs_2_, ...), custom_call_target="tpu_custom_call" | custom-call | flops 117440512 | bytes 1949696 | tf_op jit(solution)/shard_map/pallas_call | solution.py:37
  93.6 8.9 %collective-permute-done.13 = bf16[16,3584]{1,0:T(8,128)(2,1)S(1)} collective-permute-done((bf16[16,3584]{1,0:T(8,128)(2,1)}, bf16[16,3584]{1,0:T(8,128)(2,1)S(1)}, u32[]{:S(2)}, u32[]{:S(2)}) %collective-permute-start.13) | collective-permute-done | bytes 114720 | tf_op jit(solution)/shard_map/ppermute | solution.py:336
  102.6 1.9 %collective-permute-start.18 = (bf16[16,3712]{1,0:T(8,128)(2,1)S(1)}, bf16[16,3712]{1,0:T(8,128)(2,1)S(1)}, u32[]{:S(2)}, u32[]{:S(2)}) collective-permute-start(bf16[16,3712]{1,0:T(8,128)(2,1)S(1)} %pad_maximum_fusion.refs_0_.refs_10_), channel_id=1, source_target_pairs={{6,0},{7,1},{0,2},{1,3},{2,4},{3,5},{4,6},{5,7},{14,8},{15,9},{8,1... | collective-permute-start | bytes 356360 | tf_op jit(solution)/shard_map/ppermute | solution.py:284
  104.5 6.4 %collective-permute-start.17 = (bf16[16,3712]{1,0:T(8,128)(2,1)S(1)}, bf16[16,3712]{1,0:T(8,128)(2,1)S(1)}, u32[]{:S(2)}, u32[]{:S(2)}) collective-permute-start(bf16[16,3712]{1,0:T(8,128)(2,1)S(1)} %pad_maximum_fusion.refs_0_.refs_10_), channel_id=1, source_target_pairs={{4,0},{5,1},{6,2},{7,3},{0,4},{1,5},{2,6},{3,7},{12,8},{13,9},{14,... | collective-permute-start | bytes 356360 | tf_op jit(solution)/shard_map/ppermute | solution.py:284
  110.9 4.8 %collective-permute-start.16 = (bf16[16,3712]{1,0:T(8,128)(2,1)S(1)}, bf16[16,3712]{1,0:T(8,128)(2,1)S(1)}, u32[]{:S(2)}, u32[]{:S(2)}) collective-permute-start(bf16[16,3712]{1,0:T(8,128)(2,1)S(1)} %pad_maximum_fusion.refs_0_.refs_10_), channel_id=1, source_target_pairs={{2,0},{3,1},{4,2},{5,3},{6,4},{7,5},{0,6},{1,7},{10,8},{11,9},{12,... | collective-permute-start | bytes 356360 | tf_op jit(solution)/shard_map/ppermute | solution.py:284
  115.7 0.5 collective-permute-done.17.refs_2_.refs_12_
  116.2 1.9 %collective-permute-done.16.refs_1_.refs_11_ = bf16[16,3712]{1,0:T(8,128)(2,1)S(1)} collective-permute-done((bf16[16,3712]{1,0:T(8,128)(2,1)S(1)}, bf16[16,3712]{1,0:T(8,128)(2,1)S(1)}, u32[]{:S(2)}, u32[]{:S(2)}) %collective-permute-start.16) | collective-permute-done | bytes 118816 | tf_op jit(solution)/shard_map/ppermute | solution.py:284
  118.1 3.9 %shard_map.145 = (f32[16,3584]{1,0:T(8,128)S(1)}, bf16[16,3584]{1,0:T(8,128)(2,1)S(1)}, bf16[16,3584]{1,0:T(8,128)(2,1)S(1)}, bf16[16,3584]{1,0:T(8,128)(2,1)S(1)}) custom-call(bf16[16,3712]{1,0:T(8,128)(2,1)S(1)} %pad_maximum_fusion.refs_0_.refs_10_, bf16[16,3712]{1,0:T(8,128)(2,1)S(1)} %collective-permute-done.16.refs_1_.refs_11_, ...), custom_call_target="tpu_custom_call" | custom-call | flops 352321536 | bytes 6111232 | tf_op jit(solution)/shard_map/pallas_call | solution.py:37
  122.0 6.4 %collective-permute-start.19 = (bf16[16,3584]{1,0:T(8,128)(2,1)S(1)}, bf16[16,3584]{1,0:T(8,128)(2,1)S(1)}, u32[]{:S(2)}, u32[]{:S(2)}) collective-permute-start(bf16[16,3584]{1,0:T(8,128)(2,1)S(1)} %get-tuple-element.38), channel_id=1, source_target_pairs={{2,0},{3,1},{4,2},{5,3},{6,4},{7,5},{0,6},{1,7},{10,8},{11,9},{12,... | collective-permute-start | bytes 344072 | tf_op jit(solution)/shard_map/ppermute | solution.py:284
  128.3 1.9 %collective-permute-start.20 = (bf16[16,3584]{1,0:T(8,128)(2,1)S(1)}, bf16[16,3584]{1,0:T(8,128)(2,1)S(1)}, u32[]{:S(2)}, u32[]{:S(2)}) collective-permute-start(bf16[16,3584]{1,0:T(8,128)(2,1)S(1)} %get-tuple-element.39), channel_id=1, source_target_pairs={{4,0},{5,1},{6,2},{7,3},{0,4},{1,5},{2,6},{3,7},{12,8},{13,9},{14,... | collective-permute-start | bytes 344072 | tf_op jit(solution)/shard_map/ppermute | solution.py:284
  130.3 2.5 %collective-permute-start.21 = (bf16[16,3584]{1,0:T(8,128)(2,1)S(1)}, bf16[16,3584]{1,0:T(8,128)(2,1)S(1)}, u32[]{:S(2)}, u32[]{:S(2)}) collective-permute-start(bf16[16,3584]{1,0:T(8,128)(2,1)S(1)} %get-tuple-element.40), channel_id=1, source_target_pairs={{6,0},{7,1},{0,2},{1,3},{2,4},{3,5},{4,6},{5,7},{14,8},{15,9},{8,1... | collective-permute-start | bytes 344072 | tf_op jit(solution)/shard_map/ppermute | solution.py:284
  132.8 1.5 %shard_map.146 = (f32[32,3584]{1,0:T(8,128)S(1)}, f32[32,3584]{1,0:T(8,128)S(1)}) custom-call(bf16[3,8,3712]{2,1,0:T(8,128)(2,1)S(1)} %copy-done.4, bf16[3,8,3712]{2,1,0:T(8,128)(2,1)} %collective-permute-done.7.refs_1_, bf16[3,8,3712]{2,1,0:T(8,128)(2,1)S(1)} %collective-permute-done.8.refs_2_, bf16[3,8,3712]{2,1,0:T(8,128)(2,1)S(1)} %collective-permute-done.9.refs_3_, ...), custom_call_target="tpu_custom_call" | custom-call | flops 88080384 | bytes 2031616 | tf_op jit(solution)/shard_map/pallas_call | solution.py:37
  134.3 1.9 %collective-permute-start.23 = (f32[32,3584]{1,0:T(8,128)S(1)}, f32[32,3584]{1,0:T(8,128)S(1)}, u32[]{:S(2)}, u32[]{:S(2)}) collective-permute-start(f32[32,3584]{1,0:T(8,128)S(1)} %get-tuple-element.45), channel_id=1, source_target_pairs={{0,1},{1,0},{2,3},{3,2},{4,5},{5,4},{6,7},{7,6},{8,9},{9,8},{10,11... | collective-permute-start | bytes 1376264 | tf_op jit(solution)/shard_map/ppermute | solution.py:275
  136.2 0.9 collective-permute-done.20
  137.2 1.6 %collective-permute-done.21 = bf16[16,3584]{1,0:T(8,128)(2,1)S(1)} collective-permute-done((bf16[16,3584]{1,0:T(8,128)(2,1)S(1)}, bf16[16,3584]{1,0:T(8,128)(2,1)S(1)}, u32[]{:S(2)}, u32[]{:S(2)}) %collective-permute-start.21) | collective-permute-done | bytes 114720 | tf_op jit(solution)/shard_map/ppermute | solution.py:284
  138.8 0.7 add_convert_fusion.1
  139.5 3.9 %collective-permute-start.22 = (bf16[8,3584]{1,0:T(8,128)(2,1)S(1)}, bf16[8,3584]{1,0:T(8,128)(2,1)S(1)}, u32[]{:S(2)}, u32[]{:S(2)}) collective-permute-start(bf16[8,3584]{1,0:T(8,128)(2,1)S(1)} %get-tuple-element.47), channel_id=1, source_target_pairs={{0,504},{8,496},{16,488},{24,480},{32,472},{40,464},{48,456},{56,4... | collective-permute-start | bytes 172040 | tf_op jit(solution)/shard_map/ppermute | solution.py:280
  143.4 0.8 add.51
  144.2 9.5 %collective-permute-done.22 = bf16[8,3584]{1,0:T(8,128)(2,1)S(1)} collective-permute-done((bf16[8,3584]{1,0:T(8,128)(2,1)S(1)}, bf16[8,3584]{1,0:T(8,128)(2,1)S(1)}, u32[]{:S(2)}, u32[]{:S(2)}) %collective-permute-start.22) | collective-permute-done | bytes 57376 | tf_op jit(solution)/shard_map/ppermute | solution.py:280
  153.6 0.6 copy.18
  (54 shorter events, 0.2 us)
Async XLA Ops:
  2.3 30.7 %collective-permute-start = (bf16[3,8,3712]{2,1,0:T(8,128)(2,1)}, bf16[3,8,3712]{2,1,0:T(8,128)(2,1)S(1)}, u32[]{:S(2)}, u32[]{:S(2)}) collective-permute-start(bf16[3,8,3712]{2,1,0:T(8,128)(2,1)} %shard_map.139), channel_id=1, source_target_pairs={{0,504},{8,496},{16,488},{24,480},{32,472},{40,464},{48,456},{56,4... | collective-permute-start | bytes 534536 | tf_op jit(solution)/shard_map/ppermute | solution.py:280
  17.4 18.1 %collective-permute-start.1 = (bf16[3584,128]{1,0:T(8,128)(2,1)}, bf16[3584,128]{1,0:T(8,128)(2,1)}, u32[]{:S(2)}, u32[]{:S(2)}) collective-permute-start(bf16[3584,128]{1,0:T(8,128)(2,1)} %bitcast.18), channel_id=1, source_target_pairs={{0,1},{1,0},{2,3},{3,2},{4,5},{5,4},{6,7},{7,6},{8,9},{9,8},{10,11... | collective-permute-start | bytes 2752520 | tf_op jit(solution)/shard_map/ppermute | solution.py:275
  19.4 21.0 %collective-permute-start.2 = (bf16[3584,128]{1,0:T(8,128)(2,1)}, bf16[3584,128]{1,0:T(8,128)(2,1)}, u32[]{:S(2)}, u32[]{:S(2)}) collective-permute-start(bf16[3584,128]{1,0:T(8,128)(2,1)} %bitcast.22), channel_id=1, source_target_pairs={{0,1},{1,0},{2,3},{3,2},{4,5},{5,4},{6,7},{7,6},{8,9},{9,8},{10,11... | collective-permute-start | bytes 2752520 | tf_op jit(solution)/shard_map/ppermute | solution.py:275
  21.8 18.6 %collective-permute-start.3 = (bf16[128,3584]{1,0:T(8,128)(2,1)}, bf16[128,3584]{1,0:T(8,128)(2,1)}, u32[]{:S(2)}, u32[]{:S(2)}) collective-permute-start(bf16[128,3584]{1,0:T(8,128)(2,1)} %bitcast.26), channel_id=1, source_target_pairs={{0,1},{1,0},{2,3},{3,2},{4,5},{5,4},{6,7},{7,6},{8,9},{9,8},{10,11... | collective-permute-start | bytes 2752520 | tf_op jit(solution)/shard_map/ppermute | solution.py:275
  25.4 21.3 %collective-permute-start.9 = (bf16[3,8,3712]{2,1,0:T(8,128)(2,1)}, bf16[3,8,3712]{2,1,0:T(8,128)(2,1)S(1)}, u32[]{:S(2)}, u32[]{:S(2)}) collective-permute-start(bf16[3,8,3712]{2,1,0:T(8,128)(2,1)} %shard_map.141.refs_0_), channel_id=1, source_target_pairs={{6,0},{7,1},{0,2},{1,3},{2,4},{3,5},{4,6},{5,7},{14,8},{15,9},{8,1... | collective-permute-start | bytes 534536 | tf_op jit(solution)/shard_map/ppermute | solution.py:284
  33.0 7.4 %copy-start.5 = (bf16[3,8,3712]{2,1,0:T(8,128)(2,1)}, bf16[3,8,3712]{2,1,0:T(8,128)(2,1)S(1)}, u32[]{:S(2)}) copy-start(bf16[3,8,3712]{2,1,0:T(8,128)(2,1)S(1)} %collective-permute-done.value) | copy-start | bytes 534532
  33.0 18.3 %collective-permute-start.8 = (bf16[3,8,3712]{2,1,0:T(8,128)(2,1)}, bf16[3,8,3712]{2,1,0:T(8,128)(2,1)S(1)}, u32[]{:S(2)}, u32[]{:S(2)}) collective-permute-start(bf16[3,8,3712]{2,1,0:T(8,128)(2,1)} %shard_map.141.refs_0_), channel_id=1, source_target_pairs={{4,0},{5,1},{6,2},{7,3},{0,4},{1,5},{2,6},{3,7},{12,8},{13,9},{14,... | collective-permute-start | bytes 534536 | tf_op jit(solution)/shard_map/ppermute | solution.py:284
  35.5 18.1 %copy-start = (bf16[1,3584,128]{2,1,0:T(8,128)(2,1)S(1)}, bf16[1,3584,128]{2,1,0:T(8,128)(2,1)}, u32[]{:S(2)}) copy-start(bf16[1,3584,128]{2,1,0:T(8,128)(2,1)} %param.20) | copy-start | bytes 2752516
  35.5 18.1 %copy-start.1 = (bf16[1,3584,128]{2,1,0:T(8,128)(2,1)S(1)}, bf16[1,3584,128]{2,1,0:T(8,128)(2,1)}, u32[]{:S(2)}) copy-start(bf16[1,3584,128]{2,1,0:T(8,128)(2,1)} %param.21) | copy-start | bytes 2752516
  35.5 18.1 %copy-start.2 = (bf16[1,128,3584]{2,1,0:T(8,128)(2,1)S(1)}, bf16[1,128,3584]{2,1,0:T(8,128)(2,1)}, u32[]{:S(2)}) copy-start(bf16[1,128,3584]{2,1,0:T(8,128)(2,1)} %param.22) | copy-start | bytes 2752516
  35.5 18.1 %copy-start.4 = (bf16[3,8,3712]{2,1,0:T(8,128)(2,1)S(1)}, bf16[3,8,3712]{2,1,0:T(8,128)(2,1)}, u32[]{:S(2)}) copy-start(bf16[3,8,3712]{2,1,0:T(8,128)(2,1)} %shard_map.141.refs_0_) | copy-start | bytes 534532
  35.6 18.1 %collective-permute-start.7 = (bf16[3,8,3712]{2,1,0:T(8,128)(2,1)}, bf16[3,8,3712]{2,1,0:T(8,128)(2,1)}, u32[]{:S(2)}, u32[]{:S(2)}) collective-permute-start(bf16[3,8,3712]{2,1,0:T(8,128)(2,1)} %shard_map.141.refs_0_), channel_id=1, source_target_pairs={{2,0},{3,1},{4,2},{5,3},{6,4},{7,5},{0,6},{1,7},{10,8},{11,9},{12,... | collective-permute-start | bytes 534536 | tf_op jit(solution)/shard_map/ppermute | solution.py:284
  40.4 20.7 %copy-start.6 = (bf16[3,8,3712]{2,1,0:T(8,128)(2,1)S(1)}, bf16[3,8,3712]{2,1,0:T(8,128)(2,1)}, u32[]{:S(2)}) copy-start(bf16[3,8,3712]{2,1,0:T(8,128)(2,1)} %shard_map.140.refs_0_.refs_4_) | copy-start | bytes 534532
  40.4 17.7 %collective-permute-start.6 = (bf16[3,8,3712]{2,1,0:T(8,128)(2,1)}, bf16[3,8,3712]{2,1,0:T(8,128)(2,1)S(1)}, u32[]{:S(2)}, u32[]{:S(2)}) collective-permute-start(bf16[3,8,3712]{2,1,0:T(8,128)(2,1)} %shard_map.140.refs_0_.refs_4_), channel_id=1, source_target_pairs={{6,0},{7,1},{0,2},{1,3},{2,4},{3,5},{4,6},{5,7},{14,8},{15,9},{8,1... | collective-permute-start | bytes 534536 | tf_op jit(solution)/shard_map/ppermute | solution.py:284
  43.0 18.1 %collective-permute-start.5 = (bf16[3,8,3712]{2,1,0:T(8,128)(2,1)}, bf16[3,8,3712]{2,1,0:T(8,128)(2,1)S(1)}, u32[]{:S(2)}, u32[]{:S(2)}) collective-permute-start(bf16[3,8,3712]{2,1,0:T(8,128)(2,1)} %shard_map.140.refs_0_.refs_4_), channel_id=1, source_target_pairs={{4,0},{5,1},{6,2},{7,3},{0,4},{1,5},{2,6},{3,7},{12,8},{13,9},{14,... | collective-permute-start | bytes 534536 | tf_op jit(solution)/shard_map/ppermute | solution.py:284
  46.7 14.4 %collective-permute-start.4 = (bf16[3,8,3712]{2,1,0:T(8,128)(2,1)}, bf16[3,8,3712]{2,1,0:T(8,128)(2,1)S(1)}, u32[]{:S(2)}, u32[]{:S(2)}) collective-permute-start(bf16[3,8,3712]{2,1,0:T(8,128)(2,1)} %shard_map.140.refs_0_.refs_4_), channel_id=1, source_target_pairs={{2,0},{3,1},{4,2},{5,3},{6,4},{7,5},{0,6},{1,7},{10,8},{11,9},{12,... | collective-permute-start | bytes 534536 | tf_op jit(solution)/shard_map/ppermute | solution.py:284
  58.1 7.9 %copy-start.7 = (bf16[3,8,3712]{2,1,0:T(8,128)(2,1)}, bf16[3,8,3712]{2,1,0:T(8,128)(2,1)S(1)}, u32[]{:S(2)}) copy-start(bf16[3,8,3712]{2,1,0:T(8,128)(2,1)S(1)} %collective-permute-done.6.refs_3_.refs_7_) | copy-start | bytes 534532
  61.1 5.0 %copy-start.9 = (bf16[3,8,3712]{2,1,0:T(8,128)(2,1)}, bf16[3,8,3712]{2,1,0:T(8,128)(2,1)S(1)}, u32[]{:S(2)}) copy-start(bf16[3,8,3712]{2,1,0:T(8,128)(2,1)S(1)} %collective-permute-done.5.refs_2_.refs_6_) | copy-start | bytes 534532
  61.1 5.0 %copy-start.11 = (bf16[3,8,3712]{2,1,0:T(8,128)(2,1)}, bf16[3,8,3712]{2,1,0:T(8,128)(2,1)S(1)}, u32[]{:S(2)}) copy-start(bf16[3,8,3712]{2,1,0:T(8,128)(2,1)S(1)} %collective-permute-done.4.refs_1_.refs_5_) | copy-start | bytes 534532
  61.1 23.3 %copy-start.15 = (bf16[8,3584]{1,0:T(8,128)(2,1)S(1)}, bf16[8,3584]{1,0:T(8,128)(2,1)}, u32[]{:S(2)}) copy-start(bf16[8,3584]{1,0:T(8,128)(2,1)} %slice_bitcast_fusion) | copy-start | bytes 172036
  61.1 23.3 %copy-start.16 = (bf16[1,8,3584]{2,1,0:T(8,128)(2,1)S(1)}, bf16[1,8,3584]{2,1,0:T(8,128)(2,1)}, u32[]{:S(2)}) copy-start(bf16[1,8,3584]{2,1,0:T(8,128)(2,1)} %param.16) | copy-start | bytes 172036
  66.1 19.1 %copy-start.13 = (f32[32,512]{1,0:T(8,128)}, f32[32,512]{1,0:T(8,128)S(1)}, u32[]{:S(2)}) copy-start(f32[32,512]{1,0:T(8,128)S(1)} %get-tuple-element.36.refs_5_) | copy-start | bytes 196612
  66.1 13.4 %collective-permute-start.10 = (bf16[16,3584]{1,0:T(8,128)(2,1)S(1)}, bf16[16,3584]{1,0:T(8,128)(2,1)S(1)}, u32[]{:S(2)}, u32[]{:S(2)}) collective-permute-start(bf16[16,3584]{1,0:T(8,128)(2,1)S(1)} %get-tuple-element.28), channel_id=1, source_target_pairs={{2,0},{3,1},{4,2},{5,3},{6,4},{7,5},{0,6},{1,7},{10,8},{11,9},{12,... | collective-permute-start | bytes 344072 | tf_op jit(solution)/shard_map/ppermute | solution.py:284
  73.0 11.5 %collective-permute-start.11 = (bf16[16,3584]{1,0:T(8,128)(2,1)S(1)}, bf16[16,3584]{1,0:T(8,128)(2,1)S(1)}, u32[]{:S(2)}, u32[]{:S(2)}) collective-permute-start(bf16[16,3584]{1,0:T(8,128)(2,1)S(1)} %get-tuple-element.29), channel_id=1, source_target_pairs={{4,0},{5,1},{6,2},{7,3},{0,4},{1,5},{2,6},{3,7},{12,8},{13,9},{14,... | collective-permute-start | bytes 344072 | tf_op jit(solution)/shard_map/ppermute | solution.py:284
  75.6 8.8 %collective-permute-start.12 = (bf16[16,3584]{1,0:T(8,128)(2,1)S(1)}, bf16[16,3584]{1,0:T(8,128)(2,1)S(1)}, u32[]{:S(2)}, u32[]{:S(2)}) collective-permute-start(bf16[16,3584]{1,0:T(8,128)(2,1)S(1)} %get-tuple-element.30), channel_id=1, source_target_pairs={{6,0},{7,1},{0,2},{1,3},{2,4},{3,5},{4,6},{5,7},{14,8},{15,9},{8,1... | collective-permute-start | bytes 344072 | tf_op jit(solution)/shard_map/ppermute | solution.py:284
  77.5 13.6 %collective-permute-start.15 = (bf16[32,3584]{1,0:T(8,128)(2,1)}, bf16[32,3584]{1,0:T(8,128)(2,1)}, u32[]{:S(2)}, u32[]{:S(2)}) collective-permute-start(bf16[32,3584]{1,0:T(8,128)(2,1)} %bitcast.12.refs_11_), channel_id=1, source_target_pairs={{0,1},{1,0},{2,3},{3,2},{4,5},{5,4},{6,7},{7,6},{8,9},{9,8},{10,11... | collective-permute-start | bytes 688136 | tf_op jit(solution)/shard_map/ppermute | solution.py:275
  84.5 6.7 %copy-start.8 = (bf16[3,8,3712]{2,1,0:T(8,128)(2,1)S(1)}, bf16[3,8,3712]{2,1,0:T(8,128)(2,1)}, u32[]{:S(2)}) copy-start(bf16[3,8,3712]{2,1,0:T(8,128)(2,1)} %copy-done.7) | copy-start | bytes 534532
  84.5 6.6 %copy-start.10 = (bf16[3,8,3712]{2,1,0:T(8,128)(2,1)S(1)}, bf16[3,8,3712]{2,1,0:T(8,128)(2,1)}, u32[]{:S(2)}) copy-start(bf16[3,8,3712]{2,1,0:T(8,128)(2,1)} %copy-done.9) | copy-start | bytes 534532
  84.5 6.6 %copy-start.12 = (bf16[3,8,3712]{2,1,0:T(8,128)(2,1)S(1)}, bf16[3,8,3712]{2,1,0:T(8,128)(2,1)}, u32[]{:S(2)}) copy-start(bf16[3,8,3712]{2,1,0:T(8,128)(2,1)} %copy-done.11) | copy-start | bytes 534532
  85.2 17.3 %collective-permute-start.13 = (bf16[16,3584]{1,0:T(8,128)(2,1)}, bf16[16,3584]{1,0:T(8,128)(2,1)S(1)}, u32[]{:S(2)}, u32[]{:S(2)}) collective-permute-start(bf16[16,3584]{1,0:T(8,128)(2,1)} %add_convert_fusion), channel_id=1, source_target_pairs={{8,0},{16,8},{24,16},{32,24},{40,32},{48,40},{56,48},{64,56},{72,6... | collective-permute-start | bytes 344072 | tf_op jit(solution)/shard_map/ppermute | solution.py:336
  88.0 3.1 %collective-permute-start.14 = (bf16[128,128]{1,0:T(8,128)(2,1)S(1)}, bf16[128,128]{1,0:T(8,128)(2,1)S(1)}, u32[]{:S(2)}, u32[]{:S(2)}) collective-permute-start(bf16[128,128]{1,0:T(8,128)(2,1)S(1)} %pad_maximum_fusion.1), channel_id=1, source_target_pairs={{0,1},{1,0},{2,3},{3,2},{4,5},{5,4},{6,7},{7,6},{8,9},{9,8},{10,11... | collective-permute-start | bytes 98312 | tf_op jit(solution)/shard_map/ppermute | solution.py:275
  89.9 12.6 %copy-start.17 = (bf16[1,8,3584]{2,1,0:T(8,128)(2,1)S(1)}, bf16[1,8,3584]{2,1,0:T(8,128)(2,1)}, u32[]{:S(2)}) copy-start(bf16[1,8,3584]{2,1,0:T(8,128)(2,1)} %param.19) | copy-start | bytes 172036
  89.9 12.6 %copy-start.18 = (bf16[1,8,3584]{2,1,0:T(8,128)(2,1)S(1)}, bf16[1,8,3584]{2,1,0:T(8,128)(2,1)}, u32[]{:S(2)}) copy-start(bf16[1,8,3584]{2,1,0:T(8,128)(2,1)} %param.18) | copy-start | bytes 172036
  90.0 28.2 %copy-start.3 = (bf16[1,128,3584]{2,1,0:T(8,128)(2,1)S(1)}, bf16[1,128,3584]{2,1,0:T(8,128)(2,1)}, u32[]{:S(2)}) copy-start(bf16[1,128,3584]{2,1,0:T(8,128)(2,1)} %param.22) | copy-start | bytes 2752516
  102.6 15.5 %copy-start.14 = (f32[32,512]{1,0:T(8,128)S(1)}, f32[32,512]{1,0:T(8,128)}, u32[]{:S(2)}) copy-start(f32[32,512]{1,0:T(8,128)} %copy-done.13) | copy-start | bytes 196612
  102.6 13.1 %collective-permute-start.18 = (bf16[16,3712]{1,0:T(8,128)(2,1)S(1)}, bf16[16,3712]{1,0:T(8,128)(2,1)S(1)}, u32[]{:S(2)}, u32[]{:S(2)}) collective-permute-start(bf16[16,3712]{1,0:T(8,128)(2,1)S(1)} %pad_maximum_fusion.refs_0_.refs_10_), channel_id=1, source_target_pairs={{6,0},{7,1},{0,2},{1,3},{2,4},{3,5},{4,6},{5,7},{14,8},{15,9},{8,1... | collective-permute-start | bytes 356360 | tf_op jit(solution)/shard_map/ppermute | solution.py:284
  104.5 11.7 %collective-permute-start.17 = (bf16[16,3712]{1,0:T(8,128)(2,1)S(1)}, bf16[16,3712]{1,0:T(8,128)(2,1)S(1)}, u32[]{:S(2)}, u32[]{:S(2)}) collective-permute-start(bf16[16,3712]{1,0:T(8,128)(2,1)S(1)} %pad_maximum_fusion.refs_0_.refs_10_), channel_id=1, source_target_pairs={{4,0},{5,1},{6,2},{7,3},{0,4},{1,5},{2,6},{3,7},{12,8},{13,9},{14,... | collective-permute-start | bytes 356360 | tf_op jit(solution)/shard_map/ppermute | solution.py:284
  110.9 7.2 %collective-permute-start.16 = (bf16[16,3712]{1,0:T(8,128)(2,1)S(1)}, bf16[16,3712]{1,0:T(8,128)(2,1)S(1)}, u32[]{:S(2)}, u32[]{:S(2)}) collective-permute-start(bf16[16,3712]{1,0:T(8,128)(2,1)S(1)} %pad_maximum_fusion.refs_0_.refs_10_), channel_id=1, source_target_pairs={{2,0},{3,1},{4,2},{5,3},{6,4},{7,5},{0,6},{1,7},{10,8},{11,9},{12,... | collective-permute-start | bytes 356360 | tf_op jit(solution)/shard_map/ppermute | solution.py:284
  122.0 14.3 %collective-permute-start.19 = (bf16[16,3584]{1,0:T(8,128)(2,1)S(1)}, bf16[16,3584]{1,0:T(8,128)(2,1)S(1)}, u32[]{:S(2)}, u32[]{:S(2)}) collective-permute-start(bf16[16,3584]{1,0:T(8,128)(2,1)S(1)} %get-tuple-element.38), channel_id=1, source_target_pairs={{2,0},{3,1},{4,2},{5,3},{6,4},{7,5},{0,6},{1,7},{10,8},{11,9},{12,... | collective-permute-start | bytes 344072 | tf_op jit(solution)/shard_map/ppermute | solution.py:284
  128.3 8.8 %collective-permute-start.20 = (bf16[16,3584]{1,0:T(8,128)(2,1)S(1)}, bf16[16,3584]{1,0:T(8,128)(2,1)S(1)}, u32[]{:S(2)}, u32[]{:S(2)}) collective-permute-start(bf16[16,3584]{1,0:T(8,128)(2,1)S(1)} %get-tuple-element.39), channel_id=1, source_target_pairs={{4,0},{5,1},{6,2},{7,3},{0,4},{1,5},{2,6},{3,7},{12,8},{13,9},{14,... | collective-permute-start | bytes 344072 | tf_op jit(solution)/shard_map/ppermute | solution.py:284
  130.3 8.5 %collective-permute-start.21 = (bf16[16,3584]{1,0:T(8,128)(2,1)S(1)}, bf16[16,3584]{1,0:T(8,128)(2,1)S(1)}, u32[]{:S(2)}, u32[]{:S(2)}) collective-permute-start(bf16[16,3584]{1,0:T(8,128)(2,1)S(1)} %get-tuple-element.40), channel_id=1, source_target_pairs={{6,0},{7,1},{0,2},{1,3},{2,4},{3,5},{4,6},{5,7},{14,8},{15,9},{8,1... | collective-permute-start | bytes 344072 | tf_op jit(solution)/shard_map/ppermute | solution.py:284
  134.3 9.0 %collective-permute-start.23 = (f32[32,3584]{1,0:T(8,128)S(1)}, f32[32,3584]{1,0:T(8,128)S(1)}, u32[]{:S(2)}, u32[]{:S(2)}) collective-permute-start(f32[32,3584]{1,0:T(8,128)S(1)} %get-tuple-element.45), channel_id=1, source_target_pairs={{0,1},{1,0},{2,3},{3,2},{4,5},{5,4},{6,7},{7,6},{8,9},{9,8},{10,11... | collective-permute-start | bytes 1376264 | tf_op jit(solution)/shard_map/ppermute | solution.py:275
  139.5 14.2 %collective-permute-start.22 = (bf16[8,3584]{1,0:T(8,128)(2,1)S(1)}, bf16[8,3584]{1,0:T(8,128)(2,1)S(1)}, u32[]{:S(2)}, u32[]{:S(2)}) collective-permute-start(bf16[8,3584]{1,0:T(8,128)(2,1)S(1)} %get-tuple-element.47), channel_id=1, source_target_pairs={{0,504},{8,496},{16,488},{24,480},{32,472},{40,464},{48,456},{56,4... | collective-permute-start | bytes 172040 | tf_op jit(solution)/shard_map/ppermute | solution.py:280
